TPU v7x, 32 devices: a whole 2x2x4 slice. The times are simulated.
32 devices in a mesh: dp: 4 (over y, core), ctx: 2 (over x), tensor: 4 (over z).
Axes of the slice: x: 2, y: 2, z: 4, core: 2. Of those that a mesh axis runs over, the one named last changes fastest.
Arguments:
- tokens: bfloat16 [4, 1024, 2048], P('dp', ('ctx', 'tensor')), may hold values from -6 to 6
- cotangent: bfloat16 [4, 1024, 2048], P('dp', ('ctx', 'tensor')), may hold values from -6 to 6
- norm_gains: float32 [2, 2, 2048], replicated, may hold values from 0.5 to 1.5
- norm_biases: float32 [2, 2, 2048], replicated, may hold values from -1.8 to 1.8
- qkv_weight: bfloat16 [2, 2048, 3, 2048], P(None, 'dp', None, 'tensor'), may hold values from -0.125 to 0.125
- qkv_bias: float32 [2, 3, 2048], replicated, may hold values from -3 to 3
- out_weight: bfloat16 [2, 2048, 2048], P(None, 'tensor', 'dp'), may hold values from -0.75 to 0.75
- gate_up_weight: bfloat16 [2, 2048, 2, 5632], P(None, 'dp', None, 'tensor'), may hold values from -0.125 to 0.125
- down_weight: bfloat16 [2, 5632, 2048], P(None, 'tensor', 'dp'), may hold values from -0.078125 to 0.078125
Outputs:
- out: bfloat16 [4, 1024, 2048], P('dp', ('ctx', 'tensor'))
- tokens_grad: bfloat16 [4, 1024, 2048], P('dp', ('ctx', 'tensor'))
- norm_gains_grad: float32 [2, 2, 2048], replicated
- norm_biases_grad: float32 [2, 2, 2048], replicated
- qkv_weight_grad: float32 [2, 2048, 3, 2048], P(None, 'dp', None, 'tensor')
- qkv_bias_grad: float32 [2, 3, 2048], replicated
- out_weight_grad: float32 [2, 2048, 2048], P(None, 'tensor', 'dp')
- gate_up_weight_grad: float32 [2, 2048, 2, 5632], P(None, 'dp', None, 'tensor')
- down_weight_grad: float32 [2, 5632, 2048], P(None, 'tensor', 'dp')
All inputs are finite; a program needn't handle non-finite values.
Results may differ from a plain program's by a relative error of at most 0.03.
Values may be sent and summed in bfloat16 or wider, within the bound.
No kernel may reach another device: no remote copies, remote signals or barrier semaphores. Data moves between devices by JAX's collectives and lax.ppermute only.
A program may use at most 384 MiB of HBM per device.

v0:
```python
import jax
import jax.numpy as jnp
from jax import lax
from jax.sharding import PartitionSpec as P

HD = 64
ROT = 16
LAYERS = 2


MASKED = -1e30
EPSILON = 1e-05


def shifted(block, axis, distance):
    devices = range(lax.axis_size(axis))
    route = [((i - distance) % len(devices), i) for i in devices]
    return lax.ppermute(block, axis, route)


def shifted_2(value, axis, steps):
    count = lax.axis_size(axis)
    first, last = (max(0, -steps), min(count, count - steps))
    return lax.ppermute(value, axis, [(source, source + steps) for source in range(first, last)])


def gather_rows(values_low):
    return lax.all_gather(values_low, "tensor", axis=1, tiled=True)


def sum_rows(partial_value):
    return lax.psum_scatter(
        partial_value.astype(jnp.bfloat16), "tensor", scatter_dimension=1, tiled=True
    ).astype(jnp.float32)


def gather_layer(qkv_weight, out_weight, gate_up_weight, down_weight, layer_index):
    return (
        lax.all_gather(qkv_weight[layer_index], "dp", axis=0, tiled=True),
        lax.all_gather(out_weight[layer_index], "dp", axis=1, tiled=True),
        lax.all_gather(gate_up_weight[layer_index], "dp", axis=0, tiled=True),
        lax.all_gather(down_weight[layer_index], "dp", axis=1, tiled=True),
    )


def layer_norm_rows(stream, gain, bias):
    row_mean = jnp.mean(stream, axis=-1, keepdims=True)
    centered = stream - row_mean
    inverse = lax.rsqrt(jnp.mean(centered * centered, axis=-1, keepdims=True) + EPSILON)
    unit_rows = centered * inverse
    return (unit_rows * gain + bias, unit_rows, inverse)


def norm_backward(grad_rows, unit_rows, inverse, gain):
    grad_unit = grad_rows * gain
    first_mean = jnp.mean(grad_unit, axis=-1, keepdims=True)
    second_mean = jnp.mean(grad_unit * unit_rows, axis=-1, keepdims=True)
    grad_input = inverse * (grad_unit - first_mean - unit_rows * second_mean)
    return (
        grad_input,
        jnp.sum(grad_rows * unit_rows, axis=(0, 1)),
        jnp.sum(grad_rows, axis=(0, 1)),
    )


def rotary_tables(positions):
    half_rot = ROT // 2
    frequency = 10000.0 ** (-(jnp.arange(half_rot, dtype=jnp.float32) * 2.0) / ROT)
    angles = positions.astype(jnp.float32)[:, None] * frequency[None, :]
    return (jnp.cos(angles)[:, None, :], jnp.sin(angles)[:, None, :])


def rotate(heads4, cosine_table, sine_table, direction):
    half_rot = ROT // 2
    front_part = heads4[..., :half_rot]
    back_part = heads4[..., half_rot:ROT]
    new_front = front_part * cosine_table - direction * back_part * sine_table
    new_back = back_part * cosine_table + direction * front_part * sine_table
    return jnp.concatenate([new_front, new_back, heads4[..., ROT:]], axis=-1)


def attend_block(running, kv_block, key_start, queries4, query_positions):
    accumulated, row_max, row_total = running
    heads_local = queries4.shape[2]
    shape4 = (kv_block.shape[0], kv_block.shape[1], heads_local, HD)
    key_heads = kv_block[:, :, 0].reshape(shape4)
    value_heads = kv_block[:, :, 1].reshape(shape4)
    scores = jnp.einsum(
        "sqhd,skhd->shqk", queries4, key_heads, preferred_element_type=jnp.float32
    ) * HD ** (-0.5)
    key_positions = key_start + jnp.arange(kv_block.shape[1], dtype=jnp.int32)
    allowed = key_positions[None, :] <= query_positions[:, None]
    scores = jnp.where(allowed, scores, MASKED)
    new_max = jnp.maximum(row_max, jnp.max(scores, axis=-1))
    weights = jnp.where(allowed, jnp.exp(scores - new_max[..., None]), 0.0)
    factor = jnp.exp(row_max - new_max)
    row_total = row_total * factor + jnp.sum(weights, axis=-1)
    accumulated = accumulated * factor[..., None] + jnp.einsum(
        "shqk,skhd->shqd",
        weights.astype(jnp.bfloat16),
        value_heads,
        preferred_element_type=jnp.float32,
    )
    return (accumulated, new_max, row_total)


def fold_keys(running, kv_piece, queries4, query_positions, block_rows):
    block_count = kv_piece.shape[1] // block_rows
    seq_count = kv_piece.shape[0]
    blocks = jnp.moveaxis(
        kv_piece.reshape(seq_count, block_count, block_rows, 2, kv_piece.shape[3]), 1, 0
    )

    def one_block(carried, inputs):
        block_index, kv_block = inputs
        return (
            attend_block(carried, kv_block, block_index * block_rows, queries4, query_positions),
            None,
        )

    running, unused = lax.scan(
        one_block, running, (jnp.arange(block_count, dtype=jnp.int32), blocks)
    )
    return running


def shards(
    tokens,
    cotangent,
    norm_gains,
    norm_biases,
    qkv_weight,
    qkv_bias,
    out_weight,
    gate_up_weight,
    down_weight,
):
    n_ctx = lax.axis_size("ctx")
    n_tensor = lax.axis_size("tensor")
    ctx_index = lax.axis_index("ctx")
    tensor_index = lax.axis_index("tensor")
    seq_count = tokens.shape[0]
    block_rows = tokens.shape[1] * n_tensor
    local_width = qkv_weight.shape[3]
    heads_local = local_width // HD
    score_scale = HD ** (-0.5)
    query_positions = ctx_index * block_rows + jnp.arange(block_rows, dtype=jnp.int32)
    cosine_table, sine_table = rotary_tables(query_positions)
    shape4 = (seq_count, block_rows, heads_local, HD)
    stream = tokens.astype(jnp.float32)
    saved = []
    for layer_index in range(LAYERS):
        weights = gather_layer(qkv_weight, out_weight, gate_up_weight, down_weight, layer_index)
        qkv_full, out_full, gate_up_full, down_full = weights
        layer_gains = norm_gains[layer_index]
        layer_biases = norm_biases[layer_index]
        normed_one, unit_one, inverse_one = layer_norm_rows(stream, layer_gains[0], layer_biases[0])
        normed_rows = gather_rows(normed_one.astype(jnp.bfloat16))
        bias_local = lax.dynamic_slice_in_dim(
            qkv_bias[layer_index], tensor_index * local_width, local_width, 1
        )
        biased = (
            jnp.einsum("std,dce->stce", normed_rows, qkv_full, preferred_element_type=jnp.float32)
            + bias_local
        )
        queries4 = rotate(biased[:, :, 0].reshape(shape4), cosine_table, sine_table, 1.0).astype(
            jnp.bfloat16
        )
        keys4 = rotate(biased[:, :, 1].reshape(shape4), cosine_table, sine_table, 1.0).astype(
            jnp.bfloat16
        )
        kv_home = jnp.stack(
            [
                keys4.reshape(seq_count, block_rows, local_width),
                biased[:, :, 2].astype(jnp.bfloat16),
            ],
            axis=2,
        )
        start_state = (
            jnp.zeros((seq_count, heads_local, block_rows, HD), jnp.float32),
            jnp.full((seq_count, heads_local, block_rows), MASKED, jnp.float32),
            jnp.zeros((seq_count, heads_local, block_rows), jnp.float32),
        )
        accumulated, row_max, row_total = fold_keys(
            start_state,
            lax.all_gather(kv_home, "ctx", axis=1, tiled=True),
            queries4,
            query_positions,
            block_rows,
        )
        log_total = row_max + jnp.log(row_total)
        attended4 = jnp.transpose(accumulated / row_total[..., None], (0, 2, 1, 3))
        attended_low = attended4.reshape(seq_count, block_rows, local_width).astype(jnp.bfloat16)
        stream_mid = stream + sum_rows(
            jnp.einsum("stk,kd->std", attended_low, out_full, preferred_element_type=jnp.float32)
        )
        normed_two, unit_two, inverse_two = layer_norm_rows(
            stream_mid, layer_gains[1], layer_biases[1]
        )
        normed_rows_two = gather_rows(normed_two.astype(jnp.bfloat16))
        gate_up = jnp.einsum(
            "std,dcf->stcf", normed_rows_two, gate_up_full, preferred_element_type=jnp.float32
        )
        activated = (jax.nn.silu(gate_up[:, :, 0]) * gate_up[:, :, 1]).astype(jnp.bfloat16)
        stream = stream_mid + sum_rows(
            jnp.einsum("stf,fd->std", activated, down_full, preferred_element_type=jnp.float32)
        )
        kept_weights = None
        saved.append(
            (
                kept_weights,
                normed_rows,
                unit_one,
                inverse_one,
                queries4,
                kv_home,
                log_total,
                attended4,
                attended_low,
                unit_two,
                inverse_two,
                normed_rows_two,
                gate_up,
                activated,
            )
        )
    output = stream.astype(jnp.bfloat16)
    grad_stream = cotangent.astype(jnp.float32)
    qkv_grads = [None] * LAYERS
    out_grads = [None] * LAYERS
    gate_up_grads = [None] * LAYERS
    down_grads = [None] * LAYERS
    gain_grads = [None] * LAYERS
    bias_grads = [None] * LAYERS
    qkv_bias_grads = [None] * LAYERS
    for layer_index in range(LAYERS - 1, -1, -1):
        (
            kept_weights,
            normed_rows,
            unit_one,
            inverse_one,
            queries4,
            kv_home,
            log_total,
            attended4,
            attended_low,
            unit_two,
            inverse_two,
            normed_rows_two,
            gate_up,
            activated,
        ) = saved[layer_index]
        weights = gather_layer(qkv_weight, out_weight, gate_up_weight, down_weight, layer_index)
        qkv_full, out_full, gate_up_full, down_full = weights
        layer_gains = norm_gains[layer_index]
        grad_branch = gather_rows(grad_stream.astype(jnp.bfloat16))
        down_grad = jnp.einsum(
            "stf,std->fd", activated, grad_branch, preferred_element_type=jnp.float32
        )
        grad_activated = jnp.einsum(
            "std,fd->stf", grad_branch, down_full, preferred_element_type=jnp.float32
        )
        gate_part = gate_up[:, :, 0]
        up_part = gate_up[:, :, 1]
        sigmoid_gate = jax.nn.sigmoid(gate_part)
        grad_gate = (
            grad_activated * up_part * sigmoid_gate * (1.0 + gate_part * (1.0 - sigmoid_gate))
        )
        grad_up = grad_activated * jax.nn.silu(gate_part)
        grad_gate_up = jnp.stack([grad_gate, grad_up], axis=2).astype(jnp.bfloat16)
        gate_up_grad = jnp.einsum(
            "std,stcf->dcf", normed_rows_two, grad_gate_up, preferred_element_type=jnp.float32
        )
        grad_normed_two = sum_rows(
            jnp.einsum(
                "stcf,dcf->std", grad_gate_up, gate_up_full, preferred_element_type=jnp.float32
            )
        )
        grad_mid, gain_two, bias_two = norm_backward(
            grad_normed_two, unit_two, inverse_two, layer_gains[1]
        )
        grad_hidden = grad_stream + grad_mid
        grad_attention = gather_rows(grad_hidden.astype(jnp.bfloat16))
        out_grad = jnp.einsum(
            "stk,std->kd", attended_low, grad_attention, preferred_element_type=jnp.float32
        )
        grad_attended = jnp.einsum(
            "std,kd->stk", grad_attention, out_full, preferred_element_type=jnp.float32
        ).astype(jnp.bfloat16)
        grad_attended4 = grad_attended.reshape(shape4)
        delta = jnp.swapaxes(jnp.sum(grad_attended4.astype(jnp.float32) * attended4, axis=-1), 1, 2)

        def visit_turn(turn, carried):
            visiting, visiting_grads, query_grads = carried
            source = (ctx_index - turn) % n_ctx
            key_positions = source * block_rows + jnp.arange(block_rows, dtype=jnp.int32)
            allowed = key_positions[None, :] <= query_positions[:, None]
            key_heads = visiting[:, :, 0].reshape(shape4)
            value_heads = visiting[:, :, 1].reshape(shape4)
            scores = (
                jnp.einsum(
                    "sqhd,skhd->shqk", queries4, key_heads, preferred_element_type=jnp.float32
                )
                * score_scale
            )
            scores = jnp.where(allowed, scores, MASKED)
            probabilities = jnp.where(allowed, jnp.exp(scores - log_total[..., None]), 0.0)
            grad_probs = jnp.einsum(
                "sqhd,skhd->shqk", grad_attended4, value_heads, preferred_element_type=jnp.float32
            )
            grad_scores = (probabilities * (grad_probs - delta[..., None])).astype(jnp.bfloat16)
            query_grads = (
                query_grads
                + jnp.einsum(
                    "shqk,skhd->sqhd", grad_scores, key_heads, preferred_element_type=jnp.float32
                )
                * score_scale
            )
            key_grad = (
                jnp.einsum(
                    "shqk,sqhd->skhd", grad_scores, queries4, preferred_element_type=jnp.float32
                )
                * score_scale
            )
            value_grad = jnp.einsum(
                "shqk,sqhd->skhd",
                probabilities.astype(jnp.bfloat16),
                grad_attended4,
                preferred_element_type=jnp.float32,
            )
            update = jnp.stack(
                [
                    key_grad.reshape(seq_count, block_rows, local_width),
                    value_grad.reshape(seq_count, block_rows, local_width),
                ],
                axis=2,
            )
            visiting_grads = shifted(
                (visiting_grads + update).astype(jnp.bfloat16), "ctx", 1
            ).astype(jnp.float32)
            visiting = shifted_2(visiting, "ctx", 1)
            return (visiting, visiting_grads, query_grads)

        start_turns = (
            kv_home,
            jnp.zeros(kv_home.shape, jnp.float32),
            jnp.zeros(shape4, jnp.float32),
        )
        returned_kv, kv_grads, query_grads = lax.fori_loop(0, n_ctx, visit_turn, start_turns)
        grad_queries = rotate(query_grads, cosine_table, sine_table, -1.0).reshape(
            seq_count, block_rows, local_width
        )
        grad_keys = rotate(
            kv_grads[:, :, 0].reshape(shape4), cosine_table, sine_table, -1.0
        ).reshape(seq_count, block_rows, local_width)
        grad_biased = jnp.stack([grad_queries, grad_keys, kv_grads[:, :, 1]], axis=2)
        bias_grad_local = jnp.sum(grad_biased, axis=(0, 1))
        qkv_bias_grads[layer_index] = lax.dynamic_update_slice_in_dim(
            jnp.zeros((3, local_width * n_tensor), jnp.float32),
            bias_grad_local,
            tensor_index * local_width,
            1,
        )
        grad_projected = grad_biased.astype(jnp.bfloat16)
        qkv_grad = jnp.einsum(
            "std,stce->dce", normed_rows, grad_projected, preferred_element_type=jnp.float32
        )
        grad_normed_one = sum_rows(
            jnp.einsum(
                "stce,dce->std", grad_projected, qkv_full, preferred_element_type=jnp.float32
            )
        )
        grad_first, gain_one, bias_one = norm_backward(
            grad_normed_one, unit_one, inverse_one, layer_gains[0]
        )
        grad_stream = grad_hidden + grad_first
        gain_grads[layer_index] = jnp.stack([gain_one, gain_two])
        bias_grads[layer_index] = jnp.stack([bias_one, bias_two])
        owned = (
            lax.psum_scatter(
                qkv_grad.astype(jnp.bfloat16), "dp", scatter_dimension=0, tiled=True
            ).astype(jnp.float32),
            lax.psum_scatter(
                out_grad.astype(jnp.bfloat16), "dp", scatter_dimension=1, tiled=True
            ).astype(jnp.float32),
            lax.psum_scatter(
                gate_up_grad.astype(jnp.bfloat16), "dp", scatter_dimension=0, tiled=True
            ).astype(jnp.float32),
            lax.psum_scatter(
                down_grad.astype(jnp.bfloat16), "dp", scatter_dimension=1, tiled=True
            ).astype(jnp.float32),
        )
        owned = (
            lax.psum(owned[0].astype(jnp.bfloat16), "ctx").astype(jnp.float32),
            lax.psum(owned[1].astype(jnp.bfloat16), "ctx").astype(jnp.float32),
            lax.psum(owned[2].astype(jnp.bfloat16), "ctx").astype(jnp.float32),
            lax.psum(owned[3].astype(jnp.bfloat16), "ctx").astype(jnp.float32),
        )
        qkv_grads[layer_index] = owned[0]
        out_grads[layer_index] = owned[1]
        gate_up_grads[layer_index] = owned[2]
        down_grads[layer_index] = owned[3]
    small_sums = lax.psum(
        (jnp.stack(gain_grads), jnp.stack(bias_grads), jnp.stack(qkv_bias_grads)),
        ("dp", "ctx", "tensor"),
    )
    return (
        output,
        grad_stream.astype(jnp.bfloat16),
        small_sums[0],
        small_sums[1],
        jnp.stack(qkv_grads),
        small_sums[2],
        jnp.stack(out_grads),
        jnp.stack(gate_up_grads),
        jnp.stack(down_grads),
    )


def solution(mesh):
    return jax.shard_map(
        shards,
        mesh=mesh,
        in_specs=(
            P("dp", ("ctx", "tensor"), None),
            P("dp", ("ctx", "tensor"), None),
            P(),
            P(),
            P(None, "dp", None, "tensor"),
            P(),
            P(None, "tensor", "dp"),
            P(None, "dp", None, "tensor"),
            P(None, "tensor", "dp"),
        ),
        out_specs=(
            P("dp", ("ctx", "tensor"), None),
            P("dp", ("ctx", "tensor"), None),
            P(),
            P(),
            P(None, "dp", None, "tensor"),
            P(),
            P(None, "tensor", "dp"),
            P(None, "dp", None, "tensor"),
            P(None, "tensor", "dp"),
        ),
        check_vma=False,
    )
```

profile of v0, /device:TPU:0, one launch (start us, length us, event | category | flops | bytes accessed | tf_op | source)
XLA Modules:
  0.0 2390.5 jit_solution(2767286276386181525)
XLA Ops:
  20.8 42.9 %all-gather.27.cloned.1.call-done = bf16[1,512,2048]{2,1,0:T(8,128)(2,1)} async-done(((bf16[1,128,2048]{2,1,0:T(8,128)(2,1)}), bf16[1,512,2048]{2,1,0:T(8,128)(2,1)}) %all-gather.27.cloned.1.call-update) | async-done | bytes 2097168 | tf_op jit(solution)/shard_map/all_gather | solution.py:28
  63.7 47.3 %all-gather.47.cloned.1.call-done = bf16[1,2048,3,512]{1,3,2,0:T(8,128)(2,1)} async-done(((bf16[1,512,3,512]{1,3,2,0:T(8,128)(2,1)}), bf16[1,2048,3,512]{1,3,2,0:T(8,128)(2,1)}) %all-gather.47.cloned.1.call-update) | async-done | bytes 6291472 | tf_op jit(solution)/shard_map/all_gather | solution.py:39
  111.0 6.2 add_bitcast_fusion.1
  120.1 32.0 %all-gather.29.cloned.1.call-done = bf16[1,1024,2,512]{1,3,2,0:T(8,128)(2,1)} async-done(((bf16[1,512,2,512]{1,3,2,0:T(8,128)(2,1)}), bf16[1,1024,2,512]{1,3,2,0:T(8,128)(2,1)}) %all-gather.29.cloned.1.call-update) | async-done | bytes 2097168 | tf_op jit(solution)/shard_map/all_gather | solution.py:186
  153.8 32.6 %while.70 = (s32[]{:T(128)}, f32[1,8,512,64]{2,3,1,0:T(8,128)}, f32[1,8,512]{2,1,0:T(8,128)S(1)}, f32[1,8,512]{2,1,0:T(8,128)S(1)}, s32[2]{0:T(128)S(1)}, /*inde...) while((s32[]{:T(128)}, f32[1,8,512,64]{2,3,1,0:T(8,128)}, ...), condition=%wide.region_5.6_spmd.clone, body=%wide.region_2.5_spmd.clone.sunk | while | flops 565208064 | bytes 67903664 | solution.py:121
  160.4 5.0 fusion.361
  192.5 7.5 fusion.273
  202.0 34.7 %reduce-scatter.17.cloned.1.call-done = bf16[1,128,2048]{2,1,0:T(8,128)(2,1)} async-done(((bf16[1,512,2048]{2,1,0:T(8,128)(2,1)}), bf16[1,128,2048]{2,1,0:T(8,128)(2,1)}) %reduce-scatter.17.cloned.1.call-update) | async-done | bytes 524304 | tf_op jit(solution)/shard_map/reduce_scatter | solution.py:32
  243.7 70.6 %all-gather.51.cloned.1.call-done = bf16[1,2048,2,1408]{3,1,2,0:T(8,128)(2,1)} async-done(((bf16[1,512,2,1408]{3,1,2,0:T(8,128)(2,1)}), bf16[1,2048,2,1408]{3,1,2,0:T(8,128)(2,1)}) %all-gather.51.cloned.1.call-update) | async-done | bytes 11534352 | tf_op jit(solution)/shard_map/all_gather | solution.py:41
  314.3 48.2 %all-gather.31.cloned.1.call-done = bf16[1,512,2048]{2,1,0:T(8,128)(2,1)} async-done(((bf16[1,128,2048]{2,1,0:T(8,128)(2,1)}), bf16[1,512,2048]{2,1,0:T(8,128)(2,1)}) %all-gather.31.cloned.1.call-update) | async-done | bytes 2097168 | tf_op jit(solution)/shard_map/all_gather | solution.py:28
  362.5 12.5 fusion.98
  375.0 31.9 %all-gather.53.cloned.1.call-done = bf16[1,1408,2048]{2,1,0:T(8,128)(2,1)} async-done(((bf16[1,1408,512]{2,1,0:T(8,128)(2,1)}), bf16[1,1408,2048]{2,1,0:T(8,128)(2,1)}) %all-gather.53.cloned.1.call-update) | async-done | bytes 5767184 | tf_op jit(solution)/shard_map/all_gather | solution.py:42
  406.8 9.1 fusion.137
  418.8 41.3 %reduce-scatter.19.cloned.1.call-done = bf16[1,128,2048]{2,1,0:T(8,128)(2,1)} async-done(((bf16[1,512,2048]{2,1,0:T(8,128)(2,1)}), bf16[1,128,2048]{2,1,0:T(8,128)(2,1)}) %reduce-scatter.19.cloned.1.call-update) | async-done | bytes 524304 | tf_op jit(solution)/shard_map/reduce_scatter | solution.py:32
  462.8 44.9 %all-gather.55.cloned.1.call-done = bf16[1,2048,3,512]{1,3,2,0:T(8,128)(2,1)} async-done(((bf16[1,512,3,512]{1,3,2,0:T(8,128)(2,1)}), bf16[1,2048,3,512]{1,3,2,0:T(8,128)(2,1)}) %all-gather.55.cloned.1.call-update) | async-done | bytes 6291472 | tf_op jit(solution)/shard_map/all_gather | solution.py:39
  507.7 48.1 %all-gather.33.cloned.1.call-done = bf16[1,512,2048]{2,1,0:T(8,128)(2,1)} async-done(((bf16[1,128,2048]{2,1,0:T(8,128)(2,1)}), bf16[1,512,2048]{2,1,0:T(8,128)(2,1)}) %all-gather.33.cloned.1.call-update) | async-done | bytes 2097168 | tf_op jit(solution)/shard_map/all_gather | solution.py:28
  555.9 6.2 add_bitcast_fusion
  566.5 29.9 %all-gather.35.cloned.1.call-done = bf16[1,1024,2,512]{1,3,2,0:T(8,128)(2,1)} async-done(((bf16[1,512,2,512]{1,3,2,0:T(8,128)(2,1)}), bf16[1,1024,2,512]{1,3,2,0:T(8,128)(2,1)}) %all-gather.35.cloned.1.call-update) | async-done | bytes 2097168 | tf_op jit(solution)/shard_map/all_gather | solution.py:186
  599.6 32.1 %while.71 = (s32[]{:T(128)}, f32[1,8,512,64]{2,3,1,0:T(8,128)S(1)}, f32[1,8,512]{2,1,0:T(8,128)S(1)}, f32[1,8,512]{2,1,0:T(8,128)S(1)}, s32[2]{0:T(128)S(1)}, /*...) while((s32[]{:T(128)}, f32[1,8,512,64]{2,3,1,0:T(8,128)S(1)}, ...), condition=%wide.region_15.16_spmd.clone, body=%wide.region_12.15_spmd.clone.sunk | while | flops 565208064 | bytes 67903664 | solution.py:121
  640.3 40.4 %reduce-scatter.21.cloned.1.call-done = bf16[1,128,2048]{2,1,0:T(8,128)(2,1)} async-done(((bf16[1,512,2048]{2,1,0:T(8,128)(2,1)}), bf16[1,128,2048]{2,1,0:T(8,128)(2,1)}) %reduce-scatter.21.cloned.1.call-update) | async-done | bytes 524304 | tf_op jit(solution)/shard_map/reduce_scatter | solution.py:32
  684.4 8.8 reduce-scatter.25.cloned.1.call-start
  693.3 65.0 %all-gather.59.cloned.1.call-done = bf16[1,2048,2,1408]{3,1,2,0:T(8,128)(2,1)} async-done(((bf16[1,512,2,1408]{3,1,2,0:T(8,128)(2,1)}), bf16[1,2048,2,1408]{3,1,2,0:T(8,128)(2,1)}) %all-gather.59.cloned.1.call-update) | async-done | bytes 11534352 | tf_op jit(solution)/shard_map/all_gather | solution.py:41
  758.2 48.0 %all-gather.37.cloned.1.call-done = bf16[1,512,2048]{2,1,0:T(8,128)(2,1)} async-done(((bf16[1,128,2048]{2,1,0:T(8,128)(2,1)}), bf16[1,512,2048]{2,1,0:T(8,128)(2,1)}) %all-gather.37.cloned.1.call-update) | async-done | bytes 2097168 | tf_op jit(solution)/shard_map/all_gather | solution.py:28
  806.3 12.5 fusion.101
  818.8 33.7 %all-gather.39.cloned.1.call-done = bf16[1,512,2048]{2,1,0:T(8,128)(2,1)} async-done(((bf16[1,128,2048]{2,1,0:T(8,128)(2,1)}), bf16[1,512,2048]{2,1,0:T(8,128)(2,1)}) %all-gather.39.cloned.1.call-update) | async-done | bytes 2097168 | tf_op jit(solution)/shard_map/all_gather | solution.py:28
  852.5 43.6 %all-gather.61.cloned.1.call-done = bf16[1,1408,2048]{2,1,0:T(8,128)(2,1)} async-done(((bf16[1,1408,512]{2,1,0:T(8,128)(2,1)}), bf16[1,1408,2048]{2,1,0:T(8,128)(2,1)}) %all-gather.61.cloned.1.call-update) | async-done | bytes 5767184 | tf_op jit(solution)/shard_map/all_gather | solution.py:42
  896.1 9.1 fusion.203
  906.7 10.0 fusion.142
  916.8 9.1 fusion.134
  926.0 34.8 %reduce-scatter.25.cloned.1.call-done = bf16[1,128,2048]{2,1,0:T(8,128)(2,1)} async-done(((bf16[1,512,2048]{2,1,0:T(8,128)(2,1)}), bf16[1,128,2048]{2,1,0:T(8,128)(2,1)}) %reduce-scatter.25.cloned.1.call-update) | async-done | bytes 524304 | tf_op jit(solution)/shard_map/reduce_scatter | solution.py:32
  962.9 43.7 %reduce-scatter.23.cloned.1.call-done = bf16[1,128,2048]{2,1,0:T(8,128)(2,1)} async-done(((bf16[1,512,2048]{2,1,0:T(8,128)(2,1)}), bf16[1,128,2048]{2,1,0:T(8,128)(2,1)}) %reduce-scatter.23.cloned.1.call-update) | async-done | bytes 524304 | tf_op jit(solution)/shard_map/reduce_scatter | solution.py:32
  1010.1 45.1 %all-gather.41.cloned.1.call-done = bf16[1,512,2048]{2,1,0:T(8,128)(2,1)} async-done(((bf16[1,128,2048]{2,1,0:T(8,128)(2,1)}), bf16[1,512,2048]{2,1,0:T(8,128)(2,1)}) %all-gather.41.cloned.1.call-update) | async-done | bytes 2097168 | tf_op jit(solution)/shard_map/all_gather | solution.py:28
  1060.8 122.3 %while.72 = (s32[]{:T(128)}, bf16[1,512,2,512]{1,3,2,0:T(8,128)(2,1)S(1)}, f32[1,512,2,512]{1,3,2,0:T(8,128)}, f32[1,512,8,64]{1,3,2,0:T(8,128)}, s32[]{:T(128)}...) while((s32[]{:T(128)}, ...), condition=%wide.region_25.26_spmd.clone, body=%wide.region_24.25_spmd.clone.sunk | while | flops 1371276288 | bytes 92594592 | solution.py:349
  1083.9 16.8 collective-permute-done.1
  1103.5 18.4 collective-permute-done
  1145.7 17.1 collective-permute-done.1
  1165.6 17.5 collective-permute-done
  1193.8 7.5 fusion.145
  1201.8 43.7 %reduce-scatter.27.cloned.1.call-done = bf16[1,128,2048]{2,1,0:T(8,128)(2,1)} async-done(((bf16[1,512,2048]{2,1,0:T(8,128)(2,1)}), bf16[1,128,2048]{2,1,0:T(8,128)(2,1)}) %reduce-scatter.27.cloned.1.call-update) | async-done | bytes 524304 | tf_op jit(solution)/shard_map/reduce_scatter | solution.py:32
  1250.0 45.4 %all-gather.43.cloned.1.call-done = bf16[1,512,2048]{2,1,0:T(8,128)(2,1)} async-done(((bf16[1,128,2048]{2,1,0:T(8,128)(2,1)}), bf16[1,512,2048]{2,1,0:T(8,128)(2,1)}) %all-gather.43.cloned.1.call-update) | async-done | bytes 2097168 | tf_op jit(solution)/shard_map/all_gather | solution.py:28
  1295.4 9.1 fusion.202
  1306.2 10.1 fusion.148
  1316.3 42.7 %reduce-scatter.29.cloned.1.call-done = bf16[1,128,2048]{2,1,0:T(8,128)(2,1)} async-done(((bf16[1,512,2048]{2,1,0:T(8,128)(2,1)}), bf16[1,128,2048]{2,1,0:T(8,128)(2,1)}) %reduce-scatter.29.cloned.1.call-update) | async-done | bytes 524304 | tf_op jit(solution)/shard_map/reduce_scatter | solution.py:32
  1368.5 9.4 convolution_convert_fusion.2
  1379.3 7.0 convolution_convert_fusion.4
  1388.2 10.3 convolution_convert_fusion
  1400.2 7.9 convolution_convert_fusion.3
  1416.9 118.6 %while.73 = (s32[]{:T(128)}, bf16[1,512,2,512]{1,3,2,0:T(8,128)(2,1)S(1)}, f32[1,512,2,512]{1,3,2,0:T(8,128)}, f32[1,512,8,64]{1,3,2,0:T(8,128)}, s32[]{:T(128)}...) while((s32[]{:T(128)}, ...), condition=%wide.region_34.35_spmd.clone, body=%wide.region_33.34_spmd.clone.sunk | while | flops 1371276288 | bytes 94691760 | solution.py:349
  1438.1 16.7 collective-permute-done.3
  1457.8 18.3 collective-permute-done.2
  1498.0 17.1 collective-permute-done.3
  1518.0 17.5 collective-permute-done.2
  1545.3 7.0 convolution_convert_fusion.5
  1552.6 11.1 convolution_convert_fusion.1
  1563.8 7.4 fusion.151
  1571.3 85.2 %reduce-scatter.43.cloned.1.call-done = bf16[512,2,1408]{2,0,1:T(8,128)(2,1)} async-done(((bf16[2048,2,1408]{2,0,1:T(8,128)(2,1)}), bf16[512,2,1408]{2,0,1:T(8,128)(2,1)}) %reduce-scatter.43.cloned.1.call-update) | async-done | bytes 2883600 | tf_op jit(solution)/shard_map/reduce_scatter | solution.py:386
  1656.5 57.3 %reduce-scatter.45.cloned.1.call-done = bf16[1408,512]{1,0:T(8,128)(2,1)} async-done(((bf16[1408,2048]{1,0:T(8,128)(2,1)}), bf16[1408,512]{1,0:T(8,128)(2,1)}) %reduce-scatter.45.cloned.1.call-update) | async-done | bytes 1441808 | tf_op jit(solution)/shard_map/reduce_scatter | solution.py:389
  1713.8 34.1 %reduce-scatter.37.cloned.1.call-done = bf16[512,512]{1,0:T(8,128)(2,1)} async-done(((bf16[512,2048]{1,0:T(8,128)(2,1)}), bf16[512,512]{1,0:T(8,128)(2,1)}) %reduce-scatter.37.cloned.1.call-update) | async-done | bytes 524304 | tf_op jit(solution)/shard_map/reduce_scatter | solution.py:383
  1747.9 61.0 %reduce-scatter.33.cloned.1.call-done = bf16[512,3,512]{2,0,1:T(8,128)(2,1)} async-done(((bf16[2048,3,512]{2,0,1:T(8,128)(2,1)}), bf16[512,3,512]{2,0,1:T(8,128)(2,1)}) %reduce-scatter.33.cloned.1.call-update) | async-done | bytes 1572880 | tf_op jit(solution)/shard_map/reduce_scatter | solution.py:380
  1808.9 94.8 %reduce-scatter.41.cloned.1.call-done = bf16[512,2,1408]{2,0,1:T(8,128)(2,1)} async-done(((bf16[2048,2,1408]{2,0,1:T(8,128)(2,1)}), bf16[512,2,1408]{2,0,1:T(8,128)(2,1)}) %reduce-scatter.41.cloned.1.call-update) | async-done | bytes 2883600 | tf_op jit(solution)/shard_map/reduce_scatter | solution.py:386
  1921.8 28.1 %reduce-scatter.31.cloned.1.call-done = bf16[1,128,2048]{2,1,0:T(8,128)(2,1)} async-done(((bf16[1,512,2048]{2,1,0:T(8,128)(2,1)}), bf16[1,128,2048]{2,1,0:T(8,128)(2,1)}) %reduce-scatter.31.cloned.1.call-update) | async-done | bytes 524304 | tf_op jit(solution)/shard_map/reduce_scatter | solution.py:32
  1955.5 295.4 %all-reduce.7.cloned.1.call-done = (bf16[1,512,3,512]{3,1,2,0:T(8,128)(2,1)}, bf16[1,512,3,512]{3,1,2,0:T(8,128)(2,1)}, bf16[1,512,512]{2,1,0:T(8,128)(2,1)}, bf...) async-done(((bf16[1,512,3,512]{3,1,2,0:T(8,128)(2,1)}, ...) | async-done | bytes 12845072 | tf_op jit(solution)/shard_map/psum | solution.py:394
  2262.3 10.0 copy.69
  2272.3 107.1 %all-reduce.5.cloned.1.call-done = (f32[2,2,2048]{2,1,0:T(2,128)}, f32[2,2,2048]{2,1,0:T(2,128)}, f32[2,3,2048]{2,0,1:T(2,128)}) async-done(((f32[2,2,2048]{2,1,0:T(2,128)}, f32[2,2,2048]{2,1,0:T(2,128)}, f32[2,3,2048]{2,0,1:T(2,128)}), (f32[2,2,2048]{2,1,0:T(2,128)}, f32[2,2,2048]{2,1,0:T(2,128)}, f32[2,3,2048]{2,0,1:T(2,128)})) %all-reduce.5.cloned.1.call-update) | async-done | bytes 114704 | tf_op jit(solution)/shard_map/psum | solution.py:403
  (554 shorter events, 318.2 us)
Async XLA Ops:
  7.2 56.5 %all-gather.27.cloned.1.call-start = ((), (), s32[]{:S(2)}) async-start(), calls=%async_computation.16 | async-start | bytes 2621440 | tf_op jit(solution)/shard_map/all_gather | solution.py:28
  8.6 230.7 %copy-start.76 = (f32[1,1,2048]{2,1,0:T(1,128)}, f32[1,1,2048]{2,1,0:T(1,128)S(1)}, u32[]{:S(2)}) copy-start(f32[1,1,2048]{2,1,0:T(1,128)S(1)} %get-tuple-element.946) | copy-start | bytes 24580
  8.6 453.0 %copy-start.78 = (f32[1,1,2048]{2,1,0:T(1,128)}, f32[1,1,2048]{2,1,0:T(1,128)S(1)}, u32[]{:S(2)}) copy-start(f32[1,1,2048]{2,1,0:T(1,128)S(1)} %get-tuple-element.948) | copy-start | bytes 24580
  14.9 96.1 %all-gather.47.cloned.1.call-start = ((), (), s32[]{:S(2)}) async-start(), calls=%async_computation.42 | async-start | bytes 7864320 | tf_op jit(solution)/shard_map/all_gather | solution.py:39
  19.9 132.1 %all-gather.29.cloned.1.call-start = ((), (), s32[]{:S(2)}) async-start(), calls=%async_computation.17 | async-start | bytes 3145728 | tf_op jit(solution)/shard_map/all_gather | solution.py:186
  20.8 541.6 %copy-start.69 = (f32[512,8]{0,1:T(8,128)}, f32[512,8]{0,1:T(8,128)S(1)}, u32[]{:S(2)}) copy-start(f32[512,8]{0,1:T(8,128)S(1)} %get-tuple-element.959) | copy-start | bytes 49156
  118.8 69.3 %all-gather.49.cloned.1.call-start = ((), (), s32[]{:S(2)}) async-start(), calls=%async_computation.43 | async-start | bytes 2621440 | tf_op jit(solution)/shard_map/all_gather | solution.py:40
  119.9 116.8 %reduce-scatter.17.cloned.1.call-start = ((), (), s32[]{:S(2)}) async-start(), calls=%async_computation.18 | async-start | bytes 2621440 | tf_op jit(solution)/shard_map/reduce_scatter | solution.py:32
  192.5 121.8 %all-gather.51.cloned.1.call-start = ((), (), s32[]{:S(2)}) async-start(), calls=%async_computation.44 | async-start | bytes 14417920 | tf_op jit(solution)/shard_map/all_gather | solution.py:41
  202.0 160.5 %all-gather.31.cloned.1.call-start = ((), (), s32[]{:S(2)}) async-start(), calls=%async_computation.19 | async-start | bytes 2621440 | tf_op jit(solution)/shard_map/all_gather | solution.py:28
  241.5 165.3 %all-gather.53.cloned.1.call-start = ((), (), s32[]{:S(2)}) async-start(), calls=%async_computation.45 | async-start | bytes 7208960 | tf_op jit(solution)/shard_map/all_gather | solution.py:42
  243.6 216.4 %reduce-scatter.19.cloned.1.call-start = ((), (), s32[]{:S(2)}) async-start(), calls=%async_computation.20 | async-start | bytes 2621440 | tf_op jit(solution)/shard_map/reduce_scatter | solution.py:32
  416.0 44.0 %copy-start.19 = (bf16[1,128,2048]{2,1,0:T(8,128)(2,1)S(1)}, bf16[1,128,2048]{2,1,0:T(8,128)(2,1)}, u32[]{:S(2)}) copy-start(bf16[1,128,2048]{2,1,0:T(8,128)(2,1)} %reduce-scatter.17.cloned.1.call-done) | copy-start | bytes 1572868
  416.0 91.7 %all-gather.55.cloned.1.call-start = ((), (), s32[]{:S(2)}) async-start(), calls=%async_computation.46 | async-start | bytes 7864320 | tf_op jit(solution)/shard_map/all_gather | solution.py:39
  418.7 137.2 %all-gather.33.cloned.1.call-start = ((), (), s32[]{:S(2)}) async-start(), calls=%async_computation.21 | async-start | bytes 2621440 | tf_op jit(solution)/shard_map/all_gather | solution.py:28
  461.4 219.3 %copy-start.15 = (f32[1,128,2048]{2,1,0:T(8,128)}, f32[1,128,2048]{2,1,0:T(8,128)S(1)}, u32[]{:S(2)}) copy-start(f32[1,128,2048]{2,1,0:T(8,128)S(1)} %get-tuple-element.889) | copy-start | bytes 3145732
  462.7 133.7 %all-gather.35.cloned.1.call-start = ((), (), s32[]{:S(2)}) async-start(), calls=%async_computation.22 | async-start | bytes 3145728 | tf_op jit(solution)/shard_map/all_gather | solution.py:186
  564.5 67.4 %all-gather.57.cloned.1.call-start = ((), (), s32[]{:S(2)}) async-start(), calls=%async_computation.47 | async-start | bytes 2621440 | tf_op jit(solution)/shard_map/all_gather | solution.py:40
  565.2 115.5 %reduce-scatter.21.cloned.1.call-start = ((), (), s32[]{:S(2)}) async-start(), calls=%async_computation.23 | async-start | bytes 2621440 | tf_op jit(solution)/shard_map/reduce_scatter | solution.py:32
  636.4 121.8 %all-gather.59.cloned.1.call-start = ((), (), s32[]{:S(2)}) async-start(), calls=%async_computation.48 | async-start | bytes 14417920 | tf_op jit(solution)/shard_map/all_gather | solution.py:41
  640.2 42.0 %copy-start.88 = (f32[1,1,2048]{2,1,0:T(1,128)S(1)}, f32[1,1,2048]{2,1,0:T(1,128)}, u32[]{:S(2)}) copy-start(f32[1,1,2048]{2,1,0:T(1,128)} %get-tuple-element.949) | copy-start | bytes 24580
  640.2 166.0 %all-gather.37.cloned.1.call-start = ((), (), s32[]{:S(2)}) async-start(), calls=%async_computation.24 | async-start | bytes 2621440 | tf_op jit(solution)/shard_map/all_gather | solution.py:28
  683.3 169.2 %all-gather.39.cloned.1.call-start = ((), (), s32[]{:S(2)}) async-start(), calls=%async_computation.26 | async-start | bytes 2621440 | tf_op jit(solution)/shard_map/all_gather | solution.py:28
  683.8 212.3 %all-gather.61.cloned.1.call-start = ((), (), s32[]{:S(2)}) async-start(), calls=%async_computation.49 | async-start | bytes 7208960 | tf_op jit(solution)/shard_map/all_gather | solution.py:42
  684.4 276.3 %reduce-scatter.25.cloned.1.call-start = ((), (), s32[]{:S(2)}) async-start(), calls=%async_computation.27 | async-start | bytes 2621440 | tf_op jit(solution)/shard_map/reduce_scatter | solution.py:32
  916.7 89.9 %reduce-scatter.23.cloned.1.call-start = ((), (), s32[]{:S(2)}) async-start(), calls=%async_computation.25 | async-start | bytes 2621440 | tf_op jit(solution)/shard_map/reduce_scatter | solution.py:32
  925.9 80.7 %copy-start.37 = (bf16[1,128,2048]{2,1,0:T(8,128)(2,1)S(1)}, bf16[1,128,2048]{2,1,0:T(8,128)(2,1)}, u32[]{:S(2)}) copy-start(bf16[1,128,2048]{2,1,0:T(8,128)(2,1)} %param.18) | copy-start | bytes 1572868
  926.0 129.3 %all-gather.41.cloned.1.call-start = ((), (), s32[]{:S(2)}) async-start(), calls=%async_computation.28 | async-start | bytes 2621440 | tf_op jit(solution)/shard_map/all_gather | solution.py:28
  1009.8 235.7 %reduce-scatter.27.cloned.1.call-start = ((), (), s32[]{:S(2)}) async-start(), calls=%async_computation.29 | async-start | bytes 2621440 | tf_op jit(solution)/shard_map/reduce_scatter | solution.py:32
  1010.1 49.4 %copy-start.31 = (f32[1,8,512,64]{2,3,1,0:T(8,128)S(1)}, f32[1,8,512,64]{2,3,1,0:T(8,128)}, u32[]{:S(2)}) copy-start(f32[1,8,512,64]{2,3,1,0:T(8,128)} %copy-done.30) | copy-start | bytes 3145732
  1010.1 50.7 %copy-start.14 = (bf16[1,512,2,512]{1,3,2,0:T(8,128)(2,1)S(1)}, bf16[1,512,2,512]{1,3,2,0:T(8,128)(2,1)}, u32[]{:S(2)}) copy-start(bf16[1,512,2,512]{1,3,2,0:T(8,128)(2,1)} %pad_maximum_fusion.9) | copy-start | bytes 3145732
  1075.3 25.3 %collective-permute-start.1 = (bf16[1,512,2,512]{1,3,2,0:T(8,128)(2,1)}, bf16[1,512,2,512]{1,3,2,0:T(8,128)(2,1)}, u32[]{:S(2)}, u32[]{:S(2)}) collective-permute-start(bf16[1,512,2,512]{1,3,2,0:T(8,128)(2,1)} %fusion.383), channel_id=1, source_target_pairs={{4,0},{0,4},{5,1},{1,5},{6,2},{2,6},{7,3},{3,7},{12,8},{8,12},{13,... | collective-permute-start | bytes 3145736 | tf_op jit(solution)/shard_map/while/body/eval_jaxpr/ppermute | solution.py:18
  1076.8 45.1 %collective-permute-start = (bf16[1,512,2,512]{1,3,2,0:T(8,128)(2,1)S(1)}, bf16[1,512,2,512]{1,3,2,0:T(8,128)(2,1)S(1)}, u32[]{:S(2)}, u32[]{:S(2)}) collective-permute-start(bf16[1,512,2,512]{1,3,2,0:T(8,128)(2,1)S(1)} %copy.129), channel_id=1, source_target_pairs={{0,4},{1,5},{2,6},{3,7},{8,12},{9,13},{10,14},{11,15},{16,20},{17,... | collective-permute-start | bytes 3145736 | tf_op jit(solution)/shard_map/while/body/eval_jaxpr/ppermute | solution.py:24
  1136.3 26.4 %collective-permute-start.1 = (bf16[1,512,2,512]{1,3,2,0:T(8,128)(2,1)}, bf16[1,512,2,512]{1,3,2,0:T(8,128)(2,1)}, u32[]{:S(2)}, u32[]{:S(2)}) collective-permute-start(bf16[1,512,2,512]{1,3,2,0:T(8,128)(2,1)} %fusion.383), channel_id=1, source_target_pairs={{4,0},{0,4},{5,1},{1,5},{6,2},{2,6},{7,3},{3,7},{12,8},{8,12},{13,... | collective-permute-start | bytes 3145736 | tf_op jit(solution)/shard_map/while/body/eval_jaxpr/ppermute | solution.py:18
  1138.8 44.2 %collective-permute-start = (bf16[1,512,2,512]{1,3,2,0:T(8,128)(2,1)S(1)}, bf16[1,512,2,512]{1,3,2,0:T(8,128)(2,1)S(1)}, u32[]{:S(2)}, u32[]{:S(2)}) collective-permute-start(bf16[1,512,2,512]{1,3,2,0:T(8,128)(2,1)S(1)} %copy.129), channel_id=1, source_target_pairs={{0,4},{1,5},{2,6},{3,7},{8,12},{9,13},{10,14},{11,15},{16,20},{17,... | collective-permute-start | bytes 3145736 | tf_op jit(solution)/shard_map/while/body/eval_jaxpr/ppermute | solution.py:24
  1193.8 51.7 %copy-start.16 = (f32[1,128,2048]{2,1,0:T(8,128)S(1)}, f32[1,128,2048]{2,1,0:T(8,128)}, u32[]{:S(2)}) copy-start(f32[1,128,2048]{2,1,0:T(8,128)} %copy-done.15) | copy-start | bytes 3145732
  1193.8 51.7 %copy-start.79 = (f32[1,1,2048]{2,1,0:T(1,128)S(1)}, f32[1,1,2048]{2,1,0:T(1,128)}, u32[]{:S(2)}) copy-start(f32[1,1,2048]{2,1,0:T(1,128)} %copy-done.78) | copy-start | bytes 24580
  1193.8 51.7 %copy-start.94 = (f32[128]{0:T(128)S(1)}, f32[128]{0:T(128)}, u32[]{:S(2)}) copy-start(f32[128]{0:T(128)} %copy-done.93) | copy-start | bytes 1540
  1193.8 51.7 %copy-start.100 = (f32[128]{0:T(128)S(1)}, f32[128]{0:T(128)}, u32[]{:S(2)}) copy-start(f32[128]{0:T(128)} %copy-done.99) | copy-start | bytes 1540
  1201.3 46.4 %copy-start.32 = (f32[1,128,2048]{2,1,0:T(8,128)S(1)}, f32[1,128,2048]{2,1,0:T(8,128)}, u32[]{:S(2)}) copy-start(f32[1,128,2048]{2,1,0:T(8,128)} %get-tuple-element.885) | copy-start | bytes 3145732
  1201.3 94.1 %all-gather.43.cloned.1.call-start = ((), (), s32[]{:S(2)}) async-start(), calls=%async_computation.30 | async-start | bytes 2621440 | tf_op jit(solution)/shard_map/all_gather | solution.py:28
  1250.0 109.0 %reduce-scatter.29.cloned.1.call-start = ((), (), s32[]{:S(2)}) async-start(), calls=%async_computation.31 | async-start | bytes 2621440 | tf_op jit(solution)/shard_map/reduce_scatter | solution.py:32
  1306.1 52.9 %copy-start.11 = (bf16[1,128,2048]{2,1,0:T(8,128)(2,1)S(1)}, bf16[1,128,2048]{2,1,0:T(8,128)(2,1)}, u32[]{:S(2)}) copy-start(bf16[1,128,2048]{2,1,0:T(8,128)(2,1)} %param.17) | copy-start | bytes 1572868
  1306.1 52.9 %copy-start.20 = (bf16[1,128,2048]{2,1,0:T(8,128)(2,1)S(1)}, bf16[1,128,2048]{2,1,0:T(8,128)(2,1)}, u32[]{:S(2)}) copy-start(bf16[1,128,2048]{2,1,0:T(8,128)(2,1)} %reduce-scatter.17.cloned.1.call-done) | copy-start | bytes 1572868
  1306.1 52.9 %copy-start.77 = (f32[1,1,2048]{2,1,0:T(1,128)S(1)}, f32[1,1,2048]{2,1,0:T(1,128)}, u32[]{:S(2)}) copy-start(f32[1,1,2048]{2,1,0:T(1,128)} %copy-done.76) | copy-start | bytes 24580
  1306.1 52.9 %copy-start.92 = (f32[128]{0:T(128)S(1)}, f32[128]{0:T(128)}, u32[]{:S(2)}) copy-start(f32[128]{0:T(128)} %copy-done.91) | copy-start | bytes 1540
  1306.1 52.9 %copy-start.98 = (f32[128]{0:T(128)S(1)}, f32[128]{0:T(128)}, u32[]{:S(2)}) copy-start(f32[128]{0:T(128)} %copy-done.97) | copy-start | bytes 1540
  1316.3 47.8 %copy-start.58 = (bf16[1,512,8,64]{1,3,2,0:T(8,128)(2,1)S(1)}, bf16[1,512,8,64]{1,3,2,0:T(8,128)(2,1)}, u32[]{:S(2)}) copy-start(bf16[1,512,8,64]{1,3,2,0:T(8,128)(2,1)} %copy-done.57) | copy-start | bytes 1572868
  1316.3 93.2 %all-gather.45.cloned.1.call-start = ((), (), s32[]{:S(2)}) async-start(), calls=%async_computation.32 | async-start | bytes 2621440 | tf_op jit(solution)/shard_map/all_gather | solution.py:28
  1364.1 207.2 %reduce-scatter.39.cloned.1.call-start = ((), (), s32[]{:S(2)}) async-start(), calls=%async_computation.37 | async-start | bytes 2621440 | tf_op jit(solution)/shard_map/reduce_scatter | solution.py:383
  1368.3 203.0 %reduce-scatter.47.cloned.1.call-start = ((), (), s32[]{:S(2)}) async-start(), calls=%async_computation.41 | async-start | bytes 7208960 | tf_op jit(solution)/shard_map/reduce_scatter | solution.py:389
  1377.9 193.4 %reduce-scatter.35.cloned.1.call-start = ((), (), s32[]{:S(2)}) async-start(), calls=%async_computation.35 | async-start | bytes 7864320 | tf_op jit(solution)/shard_map/reduce_scatter | solution.py:380
  1386.3 270.2 %reduce-scatter.43.cloned.1.call-start = ((), (), s32[]{:S(2)}) async-start(), calls=%async_computation.39 | async-start | bytes 14417920 | tf_op jit(solution)/shard_map/reduce_scatter | solution.py:386
  1398.6 315.2 %reduce-scatter.45.cloned.1.call-start = ((), (), s32[]{:S(2)}) async-start(), calls=%async_computation.40 | async-start | bytes 7208960 | tf_op jit(solution)/shard_map/reduce_scatter | solution.py:389
  1408.1 339.8 %reduce-scatter.37.cloned.1.call-start = ((), (), s32[]{:S(2)}) async-start(), calls=%async_computation.36 | async-start | bytes 2621440 | tf_op jit(solution)/shard_map/reduce_scatter | solution.py:383
  1416.8 392.0 %reduce-scatter.33.cloned.1.call-start = ((), (), s32[]{:S(2)}) async-start(), calls=%async_computation.34 | async-start | bytes 7864320 | tf_op jit(solution)/shard_map/reduce_scatter | solution.py:380
  1429.5 25.3 %collective-permute-start.3 = (bf16[1,512,2,512]{1,3,2,0:T(8,128)(2,1)}, bf16[1,512,2,512]{1,3,2,0:T(8,128)(2,1)}, u32[]{:S(2)}, u32[]{:S(2)}) collective-permute-start(bf16[1,512,2,512]{1,3,2,0:T(8,128)(2,1)} %fusion.398), channel_id=1, source_target_pairs={{4,0},{0,4},{5,1},{1,5},{6,2},{2,6},{7,3},{3,7},{12,8},{8,12},{13,... | collective-permute-start | bytes 3145736 | tf_op jit(solution)/shard_map/while/body/eval_jaxpr/ppermute | solution.py:18
  1431.0 45.1 %collective-permute-start.2 = (bf16[1,512,2,512]{1,3,2,0:T(8,128)(2,1)S(1)}, bf16[1,512,2,512]{1,3,2,0:T(8,128)(2,1)S(1)}, u32[]{:S(2)}, u32[]{:S(2)}) collective-permute-start(bf16[1,512,2,512]{1,3,2,0:T(8,128)(2,1)S(1)} %copy.141), channel_id=1, source_target_pairs={{0,4},{1,5},{2,6},{3,7},{8,12},{9,13},{10,14},{11,15},{16,20},{17,... | collective-permute-start | bytes 3145736 | tf_op jit(solution)/shard_map/while/body/eval_jaxpr/ppermute | solution.py:24
  1488.7 26.4 %collective-permute-start.3 = (bf16[1,512,2,512]{1,3,2,0:T(8,128)(2,1)}, bf16[1,512,2,512]{1,3,2,0:T(8,128)(2,1)}, u32[]{:S(2)}, u32[]{:S(2)}) collective-permute-start(bf16[1,512,2,512]{1,3,2,0:T(8,128)(2,1)} %fusion.398), channel_id=1, source_target_pairs={{4,0},{0,4},{5,1},{1,5},{6,2},{2,6},{7,3},{3,7},{12,8},{8,12},{13,... | collective-permute-start | bytes 3145736 | tf_op jit(solution)/shard_map/while/body/eval_jaxpr/ppermute | solution.py:18
  1491.1 44.3 %collective-permute-start.2 = (bf16[1,512,2,512]{1,3,2,0:T(8,128)(2,1)S(1)}, bf16[1,512,2,512]{1,3,2,0:T(8,128)(2,1)S(1)}, u32[]{:S(2)}, u32[]{:S(2)}) collective-permute-start(bf16[1,512,2,512]{1,3,2,0:T(8,128)(2,1)S(1)} %copy.141), channel_id=1, source_target_pairs={{0,4},{1,5},{2,6},{3,7},{8,12},{9,13},{10,14},{11,15},{16,20},{17,... | collective-permute-start | bytes 3145736 | tf_op jit(solution)/shard_map/while/body/eval_jaxpr/ppermute | solution.py:24
  1552.3 351.4 %reduce-scatter.41.cloned.1.call-start = ((), (), s32[]{:S(2)}) async-start(), calls=%async_computation.38 | async-start | bytes 14417920 | tf_op jit(solution)/shard_map/reduce_scatter | solution.py:386
  1563.7 386.2 %reduce-scatter.31.cloned.1.call-start = ((), (), s32[]{:S(2)}) async-start(), calls=%async_computation.33 | async-start | bytes 2621440 | tf_op jit(solution)/shard_map/reduce_scatter | solution.py:32
  1571.2 679.7 %all-reduce.7.cloned.1.call-start = ((), (), s32[]{:S(2)}) async-start(), calls=%async_computation.51 | async-start | bytes 25690112 | tf_op jit(solution)/shard_map/psum | solution.py:394
  1903.7 475.6 %all-reduce.5.cloned.1.call-start = ((), (), s32[]{:S(2)}) async-start(), calls=%async_computation.50 | async-start | bytes 229376 | tf_op jit(solution)/shard_map/psum | solution.py:403
  (98 other events, 596.8 us)
Sparse Core Ops, SparseCore 0:
  15.0 48.6 all-gather.26
  65.8 45.0 all-gather.46
  118.9 33.1 all-gather.28
  154.0 22.5 all-gather.48
  192.6 44.0 reduce-scatter.16
  238.8 75.4 all-gather.50
  316.5 45.9 all-gather.30
  364.7 42.1 all-gather.52
  416.1 43.8 reduce-scatter.18
  462.0 45.6 all-gather.54
  509.9 45.9 all-gather.32
  564.6 31.8 all-gather.34
  598.6 22.5 all-gather.56
  636.6 44.0 reduce-scatter.20
  682.7 75.4 all-gather.58
  760.3 45.9 all-gather.36
  807.8 44.6 all-gather.38
  854.0 42.1 all-gather.60
  916.9 43.8 reduce-scatter.24
  963.5 43.0 reduce-scatter.22
  1009.9 45.2 all-gather.40
  1201.4 44.0 reduce-scatter.26
  1250.1 45.2 all-gather.42
  1316.4 42.5 reduce-scatter.28
  1364.2 45.2 all-gather.44
  1412.0 30.1 reduce-scatter.38
  1444.6 54.8 reduce-scatter.46
  1502.8 58.3 reduce-scatter.34
  1564.3 92.1 reduce-scatter.42
  1658.9 54.8 reduce-scatter.44
  1716.5 31.3 reduce-scatter.36
  1750.4 58.3 reduce-scatter.32
  1811.5 92.1 reduce-scatter.40
  1906.1 43.8 reduce-scatter.30
  1953.0 297.8 all-reduce.6
  2257.3 121.9 all-reduce.4
where the time goes:
time: 2400 us; the launch traced here: 2390 us
  waiting for transfers between devices  1860 us (78%)
  matrix products  273 us (11%)
  local copies, waits for them, and re-layouts  106 us (4%)
  other arithmetic  101 us (4%)
  starting transfers between devices  28.7 us (1%)
    all_gather x8, waiting for transfers between devices, gather_rows(): return lax.all_gather(values_low, 'tensor', axis=1, tiled=True)  312 us
    reduce_scatter x8, waiting for transfers between devices, sum_rows(): lax.psum_scatter(partial_value.astype(jnp.bfloat16), 'tensor', scatter_di...  309 us
    psum x1, waiting for transfers between devices, shards(): lax.psum(owned[0].astype(jnp.bfloat16), 'ctx').astype(jnp.float32)  295 us
    reduce_scatter x2, waiting for transfers between devices, shards(): lax.psum_scatter(gate_up_grad.astype(jnp.bfloat16), 'dp', scatter_dimensi...  180 us
    all_gather x2, waiting for transfers between devices, gather_layer(): lax.all_gather(gate_up_weight[layer_index], 'dp', axis=0, tiled=True)  136 us
    psum x1, waiting for transfers between devices, shards(): lax.psum((jnp.stack(gain_grads), jnp.stack(bias_grads), jnp.stack(qkv_bia...  107 us
    all_gather x2, waiting for transfers between devices, gather_layer(): lax.all_gather(qkv_weight[layer_index], 'dp', axis=0, tiled=True)  92.2 us
    all_gather x2, waiting for transfers between devices, gather_layer(): lax.all_gather(down_weight[layer_index], 'dp', axis=1, tiled=True)  75.5 us
  transfers between devices with their start and end apart: 44, of which 39 were waited for; matrix products, arithmetic and copies ran while one was open for 13% of the time, Pallas kernels for 0%

commit v1 on v0

v1 whole, which is shorter than its diff:
```python
import functools

import jax
import jax.numpy as jnp
from jax import lax
from jax.experimental import pallas as pl
from jax.experimental.pallas import tpu as pltpu
from jax.sharding import PartitionSpec as P

HD = 64
ROT = 16
LAYERS = 2

MASKED = -1e30
EPSILON = 1e-05
LOW = jnp.bfloat16
WIDE = jnp.float32


def layer_norm_rows(stream, gain, bias):
    row_mean = jnp.mean(stream, axis=-1, keepdims=True)
    centered = stream - row_mean
    inverse = lax.rsqrt(jnp.mean(centered * centered, axis=-1, keepdims=True) + EPSILON)
    unit_rows = centered * inverse
    return (unit_rows * gain + bias, unit_rows, inverse)


def norm_backward(grad_rows, unit_rows, inverse, gain):
    grad_unit = grad_rows * gain
    first_mean = jnp.mean(grad_unit, axis=-1, keepdims=True)
    second_mean = jnp.mean(grad_unit * unit_rows, axis=-1, keepdims=True)
    grad_input = inverse * (grad_unit - first_mean - unit_rows * second_mean)
    return (grad_input, jnp.sum(grad_rows * unit_rows, axis=0), jnp.sum(grad_rows, axis=0))


def rotary_tables(positions):
    half_rot = ROT // 2
    frequency = 10000.0 ** (-(jnp.arange(half_rot, dtype=jnp.float32) * 2.0) / ROT)
    angles = positions.astype(jnp.float32)[:, None] * frequency[None, :]
    cosine, sine = jnp.cos(angles), jnp.sin(angles)
    rest = jnp.zeros((angles.shape[0], HD - ROT), WIDE)
    none = jnp.zeros_like(sine)
    heads = lambda *parts: jnp.tile(jnp.concatenate(parts, axis=1), (1, PAIR // HD))
    return (
        heads(cosine, cosine, rest + 1.0),
        heads(-sine, none, rest),
        heads(none, sine, rest),
    )


def rotated(flat, cos_ref, right_ref, left_ref):
    shift = ROT // 2
    found = []
    for start in range(0, flat.shape[1], PAIR):
        v = flat[:, start : start + PAIR]
        right, left = pltpu.roll(v, PAIR - shift, 1), pltpu.roll(v, shift, 1)
        found.append(v * cos_ref[...] + right * right_ref[...] + left * left_ref[...])
    return jnp.concatenate(found, axis=1)


def dot(a, b, dims):
    return lax.dot_general(a, b, (dims, ((), ())), preferred_element_type=WIDE)


PAIR = 128


NN = ((1,), (0,))
NT = ((1,), (1,))
TN = ((0,), (0,))


def total_of(terms):
    return functools.reduce(lambda a, b: a + b, terms)


def work(flops):
    return pl.CostEstimate(flops=int(flops), bytes_accessed=0, transcendentals=0)


TILE = 256


def tiled(kernel, name, steps, ins, outs, flops):
    return pl.pallas_call(
        kernel,
        grid=(steps,),
        in_specs=[pl.BlockSpec(block, index) for _, block, index in ins],
        out_specs=[pl.BlockSpec(block, index) for _, block, index in outs],
        out_shape=[shape for shape, _, _ in outs],
        compiler_params=pltpu.CompilerParams(vmem_limit_bytes=48 * 1024 * 1024),
        cost_estimate=work(2.5 * flops),
        name=name,
    )(*[array for array, _, _ in ins])


def whole_block(array):
    return (array, array.shape, lambda i: (0,) * array.ndim)


def column_block(array):
    return (array, (array.shape[0], TILE), lambda i: (0, i))


def row_block(array):
    return (array, (TILE, array.shape[1]), lambda i: (i, 0))


def gate_up_kernel(rows_ref, gate_w_ref, up_w_ref, gate_ref, up_ref, activated_ref):
    rows = rows_ref[...]
    gate = dot(rows, gate_w_ref[...], NN)
    up = dot(rows, up_w_ref[...], NN)
    gate_ref[...] = gate
    up_ref[...] = up
    activated_ref[...] = (gate * jax.nn.sigmoid(gate) * up).astype(LOW)


def gate_up_rows(rows, gate_weight, up_weight):
    count, hidden = rows.shape[0], gate_weight.shape[1]
    shapes = [jax.ShapeDtypeStruct((count, hidden), t) for t in (WIDE, WIDE, LOW)]
    return tiled(
        gate_up_kernel,
        "gate_up",
        pl.cdiv(hidden, TILE),
        [whole_block(rows), column_block(gate_weight), column_block(up_weight)],
        [column_block(s) for s in shapes],
        4 * rows.size * hidden,
    )


def back_sum(rows, weight_ref):
    width = weight_ref.shape[2]
    return total_of(
        dot(rows[:, r * width : (r + 1) * width], weight_ref[r], NT)
        for r in range(weight_ref.shape[0])
    )


def tall_block(array):
    return (array, (array.shape[0], TILE, array.shape[2]), lambda i: (0, i, 0))


def gate_up_back_kernel(rows_ref, weight_ref, gate_ref, up_ref, grad_gate_ref, grad_up_ref):
    grad = back_sum(rows_ref[...], weight_ref)
    gate, up = gate_ref[...], up_ref[...]
    s = jax.nn.sigmoid(gate)
    grad_gate_ref[...] = (grad * up * s * (1.0 + gate * (1.0 - s))).astype(LOW)
    grad_up_ref[...] = (grad * (gate * s)).astype(LOW)


def gate_up_back(rows, down_weight, gate, up):
    count, hidden = gate.shape
    shape = jax.ShapeDtypeStruct((count, hidden), LOW)
    return tiled(
        gate_up_back_kernel,
        "gate_up_back",
        pl.cdiv(hidden, TILE),
        [whole_block(rows), tall_block(down_weight), column_block(gate), column_block(up)],
        [column_block(shape)] * 2,
        2 * rows.size * hidden,
    )


def out_back_kernel(rows_ref, weight_ref, out_ref):
    out_ref[...] = back_sum(rows_ref[...], weight_ref).astype(LOW)


def out_back(rows, weight):
    shape = jax.ShapeDtypeStruct((rows.shape[0], weight.shape[1]), LOW)
    return tiled(
        out_back_kernel,
        "out_back",
        shape.shape[1] // TILE,
        [whole_block(rows), tall_block(weight)],
        [column_block(shape)],
        2 * rows.size * shape.shape[1],
    )[0]


def wide_kernel(rows_ref, weight_ref, out_ref):
    out_ref[...] = dot(rows_ref[...], weight_ref[0], NN).astype(LOW)


def times_wide(rows, weight, name):
    blocks, depth, width = weight.shape
    per = width // TILE
    shape = jax.ShapeDtypeStruct((rows.shape[0], blocks * width), LOW)
    return tiled(
        wide_kernel,
        name,
        blocks * per,
        [whole_block(rows), (weight, (1, depth, TILE), lambda i: (i // per, 0, i % per))],
        [column_block(shape)],
        2 * rows.size * blocks * width,
    )[0]


def gate_up_in_kernel(gate_ref, up_ref, gate_w_ref, up_w_ref, out_ref):
    total = dot(gate_ref[...], gate_w_ref[...], NT) + dot(up_ref[...], up_w_ref[...], NT)
    out_ref[...] = total.astype(LOW)


def gate_up_in(grad_gate, grad_up, gate_weight, up_weight):
    shape = jax.ShapeDtypeStruct((grad_gate.shape[0], gate_weight.shape[0]), LOW)
    return tiled(
        gate_up_in_kernel,
        "gate_up_in",
        shape.shape[1] // TILE,
        [whole_block(grad_gate), whole_block(grad_up), row_block(gate_weight), row_block(up_weight)],
        [column_block(shape)],
        4 * grad_gate.size * shape.shape[1],
    )[0]


def project_in_kernel(rows_ref, weight_ref, out_ref):
    width = weight_ref.shape[3]
    out_ref[...] = total_of(
        dot(rows_ref[:, c * width : (c + 1) * width], weight_ref[0, c], NT) for c in range(3)
    ).astype(LOW)


def project_in(rows, weight):
    blocks, three, depth, width = weight.shape
    per = depth // TILE
    shape = jax.ShapeDtypeStruct((rows.shape[0], blocks * depth), LOW)
    return tiled(
        project_in_kernel,
        "project_in",
        blocks * per,
        [whole_block(rows), (weight, (1, three, TILE, width), lambda i: (i // per, 0, i % per, 0))],
        [column_block(shape)],
        2 * rows.size * blocks * depth,
    )[0]


def project_kernel(rows_ref, weight_ref, bias_ref, cos_ref, right_ref, left_ref, q_ref, kv_ref):
    blocks, _, depth, width = weight_ref.shape
    flat = dot(rows_ref[...], weight_ref[...].reshape(blocks * depth, width), NN) + bias_ref[0]
    step = pl.program_id(0)

    @pl.when(step == 0)
    def _():
        kv_ref[...] = rotated(flat, cos_ref, right_ref, left_ref).astype(LOW)

    @pl.when(step == 1)
    def _():
        kv_ref[...] = flat.astype(LOW)

    @pl.when(step == 2)
    def _():
        q_ref[...] = rotated(flat, cos_ref, right_ref, left_ref).astype(LOW)


def project(rows, weight, bias, tables):
    count = rows.shape[0]
    blocks, _, depth, width = weight.shape
    fixed = lambda i: (0, 0)
    shapes = [jax.ShapeDtypeStruct((k * count, width), LOW) for k in (1, 2)]
    return tiled(
        project_kernel,
        "project",
        3,
        [
            whole_block(rows),
            (weight, (blocks, 1, depth, width), lambda i: (0, (i + 1) % 3, 0, 0)),
            (bias[:, None, :], (1, 1, width), lambda i: ((i + 1) % 3, 0, 0)),
        ]
        + [(t, (count, PAIR), fixed) for t in tables],
        [
            (shapes[0], (count, width), fixed),
            (shapes[1], (count, width), lambda i: (jnp.minimum(i, 1), 0)),
        ],
        6 * rows.size * width,
    )


def project_back_kernel(far, dq_ref, dkv_ref, *refs):
    far_refs = refs[:far]
    cos_ref, right_ref, left_ref, out_ref, sum_ref = refs[far:]
    step = pl.program_id(0)

    def put(value):
        out_ref[...] = value.astype(LOW)
        sum_ref[0] = jnp.sum(value, axis=0, keepdims=True)

    def key_value():
        return total_of([dkv_ref[...]] + [r[...].astype(WIDE) for r in far_refs])

    @pl.when(step == 0)
    def _():
        put(rotated(dq_ref[...], cos_ref, right_ref, left_ref))

    @pl.when(step == 1)
    def _():
        put(rotated(key_value(), cos_ref, right_ref, left_ref))

    @pl.when(step == 2)
    def _():
        put(key_value())


def project_back(dq, dkv, far, tables):
    count, width = dq.shape
    fixed = lambda i: (0, 0)
    lower = pl.BlockSpec((count, width), lambda i: (jnp.maximum(i - 1, 0), 0))
    out, sums = pl.pallas_call(
        functools.partial(project_back_kernel, len(far)),
        grid=(3,),
        in_specs=[pl.BlockSpec((count, width), fixed)]
        + [lower] * (1 + len(far))
        + [pl.BlockSpec((count, PAIR), fixed)] * 3,
        out_specs=[
            pl.BlockSpec((count, width), lambda i: (0, i)),
            pl.BlockSpec((1, 1, width), lambda i: (i, 0, 0)),
        ],
        out_shape=[
            jax.ShapeDtypeStruct((count, 3 * width), LOW),
            jax.ShapeDtypeStruct((3, 1, width), WIDE),
        ],
        compiler_params=pltpu.CompilerParams(vmem_limit_bytes=32 * 1024 * 1024),
        cost_estimate=work(14000 * count * width),
        name="project_back",
    )(dq, dkv, *far, *tables)
    return out, sums[:, 0]


def attend_kernel(blocks, qpos_ref, kpos_ref, q_ref, *refs):
    keys, values = refs[: 2 * blocks : 2], refs[1 : 2 * blocks : 2]
    out_ref, lse_ref = refs[2 * blocks :]
    allowed = [kpos_ref[b] <= qpos_ref[...] for b in range(blocks)]
    for half in range(PAIR // HD):
        lanes = slice(half * HD, (half + 1) * HD)
        q = q_ref[:, lanes] * jnp.asarray(HD**-0.5, LOW)
        top, total, acc = None, None, None
        for b in range(blocks):
            s = jnp.where(allowed[b], dot(q, keys[b][:, lanes], NT), MASKED)
            block_top = jnp.max(s, axis=1, keepdims=True)
            new_top = block_top if b == 0 else jnp.maximum(top, block_top)
            p = jnp.exp(s - new_top)
            block_total = jnp.sum(p, axis=1, keepdims=True)
            block_acc = dot(p.astype(LOW), values[b][:, lanes], NN)
            if b == 0:
                total, acc = block_total, block_acc
            else:
                factor = jnp.exp(top - new_top)
                total = total * factor + block_total
                acc = acc * factor + block_acc
            top = new_top
        out_ref[:, lanes] = acc / total
        lse_ref[half] = top + jnp.log(total)


def attend(qpos, kpos, q, pairs_of_rows):
    rows, width = q.shape
    key_rows = pairs_of_rows[0].shape[0] // 2
    blocks = len(pairs_of_rows)
    pairs = width // PAIR
    per_pair = PAIR // HD
    column = lambda i: (0, i)
    fixed = lambda i: (0, 0)
    key_specs = [pl.BlockSpec((key_rows, PAIR), lambda i, c=c: (c, i)) for c in range(2)]
    stacked = [rows_of for rows_of in pairs_of_rows for c in range(2)]
    return pl.pallas_call(
        functools.partial(attend_kernel, blocks),
        grid=(pairs,),
        in_specs=[
            pl.BlockSpec((rows, 1), fixed),
            pl.BlockSpec((blocks, 1, key_rows), lambda i: (0, 0, 0)),
            pl.BlockSpec((rows, PAIR), column),
        ]
        + key_specs * blocks,
        out_specs=[
            pl.BlockSpec((rows, PAIR), column),
            pl.BlockSpec((per_pair, rows, 1), lambda i: (i, 0, 0)),
        ],
        out_shape=[
            jax.ShapeDtypeStruct((rows, width), WIDE),
            jax.ShapeDtypeStruct((width // HD, rows, 1), WIDE),
        ],
        compiler_params=pltpu.CompilerParams(vmem_limit_bytes=32 * 1024 * 1024),
        cost_estimate=work(43 * rows * key_rows * blocks * width),
        name="attend",
    )(qpos, kpos, q, *stacked)


def attend_back_kernel(blocks, qpos_ref, kpos_ref, q_ref, grad_ref, out_ref, lse_ref, *refs):
    keys, values = refs[: 2 * blocks : 2], refs[1 : 2 * blocks : 2]
    dq_ref = refs[2 * blocks]
    dboth = refs[2 * blocks + 1 :]
    key_rows = keys[0].shape[0]
    allowed = [kpos_ref[b] <= qpos_ref[...] for b in range(blocks)]
    scale = HD**-0.5
    for half in range(PAIR // HD):
        lanes = slice(half * HD, (half + 1) * HD)
        q = q_ref[:, lanes] * jnp.asarray(scale, LOW)
        grad = grad_ref[:, lanes]
        lse = lse_ref[half]
        delta = jnp.sum(grad.astype(WIDE) * out_ref[:, lanes], axis=1, keepdims=True)
        dq = None
        for b in range(blocks):
            k = keys[b][:, lanes]
            s = jnp.where(allowed[b], dot(q, k, NT), MASKED)
            p = jnp.exp(s - lse)
            dp = dot(grad, values[b][:, lanes], NT)
            ds = (p * (dp - delta)).astype(LOW)
            kind = dboth[b].dtype
            dboth[b][key_rows:, lanes] = dot(p.astype(LOW), grad, TN).astype(kind)
            dboth[b][:key_rows, lanes] = dot(ds, q, TN).astype(kind)
            term = dot(ds, k, NN)
            dq = term if b == 0 else dq + term
        dq_ref[:, lanes] = dq * scale


def attend_back(qpos, kpos, q, grad, out, lse, pairs_of_rows):
    rows, width = q.shape
    key_rows = pairs_of_rows[0].shape[0] // 2
    blocks = len(pairs_of_rows)
    pairs = width // PAIR
    per_pair = PAIR // HD
    column = lambda i: (0, i)
    fixed = lambda i: (0, 0)
    row_spec = pl.BlockSpec((rows, PAIR), column)
    key_specs = [pl.BlockSpec((key_rows, PAIR), lambda i, c=c: (c, i)) for c in range(2)]
    stacked = [rows_of for rows_of in pairs_of_rows for c in range(2)]
    far = [jax.ShapeDtypeStruct((2 * key_rows, width), LOW)] * (blocks - 1)
    near = [jax.ShapeDtypeStruct((2 * key_rows, width), WIDE)]
    results = pl.pallas_call(
        functools.partial(attend_back_kernel, blocks),
        grid=(pairs,),
        in_specs=[
            pl.BlockSpec((rows, 1), fixed),
            pl.BlockSpec((blocks, 1, key_rows), lambda i: (0, 0, 0)),
            row_spec,
            row_spec,
            row_spec,
            pl.BlockSpec((per_pair, rows, 1), lambda i: (i, 0, 0)),
        ]
        + key_specs * blocks,
        out_specs=[row_spec] + [pl.BlockSpec((2 * key_rows, PAIR), column)] * blocks,
        out_shape=[jax.ShapeDtypeStruct((rows, width), WIDE)] + near + far,
        compiler_params=pltpu.CompilerParams(vmem_limit_bytes=40 * 1024 * 1024),
        cost_estimate=work(75 * rows * key_rows * blocks * width),
        name="attend_back",
    )(qpos, kpos, q, grad, out, lse, *stacked)
    return results[0], results[1], results[2:]


def bits_of(count):
    return [1 << k for k in range(count.bit_length() - 1)]


def swapped(value, axis, mask):
    count = lax.axis_size(axis)
    return lax.ppermute(value, axis, [(i, i ^ mask) for i in range(count)])


class Line:
    def __init__(self, own_rows):
        n_tensor, n_ctx = lax.axis_size("tensor"), lax.axis_size("ctx")
        tensor, ctx = lax.axis_index("tensor"), lax.axis_index("ctx")
        self.count, self.tensor = n_tensor, tensor
        row = jnp.arange(own_rows, dtype=jnp.int32)
        chip = (tensor + jnp.arange(n_tensor, dtype=jnp.int32)) % n_tensor
        place = (chip[:, None] * own_rows + row[None, :]).reshape(-1)
        block = n_tensor * own_rows
        self.places = ctx * block + place
        self.key_places = [self.places] + [
            jnp.where(ctx >= s, (ctx - s) * block + place, 1 << 30) for s in range(1, n_ctx)
        ]
        self.own_rows = own_rows

    def gather_rows(self, low):
        count, t = self.count, self.tensor
        send = lambda v, *route: lax.ppermute(v, "tensor", list(route))
        if count == 4:
            far = send(low, (0, 2), (2, 0), (1, 3), (3, 1))
            above = send(low, (0, 1), (1, 2), (2, 3))
            below = send(low, (1, 0), (2, 1), (3, 2))
            end = send(far, (2, 3), (1, 0))
            found = [low, jnp.where(t == 3, end, below), far, jnp.where(t == 0, end, above)]
        else:
            found = [low] + [
                send(low, *[((i + d) % count, i) for i in range(count)]) for d in range(1, count)
            ]
        return jnp.concatenate(found, axis=0)

    def sum_rows(self, low):
        rows, count, t = self.own_rows, self.count, self.tensor
        terms = [low[d * rows : (d + 1) * rows] for d in range(count)]
        send = lambda v, *route: lax.ppermute(v, "tensor", list(route))
        wide = lambda v: v.astype(WIDE)
        if count == 4:
            end = send(jnp.where(t == 0, terms[3], terms[1]), (0, 1), (3, 2))
            above = send(terms[1], (0, 1), (1, 2), (2, 3))
            below = send(terms[3], (3, 2), (2, 1), (1, 0))
            far = (wide(terms[2]) + wide(end)).astype(LOW)
            got = [send(far, (0, 2), (2, 0), (1, 3), (3, 1)), above, below]
        else:
            got = [
                send(terms[d], *[(i, (i + d) % count) for i in range(count)])
                for d in range(1, count)
            ]
        return total_of([wide(terms[0])] + [wide(g) for g in got])

    def owner(self, low):
        count = lax.axis_size("ctx")
        if count != 2:
            return lax.psum(low, "ctx").astype(WIDE) if count > 1 else low.astype(WIDE)
        got = yield swapped(low, "ctx", 1)
        return low.astype(WIDE) + got.astype(WIDE)

    def far_keys(self, value):
        count = lax.axis_size("ctx")
        return [
            lax.ppermute(value, "ctx", [(i, i + s) for i in range(count - s)])
            for s in range(1, count)
        ]

    def far_key_grads(self, values):
        count = lax.axis_size("ctx")
        return [
            lax.ppermute(values[s - 1], "ctx", [(i + s, i) for i in range(count - s)])
            for s in range(1, count)
        ]


def weight_stages(shard):
    shard = yield shard
    return (yield lax.all_gather(shard, "dp"))


def grad_stages(plan, value, axis):
    got = yield lax.psum_scatter(value.astype(LOW), "dp", scatter_dimension=axis, tiled=True)
    return (yield from plan.owner(got))


class Job:
    def __init__(self, stages):
        self.stages, self.value, self.result, self.done = stages, None, None, False
        self.advance(None)

    def advance(self, value):
        try:
            self.value = self.stages.send(value)
        except StopIteration as end:
            self.done, self.result, self.value = True, end.value, None

    def finish(self):
        while not self.done:
            self.advance(self.value)
        return self.result


def meanwhile(value, *jobs):
    open_jobs = [j for j in jobs if j is not None and not j.done]
    if not open_jobs:
        return value
    value, held = lax.optimization_barrier((value, tuple(j.value for j in open_jobs)))
    for job, got in zip(open_jobs, held):
        job.advance(got)
    return value


def held(value, *jobs):
    open_jobs = [j for j in jobs if j is not None and not j.done]
    if not open_jobs:
        return value
    value, kept = lax.optimization_barrier((value, tuple(j.value for j in open_jobs)))
    for job, got in zip(open_jobs, kept):
        job.value = got
    return value


def shards(
    tokens,
    cotangent,
    norm_gains,
    norm_biases,
    qkv_weight,
    qkv_bias,
    out_weight,
    gate_up_weight,
    down_weight,
):
    own_rows = tokens.shape[1]
    model = tokens.shape[2]
    heads_width = qkv_weight.shape[3]
    plan = Line(own_rows)
    tables = rotary_tables(plan.places)
    tables_back = (tables[0], -tables[1], -tables[2])
    qpos = plan.places[:, None]
    kpos = jnp.stack(plan.key_places)[:, None, :]
    gains = (norm_gains)
    biases = (norm_biases)
    qkv_bias_own = lax.dynamic_slice_in_dim(qkv_bias, lax.axis_index("tensor") * heads_width, heads_width, 2)

    def weight_jobs(layer, after):
        (qkv_all, out_all, gate_up_all, down_all), after = lax.optimization_barrier(
            ((qkv_weight, out_weight, gate_up_weight, down_weight), after)
        )
        matrices = {
            "qkv": jnp.transpose(qkv_all[layer], (1, 0, 2)),
            "out": out_all[layer],
            "gate": gate_up_all[layer, :, 0],
            "up": gate_up_all[layer, :, 1],
            "down": down_all[layer],
        }
        return {n: Job(weight_stages(v)) for n, v in matrices.items()}, after

    now, unused = weight_jobs(0, ())
    for name in ("qkv", "out", "gate", "up"):
        now[name].advance(now[name].value)
    stream = tokens[0].astype(WIDE)
    moved_cotangent = cotangent[0]
    later = {}
    saved = []
    for layer in range(LAYERS):
        last = layer + 1 == LAYERS
        normed_one, unit_one, inverse_one = layer_norm_rows(
            stream, gains[layer, 0], biases[layer, 0]
        )
        rows_one = plan.gather_rows(normed_one.astype(LOW))
        if layer == 0:
            rows_one = meanwhile(rows_one, now["qkv"], now["down"])
        else:
            rows_one = meanwhile(rows_one, now["out"], now["gate"], now["down"])
        qkv_full = now["qkv"].finish()
        queries, keys_values = project(rows_one, qkv_full, qkv_bias_own[layer], tables)
        all_kv = [keys_values] + plan.far_keys(keys_values)
        attended, lse = attend(qpos, kpos, queries, all_kv)
        attended_low = meanwhile(attended.astype(LOW), now["out"])
        if layer > 0:
            attended_low = meanwhile(attended_low, now["up"])
        out_full = now["out"].finish()
        mid = stream + plan.sum_rows(times_wide(attended_low, out_full, "out"))
        mid = meanwhile(mid, now["gate"], now["up"])
        if layer > 0:
            mid = meanwhile(mid, now["down"])
        else:
            later, mid = weight_jobs(layer + 1, mid)
        normed_two, unit_two, inverse_two = layer_norm_rows(mid, gains[layer, 1], biases[layer, 1])
        rows_two = plan.gather_rows(normed_two.astype(LOW))
        rows_two = meanwhile(rows_two, now["down"], later.get("qkv"))
        if last:
            moved_cotangent, rows_two = lax.optimization_barrier((moved_cotangent, rows_two))
            grad_stream = moved_cotangent.astype(WIDE)
            branch = plan.gather_rows(grad_stream.astype(LOW))
        flat = lambda v: v.reshape(v.shape[0] * v.shape[1], v.shape[2])
        gate_full, up_full = flat(now["gate"].finish()), flat(now["up"].finish())
        gate, up, activated = gate_up_rows(rows_two, gate_full, up_full)
        if last:
            activated, branch = lax.optimization_barrier((activated, branch))
        activated = meanwhile(activated, later.get("out"), later.get("gate"))
        down_full = now["down"].finish()
        stream = mid + plan.sum_rows(times_wide(activated, down_full, "down"))
        stream = meanwhile(stream, later.get("qkv"), later.get("up"))
        saved.append(
            (
                (qkv_full, out_full, gate_full, up_full, down_full),
                (rows_one, unit_one, inverse_one),
                (queries, all_kv, attended, attended_low, lse),
                (rows_two, unit_two, inverse_two),
                (gate, up, activated),
            )
        )
        now = later
    output = (stream).astype(LOW)[None]

    grad_jobs = [None] * LAYERS
    gain_grads = [None] * LAYERS
    bias_grads = [None] * LAYERS
    qkv_bias_grads = [None] * LAYERS
    for layer in range(LAYERS - 1, -1, -1):
        (
            (qkv_full, out_full, gate_full, up_full, down_full),
            (rows_one, unit_one, inverse_one),
            (queries, all_kv, attended, attended_low, lse),
            (rows_two, unit_two, inverse_two),
            (gate, up, activated),
        ) = saved[layer]
        mine = {}
        grad_jobs[layer] = mine
        above = grad_jobs[layer + 1] if layer + 1 < LAYERS else {}
        old = lambda *keys: [above.get(k) for k in keys]

        def in_job(a, b):
            return Job(grad_stages(plan, dot(a, b, TN), 0))

        def out_job(a, b):
            return Job(grad_stages(plan, dot(a, b, TN), 1))

        if layer + 1 < LAYERS:
            branch = plan.gather_rows(grad_stream.astype(LOW))
        branch = meanwhile(branch, *old("gate", "up", "out"))
        grad_gate, grad_up = gate_up_back(branch, down_full, gate, up)
        mine["down"] = out_job(activated, branch)
        mine["gate"] = in_job(rows_two, grad_gate)
        mine["up"] = in_job(rows_two, grad_up)
        partial_in = gate_up_in(grad_gate, grad_up, gate_full, up_full)
        grad_mid, gain_two, bias_two = norm_backward(
            plan.sum_rows(partial_in), unit_two, inverse_two, gains[layer, 1]
        )
        hidden_grad = grad_stream + grad_mid
        hidden_grad = meanwhile(hidden_grad, *old("up", "out", "qkv"))
        attention = plan.gather_rows(hidden_grad.astype(LOW))
        attention = meanwhile(attention, *old("qkv"))
        attention = held(attention, mine["down"])
        grad_attended = out_back(attention, out_full)
        grad_queries, grad_kv, far_grads = attend_back(
            qpos, kpos, queries, grad_attended, attended, lse, all_kv
        )
        mine["out"] = out_job(attended_low, attention)
        projected, qkv_bias_grads[layer] = project_back(
            grad_queries, grad_kv, plan.far_key_grads(far_grads), tables_back
        )
        projected = meanwhile(projected, mine["down"], mine["gate"])
        partial_in = project_in(projected, qkv_full)
        mine["qkv"] = in_job(rows_one, projected)
        grad_first, gain_one, bias_one = norm_backward(
            plan.sum_rows(partial_in), unit_one, inverse_one, gains[layer, 0]
        )
        grad_stream = hidden_grad + grad_first
        if layer > 0:
            grad_stream = held(meanwhile(grad_stream, mine["down"], mine["gate"]), mine["up"])
        gain_grads[layer] = jnp.stack([gain_one, gain_two])
        bias_grads[layer] = jnp.stack([bias_one, bias_two])

    tokens_grad = (grad_stream).astype(LOW)[None]
    padded_bias = lax.dynamic_update_slice_in_dim(
        jnp.zeros((LAYERS, 3, qkv_bias.shape[2]), WIDE),
        jnp.stack(qkv_bias_grads),
        lax.axis_index("tensor") * heads_width,
        2,
    )
    small = jnp.concatenate(
        [
            (jnp.stack(gain_grads)).reshape(LAYERS * 2, model),
            (jnp.stack(bias_grads)).reshape(LAYERS * 2, model),
            padded_bias.reshape(LAYERS * 3, qkv_bias.shape[2]),
        ],
        axis=0,
    )
    for axis in ("dp", "ctx", "tensor"):
        for bit in bits_of(lax.axis_size(axis)):
            small = small + swapped(small, axis, bit)
    sums = [{k: j.finish() for k, j in g.items()} for g in grad_jobs]
    return (
        output,
        tokens_grad,
        small[: LAYERS * 2].reshape(LAYERS, 2, model),
        small[LAYERS * 2 : LAYERS * 4].reshape(LAYERS, 2, model),
        jnp.stack([s["qkv"].reshape(-1, 3, heads_width) for s in sums]),
        small[LAYERS * 4 :].reshape(LAYERS, 3, qkv_bias.shape[2]),
        jnp.stack([s["out"] for s in sums]),
        jnp.stack([jnp.stack([s["gate"], s["up"]], axis=1) for s in sums]),
        jnp.stack([s["down"] for s in sums]),
    )


def solution(mesh):
    rows = P("dp", ("ctx", "tensor"), None)
    wide = P(None, "dp", None, "tensor")
    tall = P(None, "tensor", "dp")
    return jax.shard_map(
        shards,
        mesh=mesh,
        in_specs=(rows, rows, P(), P(), wide, P(), tall, wide, tall),
        out_specs=(rows, rows, P(), P(), wide, P(), tall, wide, tall),
        check_vma=False,
    )
```

time: 2400 us -> 1240 us (0.52)
  waiting for transfers between devices: 1860 us -> 487 us
  starting transfers between devices: 28.7 us -> 276 us
  matrix products: 273 us -> 61.6 us
  Pallas kernels: 0 us -> 175 us
    all_gather x18 -> x10, waiting for transfers between devices: 677 us -> 19.5 us  [weight_stages(): return (yield lax.all_gather(shard, 'dp'))]
    reduce_scatter x16 -> x10, waiting for transfers between devices: 642 us -> 0.02 us  [grad_stages(): lax.psum_scatter(value.astype(LOW), 'dp', scatter_dimension=axis, tiled=T...]
    psum x2 -> x0, waiting for transfers between devices: 403 us -> none  [the longest x1 295 us: shards(): lax.psum(owned[0].astype(jnp.bfloat16), 'ctx').astype(jnp.float32)]
    ppermute x8 -> x83, waiting for transfers between devices: 139 us -> 466 us  [the longest x32 169 us: sum_rows(): send = lambda v, *route: lax.ppermute(v, 'tensor', list(route))]
    ppermute x8 -> x83, starting transfers between devices: 16.9 us -> 275 us  [the longest x32 124 us: gather_rows(): send = lambda v, *route: lax.ppermute(v, 'tensor', list(route))]
    dot_general x52 -> x10, matrix products: 273 us -> 61.6 us  [dot(): return lax.dot_general(a, b, (dims, ((), ())), preferred_element_type=WIDE)]
    pallas_call x0 -> x22, Pallas kernels: none -> 175 us  [the longest x16 117 us: tiled(): pl.pallas_call(kernel, grid=(steps,), in_specs=[pl.BlockSpec(block, index...]
    another operation x12 -> x15, other arithmetic: 12.7 us -> 46.1 us  [the longest x3 15.3 us: shards(): jnp.stack([jnp.stack([s['gate'], s['up']], axis=1) for s in sums])]
  transfers between devices with their start and end apart: 44 -> 103, of which waited for: 39 -> 52; matrix products, arithmetic and copies ran while one was open for 13% -> 15% of each run, Pallas kernels for 0% -> 14%
where the time goes in v1:
time: 1240 us; the launch traced here: 1230 us
  waiting for transfers between devices  487 us (39%)
  starting transfers between devices  276 us (22%)
  Pallas kernels  175 us (14%)
  local copies, waits for them, and re-layouts  106 us (9%)
  other arithmetic  102 us (8%)
  matrix products  61.6 us (5%)
  between operations  17 us (1%)
    ppermute x32, waiting for transfers between devices, sum_rows(): send = lambda v, *route: lax.ppermute(v, 'tensor', list(route))  169 us
    ppermute x32, waiting for transfers between devices, gather_rows(): send = lambda v, *route: lax.ppermute(v, 'tensor', list(route))  151 us
    ppermute x32, starting transfers between devices, gather_rows(): send = lambda v, *route: lax.ppermute(v, 'tensor', list(route))  124 us
    pallas_call x16, Pallas kernels, tiled(): pl.pallas_call(kernel, grid=(steps,), in_specs=[pl.BlockSpec(block, index...  117 us
    ppermute x32, starting transfers between devices, sum_rows(): send = lambda v, *route: lax.ppermute(v, 'tensor', list(route))  107 us
    ppermute x15, waiting for transfers between devices, swapped(): return lax.ppermute(value, axis, [(i, i ^ mask) for i in range(count)])  75.9 us
    unnamed x251, local copies, waits for them, and re-layouts  67.6 us
    dot_general x10, matrix products, dot(): return lax.dot_general(a, b, (dims, ((), ())), preferred_element_type=WIDE)  61.6 us
  transfers between devices with their start and end apart: 103, of which 52 were waited for; matrix products, arithmetic and copies ran while one was open for 15% of the time, Pallas kernels for 14%

profile of v1, /device:TPU:0, one launch (start us, length us, event | category | flops | bytes accessed | tf_op | source)
XLA Modules:
  0.0 1225.2 jit_solution(2681059164229950120)
XLA Ops:
  30.1 16.3 %collective-permute-done = bf16[128,2048]{1,0:T(8,128)(2,1)} collective-permute-done((bf16[128,2048]{1,0:T(8,128)(2,1)S(1)}, bf16[128,2048]{1,0:T(8,128)(2,1)}, u32[]{:S(2)}, u32[]{:S(2)}) %collective-permute-start) | collective-permute-done | bytes 524320 | tf_op jit(solution)/shard_map/ppermute | solution.py:474
  50.3 10.5 collective-permute-done.1
  62.3 8.2 project.2
  75.6 19.2 %collective-permute-done.4.refs_2_.refs_3_ = bf16[1024,512]{1,0:T(8,128)(2,1)} collective-permute-done((bf16[1024,512]{1,0:T(8,128)(2,1)}, bf16[1024,512]{1,0:T(8,128)(2,1)}, u32[]{:S(2)}, u32[]{:S(2)}) %collective-permute-start.4) | collective-permute-done | bytes 1048608 | tf_op jit(solution)/shard_map/ppermute | solution.py:515
  95.8 10.7 attend.2
  141.1 13.3 %collective-permute-done.6 = bf16[128,2048]{1,0:T(8,128)(2,1)S(1)} collective-permute-done((bf16[128,2048]{1,0:T(8,128)(2,1)S(1)}, bf16[128,2048]{1,0:T(8,128)(2,1)S(1)}, u32[]{:S(2)}, u32[]{:S(2)}) %collective-permute-start.6) | collective-permute-done | bytes 524320 | tf_op jit(solution)/shard_map/ppermute | solution.py:490
  155.7 19.4 %all-gather.26.cloned.1.call-done = bf16[4,512,1,1408]{3,1,2,0:T(8,128)(2,1)} async-done(((bf16[1,512,1,1408]{3,1,2,0:T(8,128)(2,1)}), bf16[4,512,1,1408]{3,1,2,0:T(8,128)(2,1)}) %all-gather.26.cloned.1.call-update) | async-done | bytes 5767184 | tf_op jit(solution)/shard_map/all_gather | solution.py:529
  188.5 18.0 %collective-permute-done.9 = bf16[128,2048]{1,0:T(8,128)(2,1)} collective-permute-done((bf16[128,2048]{1,0:T(8,128)(2,1)S(1)}, bf16[128,2048]{1,0:T(8,128)(2,1)}, u32[]{:S(2)}, u32[]{:S(2)}) %collective-permute-start.9) | collective-permute-done | bytes 524320 | tf_op jit(solution)/shard_map/ppermute | solution.py:474
  210.6 10.8 collective-permute-done.10
  236.9 11.5 gate_up.2
  251.8 7.7 down.2
  284.9 14.2 %collective-permute-done.14 = bf16[128,2048]{1,0:T(8,128)(2,1)S(1)} collective-permute-done((bf16[128,2048]{1,0:T(8,128)(2,1)S(1)}, bf16[128,2048]{1,0:T(8,128)(2,1)S(1)}, u32[]{:S(2)}, u32[]{:S(2)}) %collective-permute-start.14) | collective-permute-done | bytes 524320 | tf_op jit(solution)/shard_map/ppermute | solution.py:490
  306.4 8.5 collective-permute-start.20
  314.9 16.4 %collective-permute-done.17 = bf16[128,2048]{1,0:T(8,128)(2,1)} collective-permute-done((bf16[128,2048]{1,0:T(8,128)(2,1)S(1)}, bf16[128,2048]{1,0:T(8,128)(2,1)}, u32[]{:S(2)}, u32[]{:S(2)}) %collective-permute-start.17) | collective-permute-done | bytes 524320 | tf_op jit(solution)/shard_map/ppermute | solution.py:474
  335.2 7.4 collective-permute-done.18
  348.3 7.6 project.3
  359.2 17.5 %collective-permute-done.21.refs_2_.refs_3_ = bf16[1024,512]{1,0:T(8,128)(2,1)S(1)} collective-permute-done((bf16[1024,512]{1,0:T(8,128)(2,1)S(1)}, bf16[1024,512]{1,0:T(8,128)(2,1)S(1)}, u32[]{:S(2)}, u32[]{:S(2)}) %collective-permute-start.21) | collective-permute-done | bytes 1048608 | tf_op jit(solution)/shard_map/ppermute | solution.py:515
  376.7 9.9 attend.3
  410.5 10.7 collective-permute-start.23
  421.6 9.6 collective-permute-done.23
  442.5 24.3 %collective-permute-start.29 = (bf16[128,2048]{1,0:T(8,128)(2,1)S(1)}, bf16[128,2048]{1,0:T(8,128)(2,1)S(1)}, u32[]{:S(2)}, u32[]{:S(2)}) collective-permute-start(bf16[128,2048]{1,0:T(8,128)(2,1)S(1)} %add_convert_fusion.6), channel_id=1, source_target_pairs={{0,1},{1,2},{2,3},{4,5},{5,6},{6,7},{8,9},{9,10},{10,11},{12,13},{... | collective-permute-start | bytes 1572872 | tf_op jit(solution)/shard_map/ppermute | solution.py:474
  480.0 9.1 collective-permute-start.30
  495.4 13.3 %collective-permute-done.30 = bf16[128,2048]{1,0:T(8,128)(2,1)S(1)} collective-permute-done((bf16[128,2048]{1,0:T(8,128)(2,1)S(1)}, bf16[128,2048]{1,0:T(8,128)(2,1)S(1)}, u32[]{:S(2)}, u32[]{:S(2)}) %collective-permute-start.30) | collective-permute-done | bytes 524320 | tf_op jit(solution)/shard_map/ppermute | solution.py:474
  510.0 11.4 gate_up.3
  530.5 8.6 gate_up_back.2
  546.7 8.0 convolution_convert_fusion.5
  557.5 10.6 gate_up_in.2
  573.4 7.7 down.3
  599.8 8.0 collective-permute-done.41
  610.1 10.5 collective-permute-done.39
  621.3 7.5 collective-permute-done.36
  628.7 21.3 %collective-permute-done.35 = bf16[128,2048]{1,0:T(8,128)(2,1)S(1)} collective-permute-done((bf16[128,2048]{1,0:T(8,128)(2,1)S(1)}, bf16[128,2048]{1,0:T(8,128)(2,1)S(1)}, u32[]{:S(2)}, u32[]{:S(2)}) %collective-permute-start.35) | collective-permute-done | bytes 524320 | tf_op jit(solution)/shard_map/ppermute | solution.py:490
  653.3 20.9 %collective-permute-start.45 = (bf16[128,2048]{1,0:T(8,128)(2,1)S(1)}, bf16[128,2048]{1,0:T(8,128)(2,1)S(1)}, u32[]{:S(2)}, u32[]{:S(2)}) collective-permute-start(bf16[128,2048]{1,0:T(8,128)(2,1)S(1)} %get-tuple-element.235), channel_id=1, source_target_pairs={{0,1},{1,2},{2,3},{4,5},{5,6},{6,7},{8,9},{9,10},{10,11},{12,13},{... | collective-permute-start | bytes 1572872 | tf_op jit(solution)/shard_map/ppermute | solution.py:474
  675.6 7.4 collective-permute-done.44
  700.3 16.4 %attend_back.2 = (f32[512,512]{1,0:T(8,128)S(1)}, f32[1024,512]{1,0:T(8,128)S(1)}, bf16[1024,512]{1,0:T(8,128)(2,1)S(1)}) custom-call(s32[512,1]{1,0:T(8,128)S(1)} %copy-done.23, s32[2,1,512]{2,1,0:T(1,128)S(1)} %broadcast_in_dim.17.kpos_ref, bf16[512,512]{1,0:T(8,128)(2,1)S(1)} %copy-done.61, bf16[512,512]{1,0:T(8,128)(2,1)S(1)} %out_back.2.grad_ref, ...), custom_call_target="tpu_custom_call" | custom-call | flops 20132659200 | tf_op jit(solution)/shard_map/attend_back/pallas_call | solution.py:427
  718.4 18.4 %collective-permute-done.46.refs_0_ = bf16[1024,512]{1,0:T(8,128)(2,1)S(1)} collective-permute-done((bf16[1024,512]{1,0:T(8,128)(2,1)S(1)}, bf16[1024,512]{1,0:T(8,128)(2,1)S(1)}, u32[]{:S(2)}, u32[]{:S(2)}) %collective-permute-start.46) | collective-permute-done | bytes 1048608 | tf_op jit(solution)/shard_map/ppermute | solution.py:522
  740.3 8.2 convolution_convert_fusion.4
  750.0 7.9 project_in.2
  773.5 9.0 collective-permute-start.48
  784.6 12.5 %collective-permute-done.48 = bf16[128,2048]{1,0:T(8,128)(2,1)S(1)} collective-permute-done((bf16[128,2048]{1,0:T(8,128)(2,1)S(1)}, bf16[128,2048]{1,0:T(8,128)(2,1)S(1)}, u32[]{:S(2)}, u32[]{:S(2)}) %collective-permute-start.48) | collective-permute-done | bytes 524320 | tf_op jit(solution)/shard_map/ppermute | solution.py:490
  798.3 18.4 %collective-permute-done.51 = bf16[1408,512]{1,0:T(8,128)(2,1)S(1)} collective-permute-done((bf16[1408,512]{1,0:T(8,128)(2,1)S(1)}, bf16[1408,512]{1,0:T(8,128)(2,1)S(1)}, u32[]{:S(2)}, u32[]{:S(2)}) %collective-permute-start.51) | collective-permute-done | bytes 1441824 | tf_op jit(solution)/shard_map/ppermute | solution.py:454
  817.8 14.5 %collective-permute-done.52 = bf16[512,1408]{1,0:T(8,128)(2,1)} collective-permute-done((bf16[512,1408]{1,0:T(8,128)(2,1)S(1)}, bf16[512,1408]{1,0:T(8,128)(2,1)}, u32[]{:S(2)}, u32[]{:S(2)}) %collective-permute-start.52) | collective-permute-done | bytes 1441824 | tf_op jit(solution)/shard_map/ppermute | solution.py:454
  838.7 9.3 collective-permute-done.53
  852.2 6.8 collective-permute-done.54
  860.7 7.8 convolution_convert_fusion.3
  870.3 8.3 gate_up_back.3
  886.4 8.2 convolution_convert_fusion
  897.8 10.6 gate_up_in.3
  916.6 6.4 collective-permute-done.57
  929.1 10.0 collective-permute-done.58
  940.3 22.0 %collective-permute-done.62 = bf16[512,512]{1,0:T(8,128)(2,1)S(1)} collective-permute-done((bf16[512,512]{1,0:T(8,128)(2,1)S(1)}, bf16[512,512]{1,0:T(8,128)(2,1)S(1)}, u32[]{:S(2)}, u32[]{:S(2)}) %collective-permute-start.62) | collective-permute-done | bytes 524320 | tf_op jit(solution)/shard_map/ppermute | solution.py:454
  984.2 7.8 collective-permute-done.64
  999.3 17.6 %attend_back.3 = (f32[512,512]{1,0:T(8,128)S(1)}, f32[1024,512]{1,0:T(8,128)S(1)}, bf16[1024,512]{1,0:T(8,128)(2,1)S(1)}) custom-call(s32[512,1]{1,0:T(8,128)S(1)} %copy-done.24, s32[2,1,512]{2,1,0:T(1,128)S(1)} %broadcast_in_dim.17.kpos_ref, bf16[512,512]{1,0:T(8,128)(2,1)S(1)} %copy-done.59, bf16[512,512]{1,0:T(8,128)(2,1)S(1)} %out_back.3.grad_ref, ...), custom_call_target="tpu_custom_call" | custom-call | flops 20132659200 | tf_op jit(solution)/shard_map/attend_back/pallas_call | solution.py:427
  1018.2 15.4 %collective-permute-done.68.refs_0_ = bf16[1024,512]{1,0:T(8,128)(2,1)S(1)} collective-permute-done((bf16[1024,512]{1,0:T(8,128)(2,1)S(1)}, bf16[1024,512]{1,0:T(8,128)(2,1)S(1)}, u32[]{:S(2)}, u32[]{:S(2)}) %collective-permute-start.68) | collective-permute-done | bytes 1048608 | tf_op jit(solution)/shard_map/ppermute | solution.py:522
  1036.6 6.8 convolution_convert_fusion.1
  1064.0 8.0 project_in.3
  1095.3 10.7 collective-permute-done.70
  1110.4 18.4 %collective-permute-start.74 = (f32[14,2048]{1,0:T(8,128)S(1)}, f32[14,2048]{1,0:T(8,128)S(1)}, u32[]{:S(2)}, u32[]{:S(2)}) collective-permute-start(f32[14,2048]{1,0:T(8,128)S(1)} %fusion.23), channel_id=1, source_target_pairs={{0,16},{8,24},{16,0},{24,8},{1,17},{9,25},{17,1},{25,9},{2,18},{10... | collective-permute-start | bytes 344072 | tf_op jit(solution)/shard_map/ppermute | solution.py:454
  1136.3 9.8 collective-permute-done.75
  1156.3 9.5 pad_maximum_fusion
  1169.9 6.4 pad_maximum_fusion.2
  1178.0 10.0 copy.68
  1204.4 6.9 pad_maximum_fusion.1
  1211.3 6.6 copy.66
  (595 shorter events, 463.6 us)
Async XLA Ops:
  7.2 55.1 %all-gather.22.cloned.1.call-start = ((), (), s32[]{:S(2)}) async-start(), calls=%async_computation.21 | async-start | bytes 7864320 | tf_op jit(solution)/shard_map/all_gather | solution.py:529
  10.0 99.0 %all-gather.20.cloned.1.call-start = ((), (), s32[]{:S(2)}) async-start(), calls=%async_computation.10 | async-start | bytes 2621440 | tf_op jit(solution)/shard_map/all_gather | solution.py:529
  10.9 144.8 %all-gather.24.cloned.1.call-start = ((), (), s32[]{:S(2)}) async-start(), calls=%async_computation.22 | async-start | bytes 7208960 | tf_op jit(solution)/shard_map/all_gather | solution.py:529
  16.1 158.9 %all-gather.26.cloned.1.call-start = ((), (), s32[]{:S(2)}) async-start(), calls=%async_computation.23 | async-start | bytes 7208960 | tf_op jit(solution)/shard_map/all_gather | solution.py:529
  16.7 208.6 %all-gather.28.cloned.1.call-start = ((), (), s32[]{:S(2)}) async-start(), calls=%async_computation.24 | async-start | bytes 7208960 | tf_op jit(solution)/shard_map/all_gather | solution.py:529
  18.3 28.2 %collective-permute-start = (bf16[128,2048]{1,0:T(8,128)(2,1)S(1)}, bf16[128,2048]{1,0:T(8,128)(2,1)}, u32[]{:S(2)}, u32[]{:S(2)}) collective-permute-start(bf16[128,2048]{1,0:T(8,128)(2,1)S(1)} %fusion.9), channel_id=1, source_target_pairs={{0,2},{2,0},{1,3},{3,1},{4,6},{6,4},{5,7},{7,5},{8,10},{10,8},{9,1... | collective-permute-start | bytes 1572872 | tf_op jit(solution)/shard_map/ppermute | solution.py:474
  22.3 28.0 %collective-permute-start.2 = (bf16[128,2048]{1,0:T(8,128)(2,1)S(1)}, bf16[128,2048]{1,0:T(8,128)(2,1)S(1)}, u32[]{:S(2)}, u32[]{:S(2)}) collective-permute-start(bf16[128,2048]{1,0:T(8,128)(2,1)S(1)} %fusion.9), channel_id=1, source_target_pairs={{1,0},{2,1},{3,2},{5,4},{6,5},{7,6},{9,8},{10,9},{11,10},{13,12},{... | collective-permute-start | bytes 1572872 | tf_op jit(solution)/shard_map/ppermute | solution.py:474
  23.6 26.7 %collective-permute-start.3 = (bf16[128,2048]{1,0:T(8,128)(2,1)S(1)}, bf16[128,2048]{1,0:T(8,128)(2,1)S(1)}, u32[]{:S(2)}, u32[]{:S(2)}) collective-permute-start(bf16[128,2048]{1,0:T(8,128)(2,1)S(1)} %fusion.9), channel_id=1, source_target_pairs={{0,1},{1,2},{2,3},{4,5},{5,6},{6,7},{8,9},{9,10},{10,11},{12,13},{... | collective-permute-start | bytes 1572872 | tf_op jit(solution)/shard_map/ppermute | solution.py:474
  62.3 238.2 %all-gather.30.cloned.1.call-start = ((), (), s32[]{:S(2)}) async-start(), calls=%async_computation.25 | async-start | bytes 7864320 | tf_op jit(solution)/shard_map/all_gather | solution.py:529
  71.4 23.4 %collective-permute-start.4 = (bf16[1024,512]{1,0:T(8,128)(2,1)}, bf16[1024,512]{1,0:T(8,128)(2,1)}, u32[]{:S(2)}, u32[]{:S(2)}) collective-permute-start(bf16[1024,512]{1,0:T(8,128)(2,1)} %get-tuple-element.104.refs_0_.refs_1_), channel_id=1, source_target_pairs={{0,4},{1,5},{2,6},{3,7},{8,12},{9,13},{10,14},{11,15},{16,20},{17,... | collective-permute-start | bytes 3145736 | tf_op jit(solution)/shard_map/ppermute | solution.py:515
  118.8 22.3 %collective-permute-start.7 = (bf16[128,2048]{1,0:T(8,128)(2,1)S(1)}, bf16[128,2048]{1,0:T(8,128)(2,1)S(1)}, u32[]{:S(2)}, u32[]{:S(2)}) collective-permute-start(bf16[128,2048]{1,0:T(8,128)(2,1)S(1)} %get-tuple-element.264), channel_id=1, source_target_pairs={{0,1},{1,2},{2,3},{4,5},{5,6},{6,7},{8,9},{9,10},{10,11},{12,13},{... | collective-permute-start | bytes 1572872 | tf_op jit(solution)/shard_map/ppermute | solution.py:490
  129.9 24.4 %collective-permute-start.6 = (bf16[128,2048]{1,0:T(8,128)(2,1)S(1)}, bf16[128,2048]{1,0:T(8,128)(2,1)S(1)}, u32[]{:S(2)}, u32[]{:S(2)}) collective-permute-start(bf16[128,2048]{1,0:T(8,128)(2,1)S(1)} %add_convert_fusion.11), channel_id=1, source_target_pairs={{0,2},{2,0},{1,3},{3,1},{4,6},{6,4},{5,7},{7,5},{8,10},{10,8},{9,1... | collective-permute-start | bytes 1572872 | tf_op jit(solution)/shard_map/ppermute | solution.py:490
  179.4 27.1 %collective-permute-start.9 = (bf16[128,2048]{1,0:T(8,128)(2,1)S(1)}, bf16[128,2048]{1,0:T(8,128)(2,1)}, u32[]{:S(2)}, u32[]{:S(2)}) collective-permute-start(bf16[128,2048]{1,0:T(8,128)(2,1)S(1)} %add_convert_fusion.10), channel_id=1, source_target_pairs={{0,2},{2,0},{1,3},{3,1},{4,6},{6,4},{5,7},{7,5},{8,10},{10,8},{9,1... | collective-permute-start | bytes 1572872 | tf_op jit(solution)/shard_map/ppermute | solution.py:474
  181.9 28.6 %collective-permute-start.11 = (bf16[128,2048]{1,0:T(8,128)(2,1)S(1)}, bf16[128,2048]{1,0:T(8,128)(2,1)}, u32[]{:S(2)}, u32[]{:S(2)}) collective-permute-start(bf16[128,2048]{1,0:T(8,128)(2,1)S(1)} %add_convert_fusion.10), channel_id=1, source_target_pairs={{1,0},{2,1},{3,2},{5,4},{6,5},{7,6},{9,8},{10,9},{11,10},{13,12},{... | collective-permute-start | bytes 1572872 | tf_op jit(solution)/shard_map/ppermute | solution.py:474
  183.2 27.4 %collective-permute-start.12 = (bf16[128,2048]{1,0:T(8,128)(2,1)S(1)}, bf16[128,2048]{1,0:T(8,128)(2,1)}, u32[]{:S(2)}, u32[]{:S(2)}) collective-permute-start(bf16[128,2048]{1,0:T(8,128)(2,1)S(1)} %add_convert_fusion.10), channel_id=1, source_target_pairs={{0,1},{1,2},{2,3},{4,5},{5,6},{6,7},{8,9},{9,10},{10,11},{12,13},{... | collective-permute-start | bytes 1572872 | tf_op jit(solution)/shard_map/ppermute | solution.py:474
  225.3 121.3 %all-gather.32.cloned.1.call-start = ((), (), s32[]{:S(2)}) async-start(), calls=%async_computation.26 | async-start | bytes 2621440 | tf_op jit(solution)/shard_map/all_gather | solution.py:529
  249.6 97.0 %all-gather.34.cloned.1.call-start = ((), (), s32[]{:S(2)}) async-start(), calls=%async_computation.27 | async-start | bytes 7208960 | tf_op jit(solution)/shard_map/all_gather | solution.py:529
  250.3 138.5 %all-gather.36.cloned.1.call-start = ((), (), s32[]{:S(2)}) async-start(), calls=%async_computation.28 | async-start | bytes 7208960 | tf_op jit(solution)/shard_map/all_gather | solution.py:529
  262.6 22.3 %collective-permute-start.15 = (bf16[128,2048]{1,0:T(8,128)(2,1)S(1)}, bf16[128,2048]{1,0:T(8,128)(2,1)S(1)}, u32[]{:S(2)}, u32[]{:S(2)}) collective-permute-start(bf16[128,2048]{1,0:T(8,128)(2,1)S(1)} %get-tuple-element.261), channel_id=1, source_target_pairs={{0,1},{1,2},{2,3},{4,5},{5,6},{6,7},{8,9},{9,10},{10,11},{12,13},{... | collective-permute-start | bytes 1572872 | tf_op jit(solution)/shard_map/ppermute | solution.py:490
  273.8 25.3 %collective-permute-start.14 = (bf16[128,2048]{1,0:T(8,128)(2,1)S(1)}, bf16[128,2048]{1,0:T(8,128)(2,1)S(1)}, u32[]{:S(2)}, u32[]{:S(2)}) collective-permute-start(bf16[128,2048]{1,0:T(8,128)(2,1)S(1)} %add_convert_fusion.9), channel_id=1, source_target_pairs={{0,2},{2,0},{1,3},{3,1},{4,6},{6,4},{5,7},{7,5},{8,10},{10,8},{9,1... | collective-permute-start | bytes 1572872 | tf_op jit(solution)/shard_map/ppermute | solution.py:490
  300.5 132.1 %all-gather.38.cloned.1.call-start = ((), (), s32[]{:S(2)}) async-start(), calls=%async_computation.29 | async-start | bytes 7208960 | tf_op jit(solution)/shard_map/all_gather | solution.py:529
  305.0 26.3 %collective-permute-start.17 = (bf16[128,2048]{1,0:T(8,128)(2,1)S(1)}, bf16[128,2048]{1,0:T(8,128)(2,1)}, u32[]{:S(2)}, u32[]{:S(2)}) collective-permute-start(bf16[128,2048]{1,0:T(8,128)(2,1)S(1)} %add_convert_fusion.8), channel_id=1, source_target_pairs={{0,2},{2,0},{1,3},{3,1},{4,6},{6,4},{5,7},{7,5},{8,10},{10,8},{9,1... | collective-permute-start | bytes 1572872 | tf_op jit(solution)/shard_map/ppermute | solution.py:474
  305.1 30.1 %collective-permute-start.19 = (bf16[128,2048]{1,0:T(8,128)(2,1)S(1)}, bf16[128,2048]{1,0:T(8,128)(2,1)}, u32[]{:S(2)}, u32[]{:S(2)}) collective-permute-start(bf16[128,2048]{1,0:T(8,128)(2,1)S(1)} %add_convert_fusion.8), channel_id=1, source_target_pairs={{1,0},{2,1},{3,2},{5,4},{6,5},{7,6},{9,8},{10,9},{11,10},{13,12},{... | collective-permute-start | bytes 1572872 | tf_op jit(solution)/shard_map/ppermute | solution.py:474
  306.4 28.8 %collective-permute-start.20 = (bf16[128,2048]{1,0:T(8,128)(2,1)S(1)}, bf16[128,2048]{1,0:T(8,128)(2,1)}, u32[]{:S(2)}, u32[]{:S(2)}) collective-permute-start(bf16[128,2048]{1,0:T(8,128)(2,1)S(1)} %add_convert_fusion.8), channel_id=1, source_target_pairs={{0,1},{1,2},{2,3},{4,5},{5,6},{6,7},{8,9},{9,10},{10,11},{12,13},{... | collective-permute-start | bytes 1572872 | tf_op jit(solution)/shard_map/ppermute | solution.py:474
  346.7 343.6 %reduce-scatter.11.cloned.1.call-start = ((), (), s32[]{:S(2)}) async-start(), calls=%async_computation.11 | async-start | bytes 7208960 | tf_op jit(solution)/shard_map/reduce_scatter | solution.py:533
  398.1 23.2 %collective-permute-start.25 = (bf16[128,2048]{1,0:T(8,128)(2,1)S(1)}, bf16[128,2048]{1,0:T(8,128)(2,1)S(1)}, u32[]{:S(2)}, u32[]{:S(2)}) collective-permute-start(bf16[128,2048]{1,0:T(8,128)(2,1)S(1)} %get-tuple-element.259), channel_id=1, source_target_pairs={{3,2},{2,1},{1,0},{7,6},{6,5},{5,4},{11,10},{10,9},{9,8},{15,14},{... | collective-permute-start | bytes 1572872 | tf_op jit(solution)/shard_map/ppermute | solution.py:490
  399.4 22.3 %collective-permute-start.24 = (bf16[128,2048]{1,0:T(8,128)(2,1)S(1)}, bf16[128,2048]{1,0:T(8,128)(2,1)S(1)}, u32[]{:S(2)}, u32[]{:S(2)}) collective-permute-start(bf16[128,2048]{1,0:T(8,128)(2,1)S(1)} %get-tuple-element.258), channel_id=1, source_target_pairs={{0,1},{1,2},{2,3},{4,5},{5,6},{6,7},{8,9},{9,10},{10,11},{12,13},{... | collective-permute-start | bytes 1572872 | tf_op jit(solution)/shard_map/ppermute | solution.py:490
  437.0 29.9 %collective-permute-start.26 = (bf16[128,2048]{1,0:T(8,128)(2,1)S(1)}, bf16[128,2048]{1,0:T(8,128)(2,1)S(1)}, u32[]{:S(2)}, u32[]{:S(2)}) collective-permute-start(bf16[128,2048]{1,0:T(8,128)(2,1)S(1)} %add_convert_fusion.6), channel_id=1, source_target_pairs={{0,2},{2,0},{1,3},{3,1},{4,6},{6,4},{5,7},{7,5},{8,10},{10,8},{9,1... | collective-permute-start | bytes 1572872 | tf_op jit(solution)/shard_map/ppermute | solution.py:474
  441.2 31.3 %collective-permute-start.28 = (bf16[128,2048]{1,0:T(8,128)(2,1)S(1)}, bf16[128,2048]{1,0:T(8,128)(2,1)S(1)}, u32[]{:S(2)}, u32[]{:S(2)}) collective-permute-start(bf16[128,2048]{1,0:T(8,128)(2,1)S(1)} %add_convert_fusion.6), channel_id=1, source_target_pairs={{1,0},{2,1},{3,2},{5,4},{6,5},{7,6},{9,8},{10,9},{11,10},{13,12},{... | collective-permute-start | bytes 1572872 | tf_op jit(solution)/shard_map/ppermute | solution.py:474
  442.5 31.0 %collective-permute-start.29 = (bf16[128,2048]{1,0:T(8,128)(2,1)S(1)}, bf16[128,2048]{1,0:T(8,128)(2,1)S(1)}, u32[]{:S(2)}, u32[]{:S(2)}) collective-permute-start(bf16[128,2048]{1,0:T(8,128)(2,1)S(1)} %add_convert_fusion.6), channel_id=1, source_target_pairs={{0,1},{1,2},{2,3},{4,5},{5,6},{6,7},{8,9},{9,10},{10,11},{12,13},{... | collective-permute-start | bytes 1572872 | tf_op jit(solution)/shard_map/ppermute | solution.py:474
  480.0 28.7 %collective-permute-start.30 = (bf16[128,2048]{1,0:T(8,128)(2,1)S(1)}, bf16[128,2048]{1,0:T(8,128)(2,1)S(1)}, u32[]{:S(2)}, u32[]{:S(2)}) collective-permute-start(bf16[128,2048]{1,0:T(8,128)(2,1)S(1)} %bitcast.160), channel_id=1, source_target_pairs={{0,2},{2,0},{1,3},{3,1},{4,6},{6,4},{5,7},{7,5},{8,10},{10,8},{9,1... | collective-permute-start | bytes 1572872 | tf_op jit(solution)/shard_map/ppermute | solution.py:474
  489.1 32.3 %collective-permute-start.32 = (bf16[128,2048]{1,0:T(8,128)(2,1)S(1)}, bf16[128,2048]{1,0:T(8,128)(2,1)S(1)}, u32[]{:S(2)}, u32[]{:S(2)}) collective-permute-start(bf16[128,2048]{1,0:T(8,128)(2,1)S(1)} %bitcast.161), channel_id=1, source_target_pairs={{1,0},{2,1},{3,2},{5,4},{6,5},{7,6},{9,8},{10,9},{11,10},{13,12},{... | collective-permute-start | bytes 1572872 | tf_op jit(solution)/shard_map/ppermute | solution.py:474
  490.4 31.0 %collective-permute-start.33 = (bf16[128,2048]{1,0:T(8,128)(2,1)S(1)}, bf16[128,2048]{1,0:T(8,128)(2,1)S(1)}, u32[]{:S(2)}, u32[]{:S(2)}) collective-permute-start(bf16[128,2048]{1,0:T(8,128)(2,1)S(1)} %bitcast.162), channel_id=1, source_target_pairs={{0,1},{1,2},{2,3},{4,5},{5,6},{6,7},{8,9},{9,10},{10,11},{12,13},{... | collective-permute-start | bytes 1572872 | tf_op jit(solution)/shard_map/ppermute | solution.py:474
  528.9 211.4 %reduce-scatter.13.cloned.1.call-start = ((), (), s32[]{:S(2)}) async-start(), calls=%async_computation.12 | async-start | bytes 7208960 | tf_op jit(solution)/shard_map/reduce_scatter | solution.py:533
  546.6 285.6 %reduce-scatter.15.cloned.1.call-start = ((), (), s32[]{:S(2)}) async-start(), calls=%async_computation.13 | async-start | bytes 7208960 | tf_op jit(solution)/shard_map/reduce_scatter | solution.py:533
  554.7 306.0 %reduce-scatter.17.cloned.1.call-start = ((), (), s32[]{:S(2)}) async-start(), calls=%async_computation.14 | async-start | bytes 2621440 | tf_op jit(solution)/shard_map/reduce_scatter | solution.py:533
  582.7 25.1 %collective-permute-start.41 = (bf16[128,2048]{1,0:T(8,128)(2,1)S(1)}, bf16[128,2048]{1,0:T(8,128)(2,1)S(1)}, u32[]{:S(2)}, u32[]{:S(2)}) collective-permute-start(bf16[128,2048]{1,0:T(8,128)(2,1)S(1)} %get-tuple-element.253), channel_id=1, source_target_pairs={{3,2},{2,1},{1,0},{7,6},{6,5},{5,4},{11,10},{10,9},{9,8},{15,14},{... | collective-permute-start | bytes 1572872 | tf_op jit(solution)/shard_map/ppermute | solution.py:490
  584.0 26.1 %collective-permute-start.40 = (bf16[128,2048]{1,0:T(8,128)(2,1)S(1)}, bf16[128,2048]{1,0:T(8,128)(2,1)S(1)}, u32[]{:S(2)}, u32[]{:S(2)}) collective-permute-start(bf16[128,2048]{1,0:T(8,128)(2,1)S(1)} %get-tuple-element.252), channel_id=1, source_target_pairs={{0,1},{1,2},{2,3},{4,5},{5,6},{6,7},{8,9},{9,10},{10,11},{12,13},{... | collective-permute-start | bytes 1572872 | tf_op jit(solution)/shard_map/ppermute | solution.py:490
  588.7 31.9 %collective-permute-start.39 = (bf16[128,2048]{1,0:T(8,128)(2,1)S(1)}, bf16[128,2048]{1,0:T(8,128)(2,1)S(1)}, u32[]{:S(2)}, u32[]{:S(2)}) collective-permute-start(bf16[128,2048]{1,0:T(8,128)(2,1)S(1)} %add_convert_fusion.3), channel_id=1, source_target_pairs={{0,2},{2,0},{1,3},{3,1},{4,6},{6,4},{5,7},{7,5},{8,10},{10,8},{9,1... | collective-permute-start | bytes 1572872 | tf_op jit(solution)/shard_map/ppermute | solution.py:490
  589.5 31.8 %collective-permute-start.37 = (bf16[128,2048]{1,0:T(8,128)(2,1)S(1)}, bf16[128,2048]{1,0:T(8,128)(2,1)S(1)}, u32[]{:S(2)}, u32[]{:S(2)}) collective-permute-start(bf16[128,2048]{1,0:T(8,128)(2,1)S(1)} %get-tuple-element.256), channel_id=1, source_target_pairs={{3,2},{2,1},{1,0},{7,6},{6,5},{5,4},{11,10},{10,9},{9,8},{15,14},{... | collective-permute-start | bytes 1572872 | tf_op jit(solution)/shard_map/ppermute | solution.py:490
  595.0 33.8 %collective-permute-start.36 = (bf16[128,2048]{1,0:T(8,128)(2,1)S(1)}, bf16[128,2048]{1,0:T(8,128)(2,1)S(1)}, u32[]{:S(2)}, u32[]{:S(2)}) collective-permute-start(bf16[128,2048]{1,0:T(8,128)(2,1)S(1)} %get-tuple-element.255), channel_id=1, source_target_pairs={{0,1},{1,2},{2,3},{4,5},{5,6},{6,7},{8,9},{9,10},{10,11},{12,13},{... | collective-permute-start | bytes 1572872 | tf_op jit(solution)/shard_map/ppermute | solution.py:490
  607.8 42.3 %collective-permute-start.35 = (bf16[128,2048]{1,0:T(8,128)(2,1)S(1)}, bf16[128,2048]{1,0:T(8,128)(2,1)S(1)}, u32[]{:S(2)}, u32[]{:S(2)}) collective-permute-start(bf16[128,2048]{1,0:T(8,128)(2,1)S(1)} %add_convert_fusion.5), channel_id=1, source_target_pairs={{0,2},{2,0},{1,3},{3,1},{4,6},{6,4},{5,7},{7,5},{8,10},{10,8},{9,1... | collective-permute-start | bytes 1572872 | tf_op jit(solution)/shard_map/ppermute | solution.py:490
  652.0 30.9 %collective-permute-start.44 = (bf16[128,2048]{1,0:T(8,128)(2,1)S(1)}, bf16[128,2048]{1,0:T(8,128)(2,1)S(1)}, u32[]{:S(2)}, u32[]{:S(2)}) collective-permute-start(bf16[128,2048]{1,0:T(8,128)(2,1)S(1)} %get-tuple-element.235), channel_id=1, source_target_pairs={{1,0},{2,1},{3,2},{5,4},{6,5},{7,6},{9,8},{10,9},{11,10},{13,12},{... | collective-permute-start | bytes 1572872 | tf_op jit(solution)/shard_map/ppermute | solution.py:474
  653.3 29.6 %collective-permute-start.45 = (bf16[128,2048]{1,0:T(8,128)(2,1)S(1)}, bf16[128,2048]{1,0:T(8,128)(2,1)S(1)}, u32[]{:S(2)}, u32[]{:S(2)}) collective-permute-start(bf16[128,2048]{1,0:T(8,128)(2,1)S(1)} %get-tuple-element.235), channel_id=1, source_target_pairs={{0,1},{1,2},{2,3},{4,5},{5,6},{6,7},{8,9},{9,10},{10,11},{12,13},{... | collective-permute-start | bytes 1572872 | tf_op jit(solution)/shard_map/ppermute | solution.py:474
  694.6 268.5 %reduce-scatter.19.cloned.1.call-start = ((), (), s32[]{:S(2)}) async-start(), calls=%async_computation.15 | async-start | bytes 7864320 | tf_op jit(solution)/shard_map/reduce_scatter | solution.py:533
  748.6 245.1 %reduce-scatter.21.cloned.1.call-start = ((), (), s32[]{:S(2)}) async-start(), calls=%async_computation.16 | async-start | bytes 7208960 | tf_op jit(solution)/shard_map/reduce_scatter | solution.py:533
  761.1 23.5 %collective-permute-start.50 = (bf16[128,2048]{1,0:T(8,128)(2,1)S(1)}, bf16[128,2048]{1,0:T(8,128)(2,1)S(1)}, u32[]{:S(2)}, u32[]{:S(2)}) collective-permute-start(bf16[128,2048]{1,0:T(8,128)(2,1)S(1)} %get-tuple-element.250), channel_id=1, source_target_pairs={{3,2},{2,1},{1,0},{7,6},{6,5},{5,4},{11,10},{10,9},{9,8},{15,14},{... | collective-permute-start | bytes 1572872 | tf_op jit(solution)/shard_map/ppermute | solution.py:490
  773.5 23.5 %collective-permute-start.48 = (bf16[128,2048]{1,0:T(8,128)(2,1)S(1)}, bf16[128,2048]{1,0:T(8,128)(2,1)S(1)}, u32[]{:S(2)}, u32[]{:S(2)}) collective-permute-start(bf16[128,2048]{1,0:T(8,128)(2,1)S(1)} %add_convert_fusion.2), channel_id=1, source_target_pairs={{0,2},{2,0},{1,3},{3,1},{4,6},{6,4},{5,7},{7,5},{8,10},{10,8},{9,1... | collective-permute-start | bytes 1572872 | tf_op jit(solution)/shard_map/ppermute | solution.py:490
  782.5 34.2 %collective-permute-start.51 = (bf16[1408,512]{1,0:T(8,128)(2,1)S(1)}, bf16[1408,512]{1,0:T(8,128)(2,1)S(1)}, u32[]{:S(2)}, u32[]{:S(2)}) collective-permute-start(bf16[1408,512]{1,0:T(8,128)(2,1)S(1)} %copy-done.88), channel_id=1, source_target_pairs={{0,4},{4,0},{1,5},{5,1},{2,6},{6,2},{3,7},{7,3},{8,12},{12,8},{9,1... | collective-permute-start | bytes 4325384 | tf_op jit(solution)/shard_map/ppermute | solution.py:454
  782.5 49.7 %collective-permute-start.52 = (bf16[512,1408]{1,0:T(8,128)(2,1)S(1)}, bf16[512,1408]{1,0:T(8,128)(2,1)}, u32[]{:S(2)}, u32[]{:S(2)}) collective-permute-start(bf16[512,1408]{1,0:T(8,128)(2,1)S(1)} %copy-done.90), channel_id=1, source_target_pairs={{0,4},{4,0},{1,5},{5,1},{2,6},{6,2},{3,7},{7,3},{8,12},{12,8},{9,1... | collective-permute-start | bytes 4325384 | tf_op jit(solution)/shard_map/ppermute | solution.py:454
  868.5 168.1 %reduce-scatter.23.cloned.1.call-start = ((), (), s32[]{:S(2)}) async-start(), calls=%async_computation.17 | async-start | bytes 7208960 | tf_op jit(solution)/shard_map/reduce_scatter | solution.py:533
  886.4 175.9 %reduce-scatter.29.cloned.1.call-start = ((), (), s32[]{:S(2)}) async-start(), calls=%async_computation.20 | async-start | bytes 7208960 | tf_op jit(solution)/shard_map/reduce_scatter | solution.py:533
  894.6 260.2 %reduce-scatter.25.cloned.1.call-start = ((), (), s32[]{:S(2)}) async-start(), calls=%async_computation.18 | async-start | bytes 7864320 | tf_op jit(solution)/shard_map/reduce_scatter | solution.py:533
  924.5 38.7 %collective-permute-start.61 = (bf16[512,1408]{1,0:T(8,128)(2,1)S(1)}, bf16[512,1408]{1,0:T(8,128)(2,1)}, u32[]{:S(2)}, u32[]{:S(2)}) collective-permute-start(bf16[512,1408]{1,0:T(8,128)(2,1)S(1)} %copy-done.91), channel_id=1, source_target_pairs={{0,4},{4,0},{1,5},{5,1},{2,6},{6,2},{3,7},{7,3},{8,12},{12,8},{9,1... | collective-permute-start | bytes 4325384 | tf_op jit(solution)/shard_map/ppermute | solution.py:454
  924.5 37.8 %collective-permute-start.62 = (bf16[512,512]{1,0:T(8,128)(2,1)S(1)}, bf16[512,512]{1,0:T(8,128)(2,1)S(1)}, u32[]{:S(2)}, u32[]{:S(2)}) collective-permute-start(bf16[512,512]{1,0:T(8,128)(2,1)S(1)} %copy-done.99), channel_id=1, source_target_pairs={{0,4},{4,0},{1,5},{5,1},{2,6},{6,2},{3,7},{7,3},{8,12},{12,8},{9,1... | collective-permute-start | bytes 1572872 | tf_op jit(solution)/shard_map/ppermute | solution.py:454
  968.0 25.6 %collective-permute-start.67 = (bf16[512,1536]{1,0:T(8,128)(2,1)}, bf16[512,1536]{1,0:T(8,128)(2,1)}, u32[]{:S(2)}, u32[]{:S(2)}) collective-permute-start(bf16[512,1536]{1,0:T(8,128)(2,1)} %reduce-scatter.19.cloned.1.call-done), channel_id=1, source_target_pairs={{0,4},{4,0},{1,5},{5,1},{2,6},{6,2},{3,7},{7,3},{8,12},{12,8},{9,1... | collective-permute-start | bytes 4718600 | tf_op jit(solution)/shard_map/ppermute | solution.py:454
  1043.3 124.9 %reduce-scatter.27.cloned.1.call-start = ((), (), s32[]{:S(2)}) async-start(), calls=%async_computation.19 | async-start | bytes 2621440 | tf_op jit(solution)/shard_map/reduce_scatter | solution.py:533
  1062.2 28.0 %collective-permute-start.81 = (bf16[512,1408]{1,0:T(8,128)(2,1)}, bf16[512,1408]{1,0:T(8,128)(2,1)}, u32[]{:S(2)}, u32[]{:S(2)}) collective-permute-start(bf16[512,1408]{1,0:T(8,128)(2,1)} %reduce-scatter.29.cloned.1.call-done), channel_id=1, source_target_pairs={{0,4},{4,0},{1,5},{5,1},{2,6},{6,2},{3,7},{7,3},{8,12},{12,8},{9,1... | collective-permute-start | bytes 4325384 | tf_op jit(solution)/shard_map/ppermute | solution.py:454
  1085.0 61.8 %collective-permute-start.80 = (bf16[512,1408]{1,0:T(8,128)(2,1)}, bf16[512,1408]{1,0:T(8,128)(2,1)}, u32[]{:S(2)}, u32[]{:S(2)}) collective-permute-start(bf16[512,1408]{1,0:T(8,128)(2,1)} %reduce-scatter.23.cloned.1.call-done), channel_id=1, source_target_pairs={{0,4},{4,0},{1,5},{5,1},{2,6},{6,2},{3,7},{7,3},{8,12},{12,8},{9,1... | collective-permute-start | bytes 4325384 | tf_op jit(solution)/shard_map/ppermute | solution.py:454
  1087.3 64.2 %collective-permute-start.82 = (bf16[1408,512]{1,0:T(8,128)(2,1)}, bf16[1408,512]{1,0:T(8,128)(2,1)}, u32[]{:S(2)}, u32[]{:S(2)}) collective-permute-start(bf16[1408,512]{1,0:T(8,128)(2,1)} %reduce-scatter.21.cloned.1.call-done), channel_id=1, source_target_pairs={{0,4},{4,0},{1,5},{5,1},{2,6},{6,2},{3,7},{7,3},{8,12},{12,8},{9,1... | collective-permute-start | bytes 4325384 | tf_op jit(solution)/shard_map/ppermute | solution.py:454
  1110.4 23.3 %collective-permute-start.74 = (f32[14,2048]{1,0:T(8,128)S(1)}, f32[14,2048]{1,0:T(8,128)S(1)}, u32[]{:S(2)}, u32[]{:S(2)}) collective-permute-start(f32[14,2048]{1,0:T(8,128)S(1)} %fusion.23), channel_id=1, source_target_pairs={{0,16},{8,24},{16,0},{24,8},{1,17},{9,25},{17,1},{25,9},{2,18},{10... | collective-permute-start | bytes 344072 | tf_op jit(solution)/shard_map/ppermute | solution.py:454
  1154.9 41.9 %collective-permute-start.78 = (bf16[512,1536]{1,0:T(8,128)(2,1)}, bf16[512,1536]{1,0:T(8,128)(2,1)}, u32[]{:S(2)}, u32[]{:S(2)}) collective-permute-start(bf16[512,1536]{1,0:T(8,128)(2,1)} %reduce-scatter.25.cloned.1.call-done), channel_id=1, source_target_pairs={{0,4},{4,0},{1,5},{5,1},{2,6},{6,2},{3,7},{7,3},{8,12},{12,8},{9,1... | collective-permute-start | bytes 4718600 | tf_op jit(solution)/shard_map/ppermute | solution.py:454
  1165.8 22.2 %collective-permute-start.77 = (f32[14,2048]{1,0:T(8,128)S(1)}, f32[14,2048]{1,0:T(8,128)S(1)}, u32[]{:S(2)}, u32[]{:S(2)}) collective-permute-start(f32[14,2048]{1,0:T(8,128)S(1)} %add.440), channel_id=1, source_target_pairs={{0,2},{1,3},{2,0},{3,1},{4,6},{5,7},{6,4},{7,5},{8,10},{9,11},{10,... | collective-permute-start | bytes 344072 | tf_op jit(solution)/shard_map/ppermute | solution.py:454
  1168.3 26.8 %collective-permute-start.79 = (bf16[512,512]{1,0:T(8,128)(2,1)}, bf16[512,512]{1,0:T(8,128)(2,1)S(1)}, u32[]{:S(2)}, u32[]{:S(2)}) collective-permute-start(bf16[512,512]{1,0:T(8,128)(2,1)} %reduce-scatter.27.cloned.1.call-done), channel_id=1, source_target_pairs={{0,4},{4,0},{1,5},{5,1},{2,6},{6,2},{3,7},{7,3},{8,12},{12,8},{9,1... | collective-permute-start | bytes 1572872 | tf_op jit(solution)/shard_map/ppermute | solution.py:454
  (163 other events, 3303.6 us)
Sparse Core Ops, SparseCore 0:
  10.2 49.0 all-gather.21
  61.4 22.5 all-gather.19
  86.2 43.3 all-gather.23
  131.6 43.3 all-gather.25
  177.0 43.3 all-gather.27
  225.4 46.9 all-gather.29
  274.0 22.5 all-gather.31
  298.2 43.3 all-gather.33
  343.8 43.4 all-gather.35
  389.2 43.3 all-gather.37
  529.0 57.4 reduce-scatter.10
  589.6 54.8 reduce-scatter.12
  647.6 54.8 reduce-scatter.14
  705.7 31.4 reduce-scatter.16
  748.7 65.7 reduce-scatter.18
  868.6 62.5 reduce-scatter.20
  934.2 54.8 reduce-scatter.22
  992.2 54.8 reduce-scatter.28
  1050.2 60.4 reduce-scatter.24
  1113.8 31.4 reduce-scatter.26

commit v2 on v1

--- a/solution.py
+++ b/solution.py
@@ -230,6 +230,22 @@
         [whole_block(rows), (weight, (1, three, TILE, width), lambda i: (i // per, 0, i % per, 0))],
         [column_block(shape)],
         2 * rows.size * blocks * depth,
+    )[0]
+
+
+def outer_kernel(a_ref, b_ref, out_ref):
+    out_ref[...] = dot(a_ref[...], b_ref[...], TN).astype(LOW)
+
+
+def outer(a, b):
+    shape = jax.ShapeDtypeStruct((a.shape[1], b.shape[1]), LOW)
+    return tiled(
+        outer_kernel,
+        "outer",
+        pl.cdiv(a.shape[1], TILE),
+        [column_block(a), whole_block(b)],
+        [row_block(shape)],
+        a.size * b.shape[1] * 0.8,
     )[0]
 
 
@@ -445,6 +461,59 @@
     return results[0], results[1], results[2:]
 
 
+def finish(buffer, layer, terms, make, steps, ins, out, name):
+    shape, block, place = out
+
+    def kernel(*refs):
+        refs[-1][...] = make(*[r[...].astype(WIDE) for r in refs[: len(terms)]])
+
+    operands = list(terms)
+    specs = [pl.BlockSpec(b, index) for b, index in ins]
+    if buffer is not None:
+        operands.append(buffer)
+        specs.append(pl.BlockSpec(memory_space=pl.ANY))
+    return pl.pallas_call(
+        kernel,
+        grid=(steps,),
+        in_specs=specs,
+        out_specs=pl.BlockSpec((1,) + block, lambda i: (layer,) + place(i)),
+        out_shape=jax.ShapeDtypeStruct(shape, WIDE),
+        input_output_aliases={} if buffer is None else {len(terms): 0},
+        compiler_params=pltpu.CompilerParams(vmem_limit_bytes=48 * 1024 * 1024),
+        cost_estimate=work(1e9),
+        name=name,
+    )(*operands)
+
+
+def finish_matrix(buffer, layer, terms, name):
+    rows, columns = terms[0].shape
+    block = (rows // 4, columns)
+    place = lambda i: (i, 0)
+    out = ((LAYERS, rows, columns), block, place)
+    make = lambda *t: total_of(t)[None]
+    return finish(buffer, layer, terms, make, 4, [(block, place)] * len(terms), out, name)
+
+
+def finish_projections(buffer, layer, terms):
+    rows, columns = terms[0].shape
+    width = columns // 3
+    out = ((LAYERS, 3, rows, width), (1, rows, width), lambda i: (i, 0, 0))
+    make = lambda *t: total_of(t)[None, None]
+    ins = [((rows, width), lambda i: (0, i))] * len(terms)
+    return finish(buffer, layer, terms, make, 3, ins, out, "finish_qkv")
+
+
+def finish_gate_up(buffer, layer, gate_terms, up_terms):
+    rows, columns = gate_terms[0].shape
+    steps = 8
+    block = (rows // steps, columns)
+    out = ((LAYERS, rows, 2, columns), (rows // steps, 2, columns), lambda i: (i, 0, 0))
+    count = len(gate_terms)
+    make = lambda *t: jnp.stack([total_of(t[:count]), total_of(t[count:])], axis=1)[None]
+    ins = [(block, lambda i: (i, 0))] * (2 * count)
+    return finish(buffer, layer, gate_terms + up_terms, make, steps, ins, out, "finish_gate_up")
+
+
 def bits_of(count):
     return [1 << k for k in range(count.bit_length() - 1)]
 
@@ -452,6 +521,10 @@
 def swapped(value, axis, mask):
     count = lax.axis_size(axis)
     return lax.ppermute(value, axis, [(i, i ^ mask) for i in range(count)])
+
+
+def joined(pieces, axis):
+    return pieces[0] if len(pieces) == 1 else jnp.concatenate(pieces, axis=axis)
 
 
 class Line:
@@ -505,9 +578,9 @@
     def owner(self, low):
         count = lax.axis_size("ctx")
         if count != 2:
-            return lax.psum(low, "ctx").astype(WIDE) if count > 1 else low.astype(WIDE)
+            return (lax.psum(low, "ctx") if count > 1 else low,)
         got = yield swapped(low, "ctx", 1)
-        return low.astype(WIDE) + got.astype(WIDE)
+        return (low, got)
 
     def far_keys(self, value):
         count = lax.axis_size("ctx")
@@ -532,6 +605,32 @@
 def grad_stages(plan, value, axis):
     got = yield lax.psum_scatter(value.astype(LOW), "dp", scatter_dimension=axis, tiled=True)
     return (yield from plan.owner(got))
+
+
+def low_first(count):
+    width = count.bit_length() - 1
+    return sorted(range(count), key=lambda r: int(format(r, "b").zfill(width)[::-1] or "0", 2))
+
+
+def pair_stages(plan, terms_of, axis):
+    count = lax.axis_size("dp")
+
+    def term(parts):
+        factors = [terms_of(r) for r in parts]
+        a = joined([f[0] for f in factors], 1) if axis == 0 else factors[0][0]
+        b = joined([f[1] for f in factors], 1) if axis == 1 else factors[0][1]
+        return outer(a, b)
+
+    order = low_first(count)
+    kept = None
+    for bit in bits_of(count):
+        if kept is None:
+            sent = yield term(order[count // 2 :])
+        else:
+            kept, sent = jnp.split(kept, 2, axis=axis)
+        got = yield swapped(sent.astype(LOW), "dp", bit)
+        kept = (term(order[: count // 2]).astype(WIDE) if kept is None else kept) + got.astype(WIDE)
+    return (yield from plan.owner(kept.astype(LOW)))
 
 
 class Job:
@@ -611,7 +710,6 @@
     for name in ("qkv", "out", "gate", "up"):
         now[name].advance(now[name].value)
     stream = tokens[0].astype(WIDE)
-    moved_cotangent = cotangent[0]
     later = {}
     saved = []
     for layer in range(LAYERS):
@@ -626,10 +724,16 @@
             rows_one = meanwhile(rows_one, now["out"], now["gate"], now["down"])
         qkv_full = now["qkv"].finish()
         queries, keys_values = project(rows_one, qkv_full, qkv_bias_own[layer], tables)
+        if layer == 0:
+            late_cotangent, queries = lax.optimization_barrier((cotangent[0], queries))
+            grad_stream = late_cotangent.astype(WIDE)
+            branch = plan.gather_rows(late_cotangent)
         all_kv = [keys_values] + plan.far_keys(keys_values)
         attended, lse = attend(qpos, kpos, queries, all_kv)
         attended_low = meanwhile(attended.astype(LOW), now["out"])
-        if layer > 0:
+        if layer == 0:
+            attended_low, branch = lax.optimization_barrier((attended_low, branch))
+        else:
             attended_low = meanwhile(attended_low, now["up"])
         out_full = now["out"].finish()
         mid = stream + plan.sum_rows(times_wide(attended_low, out_full, "out"))
@@ -641,19 +745,14 @@
         normed_two, unit_two, inverse_two = layer_norm_rows(mid, gains[layer, 1], biases[layer, 1])
         rows_two = plan.gather_rows(normed_two.astype(LOW))
         rows_two = meanwhile(rows_two, now["down"], later.get("qkv"))
-        if last:
-            moved_cotangent, rows_two = lax.optimization_barrier((moved_cotangent, rows_two))
-            grad_stream = moved_cotangent.astype(WIDE)
-            branch = plan.gather_rows(grad_stream.astype(LOW))
         flat = lambda v: v.reshape(v.shape[0] * v.shape[1], v.shape[2])
         gate_full, up_full = flat(now["gate"].finish()), flat(now["up"].finish())
         gate, up, activated = gate_up_rows(rows_two, gate_full, up_full)
-        if last:
-            activated, branch = lax.optimization_barrier((activated, branch))
         activated = meanwhile(activated, later.get("out"), later.get("gate"))
         down_full = now["down"].finish()
-        stream = mid + plan.sum_rows(times_wide(activated, down_full, "down"))
-        stream = meanwhile(stream, later.get("qkv"), later.get("up"))
+        if not last:
+            stream = mid + plan.sum_rows(times_wide(activated, down_full, "down"))
+            stream = meanwhile(stream, later.get("qkv"), later.get("up"))
         saved.append(
             (
                 (qkv_full, out_full, gate_full, up_full, down_full),
@@ -664,8 +763,6 @@
             )
         )
         now = later
-    output = (stream).astype(LOW)[None]
-
     grad_jobs = [None] * LAYERS
     gain_grads = [None] * LAYERS
     bias_grads = [None] * LAYERS
@@ -683,45 +780,102 @@
         above = grad_jobs[layer + 1] if layer + 1 < LAYERS else {}
         old = lambda *keys: [above.get(k) for k in keys]
 
+        def own_part(value, r):
+            index = lax.axis_index("dp") ^ r
+            width = value.shape[1] // lax.axis_size("dp")
+            return lax.dynamic_slice_in_dim(value, index * width, width, 1)
+
         def in_job(a, b):
-            return Job(grad_stages(plan, dot(a, b, TN), 0))
+            return Job(grad_stages(plan, outer(a, b), 0))
 
         def out_job(a, b):
-            return Job(grad_stages(plan, dot(a, b, TN), 1))
+            return Job(grad_stages(plan, outer(a, b), 1))
 
         if layer + 1 < LAYERS:
             branch = plan.gather_rows(grad_stream.astype(LOW))
         branch = meanwhile(branch, *old("gate", "up", "out"))
+        if layer == 0:
+            down_grad, branch = lax.optimization_barrier(
+                (outer(activated, branch), branch)
+            )
+            mine["down"] = Job(grad_stages(plan, down_grad, 1))
         grad_gate, grad_up = gate_up_back(branch, down_full, gate, up)
-        mine["down"] = out_job(activated, branch)
+        partial_in = gate_up_in(grad_gate, grad_up, gate_full, up_full)
+        summed = plan.sum_rows(partial_in)
+        if layer > 0:
+            summed, (branch, grad_gate, grad_up) = lax.optimization_barrier(
+                (summed, (branch, grad_gate, grad_up))
+            )
+        if layer > 0:
+            mine["down"] = out_job(activated, branch)
         mine["gate"] = in_job(rows_two, grad_gate)
         mine["up"] = in_job(rows_two, grad_up)
-        partial_in = gate_up_in(grad_gate, grad_up, gate_full, up_full)
         grad_mid, gain_two, bias_two = norm_backward(
-            plan.sum_rows(partial_in), unit_two, inverse_two, gains[layer, 1]
+            summed, unit_two, inverse_two, gains[layer, 1]
         )
         hidden_grad = grad_stream + grad_mid
         hidden_grad = meanwhile(hidden_grad, *old("up", "out", "qkv"))
+        top = layer + 1 == LAYERS
+        if top:
+            late, hidden_grad = lax.optimization_barrier((activated, hidden_grad))
+            partial_out = times_wide(late, down_full, "down")
         attention = plan.gather_rows(hidden_grad.astype(LOW))
         attention = meanwhile(attention, *old("qkv"))
-        attention = held(attention, mine["down"])
+        if layer == 0:
+            attention = meanwhile(attention, mine["down"])
+        if top:
+            attention, partial_out = lax.optimization_barrier((attention, partial_out))
+            output = (mid + plan.sum_rows(partial_out)).astype(LOW)[None]
         grad_attended = out_back(attention, out_full)
         grad_queries, grad_kv, far_grads = attend_back(
             qpos, kpos, queries, grad_attended, attended, lse, all_kv
         )
-        mine["out"] = out_job(attended_low, attention)
+        grad_queries, attention = lax.optimization_barrier((grad_queries, attention))
+        if layer == 0:
+            mine["out"] = Job(
+                pair_stages(plan, lambda r, a=attention: (attended_low, own_part(a, r)), 1)
+            )
+        else:
+            mine["out"] = out_job(attended_low, attention)
         projected, qkv_bias_grads[layer] = project_back(
             grad_queries, grad_kv, plan.far_key_grads(far_grads), tables_back
         )
-        projected = meanwhile(projected, mine["down"], mine["gate"])
+        projected = meanwhile(projected, mine["down"], *old("qkv"))
+        if not top:
+            above_done, projected = lax.optimization_barrier(
+                ({k: j.finish() for k, j in above.items()}, projected)
+            )
+            sums = above_done
+            results = [
+                finish_projections(None, layer + 1, sums["qkv"]),
+                finish_matrix(None, layer + 1, sums["out"], "finish_out"),
+                finish_gate_up(None, layer + 1, sums["gate"], sums["up"]),
+                finish_matrix(None, layer + 1, sums["down"], "finish_down"),
+            ]
+        if layer == 0:
+            mine["qkv"] = Job(
+                pair_stages(plan, lambda r, b=projected: (own_part(rows_one, r), b), 0)
+            )
+            projected = meanwhile(projected, *map(mine.get, ("qkv", "out", "gate")))
         partial_in = project_in(projected, qkv_full)
-        mine["qkv"] = in_job(rows_one, projected)
+        if top:
+            partial_in, output = lax.optimization_barrier((partial_in, output))
+        if layer == 0:
+            partial_in = meanwhile(partial_in, *map(mine.get, ("up", "out", "qkv")))
+        summed = plan.sum_rows(partial_in)
+        if layer > 0:
+            summed, projected = lax.optimization_barrier((summed, projected))
+            mine["qkv"] = in_job(rows_one, projected)
+        else:
+            summed, results = lax.optimization_barrier((summed, results))
         grad_first, gain_one, bias_one = norm_backward(
-            plan.sum_rows(partial_in), unit_one, inverse_one, gains[layer, 0]
+            summed, unit_one, inverse_one, gains[layer, 0]
         )
         grad_stream = hidden_grad + grad_first
         if layer > 0:
-            grad_stream = held(meanwhile(grad_stream, mine["down"], mine["gate"]), mine["up"])
+            grad_stream = meanwhile(grad_stream, mine["down"], mine["gate"])
+        else:
+            grad_stream = meanwhile(grad_stream, *map(mine.get, ("gate", "up", "out", "qkv")))
         gain_grads[layer] = jnp.stack([gain_one, gain_two])
         bias_grads[layer] = jnp.stack([bias_one, bias_two])
 
@@ -740,20 +894,24 @@
         ],
         axis=0,
     )
-    for axis in ("dp", "ctx", "tensor"):
+    for axis in ("ctx", "dp", "tensor"):
         for bit in bits_of(lax.axis_size(axis)):
             small = small + swapped(small, axis, bit)
-    sums = [{k: j.finish() for k, j in g.items()} for g in grad_jobs]
+    sums = {k: j.finish() for k, j in grad_jobs[0].items()}
+    results = [
+        finish_projections(results[0], 0, sums["qkv"]),
+        finish_matrix(results[1], 0, sums["out"], "finish_out"),
+        finish_gate_up(results[2], 0, sums["gate"], sums["up"]),
+        finish_matrix(results[3], 0, sums["down"], "finish_down"),
+    ]
     return (
         output,
         tokens_grad,
         small[: LAYERS * 2].reshape(LAYERS, 2, model),
         small[LAYERS * 2 : LAYERS * 4].reshape(LAYERS, 2, model),
-        jnp.stack([s["qkv"].reshape(-1, 3, heads_width) for s in sums]),
+        jnp.transpose(results[0], (0, 2, 1, 3)),
         small[LAYERS * 4 :].reshape(LAYERS, 3, qkv_bias.shape[2]),
-        jnp.stack([s["out"] for s in sums]),
-        jnp.stack([jnp.stack([s["gate"], s["up"]], axis=1) for s in sums]),
-        jnp.stack([s["down"] for s in sums]),
+        *results[1:],
     )
 
 

time: 1240 us -> 1220 us (0.984)
  Pallas kernels: 175 us -> 269 us
  matrix products: 61.6 us -> 0 us
  other arithmetic: 102 us -> 76.5 us
  starting transfers between devices: 276 us -> 263 us
    dot_general x10 -> x0, matrix products: 61.6 us -> none  [dot(): return lax.dot_general(a, b, (dims, ((), ())), preferred_element_type=WIDE)]
    pallas_call x16 -> x28, Pallas kernels: 117 us -> 174 us  [tiled(): pl.pallas_call(kernel, grid=(steps,), in_specs=[pl.BlockSpec(block, index...]
    another operation x14 -> x0, other arithmetic: 46.1 us -> none  [the longest x3 15.3 us: shards(): jnp.stack([jnp.stack([s['gate'], s['up']], axis=1) for s in sums])]
    pallas_call x0 -> x8, Pallas kernels: none -> 35.3 us  [finish(): pl.pallas_call(kernel, grid=(steps,), in_specs=specs, out_specs=pl.BlockS...]
    ppermute x32, waiting for transfers between devices: 151 us -> 180 us  [gather_rows(): send = lambda v, *route: lax.ppermute(v, 'tensor', list(route))]
    ppermute x2, waiting for transfers between devices: 36.7 us -> 17.8 us  [far_keys(): lax.ppermute(value, 'ctx', [(i, i + s) for i in range(count - s)])]
    ppermute x15 -> x19, starting transfers between devices: 33.6 us -> 18.7 us  [swapped(): return lax.ppermute(value, axis, [(i, i ^ mask) for i in range(count)])]
    ppermute x2, waiting for transfers between devices: 33.8 us -> 19.9 us  [far_key_grads(): lax.ppermute(values[s - 1], 'ctx', [(i + s, i) for i in range(count - s)])]
  transfers between devices with their start and end apart: 103 -> 105, of which waited for: 52 -> 48; matrix products, arithmetic and copies ran while one was open for 15% -> 9% of each run, Pallas kernels for 14% -> 19%
where the time goes in v2:
time: 1220 us; the launch traced here: 1210 us
  waiting for transfers between devices  489 us (40%)
  Pallas kernels  269 us (22%)
  starting transfers between devices  263 us (22%)
  local copies, waits for them, and re-layouts  99.7 us (8%)
  other arithmetic  76.5 us (6%)
  between operations  16.9 us (1%)
    ppermute x32, waiting for transfers between devices, sum_rows(): send = lambda v, *route: lax.ppermute(v, 'tensor', list(route))  181 us
    ppermute x32, waiting for transfers between devices, gather_rows(): send = lambda v, *route: lax.ppermute(v, 'tensor', list(route))  180 us
    pallas_call x28, Pallas kernels, tiled(): pl.pallas_call(kernel, grid=(steps,), in_specs=[pl.BlockSpec(block, index...  174 us
    ppermute x32, starting transfers between devices, sum_rows(): send = lambda v, *route: lax.ppermute(v, 'tensor', list(route))  120 us
    ppermute x32, starting transfers between devices, gather_rows(): send = lambda v, *route: lax.ppermute(v, 'tensor', list(route))  113 us
    ppermute x19, waiting for transfers between devices, swapped(): return lax.ppermute(value, axis, [(i, i ^ mask) for i in range(count)])  79.1 us
    unnamed x269, local copies, waits for them, and re-layouts  64.2 us
    pallas_call x8, Pallas kernels, finish(): pl.pallas_call(kernel, grid=(steps,), in_specs=specs, out_specs=pl.BlockS...  35.3 us
  transfers between devices with their start and end apart: 105, of which 48 were waited for; matrix products, arithmetic and copies ran while one was open for 9% of the time, Pallas kernels for 19%

profile of v2, /device:TPU:0, one launch (start us, length us, event | category | flops | bytes accessed | tf_op | source)
XLA Modules:
  0.0 1213.6 jit_solution(8503842153071216791)
XLA Ops:
  30.1 16.3 %collective-permute-done = bf16[128,2048]{1,0:T(8,128)(2,1)} collective-permute-done((bf16[128,2048]{1,0:T(8,128)(2,1)S(1)}, bf16[128,2048]{1,0:T(8,128)(2,1)}, u32[]{:S(2)}, u32[]{:S(2)}) %collective-permute-start) | collective-permute-done | bytes 524320 | tf_op jit(solution)/shard_map/ppermute | solution.py:547
  50.3 10.5 collective-permute-done.1
  62.3 8.3 project.2
  85.5 16.4 %collective-permute-done.5 = bf16[128,2048]{1,0:T(8,128)(2,1)} collective-permute-done((bf16[128,2048]{1,0:T(8,128)(2,1)}, bf16[128,2048]{1,0:T(8,128)(2,1)}, u32[]{:S(2)}, u32[]{:S(2)}) %collective-permute-start.5) | collective-permute-done | bytes 524320 | tf_op jit(solution)/shard_map/ppermute | solution.py:547
  104.1 10.7 attend.2
  135.9 6.4 collective-permute-done.9
  145.2 8.4 collective-permute-done.11
  153.6 12.3 %collective-permute-done.10 = bf16[128,2048]{1,0:T(8,128)(2,1)S(1)} collective-permute-done((bf16[128,2048]{1,0:T(8,128)(2,1)S(1)}, bf16[128,2048]{1,0:T(8,128)(2,1)S(1)}, u32[]{:S(2)}, u32[]{:S(2)}) %collective-permute-start.10) | collective-permute-done | bytes 524320 | tf_op jit(solution)/shard_map/ppermute | solution.py:563
  167.4 7.6 all-gather.26.cloned.1.call-done
  189.3 18.1 %collective-permute-done.13 = bf16[128,2048]{1,0:T(8,128)(2,1)} collective-permute-done((bf16[128,2048]{1,0:T(8,128)(2,1)}, bf16[128,2048]{1,0:T(8,128)(2,1)}, u32[]{:S(2)}, u32[]{:S(2)}) %collective-permute-start.13) | collective-permute-done | bytes 524320 | tf_op jit(solution)/shard_map/ppermute | solution.py:547
  211.4 10.8 collective-permute-done.14
  237.9 11.5 gate_up.2
  252.8 7.7 down.2
  267.9 6.4 collective-permute-done.17
  285.6 14.1 %collective-permute-done.18 = bf16[128,2048]{1,0:T(8,128)(2,1)S(1)} collective-permute-done((bf16[128,2048]{1,0:T(8,128)(2,1)S(1)}, bf16[128,2048]{1,0:T(8,128)(2,1)S(1)}, u32[]{:S(2)}, u32[]{:S(2)}) %collective-permute-start.18) | collective-permute-done | bytes 524320 | tf_op jit(solution)/shard_map/ppermute | solution.py:563
  307.5 8.6 collective-permute-start.24
  316.1 16.3 %collective-permute-done.21 = bf16[128,2048]{1,0:T(8,128)(2,1)} collective-permute-done((bf16[128,2048]{1,0:T(8,128)(2,1)}, bf16[128,2048]{1,0:T(8,128)(2,1)}, u32[]{:S(2)}, u32[]{:S(2)}) %collective-permute-start.21) | collective-permute-done | bytes 524320 | tf_op jit(solution)/shard_map/ppermute | solution.py:547
  336.3 7.5 collective-permute-done.22
  349.6 7.8 project.3
  360.5 17.8 %collective-permute-done.25.refs_2_.refs_3_ = bf16[1024,512]{1,0:T(8,128)(2,1)S(1)} collective-permute-done((bf16[1024,512]{1,0:T(8,128)(2,1)S(1)}, bf16[1024,512]{1,0:T(8,128)(2,1)S(1)}, u32[]{:S(2)}, u32[]{:S(2)}) %collective-permute-start.25) | collective-permute-done | bytes 1048608 | tf_op jit(solution)/shard_map/ppermute | solution.py:588
  378.3 9.9 attend.3
  411.3 9.9 collective-permute-start.27
  422.2 8.7 collective-permute-done.27
  442.5 12.0 collective-permute-start.33
  454.5 10.7 collective-permute-done.30
  465.2 13.7 %collective-permute-start.31 = (bf16[128,2048]{1,0:T(8,128)(2,1)S(1)}, bf16[128,2048]{1,0:T(8,128)(2,1)S(1)}, u32[]{:S(2)}, u32[]{:S(2)}) collective-permute-start(bf16[128,2048]{1,0:T(8,128)(2,1)S(1)} %collective-permute-done.30), channel_id=1, source_target_pairs={{2,3},{1,0},{6,7},{5,4},{10,11},{9,8},{14,15},{13,12},{18,19},{17,... | collective-permute-start | bytes 1572872 | tf_op jit(solution)/shard_map/ppermute | solution.py:547
  479.0 12.6 %collective-permute-done.31 = bf16[128,2048]{1,0:T(8,128)(2,1)S(1)} collective-permute-done((bf16[128,2048]{1,0:T(8,128)(2,1)S(1)}, bf16[128,2048]{1,0:T(8,128)(2,1)S(1)}, u32[]{:S(2)}, u32[]{:S(2)}) %collective-permute-start.31) | collective-permute-done | bytes 524320 | tf_op jit(solution)/shard_map/ppermute | solution.py:547
  492.0 12.2 %gate_up.3 = (f32[512,1408]{1,0:T(8,128)}, f32[512,1408]{1,0:T(8,128)}, bf16[512,1408]{1,0:T(8,128)(2,1)S(1)}) custom-call(bf16[512,2048]{1,0:T(8,128)(2,1)S(1)} %pad_maximum_fusion.4.rows_ref.a_ref, bf16[2048,1408]{1,0:T(8,128)(2,1)} %all-gather.34.cloned.1.call-done, bf16[2048,1408]{1,0:T(8,128)(2,1)} %all-gather.36.cloned.1.call-done), custom_call_target="tpu_custom_call" | custom-call | flops 14763950080 | tf_op jit(solution)/shard_map/gate_up/pallas_call | solution.py:85
  504.2 8.7 gate_up_back.2
  512.9 11.6 gate_up_in.2
  549.7 7.7 collective-permute-done.35
  567.6 6.6 outer.13
  583.2 11.0 collective-permute-start.41
  594.2 7.6 collective-permute-done.38
  603.1 7.7 down.3
  620.6 16.4 %attend_back.2 = (f32[512,512]{1,0:T(8,128)S(1)}, f32[1024,512]{1,0:T(8,128)S(1)}, bf16[1024,512]{1,0:T(8,128)(2,1)S(1)}) custom-call(s32[512,1]{1,0:T(8,128)S(1)} %copy-done.42, s32[2,1,512]{2,1,0:T(1,128)S(1)} %broadcast_in_dim.17.kpos_ref, bf16[512,512]{1,0:T(8,128)(2,1)S(1)} %copy-done.93, bf16[512,512]{1,0:T(8,128)(2,1)S(1)} %out_back.2.grad_ref, ...), custom_call_target="tpu_custom_call" | custom-call | flops 20132659200 | tf_op jit(solution)/shard_map/attend_back/pallas_call | solution.py:443
  646.3 6.6 outer.14
  668.9 13.3 %collective-permute-start.44 = (bf16[128,2048]{1,0:T(8,128)(2,1)S(1)}, bf16[128,2048]{1,0:T(8,128)(2,1)S(1)}, u32[]{:S(2)}, u32[]{:S(2)}) collective-permute-start(bf16[128,2048]{1,0:T(8,128)(2,1)S(1)} %add_convert_fusion.4), channel_id=1, source_target_pairs={{0,2},{2,0},{1,3},{3,1},{4,6},{6,4},{5,7},{7,5},{8,10},{10,8},{9,1... | collective-permute-start | bytes 1572872 | tf_op jit(solution)/shard_map/ppermute | solution.py:563
  686.4 18.0 %collective-permute-done.44 = bf16[128,2048]{1,0:T(8,128)(2,1)S(1)} collective-permute-done((bf16[128,2048]{1,0:T(8,128)(2,1)S(1)}, bf16[128,2048]{1,0:T(8,128)(2,1)S(1)}, u32[]{:S(2)}, u32[]{:S(2)}) %collective-permute-start.44) | collective-permute-done | bytes 524320 | tf_op jit(solution)/shard_map/ppermute | solution.py:563
  707.0 8.0 project_in.2
  734.5 9.1 collective-permute-done.50
  743.6 11.5 collective-permute-done.48
  756.5 6.7 outer.17
  770.4 22.4 %collective-permute-done.51.refs_1_ = bf16[1408,512]{1,0:T(8,128)(2,1)} collective-permute-done((bf16[1408,512]{1,0:T(8,128)(2,1)}, bf16[1408,512]{1,0:T(8,128)(2,1)}, u32[]{:S(2)}, u32[]{:S(2)}) %collective-permute-start.51) | collective-permute-done | bytes 1441824 | tf_op jit(solution)/shard_map/ppermute | solution.py:523
  800.3 8.1 collective-permute-start.55
  808.4 13.2 %collective-permute-done.52 = bf16[128,2048]{1,0:T(8,128)(2,1)S(1)} collective-permute-done((bf16[128,2048]{1,0:T(8,128)(2,1)S(1)}, bf16[128,2048]{1,0:T(8,128)(2,1)S(1)}, u32[]{:S(2)}, u32[]{:S(2)}) %collective-permute-start.52) | collective-permute-done | bytes 524320 | tf_op jit(solution)/shard_map/ppermute | solution.py:547
  822.9 9.8 collective-permute-done.53
  844.9 8.3 gate_up_back.3
  854.4 6.6 outer.20
  865.0 10.9 gate_up_in.3
  880.9 6.6 outer.21
  894.9 7.9 collective-permute-start.58
  906.2 21.3 %collective-permute-done.58 = bf16[128,2048]{1,0:T(8,128)(2,1)S(1)} collective-permute-done((bf16[128,2048]{1,0:T(8,128)(2,1)S(1)}, bf16[128,2048]{1,0:T(8,128)(2,1)S(1)}, u32[]{:S(2)}, u32[]{:S(2)}) %collective-permute-start.58) | collective-permute-done | bytes 524320 | tf_op jit(solution)/shard_map/ppermute | solution.py:563
  930.9 12.6 %collective-permute-done.62.refs_1_ = bf16[512,512]{1,0:T(8,128)(2,1)S(1)} collective-permute-done((bf16[512,512]{1,0:T(8,128)(2,1)}, bf16[512,512]{1,0:T(8,128)(2,1)S(1)}, u32[]{:S(2)}, u32[]{:S(2)}) %collective-permute-start.62) | collective-permute-done | bytes 524320 | tf_op jit(solution)/shard_map/ppermute | solution.py:523
  954.1 13.7 %collective-permute-done.63 = bf16[128,2048]{1,0:T(8,128)(2,1)S(1)} collective-permute-done((bf16[128,2048]{1,0:T(8,128)(2,1)S(1)}, bf16[128,2048]{1,0:T(8,128)(2,1)S(1)}, u32[]{:S(2)}, u32[]{:S(2)}) %collective-permute-start.63) | collective-permute-done | bytes 524320 | tf_op jit(solution)/shard_map/ppermute | solution.py:547
  969.6 11.9 collective-permute-done.64
  990.8 17.6 %attend_back.3 = (f32[512,512]{1,0:T(8,128)S(1)}, f32[1024,512]{1,0:T(8,128)S(1)}, bf16[1024,512]{1,0:T(8,128)(2,1)}) custom-call(s32[512,1]{1,0:T(8,128)S(1)} %copy-done.43, s32[2,1,512]{2,1,0:T(1,128)S(1)} %broadcast_in_dim.17.kpos_ref, bf16[512,512]{1,0:T(8,128)(2,1)S(1)} %copy-done.91, bf16[512,512]{1,0:T(8,128)(2,1)S(1)} %out_back.3.grad_ref, ...), custom_call_target="tpu_custom_call" | custom-call | flops 20132659200 | tf_op jit(solution)/shard_map/attend_back/pallas_call | solution.py:443
  1018.1 19.8 %collective-permute-done.68.refs_0_ = bf16[1024,512]{1,0:T(8,128)(2,1)} collective-permute-done((bf16[1024,512]{1,0:T(8,128)(2,1)}, bf16[1024,512]{1,0:T(8,128)(2,1)}, u32[]{:S(2)}, u32[]{:S(2)}) %collective-permute-start.68) | collective-permute-done | bytes 1048608 | tf_op jit(solution)/shard_map/ppermute | solution.py:595
  1061.2 8.0 project_in.3
  1074.9 8.6 finish_gate_up.2.refs_4_
  1106.3 18.9 %collective-permute-done.73 = bf16[128,2048]{1,0:T(8,128)(2,1)S(1)} collective-permute-done((bf16[128,2048]{1,0:T(8,128)(2,1)S(1)}, bf16[128,2048]{1,0:T(8,128)(2,1)S(1)}, u32[]{:S(2)}, u32[]{:S(2)}) %collective-permute-start.73) | collective-permute-done | bytes 524320 | tf_op jit(solution)/shard_map/ppermute | solution.py:563
  1131.4 19.4 %collective-permute-done.79 = bf16[512,1536]{1,0:T(8,128)(2,1)} collective-permute-done((bf16[512,1536]{1,0:T(8,128)(2,1)}, bf16[512,1536]{1,0:T(8,128)(2,1)}, u32[]{:S(2)}, u32[]{:S(2)}) %collective-permute-start.79) | collective-permute-done | bytes 1572896 | tf_op jit(solution)/shard_map/ppermute | solution.py:523
  1171.5 9.1 finish_gate_up.3
  1182.6 18.0 %collective-permute-done.86.refs_1_ = bf16[512,512]{1,0:T(8,128)(2,1)S(1)} collective-permute-done((bf16[512,512]{1,0:T(8,128)(2,1)S(1)}, bf16[512,512]{1,0:T(8,128)(2,1)S(1)}, u32[]{:S(2)}, u32[]{:S(2)}) %collective-permute-start.86) | collective-permute-done | bytes 524320 | tf_op jit(solution)/shard_map/ppermute | solution.py:523
  (624 shorter events, 459.9 us)
Async XLA Ops:
  7.2 55.1 %all-gather.22.cloned.1.call-start = ((), (), s32[]{:S(2)}) async-start(), calls=%async_computation.17 | async-start | bytes 7864320 | tf_op jit(solution)/shard_map/all_gather | solution.py:602
  10.0 107.2 %all-gather.20.cloned.1.call-start = ((), (), s32[]{:S(2)}) async-start(), calls=%async_computation.8 | async-start | bytes 2621440 | tf_op jit(solution)/shard_map/all_gather | solution.py:602
  10.9 156.5 %all-gather.24.cloned.1.call-start = ((), (), s32[]{:S(2)}) async-start(), calls=%async_computation.18 | async-start | bytes 7208960 | tf_op jit(solution)/shard_map/all_gather | solution.py:602
  16.1 158.9 %all-gather.26.cloned.1.call-start = ((), (), s32[]{:S(2)}) async-start(), calls=%async_computation.19 | async-start | bytes 7208960 | tf_op jit(solution)/shard_map/all_gather | solution.py:602
  16.7 209.6 %all-gather.28.cloned.1.call-start = ((), (), s32[]{:S(2)}) async-start(), calls=%async_computation.20 | async-start | bytes 7208960 | tf_op jit(solution)/shard_map/all_gather | solution.py:602
  18.3 28.2 %collective-permute-start = (bf16[128,2048]{1,0:T(8,128)(2,1)S(1)}, bf16[128,2048]{1,0:T(8,128)(2,1)}, u32[]{:S(2)}, u32[]{:S(2)}) collective-permute-start(bf16[128,2048]{1,0:T(8,128)(2,1)S(1)} %fusion.10), channel_id=1, source_target_pairs={{0,2},{2,0},{1,3},{3,1},{4,6},{6,4},{5,7},{7,5},{8,10},{10,8},{9,1... | collective-permute-start | bytes 1572872 | tf_op jit(solution)/shard_map/ppermute | solution.py:547
  22.3 28.0 %collective-permute-start.2 = (bf16[128,2048]{1,0:T(8,128)(2,1)S(1)}, bf16[128,2048]{1,0:T(8,128)(2,1)S(1)}, u32[]{:S(2)}, u32[]{:S(2)}) collective-permute-start(bf16[128,2048]{1,0:T(8,128)(2,1)S(1)} %fusion.10), channel_id=1, source_target_pairs={{1,0},{2,1},{3,2},{5,4},{6,5},{7,6},{9,8},{10,9},{11,10},{13,12},{... | collective-permute-start | bytes 1572872 | tf_op jit(solution)/shard_map/ppermute | solution.py:547
  23.6 26.7 %collective-permute-start.3 = (bf16[128,2048]{1,0:T(8,128)(2,1)S(1)}, bf16[128,2048]{1,0:T(8,128)(2,1)S(1)}, u32[]{:S(2)}, u32[]{:S(2)}) collective-permute-start(bf16[128,2048]{1,0:T(8,128)(2,1)S(1)} %fusion.10), channel_id=1, source_target_pairs={{0,1},{1,2},{2,3},{4,5},{5,6},{6,7},{8,9},{9,10},{10,11},{12,13},{... | collective-permute-start | bytes 1572872 | tf_op jit(solution)/shard_map/ppermute | solution.py:547
  70.5 32.6 %collective-permute-start.4 = (bf16[1024,512]{1,0:T(8,128)(2,1)}, bf16[1024,512]{1,0:T(8,128)(2,1)}, u32[]{:S(2)}, u32[]{:S(2)}) collective-permute-start(bf16[1024,512]{1,0:T(8,128)(2,1)} %get-tuple-element.147.refs_0_.refs_1_), channel_id=1, source_target_pairs={{0,4},{1,5},{2,6},{3,7},{8,12},{9,13},{10,14},{11,15},{16,20},{17,... | collective-permute-start | bytes 3145736 | tf_op jit(solution)/shard_map/ppermute | solution.py:588
  74.6 226.4 %all-gather.30.cloned.1.call-start = ((), (), s32[]{:S(2)}) async-start(), calls=%async_computation.21 | async-start | bytes 7864320 | tf_op jit(solution)/shard_map/all_gather | solution.py:602
  74.6 27.2 %collective-permute-start.5 = (bf16[128,2048]{1,0:T(8,128)(2,1)}, bf16[128,2048]{1,0:T(8,128)(2,1)}, u32[]{:S(2)}, u32[]{:S(2)}) collective-permute-start(bf16[128,2048]{1,0:T(8,128)(2,1)} %bitcast.115), channel_id=1, source_target_pairs={{0,2},{2,0},{1,3},{3,1},{4,6},{6,4},{5,7},{7,5},{8,10},{10,8},{9,1... | collective-permute-start | bytes 1572872 | tf_op jit(solution)/shard_map/ppermute | solution.py:547
  78.3 38.9 %collective-permute-start.7 = (bf16[128,2048]{1,0:T(8,128)(2,1)}, bf16[128,2048]{1,0:T(8,128)(2,1)}, u32[]{:S(2)}, u32[]{:S(2)}) collective-permute-start(bf16[128,2048]{1,0:T(8,128)(2,1)} %bitcast.116), channel_id=1, source_target_pairs={{1,0},{2,1},{3,2},{5,4},{6,5},{7,6},{9,8},{10,9},{11,10},{13,12},{... | collective-permute-start | bytes 1572872 | tf_op jit(solution)/shard_map/ppermute | solution.py:547
  79.6 37.6 %collective-permute-start.8 = (bf16[128,2048]{1,0:T(8,128)(2,1)}, bf16[128,2048]{1,0:T(8,128)(2,1)}, u32[]{:S(2)}, u32[]{:S(2)}) collective-permute-start(bf16[128,2048]{1,0:T(8,128)(2,1)} %bitcast.117), channel_id=1, source_target_pairs={{0,1},{1,2},{2,3},{4,5},{5,6},{6,7},{8,9},{9,10},{10,11},{12,13},{... | collective-permute-start | bytes 1572872 | tf_op jit(solution)/shard_map/ppermute | solution.py:547
  180.2 27.2 %collective-permute-start.13 = (bf16[128,2048]{1,0:T(8,128)(2,1)}, bf16[128,2048]{1,0:T(8,128)(2,1)}, u32[]{:S(2)}, u32[]{:S(2)}) collective-permute-start(bf16[128,2048]{1,0:T(8,128)(2,1)} %add_convert_fusion.10), channel_id=1, source_target_pairs={{0,2},{2,0},{1,3},{3,1},{4,6},{6,4},{5,7},{7,5},{8,10},{10,8},{9,1... | collective-permute-start | bytes 1572872 | tf_op jit(solution)/shard_map/ppermute | solution.py:547
  182.6 28.8 %collective-permute-start.15 = (bf16[128,2048]{1,0:T(8,128)(2,1)}, bf16[128,2048]{1,0:T(8,128)(2,1)}, u32[]{:S(2)}, u32[]{:S(2)}) collective-permute-start(bf16[128,2048]{1,0:T(8,128)(2,1)} %add_convert_fusion.10), channel_id=1, source_target_pairs={{1,0},{2,1},{3,2},{5,4},{6,5},{7,6},{9,8},{10,9},{11,10},{13,12},{... | collective-permute-start | bytes 1572872 | tf_op jit(solution)/shard_map/ppermute | solution.py:547
  183.9 27.5 %collective-permute-start.16 = (bf16[128,2048]{1,0:T(8,128)(2,1)}, bf16[128,2048]{1,0:T(8,128)(2,1)}, u32[]{:S(2)}, u32[]{:S(2)}) collective-permute-start(bf16[128,2048]{1,0:T(8,128)(2,1)} %add_convert_fusion.10), channel_id=1, source_target_pairs={{0,1},{1,2},{2,3},{4,5},{5,6},{6,7},{8,9},{9,10},{10,11},{12,13},{... | collective-permute-start | bytes 1572872 | tf_op jit(solution)/shard_map/ppermute | solution.py:547
  226.3 121.5 %all-gather.32.cloned.1.call-start = ((), (), s32[]{:S(2)}) async-start(), calls=%async_computation.22 | async-start | bytes 2621440 | tf_op jit(solution)/shard_map/all_gather | solution.py:602
  250.6 97.3 %all-gather.34.cloned.1.call-start = ((), (), s32[]{:S(2)}) async-start(), calls=%async_computation.23 | async-start | bytes 7208960 | tf_op jit(solution)/shard_map/all_gather | solution.py:602
  251.3 139.3 %all-gather.36.cloned.1.call-start = ((), (), s32[]{:S(2)}) async-start(), calls=%async_computation.24 | async-start | bytes 7208960 | tf_op jit(solution)/shard_map/all_gather | solution.py:602
  274.5 25.2 %collective-permute-start.18 = (bf16[128,2048]{1,0:T(8,128)(2,1)S(1)}, bf16[128,2048]{1,0:T(8,128)(2,1)S(1)}, u32[]{:S(2)}, u32[]{:S(2)}) collective-permute-start(bf16[128,2048]{1,0:T(8,128)(2,1)S(1)} %add_convert_fusion.9), channel_id=1, source_target_pairs={{0,2},{2,0},{1,3},{3,1},{4,6},{6,4},{5,7},{7,5},{8,10},{10,8},{9,1... | collective-permute-start | bytes 1572872 | tf_op jit(solution)/shard_map/ppermute | solution.py:563
  301.1 132.6 %all-gather.38.cloned.1.call-start = ((), (), s32[]{:S(2)}) async-start(), calls=%async_computation.25 | async-start | bytes 7208960 | tf_op jit(solution)/shard_map/all_gather | solution.py:602
  306.2 26.2 %collective-permute-start.21 = (bf16[128,2048]{1,0:T(8,128)(2,1)}, bf16[128,2048]{1,0:T(8,128)(2,1)}, u32[]{:S(2)}, u32[]{:S(2)}) collective-permute-start(bf16[128,2048]{1,0:T(8,128)(2,1)} %add_convert_fusion.8), channel_id=1, source_target_pairs={{0,2},{2,0},{1,3},{3,1},{4,6},{6,4},{5,7},{7,5},{8,10},{10,8},{9,1... | collective-permute-start | bytes 1572872 | tf_op jit(solution)/shard_map/ppermute | solution.py:547
  306.2 30.1 %collective-permute-start.23 = (bf16[128,2048]{1,0:T(8,128)(2,1)}, bf16[128,2048]{1,0:T(8,128)(2,1)}, u32[]{:S(2)}, u32[]{:S(2)}) collective-permute-start(bf16[128,2048]{1,0:T(8,128)(2,1)} %add_convert_fusion.8), channel_id=1, source_target_pairs={{1,0},{2,1},{3,2},{5,4},{6,5},{7,6},{9,8},{10,9},{11,10},{13,12},{... | collective-permute-start | bytes 1572872 | tf_op jit(solution)/shard_map/ppermute | solution.py:547
  307.5 28.8 %collective-permute-start.24 = (bf16[128,2048]{1,0:T(8,128)(2,1)}, bf16[128,2048]{1,0:T(8,128)(2,1)}, u32[]{:S(2)}, u32[]{:S(2)}) collective-permute-start(bf16[128,2048]{1,0:T(8,128)(2,1)} %add_convert_fusion.8), channel_id=1, source_target_pairs={{0,1},{1,2},{2,3},{4,5},{5,6},{6,7},{8,9},{9,10},{10,11},{12,13},{... | collective-permute-start | bytes 1572872 | tf_op jit(solution)/shard_map/ppermute | solution.py:547
  347.9 357.7 %reduce-scatter.9.cloned.1.call-start = ((), (), s32[]{:S(2)}) async-start(), calls=%async_computation.9 | async-start | bytes 7208960 | tf_op jit(solution)/shard_map/reduce_scatter | solution.py:606
  438.0 27.2 %collective-permute-start.30 = (bf16[128,2048]{1,0:T(8,128)(2,1)S(1)}, bf16[128,2048]{1,0:T(8,128)(2,1)S(1)}, u32[]{:S(2)}, u32[]{:S(2)}) collective-permute-start(bf16[128,2048]{1,0:T(8,128)(2,1)S(1)} %add_convert_fusion.6), channel_id=1, source_target_pairs={{0,2},{2,0},{1,3},{3,1},{4,6},{6,4},{5,7},{7,5},{8,10},{10,8},{9,1... | collective-permute-start | bytes 1572872 | tf_op jit(solution)/shard_map/ppermute | solution.py:547
  441.2 37.8 %collective-permute-start.32 = (bf16[128,2048]{1,0:T(8,128)(2,1)S(1)}, bf16[128,2048]{1,0:T(8,128)(2,1)S(1)}, u32[]{:S(2)}, u32[]{:S(2)}) collective-permute-start(bf16[128,2048]{1,0:T(8,128)(2,1)S(1)} %add_convert_fusion.6), channel_id=1, source_target_pairs={{1,0},{2,1},{3,2},{5,4},{6,5},{7,6},{9,8},{10,9},{11,10},{13,12},{... | collective-permute-start | bytes 1572872 | tf_op jit(solution)/shard_map/ppermute | solution.py:547
  442.5 36.5 %collective-permute-start.33 = (bf16[128,2048]{1,0:T(8,128)(2,1)S(1)}, bf16[128,2048]{1,0:T(8,128)(2,1)S(1)}, u32[]{:S(2)}, u32[]{:S(2)}) collective-permute-start(bf16[128,2048]{1,0:T(8,128)(2,1)S(1)} %add_convert_fusion.6), channel_id=1, source_target_pairs={{0,1},{1,2},{2,3},{4,5},{5,6},{6,7},{8,9},{9,10},{10,11},{12,13},{... | collective-permute-start | bytes 1572872 | tf_op jit(solution)/shard_map/ppermute | solution.py:547
  465.2 26.4 %collective-permute-start.31 = (bf16[128,2048]{1,0:T(8,128)(2,1)S(1)}, bf16[128,2048]{1,0:T(8,128)(2,1)S(1)}, u32[]{:S(2)}, u32[]{:S(2)}) collective-permute-start(bf16[128,2048]{1,0:T(8,128)(2,1)S(1)} %collective-permute-done.30), channel_id=1, source_target_pairs={{2,3},{1,0},{6,7},{5,4},{10,11},{9,8},{14,15},{13,12},{18,19},{17,... | collective-permute-start | bytes 1572872 | tf_op jit(solution)/shard_map/ppermute | solution.py:547
  564.6 205.8 %reduce-scatter.11.cloned.1.call-start = ((), (), s32[]{:S(2)}) async-start(), calls=%async_computation.10 | async-start | bytes 7208960 | tf_op jit(solution)/shard_map/reduce_scatter | solution.py:606
  574.2 260.1 %reduce-scatter.15.cloned.1.call-start = ((), (), s32[]{:S(2)}) async-start(), calls=%async_computation.12 | async-start | bytes 2621440 | tf_op jit(solution)/shard_map/reduce_scatter | solution.py:606
  578.2 23.6 %collective-permute-start.38 = (bf16[128,2048]{1,0:T(8,128)(2,1)S(1)}, bf16[128,2048]{1,0:T(8,128)(2,1)S(1)}, u32[]{:S(2)}, u32[]{:S(2)}) collective-permute-start(bf16[128,2048]{1,0:T(8,128)(2,1)S(1)} %convert_element_type.285), channel_id=1, source_target_pairs={{0,2},{2,0},{1,3},{3,1},{4,6},{6,4},{5,7},{7,5},{8,10},{10,8},{9,1... | collective-permute-start | bytes 1572872 | tf_op jit(solution)/shard_map/ppermute | solution.py:547
  581.9 29.0 %collective-permute-start.40 = (bf16[128,2048]{1,0:T(8,128)(2,1)S(1)}, bf16[128,2048]{1,0:T(8,128)(2,1)S(1)}, u32[]{:S(2)}, u32[]{:S(2)}) collective-permute-start(bf16[128,2048]{1,0:T(8,128)(2,1)S(1)} %convert_element_type.285), channel_id=1, source_target_pairs={{1,0},{2,1},{3,2},{5,4},{6,5},{7,6},{9,8},{10,9},{11,10},{13,12},{... | collective-permute-start | bytes 1572872 | tf_op jit(solution)/shard_map/ppermute | solution.py:547
  583.2 27.7 %collective-permute-start.41 = (bf16[128,2048]{1,0:T(8,128)(2,1)S(1)}, bf16[128,2048]{1,0:T(8,128)(2,1)S(1)}, u32[]{:S(2)}, u32[]{:S(2)}) collective-permute-start(bf16[128,2048]{1,0:T(8,128)(2,1)S(1)} %convert_element_type.285), channel_id=1, source_target_pairs={{0,1},{1,2},{2,3},{4,5},{5,6},{6,7},{8,9},{9,10},{10,11},{12,13},{... | collective-permute-start | bytes 1572872 | tf_op jit(solution)/shard_map/ppermute | solution.py:547
  643.3 191.1 %reduce-scatter.13.cloned.1.call-start = ((), (), s32[]{:S(2)}) async-start(), calls=%async_computation.11 | async-start | bytes 7208960 | tf_op jit(solution)/shard_map/reduce_scatter | solution.py:606
  653.0 292.4 %reduce-scatter.17.cloned.1.call-start = ((), (), s32[]{:S(2)}) async-start(), calls=%async_computation.13 | async-start | bytes 7864320 | tf_op jit(solution)/shard_map/reduce_scatter | solution.py:606
  656.4 25.9 %collective-permute-start.42 = (bf16[1024,512]{1,0:T(8,128)(2,1)}, bf16[1024,512]{1,0:T(8,128)(2,1)S(1)}, u32[]{:S(2)}, u32[]{:S(2)}) collective-permute-start(bf16[1024,512]{1,0:T(8,128)(2,1)} %copy-done.55), channel_id=1, source_target_pairs={{4,0},{5,1},{6,2},{7,3},{12,8},{13,9},{14,10},{15,11},{20,16},{21,... | collective-permute-start | bytes 3145736 | tf_op jit(solution)/shard_map/ppermute | solution.py:595
  657.7 28.7 %collective-permute-start.46 = (bf16[128,2048]{1,0:T(8,128)(2,1)S(1)}, bf16[128,2048]{1,0:T(8,128)(2,1)S(1)}, u32[]{:S(2)}, u32[]{:S(2)}) collective-permute-start(bf16[128,2048]{1,0:T(8,128)(2,1)S(1)} %get-tuple-element.331), channel_id=1, source_target_pairs={{3,2},{2,1},{1,0},{7,6},{6,5},{5,4},{11,10},{10,9},{9,8},{15,14},{... | collective-permute-start | bytes 1572872 | tf_op jit(solution)/shard_map/ppermute | solution.py:563
  659.0 27.4 %collective-permute-start.45 = (bf16[128,2048]{1,0:T(8,128)(2,1)S(1)}, bf16[128,2048]{1,0:T(8,128)(2,1)S(1)}, u32[]{:S(2)}, u32[]{:S(2)}) collective-permute-start(bf16[128,2048]{1,0:T(8,128)(2,1)S(1)} %get-tuple-element.330), channel_id=1, source_target_pairs={{0,1},{1,2},{2,3},{4,5},{5,6},{6,7},{8,9},{9,10},{10,11},{12,13},{... | collective-permute-start | bytes 1572872 | tf_op jit(solution)/shard_map/ppermute | solution.py:563
  668.9 35.5 %collective-permute-start.44 = (bf16[128,2048]{1,0:T(8,128)(2,1)S(1)}, bf16[128,2048]{1,0:T(8,128)(2,1)S(1)}, u32[]{:S(2)}, u32[]{:S(2)}) collective-permute-start(bf16[128,2048]{1,0:T(8,128)(2,1)S(1)} %add_convert_fusion.4), channel_id=1, source_target_pairs={{0,2},{2,0},{1,3},{3,1},{4,6},{6,4},{5,7},{7,5},{8,10},{10,8},{9,1... | collective-permute-start | bytes 1572872 | tf_op jit(solution)/shard_map/ppermute | solution.py:563
  718.8 24.9 %collective-permute-start.50 = (bf16[128,2048]{1,0:T(8,128)(2,1)S(1)}, bf16[128,2048]{1,0:T(8,128)(2,1)S(1)}, u32[]{:S(2)}, u32[]{:S(2)}) collective-permute-start(bf16[128,2048]{1,0:T(8,128)(2,1)S(1)} %get-tuple-element.328), channel_id=1, source_target_pairs={{3,2},{2,1},{1,0},{7,6},{6,5},{5,4},{11,10},{10,9},{9,8},{15,14},{... | collective-permute-start | bytes 1572872 | tf_op jit(solution)/shard_map/ppermute | solution.py:563
  731.2 23.9 %collective-permute-start.48 = (bf16[128,2048]{1,0:T(8,128)(2,1)S(1)}, bf16[128,2048]{1,0:T(8,128)(2,1)S(1)}, u32[]{:S(2)}, u32[]{:S(2)}) collective-permute-start(bf16[128,2048]{1,0:T(8,128)(2,1)S(1)} %add_convert_fusion.2), channel_id=1, source_target_pairs={{0,2},{2,0},{1,3},{3,1},{4,6},{6,4},{5,7},{7,5},{8,10},{10,8},{9,1... | collective-permute-start | bytes 1572872 | tf_op jit(solution)/shard_map/ppermute | solution.py:563
  763.2 221.2 %reduce-scatter.19.cloned.1.call-start = ((), (), s32[]{:S(2)}) async-start(), calls=%async_computation.14 | async-start | bytes 7208960 | tf_op jit(solution)/shard_map/reduce_scatter | solution.py:606
  763.7 29.1 %collective-permute-start.51 = (bf16[1408,512]{1,0:T(8,128)(2,1)}, bf16[1408,512]{1,0:T(8,128)(2,1)}, u32[]{:S(2)}, u32[]{:S(2)}) collective-permute-start(bf16[1408,512]{1,0:T(8,128)(2,1)} %reduce-scatter.9.cloned.1.call-done.refs_0_), channel_id=1, source_target_pairs={{0,4},{4,0},{1,5},{5,1},{2,6},{6,2},{3,7},{7,3},{8,12},{12,8},{9,1... | collective-permute-start | bytes 4325384 | tf_op jit(solution)/shard_map/ppermute | solution.py:523
  794.1 27.5 %collective-permute-start.52 = (bf16[128,2048]{1,0:T(8,128)(2,1)S(1)}, bf16[128,2048]{1,0:T(8,128)(2,1)S(1)}, u32[]{:S(2)}, u32[]{:S(2)}) collective-permute-start(bf16[128,2048]{1,0:T(8,128)(2,1)S(1)} %convert_element_type.301), channel_id=1, source_target_pairs={{0,2},{2,0},{1,3},{3,1},{4,6},{6,4},{5,7},{7,5},{8,10},{10,8},{9,1... | collective-permute-start | bytes 1572872 | tf_op jit(solution)/shard_map/ppermute | solution.py:547
  797.6 36.8 %collective-permute-start.56 = (bf16[512,1408]{1,0:T(8,128)(2,1)}, bf16[512,1408]{1,0:T(8,128)(2,1)}, u32[]{:S(2)}, u32[]{:S(2)}) collective-permute-start(bf16[512,1408]{1,0:T(8,128)(2,1)} %reduce-scatter.11.cloned.1.call-done.refs_0_), channel_id=1, source_target_pairs={{0,4},{4,0},{1,5},{5,1},{2,6},{6,2},{3,7},{7,3},{8,12},{12,8},{9,1... | collective-permute-start | bytes 4325384 | tf_op jit(solution)/shard_map/ppermute | solution.py:523
  799.0 23.9 %collective-permute-start.54 = (bf16[128,2048]{1,0:T(8,128)(2,1)S(1)}, bf16[128,2048]{1,0:T(8,128)(2,1)S(1)}, u32[]{:S(2)}, u32[]{:S(2)}) collective-permute-start(bf16[128,2048]{1,0:T(8,128)(2,1)S(1)} %convert_element_type.301), channel_id=1, source_target_pairs={{1,0},{2,1},{3,2},{5,4},{6,5},{7,6},{9,8},{10,9},{11,10},{13,12},{... | collective-permute-start | bytes 1572872 | tf_op jit(solution)/shard_map/ppermute | solution.py:547
  843.3 203.1 %reduce-scatter.21.cloned.1.call-start = ((), (), s32[]{:S(2)}) async-start(), calls=%async_computation.15 | async-start | bytes 7208960 | tf_op jit(solution)/shard_map/reduce_scatter | solution.py:606
  862.2 207.1 %reduce-scatter.23.cloned.1.call-start = ((), (), s32[]{:S(2)}) async-start(), calls=%async_computation.16 | async-start | bytes 7208960 | tf_op jit(solution)/shard_map/reduce_scatter | solution.py:606
  894.9 32.6 %collective-permute-start.58 = (bf16[128,2048]{1,0:T(8,128)(2,1)S(1)}, bf16[128,2048]{1,0:T(8,128)(2,1)S(1)}, u32[]{:S(2)}, u32[]{:S(2)}) collective-permute-start(bf16[128,2048]{1,0:T(8,128)(2,1)S(1)} %add_convert_fusion.1), channel_id=1, source_target_pairs={{0,2},{2,0},{1,3},{3,1},{4,6},{6,4},{5,7},{7,5},{8,10},{10,8},{9,1... | collective-permute-start | bytes 1572872 | tf_op jit(solution)/shard_map/ppermute | solution.py:563
  902.8 41.4 %collective-permute-start.61 = (bf16[512,1408]{1,0:T(8,128)(2,1)}, bf16[512,1408]{1,0:T(8,128)(2,1)S(1)}, u32[]{:S(2)}, u32[]{:S(2)}) collective-permute-start(bf16[512,1408]{1,0:T(8,128)(2,1)} %reduce-scatter.13.cloned.1.call-done.refs_2_), channel_id=1, source_target_pairs={{0,4},{4,0},{1,5},{5,1},{2,6},{6,2},{3,7},{7,3},{8,12},{12,8},{9,1... | collective-permute-start | bytes 4325384 | tf_op jit(solution)/shard_map/ppermute | solution.py:523
  903.9 39.6 %collective-permute-start.62 = (bf16[512,512]{1,0:T(8,128)(2,1)}, bf16[512,512]{1,0:T(8,128)(2,1)S(1)}, u32[]{:S(2)}, u32[]{:S(2)}) collective-permute-start(bf16[512,512]{1,0:T(8,128)(2,1)} %reduce-scatter.15.cloned.1.call-done.refs_0_), channel_id=1, source_target_pairs={{0,4},{4,0},{1,5},{5,1},{2,6},{6,2},{3,7},{7,3},{8,12},{12,8},{9,1... | collective-permute-start | bytes 1572872 | tf_op jit(solution)/shard_map/ppermute | solution.py:523
  947.1 36.1 %collective-permute-start.67 = (bf16[512,1536]{1,0:T(8,128)(2,1)}, bf16[512,1536]{1,0:T(8,128)(2,1)S(1)}, u32[]{:S(2)}, u32[]{:S(2)}) collective-permute-start(bf16[512,1536]{1,0:T(8,128)(2,1)} %reduce-scatter.17.cloned.1.call-done.refs_0_), channel_id=1, source_target_pairs={{0,4},{4,0},{1,5},{5,1},{2,6},{6,2},{3,7},{7,3},{8,12},{12,8},{9,1... | collective-permute-start | bytes 4718600 | tf_op jit(solution)/shard_map/ppermute | solution.py:523
  984.4 56.5 %collective-permute-start.69 = (bf16[1408,512]{1,0:T(8,128)(2,1)}, bf16[1408,512]{1,0:T(8,128)(2,1)}, u32[]{:S(2)}, u32[]{:S(2)}) collective-permute-start(bf16[1408,512]{1,0:T(8,128)(2,1)} %reduce-scatter.19.cloned.1.call-done.refs_0_), channel_id=1, source_target_pairs={{0,4},{4,0},{1,5},{5,1},{2,6},{6,2},{3,7},{7,3},{8,12},{12,8},{9,1... | collective-permute-start | bytes 4325384 | tf_op jit(solution)/shard_map/ppermute | solution.py:523
  1010.8 27.1 %collective-permute-start.68 = (bf16[1024,512]{1,0:T(8,128)(2,1)}, bf16[1024,512]{1,0:T(8,128)(2,1)}, u32[]{:S(2)}, u32[]{:S(2)}) collective-permute-start(bf16[1024,512]{1,0:T(8,128)(2,1)} %get-tuple-element.236), channel_id=1, source_target_pairs={{4,0},{5,1},{6,2},{7,3},{12,8},{13,9},{14,10},{15,11},{20,16},{21,... | collective-permute-start | bytes 3145736 | tf_op jit(solution)/shard_map/ppermute | solution.py:595
  1050.5 80.9 %collective-permute-start.76 = (bf16[512,1408]{1,0:T(8,128)(2,1)}, bf16[512,1408]{1,0:T(8,128)(2,1)}, u32[]{:S(2)}, u32[]{:S(2)}) collective-permute-start(bf16[512,1408]{1,0:T(8,128)(2,1)} %reduce-scatter.21.cloned.1.call-done.refs_0_), channel_id=1, source_target_pairs={{0,4},{4,0},{1,5},{5,1},{2,6},{6,2},{3,7},{7,3},{8,12},{12,8},{9,1... | collective-permute-start | bytes 4325384 | tf_op jit(solution)/shard_map/ppermute | solution.py:523
  1070.7 25.4 %collective-permute-start.72 = (bf16[128,2048]{1,0:T(8,128)(2,1)S(1)}, bf16[128,2048]{1,0:T(8,128)(2,1)S(1)}, u32[]{:S(2)}, u32[]{:S(2)}) collective-permute-start(bf16[128,2048]{1,0:T(8,128)(2,1)S(1)} %get-tuple-element.320), channel_id=1, source_target_pairs={{0,1},{3,2},{4,5},{7,6},{8,9},{11,10},{12,13},{15,14},{16,17},{19,... | collective-permute-start | bytes 1572872 | tf_op jit(solution)/shard_map/ppermute | solution.py:563
  1092.3 39.1 %collective-permute-start.77 = (bf16[512,1408]{1,0:T(8,128)(2,1)}, bf16[512,1408]{1,0:T(8,128)(2,1)}, u32[]{:S(2)}, u32[]{:S(2)}) collective-permute-start(bf16[512,1408]{1,0:T(8,128)(2,1)} %reduce-scatter.23.cloned.1.call-done.refs_2_), channel_id=1, source_target_pairs={{0,4},{4,0},{1,5},{5,1},{2,6},{6,2},{3,7},{7,3},{8,12},{12,8},{9,1... | collective-permute-start | bytes 4325384 | tf_op jit(solution)/shard_map/ppermute | solution.py:523
  1097.3 27.9 %collective-permute-start.73 = (bf16[128,2048]{1,0:T(8,128)(2,1)S(1)}, bf16[128,2048]{1,0:T(8,128)(2,1)S(1)}, u32[]{:S(2)}, u32[]{:S(2)}) collective-permute-start(bf16[128,2048]{1,0:T(8,128)(2,1)S(1)} %add_convert_fusion), channel_id=1, source_target_pairs={{0,2},{2,0},{1,3},{3,1},{4,6},{6,4},{5,7},{7,5},{8,10},{10,8},{9,1... | collective-permute-start | bytes 1572872 | tf_op jit(solution)/shard_map/ppermute | solution.py:563
  1104.2 27.2 %collective-permute-start.78 = (bf16[512,512]{1,0:T(8,128)(2,1)S(1)}, bf16[512,512]{1,0:T(8,128)(2,1)}, u32[]{:S(2)}, u32[]{:S(2)}) collective-permute-start(bf16[512,512]{1,0:T(8,128)(2,1)S(1)} %split.31), channel_id=1, source_target_pairs={{0,16},{8,24},{16,0},{24,8},{1,17},{9,25},{17,1},{25,9},{2,18},{10... | collective-permute-start | bytes 1572872 | tf_op jit(solution)/shard_map/ppermute | solution.py:523
  1104.4 46.4 %collective-permute-start.79 = (bf16[512,1536]{1,0:T(8,128)(2,1)}, bf16[512,1536]{1,0:T(8,128)(2,1)}, u32[]{:S(2)}, u32[]{:S(2)}) collective-permute-start(bf16[512,1536]{1,0:T(8,128)(2,1)} %split.30), channel_id=1, source_target_pairs={{0,16},{8,24},{16,0},{24,8},{1,17},{9,25},{17,1},{25,9},{2,18},{10... | collective-permute-start | bytes 4718600 | tf_op jit(solution)/shard_map/ppermute | solution.py:523
  1126.8 28.4 %collective-permute-start.80 = (f32[14,2048]{1,0:T(8,128)S(1)}, f32[14,2048]{1,0:T(8,128)S(1)}, u32[]{:S(2)}, u32[]{:S(2)}) collective-permute-start(f32[14,2048]{1,0:T(8,128)S(1)} %pad_maximum_fusion.12), channel_id=1, source_target_pairs={{0,4},{4,0},{1,5},{5,1},{2,6},{6,2},{3,7},{7,3},{8,12},{12,8},{9,1... | collective-permute-start | bytes 344072 | tf_op jit(solution)/shard_map/ppermute | solution.py:523
  1154.9 47.3 %collective-permute-start.85 = (bf16[512,1536]{1,0:T(8,128)(2,1)}, bf16[512,1536]{1,0:T(8,128)(2,1)}, u32[]{:S(2)}, u32[]{:S(2)}) collective-permute-start(bf16[512,1536]{1,0:T(8,128)(2,1)} %fusion.refs_0_), channel_id=1, source_target_pairs={{0,4},{4,0},{1,5},{5,1},{2,6},{6,2},{3,7},{7,3},{8,12},{12,8},{9,1... | collective-permute-start | bytes 4718600 | tf_op jit(solution)/shard_map/ppermute | solution.py:523
  1170.8 29.8 %collective-permute-start.86 = (bf16[512,512]{1,0:T(8,128)(2,1)S(1)}, bf16[512,512]{1,0:T(8,128)(2,1)S(1)}, u32[]{:S(2)}, u32[]{:S(2)}) collective-permute-start(bf16[512,512]{1,0:T(8,128)(2,1)S(1)} %fusion.17.refs_0_), channel_id=1, source_target_pairs={{0,4},{4,0},{1,5},{5,1},{2,6},{6,2},{3,7},{7,3},{8,12},{12,8},{9,1... | collective-permute-start | bytes 1572872 | tf_op jit(solution)/shard_map/ppermute | solution.py:523
  (175 other events, 2789.7 us)
Sparse Core Ops, SparseCore 0:
  10.2 49.0 all-gather.21
  61.4 22.5 all-gather.19
  86.2 43.3 all-gather.23
  131.6 43.3 all-gather.25
  176.5 43.3 all-gather.27
  226.5 46.9 all-gather.29
  275.6 22.5 all-gather.31
  299.8 43.3 all-gather.33
  344.8 43.3 all-gather.35
  390.2 43.4 all-gather.37
  564.7 62.5 reduce-scatter.8
  630.4 54.8 reduce-scatter.10
  687.8 31.4 reduce-scatter.14
  722.4 54.8 reduce-scatter.12
  780.3 58.3 reduce-scatter.16
  843.4 60.0 reduce-scatter.18
  906.4 54.8 reduce-scatter.20
  964.5 54.8 reduce-scatter.22

commit v3 on v2

--- a/solution.py
+++ b/solution.py
@@ -23,14 +23,6 @@
     inverse = lax.rsqrt(jnp.mean(centered * centered, axis=-1, keepdims=True) + EPSILON)
     unit_rows = centered * inverse
     return (unit_rows * gain + bias, unit_rows, inverse)
-
-
-def norm_backward(grad_rows, unit_rows, inverse, gain):
-    grad_unit = grad_rows * gain
-    first_mean = jnp.mean(grad_unit, axis=-1, keepdims=True)
-    second_mean = jnp.mean(grad_unit * unit_rows, axis=-1, keepdims=True)
-    grad_input = inverse * (grad_unit - first_mean - unit_rows * second_mean)
-    return (grad_input, jnp.sum(grad_rows * unit_rows, axis=0), jnp.sum(grad_rows, axis=0))
 
 
 def rotary_tables(positions):
@@ -78,7 +70,7 @@
     return pl.CostEstimate(flops=int(flops), bytes_accessed=0, transcendentals=0)
 
 
-TILE = 256
+TILE = 512
 
 
 def tiled(kernel, name, steps, ins, outs, flops):
@@ -340,71 +332,85 @@
     return out, sums[:, 0]
 
 
-def attend_kernel(blocks, qpos_ref, kpos_ref, q_ref, *refs):
+def attend_kernel(blocks, ctx_ref, qpos_ref, kpos_ref, q_ref, *refs):
     keys, values = refs[: 2 * blocks : 2], refs[1 : 2 * blocks : 2]
-    out_ref, lse_ref = refs[2 * blocks :]
-    allowed = [kpos_ref[b] <= qpos_ref[...] for b in range(blocks)]
+    out_ref, lse_ref, acc_ref, top_ref, total_ref = refs[2 * blocks :]
+    allowed = kpos_ref[...] <= qpos_ref[...]
     for half in range(PAIR // HD):
         lanes = slice(half * HD, (half + 1) * HD)
         q = q_ref[:, lanes] * jnp.asarray(HD**-0.5, LOW)
-        top, total, acc = None, None, None
-        for b in range(blocks):
-            s = jnp.where(allowed[b], dot(q, keys[b][:, lanes], NT), MASKED)
-            block_top = jnp.max(s, axis=1, keepdims=True)
-            new_top = block_top if b == 0 else jnp.maximum(top, block_top)
-            p = jnp.exp(s - new_top)
-            block_total = jnp.sum(p, axis=1, keepdims=True)
-            block_acc = dot(p.astype(LOW), values[b][:, lanes], NN)
-            if b == 0:
-                total, acc = block_total, block_acc
-            else:
+        s = jnp.where(allowed, dot(q, keys[0][:, lanes], NT), MASKED)
+        top = jnp.max(s, axis=1, keepdims=True)
+        p = jnp.exp(s - top)
+        top_ref[half] = top
+        total_ref[half] = jnp.sum(p, axis=1, keepdims=True)
+        acc_ref[half] = dot(p.astype(LOW), values[0][:, lanes], NN)
+        for b in range(1, blocks):
+
+            @pl.when(ctx_ref[0] >= b)
+            def _():
+                s = dot(q, keys[b][:, lanes], NT)
+                top = top_ref[half]
+                new_top = jnp.maximum(top, jnp.max(s, axis=1, keepdims=True))
+                p = jnp.exp(s - new_top)
                 factor = jnp.exp(top - new_top)
-                total = total * factor + block_total
-                acc = acc * factor + block_acc
-            top = new_top
-        out_ref[:, lanes] = acc / total
-        lse_ref[half] = top + jnp.log(total)
-
-
-def attend(qpos, kpos, q, pairs_of_rows):
-    rows, width = q.shape
-    key_rows = pairs_of_rows[0].shape[0] // 2
-    blocks = len(pairs_of_rows)
-    pairs = width // PAIR
-    per_pair = PAIR // HD
+                top_ref[half] = new_top
+                total_ref[half] = total_ref[half] * factor + jnp.sum(p, axis=1, keepdims=True)
+                acc_ref[half] = acc_ref[half] * factor + dot(
+                    p.astype(LOW), values[b][:, lanes], NN
+                )
+
+        out_ref[:, lanes] = acc_ref[half] / total_ref[half]
+        lse_ref[half] = top_ref[half] + jnp.log(total_ref[half])
+
+
+def attention_specs(rows, key_rows, blocks):
     column = lambda i: (0, i)
     fixed = lambda i: (0, 0)
-    key_specs = [pl.BlockSpec((key_rows, PAIR), lambda i, c=c: (c, i)) for c in range(2)]
-    stacked = [rows_of for rows_of in pairs_of_rows for c in range(2)]
+    common = [
+        pl.BlockSpec(memory_space=pltpu.SMEM),
+        pl.BlockSpec((rows, 1), fixed),
+        pl.BlockSpec((1, key_rows), fixed),
+    ]
+    row = pl.BlockSpec((rows, PAIR), column)
+    lse = pl.BlockSpec((PAIR // HD, rows, 1), lambda i: (i, 0, 0))
+    halves = [pl.BlockSpec((key_rows, PAIR), lambda i, c=c: (c, i)) for c in range(2)]
+    return common, row, lse, halves * blocks
+
+
+def attend(ctx, qpos, kpos, q, pairs_of_rows):
+    rows, width = q.shape
+    key_rows, blocks, heads = pairs_of_rows[0].shape[0] // 2, len(pairs_of_rows), width // HD
+    common, row, lse, keys = attention_specs(rows, key_rows, blocks)
+    per_pair = PAIR // HD
     return pl.pallas_call(
         functools.partial(attend_kernel, blocks),
-        grid=(pairs,),
-        in_specs=[
-            pl.BlockSpec((rows, 1), fixed),
-            pl.BlockSpec((blocks, 1, key_rows), lambda i: (0, 0, 0)),
-            pl.BlockSpec((rows, PAIR), column),
-        ]
-        + key_specs * blocks,
-        out_specs=[
-            pl.BlockSpec((rows, PAIR), column),
-            pl.BlockSpec((per_pair, rows, 1), lambda i: (i, 0, 0)),
-        ],
+        grid=(width // PAIR,),
+        in_specs=common + [row] + keys,
+        out_specs=[row, lse],
         out_shape=[
             jax.ShapeDtypeStruct((rows, width), WIDE),
-            jax.ShapeDtypeStruct((width // HD, rows, 1), WIDE),
+            jax.ShapeDtypeStruct((heads, rows, 1), WIDE),
+        ],
+        scratch_shapes=[
+            pltpu.VMEM((per_pair, rows, HD), WIDE),
+            pltpu.VMEM((per_pair, rows, 1), WIDE),
+            pltpu.VMEM((per_pair, rows, 1), WIDE),
         ],
         compiler_params=pltpu.CompilerParams(vmem_limit_bytes=32 * 1024 * 1024),
         cost_estimate=work(43 * rows * key_rows * blocks * width),
         name="attend",
-    )(qpos, kpos, q, *stacked)
-
-
-def attend_back_kernel(blocks, qpos_ref, kpos_ref, q_ref, grad_ref, out_ref, lse_ref, *refs):
+    )(ctx, qpos, kpos, q, *[p for p in pairs_of_rows for c in range(2)])
+
+
+def attend_back_kernel(
+    blocks, ctx_ref, qpos_ref, kpos_ref, q_ref, grad_ref, out_ref, lse_ref, *refs
+):
     keys, values = refs[: 2 * blocks : 2], refs[1 : 2 * blocks : 2]
     dq_ref = refs[2 * blocks]
     dboth = refs[2 * blocks + 1 :]
     key_rows = keys[0].shape[0]
-    allowed = [kpos_ref[b] <= qpos_ref[...] for b in range(blocks)]
+    allowed = kpos_ref[...] <= qpos_ref[...]
     scale = HD**-0.5
     for half in range(PAIR // HD):
         lanes = slice(half * HD, (half + 1) * HD)
@@ -412,53 +418,84 @@
         grad = grad_ref[:, lanes]
         lse = lse_ref[half]
         delta = jnp.sum(grad.astype(WIDE) * out_ref[:, lanes], axis=1, keepdims=True)
-        dq = None
-        for b in range(blocks):
+
+        def block(b):
             k = keys[b][:, lanes]
-            s = jnp.where(allowed[b], dot(q, k, NT), MASKED)
+            s = dot(q, k, NT)
+            if b == 0:
+                s = jnp.where(allowed, s, MASKED)
             p = jnp.exp(s - lse)
             dp = dot(grad, values[b][:, lanes], NT)
             ds = (p * (dp - delta)).astype(LOW)
             kind = dboth[b].dtype
             dboth[b][key_rows:, lanes] = dot(p.astype(LOW), grad, TN).astype(kind)
             dboth[b][:key_rows, lanes] = dot(ds, q, TN).astype(kind)
-            term = dot(ds, k, NN)
-            dq = term if b == 0 else dq + term
-        dq_ref[:, lanes] = dq * scale
-
-
-def attend_back(qpos, kpos, q, grad, out, lse, pairs_of_rows):
+            return dot(ds, k, NN) * scale
+
+        dq_ref[:, lanes] = block(0)
+        for b in range(1, blocks):
+
+            @pl.when(ctx_ref[0] >= b)
+            def _():
+                dq_ref[:, lanes] += block(b)
+
+            @pl.when(ctx_ref[0] < b)
+            def _():
+                dboth[b][:, lanes] = jnp.zeros((2 * key_rows, HD), LOW)
+
+
+def attend_back(ctx, qpos, kpos, q, grad, out, lse, pairs_of_rows):
     rows, width = q.shape
-    key_rows = pairs_of_rows[0].shape[0] // 2
-    blocks = len(pairs_of_rows)
-    pairs = width // PAIR
-    per_pair = PAIR // HD
-    column = lambda i: (0, i)
-    fixed = lambda i: (0, 0)
-    row_spec = pl.BlockSpec((rows, PAIR), column)
-    key_specs = [pl.BlockSpec((key_rows, PAIR), lambda i, c=c: (c, i)) for c in range(2)]
-    stacked = [rows_of for rows_of in pairs_of_rows for c in range(2)]
+    key_rows, blocks = pairs_of_rows[0].shape[0] // 2, len(pairs_of_rows)
+    common, row, lse_spec, keys = attention_specs(rows, key_rows, blocks)
+    both = pl.BlockSpec((2 * key_rows, PAIR), lambda i: (0, i))
+    near = [jax.ShapeDtypeStruct((2 * key_rows, width), WIDE)]
     far = [jax.ShapeDtypeStruct((2 * key_rows, width), LOW)] * (blocks - 1)
-    near = [jax.ShapeDtypeStruct((2 * key_rows, width), WIDE)]
     results = pl.pallas_call(
         functools.partial(attend_back_kernel, blocks),
-        grid=(pairs,),
-        in_specs=[
-            pl.BlockSpec((rows, 1), fixed),
-            pl.BlockSpec((blocks, 1, key_rows), lambda i: (0, 0, 0)),
-            row_spec,
-            row_spec,
-            row_spec,
-            pl.BlockSpec((per_pair, rows, 1), lambda i: (i, 0, 0)),
-        ]
-        + key_specs * blocks,
-        out_specs=[row_spec] + [pl.BlockSpec((2 * key_rows, PAIR), column)] * blocks,
+        grid=(width // PAIR,),
+        in_specs=common + [row, row, row, lse_spec] + keys,
+        out_specs=[row] + [both] * blocks,
         out_shape=[jax.ShapeDtypeStruct((rows, width), WIDE)] + near + far,
         compiler_params=pltpu.CompilerParams(vmem_limit_bytes=40 * 1024 * 1024),
         cost_estimate=work(75 * rows * key_rows * blocks * width),
         name="attend_back",
-    )(qpos, kpos, q, grad, out, lse, *stacked)
+    )(ctx, qpos, kpos, q, grad, out, lse, *[p for p in pairs_of_rows for c in range(2)])
     return results[0], results[1], results[2:]
+
+
+def norm_back_kernel(count, *refs):
+    terms = refs[:count]
+    unit_ref, inverse_ref, gain_ref, base_ref = refs[count : count + 4]
+    grad_ref, low_ref, gain_out_ref, bias_out_ref = refs[count + 4 :]
+    grad_rows = total_of([t[...].astype(WIDE) for t in terms])
+    unit = unit_ref[...]
+    grad_unit = grad_rows * gain_ref[...]
+    first_mean = jnp.mean(grad_unit, axis=-1, keepdims=True)
+    second_mean = jnp.mean(grad_unit * unit, axis=-1, keepdims=True)
+    total = base_ref[...] + inverse_ref[...] * (grad_unit - first_mean - unit * second_mean)
+    grad_ref[...] = total
+    low_ref[...] = total.astype(LOW)
+    gain_out_ref[...] = jnp.sum(grad_rows * unit, axis=0, keepdims=True)
+    bias_out_ref[...] = jnp.sum(grad_rows, axis=0, keepdims=True)
+
+
+def norm_back(terms, unit, inverse, gain, base):
+    rows, model = unit.shape
+    fixed = lambda i: (0, 0)
+    line = (1, model)
+    operands = [*terms, unit, inverse, gain[None], base]
+    shapes = [(rows, model)] * (len(terms) + 1) + [(rows, 1), line, (rows, model)]
+    outs = [((rows, model), WIDE), ((rows, model), LOW), (line, WIDE), (line, WIDE)]
+    results = tiled(
+        functools.partial(norm_back_kernel, len(terms)),
+        "norm_back",
+        1,
+        [(o, s, fixed) for o, s in zip(operands, shapes)],
+        [(jax.ShapeDtypeStruct(s, t), s, fixed) for s, t in outs],
+        1e9,
+    )
+    return results[0], results[1], results[2][0], results[3][0]
 
 
 def finish(buffer, layer, terms, make, steps, ins, out, name):
@@ -529,7 +566,7 @@
 
 class Line:
     def __init__(self, own_rows):
-        n_tensor, n_ctx = lax.axis_size("tensor"), lax.axis_size("ctx")
+        n_tensor = lax.axis_size("tensor")
         tensor, ctx = lax.axis_index("tensor"), lax.axis_index("ctx")
         self.count, self.tensor = n_tensor, tensor
         row = jnp.arange(own_rows, dtype=jnp.int32)
@@ -537,9 +574,7 @@
         place = (chip[:, None] * own_rows + row[None, :]).reshape(-1)
         block = n_tensor * own_rows
         self.places = ctx * block + place
-        self.key_places = [self.places] + [
-            jnp.where(ctx >= s, (ctx - s) * block + place, 1 << 30) for s in range(1, n_ctx)
-        ]
+        self.ctx = ctx.astype(jnp.int32).reshape(1)
         self.own_rows = own_rows
 
     def gather_rows(self, low):
@@ -573,7 +608,10 @@
                 send(terms[d], *[(i, (i + d) % count) for i in range(count)])
                 for d in range(1, count)
             ]
-        return total_of([wide(terms[0])] + [wide(g) for g in got])
+        return (low, *got)
+
+    def sum_of(self, terms):
+        return total_of([terms[0][: self.own_rows].astype(WIDE)] + [t.astype(WIDE) for t in terms[1:]])
 
     def owner(self, low):
         count = lax.axis_size("ctx")
@@ -688,7 +726,7 @@
     tables = rotary_tables(plan.places)
     tables_back = (tables[0], -tables[1], -tables[2])
     qpos = plan.places[:, None]
-    kpos = jnp.stack(plan.key_places)[:, None, :]
+    kpos = plan.places[None, :]
     gains = (norm_gains)
     biases = (norm_biases)
     qkv_bias_own = lax.dynamic_slice_in_dim(qkv_bias, lax.axis_index("tensor") * heads_width, heads_width, 2)
@@ -729,14 +767,14 @@
             grad_stream = late_cotangent.astype(WIDE)
             branch = plan.gather_rows(late_cotangent)
         all_kv = [keys_values] + plan.far_keys(keys_values)
-        attended, lse = attend(qpos, kpos, queries, all_kv)
+        attended, lse = attend(plan.ctx, qpos, kpos, queries, all_kv)
         attended_low = meanwhile(attended.astype(LOW), now["out"])
         if layer == 0:
             attended_low, branch = lax.optimization_barrier((attended_low, branch))
         else:
             attended_low = meanwhile(attended_low, now["up"])
         out_full = now["out"].finish()
-        mid = stream + plan.sum_rows(times_wide(attended_low, out_full, "out"))
+        mid = stream + plan.sum_of(plan.sum_rows(times_wide(attended_low, out_full, "out")))
         mid = meanwhile(mid, now["gate"], now["up"])
         if layer > 0:
             mid = meanwhile(mid, now["down"])
@@ -751,7 +789,9 @@
         activated = meanwhile(activated, later.get("out"), later.get("gate"))
         down_full = now["down"].finish()
         if not last:
-            stream = mid + plan.sum_rows(times_wide(activated, down_full, "down"))
+            stream = mid + plan.sum_of(
+                plan.sum_rows(times_wide(activated, down_full, "down"))
+            )
             stream = meanwhile(stream, later.get("qkv"), later.get("up"))
         saved.append(
             (
@@ -792,7 +832,7 @@
             return Job(grad_stages(plan, outer(a, b), 1))
 
         if layer + 1 < LAYERS:
-            branch = plan.gather_rows(grad_stream.astype(LOW))
+            branch = plan.gather_rows(grad_low)
         branch = meanwhile(branch, *old("gate", "up", "out"))
         if layer == 0:
             down_grad, branch = lax.optimization_barrier(
@@ -802,33 +842,31 @@
         grad_gate, grad_up = gate_up_back(branch, down_full, gate, up)
         partial_in = gate_up_in(grad_gate, grad_up, gate_full, up_full)
         summed = plan.sum_rows(partial_in)
-        if layer > 0:
-            summed, (branch, grad_gate, grad_up) = lax.optimization_barrier(
-                (summed, (branch, grad_gate, grad_up))
-            )
+        summed = meanwhile(summed, *old("up", "out", "qkv"))
+        hidden_grad, hidden_low, gain_two, bias_two = norm_back(
+            summed, unit_two, inverse_two, gains[layer, 1], grad_stream
+        )
+        hidden_low, (branch, grad_gate, grad_up) = lax.optimization_barrier(
+            (hidden_low, (branch, grad_gate, grad_up))
+        )
         if layer > 0:
             mine["down"] = out_job(activated, branch)
         mine["gate"] = in_job(rows_two, grad_gate)
         mine["up"] = in_job(rows_two, grad_up)
-        grad_mid, gain_two, bias_two = norm_backward(
-            summed, unit_two, inverse_two, gains[layer, 1]
-        )
-        hidden_grad = grad_stream + grad_mid
-        hidden_grad = meanwhile(hidden_grad, *old("up", "out", "qkv"))
         top = layer + 1 == LAYERS
         if top:
-            late, hidden_grad = lax.optimization_barrier((activated, hidden_grad))
+            late, hidden_low = lax.optimization_barrier((activated, hidden_low))
             partial_out = times_wide(late, down_full, "down")
-        attention = plan.gather_rows(hidden_grad.astype(LOW))
+        attention = plan.gather_rows(hidden_low)
         attention = meanwhile(attention, *old("qkv"))
         if layer == 0:
             attention = meanwhile(attention, mine["down"])
         if top:
             attention, partial_out = lax.optimization_barrier((attention, partial_out))
-            output = (mid + plan.sum_rows(partial_out)).astype(LOW)[None]
+            output = (mid + plan.sum_of(plan.sum_rows(partial_out))).astype(LOW)[None]
         grad_attended = out_back(attention, out_full)
         grad_queries, grad_kv, far_grads = attend_back(
-            qpos, kpos, queries, grad_attended, attended, lse, all_kv
+            plan.ctx, qpos, kpos, queries, grad_attended, attended, lse, all_kv
         )
         grad_queries, attention = lax.optimization_barrier((grad_queries, attention))
         if layer == 0:
@@ -861,25 +899,23 @@
         if top:
             partial_in, output = lax.optimization_barrier((partial_in, output))
         if layer == 0:
-            partial_in = meanwhile(partial_in, *map(mine.get, ("up", "out", "qkv")))
+            partial_in = held(meanwhile(partial_in, mine["up"], mine["qkv"]), mine["out"])
         summed = plan.sum_rows(partial_in)
         if layer > 0:
-            summed, projected = lax.optimization_barrier((summed, projected))
+            summed = meanwhile(summed, mine["down"])
+        else:
+            summed = meanwhile(summed, *map(mine.get, ("gate", "out", "qkv")))
+        grad_stream, grad_low, gain_one, bias_one = norm_back(
+            summed, unit_one, inverse_one, gains[layer, 0], hidden_grad
+        )
+        if layer > 0:
+            grad_low, projected = lax.optimization_barrier((grad_low, projected))
             mine["qkv"] = in_job(rows_one, projected)
-        else:
-            summed, results = lax.optimization_barrier((summed, results))
-        grad_first, gain_one, bias_one = norm_backward(
-            summed, unit_one, inverse_one, gains[layer, 0]
-        )
-        grad_stream = hidden_grad + grad_first
-        if layer > 0:
-            grad_stream = meanwhile(grad_stream, mine["down"], mine["gate"])
-        else:
-            grad_stream = meanwhile(grad_stream, *map(mine.get, ("gate", "up", "out", "qkv")))
+            grad_low = meanwhile(grad_low, mine["gate"])
         gain_grads[layer] = jnp.stack([gain_one, gain_two])
         bias_grads[layer] = jnp.stack([bias_one, bias_two])
 
-    tokens_grad = (grad_stream).astype(LOW)[None]
+    tokens_grad = grad_low[None]
     padded_bias = lax.dynamic_update_slice_in_dim(
         jnp.zeros((LAYERS, 3, qkv_bias.shape[2]), WIDE),
         jnp.stack(qkv_bias_grads),
@@ -897,6 +933,7 @@
     for axis in ("ctx", "dp", "tensor"):
         for bit in bits_of(lax.axis_size(axis)):
             small = small + swapped(small, axis, bit)
+        small, results = lax.optimization_barrier((small, results))
     sums = {k: j.finish() for k, j in grad_jobs[0].items()}
     results = [
         finish_projections(results[0], 0, sums["qkv"]),

time: 1220 us -> 1180 us (0.967)
  starting transfers between devices: 263 us -> 211 us
  waiting for transfers between devices: 489 us -> 514 us
  Pallas kernels: 269 us -> 246 us
    ppermute x2, waiting for transfers between devices: 19.9 us -> 60.4 us  [far_key_grads(): lax.ppermute(values[s - 1], 'ctx', [(i + s, i) for i in range(count - s)])]
    ppermute x32, starting transfers between devices: 113 us -> 75.4 us  [gather_rows(): send = lambda v, *route: lax.ppermute(v, 'tensor', list(route))]
    ppermute x19, waiting for transfers between devices: 79.1 us -> 53.3 us  [swapped(): return lax.ppermute(value, axis, [(i, i ^ mask) for i in range(count)])]
    ppermute x32, starting transfers between devices: 120 us -> 95.2 us  [sum_rows(): send = lambda v, *route: lax.ppermute(v, 'tensor', list(route))]
    ppermute x32, waiting for transfers between devices: 180 us -> 203 us  [gather_rows(): send = lambda v, *route: lax.ppermute(v, 'tensor', list(route))]
    ppermute x32, waiting for transfers between devices: 181 us -> 168 us  [sum_rows(): send = lambda v, *route: lax.ppermute(v, 'tensor', list(route))]
    pallas_call x28 -> x32, Pallas kernels: 174 us -> 161 us  [tiled(): pl.pallas_call(kernel, grid=(steps,), in_specs=[pl.BlockSpec(block, index...]
    pallas_call x4, Pallas kernels: 54.6 us -> 41.9 us  [the longest x2 23.9 us: attend_back(): pl.pallas_call(functools.partial(attend_back_kernel, blocks), grid=(width...]
  transfers between devices with their start and end apart: 105 -> 105, of which waited for: 48 -> 48; matrix products, arithmetic and copies ran while one was open for 9% -> 8% of each run, Pallas kernels for 19% -> 18%
where the time goes in v3:
time: 1180 us; the launch traced here: 1160 us
  waiting for transfers between devices  514 us (44%)
  Pallas kernels  246 us (21%)
  starting transfers between devices  211 us (18%)
  local copies, waits for them, and re-layouts  108 us (9%)
  other arithmetic  67 us (6%)
  between operations  16.9 us (1%)
    ppermute x32, waiting for transfers between devices, gather_rows(): send = lambda v, *route: lax.ppermute(v, 'tensor', list(route))  203 us
    ppermute x32, waiting for transfers between devices, sum_rows(): send = lambda v, *route: lax.ppermute(v, 'tensor', list(route))  168 us
    pallas_call x32, Pallas kernels, tiled(): pl.pallas_call(kernel, grid=(steps,), in_specs=[pl.BlockSpec(block, index...  161 us
    ppermute x32, starting transfers between devices, sum_rows(): send = lambda v, *route: lax.ppermute(v, 'tensor', list(route))  95.2 us
    unnamed x263, local copies, waits for them, and re-layouts  75.6 us
    ppermute x32, starting transfers between devices, gather_rows(): send = lambda v, *route: lax.ppermute(v, 'tensor', list(route))  75.4 us
    ppermute x2, waiting for transfers between devices, far_key_grads(): lax.ppermute(values[s - 1], 'ctx', [(i + s, i) for i in range(count - s)])  60.4 us
    ppermute x19, waiting for transfers between devices, swapped(): return lax.ppermute(value, axis, [(i, i ^ mask) for i in range(count)])  53.3 us
  transfers between devices with their start and end apart: 105, of which 48 were waited for; matrix products, arithmetic and copies ran while one was open for 8% of the time, Pallas kernels for 18%

profile of v3, /device:TPU:0, one launch (start us, length us, event | category | flops | bytes accessed | tf_op | source)
XLA Modules:
  0.0 1163.9 jit_solution(8100344764691229735)
XLA Ops:
  31.5 16.3 %collective-permute-done = bf16[128,2048]{1,0:T(8,128)(2,1)} collective-permute-done((bf16[128,2048]{1,0:T(8,128)(2,1)S(1)}, bf16[128,2048]{1,0:T(8,128)(2,1)}, u32[]{:S(2)}, u32[]{:S(2)}) %collective-permute-start) | collective-permute-done | bytes 524320 | tf_op jit(solution)/shard_map/ppermute | solution.py:582
  51.7 10.5 collective-permute-done.1
  63.6 8.3 project.2
  81.0 5.7 collective-permute-start.8
  86.7 16.6 %collective-permute-done.5 = bf16[128,2048]{1,0:T(8,128)(2,1)} collective-permute-done((bf16[128,2048]{1,0:T(8,128)(2,1)}, bf16[128,2048]{1,0:T(8,128)(2,1)}, u32[]{:S(2)}, u32[]{:S(2)}) %collective-permute-start.5) | collective-permute-done | bytes 524320 | tf_op jit(solution)/shard_map/ppermute | solution.py:582
  105.6 9.4 attend.2
  123.5 5.7 collective-permute-start.9
  135.3 6.3 collective-permute-done.9
  144.3 8.4 collective-permute-done.11
  152.8 12.3 %collective-permute-done.10 = bf16[128,2048]{1,0:T(8,128)(2,1)S(1)} collective-permute-done((bf16[128,2048]{1,0:T(8,128)(2,1)S(1)}, bf16[128,2048]{1,0:T(8,128)(2,1)S(1)}, u32[]{:S(2)}, u32[]{:S(2)}) %collective-permute-start.10) | collective-permute-done | bytes 524320 | tf_op jit(solution)/shard_map/ppermute | solution.py:598
  166.5 8.6 all-gather.26.cloned.1.call-done
  190.3 18.2 %collective-permute-done.13 = bf16[128,2048]{1,0:T(8,128)(2,1)} collective-permute-done((bf16[128,2048]{1,0:T(8,128)(2,1)}, bf16[128,2048]{1,0:T(8,128)(2,1)}, u32[]{:S(2)}, u32[]{:S(2)}) %collective-permute-start.13) | collective-permute-done | bytes 524320 | tf_op jit(solution)/shard_map/ppermute | solution.py:582
  211.0 12.2 %collective-permute-done.14 = bf16[128,2048]{1,0:T(8,128)(2,1)} collective-permute-done((bf16[128,2048]{1,0:T(8,128)(2,1)}, bf16[128,2048]{1,0:T(8,128)(2,1)}, u32[]{:S(2)}, u32[]{:S(2)}) %collective-permute-start.14) | collective-permute-done | bytes 524320 | tf_op jit(solution)/shard_map/ppermute | solution.py:582
  227.4 6.0 copy.56
  238.4 11.1 gate_up.2
  252.8 5.9 down.2
  266.4 6.4 collective-permute-done.17
  278.2 5.9 collective-permute-done.19
  284.1 14.5 %collective-permute-done.18 = bf16[128,2048]{1,0:T(8,128)(2,1)S(1)} collective-permute-done((bf16[128,2048]{1,0:T(8,128)(2,1)S(1)}, bf16[128,2048]{1,0:T(8,128)(2,1)S(1)}, u32[]{:S(2)}, u32[]{:S(2)}) %collective-permute-start.18) | collective-permute-done | bytes 524320 | tf_op jit(solution)/shard_map/ppermute | solution.py:598
  306.9 8.4 collective-permute-start.24
  315.3 16.8 %collective-permute-done.21 = bf16[128,2048]{1,0:T(8,128)(2,1)} collective-permute-done((bf16[128,2048]{1,0:T(8,128)(2,1)}, bf16[128,2048]{1,0:T(8,128)(2,1)}, u32[]{:S(2)}, u32[]{:S(2)}) %collective-permute-start.21) | collective-permute-done | bytes 524320 | tf_op jit(solution)/shard_map/ppermute | solution.py:582
  334.6 8.9 collective-permute-done.22
  349.3 7.5 project.3
  360.5 18.9 %collective-permute-done.25.refs_2_.refs_3_ = bf16[1024,512]{1,0:T(8,128)(2,1)S(1)} collective-permute-done((bf16[1024,512]{1,0:T(8,128)(2,1)S(1)}, bf16[1024,512]{1,0:T(8,128)(2,1)S(1)}, u32[]{:S(2)}, u32[]{:S(2)}) %collective-permute-start.25) | collective-permute-done | bytes 1048608 | tf_op jit(solution)/shard_map/ppermute | solution.py:626
  379.3 8.6 attend.3
  403.5 6.4 collective-permute-done.26
  410.0 9.2 collective-permute-start.27
  421.1 17.5 %collective-permute-done.27 = bf16[128,2048]{1,0:T(8,128)(2,1)S(1)} collective-permute-done((bf16[128,2048]{1,0:T(8,128)(2,1)S(1)}, bf16[128,2048]{1,0:T(8,128)(2,1)S(1)}, u32[]{:S(2)}, u32[]{:S(2)}) %collective-permute-start.27) | collective-permute-done | bytes 524320 | tf_op jit(solution)/shard_map/ppermute | solution.py:598
  446.6 7.7 collective-permute-start.33
  454.3 16.8 %collective-permute-done.30 = bf16[128,2048]{1,0:T(8,128)(2,1)S(1)} collective-permute-done((bf16[128,2048]{1,0:T(8,128)(2,1)S(1)}, bf16[128,2048]{1,0:T(8,128)(2,1)S(1)}, u32[]{:S(2)}, u32[]{:S(2)}) %collective-permute-start.30) | collective-permute-done | bytes 524320 | tf_op jit(solution)/shard_map/ppermute | solution.py:582
  472.4 9.8 collective-permute-done.31
  482.5 11.5 gate_up.3
  495.2 7.3 gate_up_back.2
  502.5 10.3 gate_up_in.2.refs_0_
  519.2 8.5 collective-permute-done.34
  528.6 7.7 collective-permute-start.35
  537.9 20.7 %collective-permute-done.35.refs_1_ = bf16[128,2048]{1,0:T(8,128)(2,1)} collective-permute-done((bf16[128,2048]{1,0:T(8,128)(2,1)}, bf16[128,2048]{1,0:T(8,128)(2,1)}, u32[]{:S(2)}, u32[]{:S(2)}) %collective-permute-start.35) | collective-permute-done | bytes 524320 | tf_op jit(solution)/shard_map/ppermute | solution.py:598
  585.3 13.6 %collective-permute-done.38 = bf16[128,2048]{1,0:T(8,128)(2,1)S(1)} collective-permute-done((bf16[128,2048]{1,0:T(8,128)(2,1)}, bf16[128,2048]{1,0:T(8,128)(2,1)S(1)}, u32[]{:S(2)}, u32[]{:S(2)}) %collective-permute-start.38) | collective-permute-done | bytes 524320 | tf_op jit(solution)/shard_map/ppermute | solution.py:582
  601.6 6.1 down.3
  607.8 6.7 collective-permute-done.39
  619.9 11.3 attend_back.2
  666.0 35.3 %collective-permute-done.42.refs_0_ = bf16[1024,512]{1,0:T(8,128)(2,1)S(1)} collective-permute-done((bf16[1024,512]{1,0:T(8,128)(2,1)}, bf16[1024,512]{1,0:T(8,128)(2,1)S(1)}, u32[]{:S(2)}, u32[]{:S(2)}) %collective-permute-start.42) | collective-permute-done | bytes 1048608 | tf_op jit(solution)/shard_map/ppermute | solution.py:633
  708.3 6.1 project_in.2.refs_0_
  717.1 12.5 %collective-permute-start.51 = (bf16[1408,512]{1,0:T(8,128)(2,1)}, bf16[1408,512]{1,0:T(8,128)(2,1)}, u32[]{:S(2)}, u32[]{:S(2)}) collective-permute-start(bf16[1408,512]{1,0:T(8,128)(2,1)} %reduce-scatter.9.cloned.1.call-done.refs_0_), channel_id=1, source_target_pairs={{0,4},{4,0},{1,5},{5,1},{2,6},{6,2},{3,7},{7,3},{8,12},{12,8},{9,1... | collective-permute-start | bytes 4325384 | tf_op jit(solution)/shard_map/ppermute | solution.py:560
  737.1 6.6 collective-permute-done.49.refs_2_
  744.9 23.7 %collective-permute-done.48.refs_1_ = bf16[128,2048]{1,0:T(8,128)(2,1)} collective-permute-done((bf16[128,2048]{1,0:T(8,128)(2,1)}, bf16[128,2048]{1,0:T(8,128)(2,1)}, u32[]{:S(2)}, u32[]{:S(2)}) %collective-permute-start.48) | collective-permute-done | bytes 524320 | tf_op jit(solution)/shard_map/ppermute | solution.py:598
  787.6 11.9 %collective-permute-done.52 = bf16[128,2048]{1,0:T(8,128)(2,1)S(1)} collective-permute-done((bf16[128,2048]{1,0:T(8,128)(2,1)S(1)}, bf16[128,2048]{1,0:T(8,128)(2,1)S(1)}, u32[]{:S(2)}, u32[]{:S(2)}) %collective-permute-start.52) | collective-permute-done | bytes 524320 | tf_op jit(solution)/shard_map/ppermute | solution.py:582
  800.8 6.9 collective-permute-done.54
  807.7 9.2 collective-permute-done.53
  828.4 7.4 gate_up_back.3
  835.8 10.3 gate_up_in.3.refs_0_
  854.4 6.6 collective-permute-done.57
  865.0 7.2 collective-permute-done.59.refs_2_
  872.3 19.4 %collective-permute-done.62.refs_1_ = bf16[512,512]{1,0:T(8,128)(2,1)} collective-permute-done((bf16[512,512]{1,0:T(8,128)(2,1)S(1)}, bf16[512,512]{1,0:T(8,128)(2,1)}, u32[]{:S(2)}, u32[]{:S(2)}) %collective-permute-start.62) | collective-permute-done | bytes 524320 | tf_op jit(solution)/shard_map/ppermute | solution.py:560
  919.6 14.6 %collective-permute-done.63 = bf16[128,2048]{1,0:T(8,128)(2,1)S(1)} collective-permute-done((bf16[128,2048]{1,0:T(8,128)(2,1)S(1)}, bf16[128,2048]{1,0:T(8,128)(2,1)S(1)}, u32[]{:S(2)}, u32[]{:S(2)}) %collective-permute-start.63) | collective-permute-done | bytes 524320 | tf_op jit(solution)/shard_map/ppermute | solution.py:582
  937.8 12.1 %collective-permute-done.64 = bf16[128,2048]{1,0:T(8,128)(2,1)S(1)} collective-permute-done((bf16[128,2048]{1,0:T(8,128)(2,1)S(1)}, bf16[128,2048]{1,0:T(8,128)(2,1)S(1)}, u32[]{:S(2)}, u32[]{:S(2)}) %collective-permute-start.64) | collective-permute-done | bytes 524320 | tf_op jit(solution)/shard_map/ppermute | solution.py:582
  961.0 12.6 %attend_back.3 = (f32[512,512]{1,0:T(8,128)S(1)}, f32[1024,512]{1,0:T(8,128)S(1)}, bf16[1024,512]{1,0:T(8,128)(2,1)}) custom-call(s32[1]{0:T(128)} %bitcast.ctx_ref, s32[512,1]{1,0:T(8,128)S(1)} %copy-done.48, s32[1,512]{1,0:T(1,128)S(1)} %bitcast.100, bf16[512,512]{1,0:T(8,128)(2,1)S(1)} %copy-done.108, bf16[512,512]{1,0:T(8,128)(2,1)S(1)} %out_back.3.grad_ref, ...), custom_call_target="tpu_custom_call" | custom-call | flops 20132659200 | tf_op jit(solution)/shard_map/attend_back/pallas_call | solution.py:454
  983.6 25.1 %collective-permute-done.68.refs_0_ = bf16[1024,512]{1,0:T(8,128)(2,1)} collective-permute-done((bf16[1024,512]{1,0:T(8,128)(2,1)}, bf16[1024,512]{1,0:T(8,128)(2,1)}, u32[]{:S(2)}, u32[]{:S(2)}) %collective-permute-start.68) | collective-permute-done | bytes 1048608 | tf_op jit(solution)/shard_map/ppermute | solution.py:633
  1022.5 6.0 project_in.3.refs_0_
  1060.5 9.2 finish_gate_up.2.refs_4_
  1072.6 8.9 collective-permute-done.73.refs_1_
  1094.2 13.1 %collective-permute-done.78 = f32[14,2048]{1,0:T(8,128)S(1)} collective-permute-done((f32[14,2048]{1,0:T(8,128)S(1)}, f32[14,2048]{1,0:T(8,128)S(1)}, u32[]{:S(2)}, u32[]{:S(2)}) %collective-permute-start.78) | collective-permute-done | bytes 114720 | tf_op jit(solution)/shard_map/ppermute | solution.py:560
  1122.8 5.7 collective-permute-done.82
  1135.7 9.4 finish_gate_up.3
  (603 shorter events, 438.7 us)
Async XLA Ops:
  7.2 56.4 %all-gather.22.cloned.1.call-start = ((), (), s32[]{:S(2)}) async-start(), calls=%async_computation.17 | async-start | bytes 7864320 | tf_op jit(solution)/shard_map/all_gather | solution.py:640
  10.0 107.4 %all-gather.20.cloned.1.call-start = ((), (), s32[]{:S(2)}) async-start(), calls=%async_computation.8 | async-start | bytes 2621440 | tf_op jit(solution)/shard_map/all_gather | solution.py:640
  10.9 155.6 %all-gather.24.cloned.1.call-start = ((), (), s32[]{:S(2)}) async-start(), calls=%async_computation.18 | async-start | bytes 7208960 | tf_op jit(solution)/shard_map/all_gather | solution.py:640
  16.1 158.9 %all-gather.26.cloned.1.call-start = ((), (), s32[]{:S(2)}) async-start(), calls=%async_computation.19 | async-start | bytes 7208960 | tf_op jit(solution)/shard_map/all_gather | solution.py:640
  16.7 210.6 %all-gather.28.cloned.1.call-start = ((), (), s32[]{:S(2)}) async-start(), calls=%async_computation.20 | async-start | bytes 7208960 | tf_op jit(solution)/shard_map/all_gather | solution.py:640
  19.7 28.2 %collective-permute-start = (bf16[128,2048]{1,0:T(8,128)(2,1)S(1)}, bf16[128,2048]{1,0:T(8,128)(2,1)}, u32[]{:S(2)}, u32[]{:S(2)}) collective-permute-start(bf16[128,2048]{1,0:T(8,128)(2,1)S(1)} %get-tuple-element.410), channel_id=1, source_target_pairs={{0,2},{2,0},{1,3},{3,1},{4,6},{6,4},{5,7},{7,5},{8,10},{10,8},{9,1... | collective-permute-start | bytes 1572872 | tf_op jit(solution)/shard_map/ppermute | solution.py:582
  23.7 28.0 %collective-permute-start.2 = (bf16[128,2048]{1,0:T(8,128)(2,1)S(1)}, bf16[128,2048]{1,0:T(8,128)(2,1)S(1)}, u32[]{:S(2)}, u32[]{:S(2)}) collective-permute-start(bf16[128,2048]{1,0:T(8,128)(2,1)S(1)} %get-tuple-element.410), channel_id=1, source_target_pairs={{1,0},{2,1},{3,2},{5,4},{6,5},{7,6},{9,8},{10,9},{11,10},{13,12},{... | collective-permute-start | bytes 1572872 | tf_op jit(solution)/shard_map/ppermute | solution.py:582
  25.0 26.7 %collective-permute-start.3 = (bf16[128,2048]{1,0:T(8,128)(2,1)S(1)}, bf16[128,2048]{1,0:T(8,128)(2,1)S(1)}, u32[]{:S(2)}, u32[]{:S(2)}) collective-permute-start(bf16[128,2048]{1,0:T(8,128)(2,1)S(1)} %get-tuple-element.410), channel_id=1, source_target_pairs={{0,1},{1,2},{2,3},{4,5},{5,6},{6,7},{8,9},{9,10},{10,11},{12,13},{... | collective-permute-start | bytes 1572872 | tf_op jit(solution)/shard_map/ppermute | solution.py:582
  71.9 32.7 %collective-permute-start.4 = (bf16[1024,512]{1,0:T(8,128)(2,1)}, bf16[1024,512]{1,0:T(8,128)(2,1)}, u32[]{:S(2)}, u32[]{:S(2)}) collective-permute-start(bf16[1024,512]{1,0:T(8,128)(2,1)} %get-tuple-element.185.refs_0_.refs_1_), channel_id=1, source_target_pairs={{0,4},{1,5},{2,6},{3,7},{8,12},{9,13},{10,14},{11,15},{16,20},{17,... | collective-permute-start | bytes 3145736 | tf_op jit(solution)/shard_map/ppermute | solution.py:626
  76.0 223.9 %all-gather.30.cloned.1.call-start = ((), (), s32[]{:S(2)}) async-start(), calls=%async_computation.21 | async-start | bytes 7864320 | tf_op jit(solution)/shard_map/all_gather | solution.py:640
  76.1 27.2 %collective-permute-start.5 = (bf16[128,2048]{1,0:T(8,128)(2,1)}, bf16[128,2048]{1,0:T(8,128)(2,1)}, u32[]{:S(2)}, u32[]{:S(2)}) collective-permute-start(bf16[128,2048]{1,0:T(8,128)(2,1)} %bitcast.106), channel_id=1, source_target_pairs={{0,2},{2,0},{1,3},{3,1},{4,6},{6,4},{5,7},{7,5},{8,10},{10,8},{9,1... | collective-permute-start | bytes 1572872 | tf_op jit(solution)/shard_map/ppermute | solution.py:582
  79.7 37.6 %collective-permute-start.7 = (bf16[128,2048]{1,0:T(8,128)(2,1)}, bf16[128,2048]{1,0:T(8,128)(2,1)}, u32[]{:S(2)}, u32[]{:S(2)}) collective-permute-start(bf16[128,2048]{1,0:T(8,128)(2,1)} %bitcast.107), channel_id=1, source_target_pairs={{1,0},{2,1},{3,2},{5,4},{6,5},{7,6},{9,8},{10,9},{11,10},{13,12},{... | collective-permute-start | bytes 1572872 | tf_op jit(solution)/shard_map/ppermute | solution.py:582
  81.0 36.4 %collective-permute-start.8 = (bf16[128,2048]{1,0:T(8,128)(2,1)}, bf16[128,2048]{1,0:T(8,128)(2,1)}, u32[]{:S(2)}, u32[]{:S(2)}) collective-permute-start(bf16[128,2048]{1,0:T(8,128)(2,1)} %bitcast.108), channel_id=1, source_target_pairs={{0,1},{1,2},{2,3},{4,5},{5,6},{6,7},{8,9},{9,10},{10,11},{12,13},{... | collective-permute-start | bytes 1572872 | tf_op jit(solution)/shard_map/ppermute | solution.py:582
  181.2 27.2 %collective-permute-start.13 = (bf16[128,2048]{1,0:T(8,128)(2,1)}, bf16[128,2048]{1,0:T(8,128)(2,1)}, u32[]{:S(2)}, u32[]{:S(2)}) collective-permute-start(bf16[128,2048]{1,0:T(8,128)(2,1)} %get-tuple-element.371), channel_id=1, source_target_pairs={{0,2},{2,0},{1,3},{3,1},{4,6},{6,4},{5,7},{7,5},{8,10},{10,8},{9,1... | collective-permute-start | bytes 1572872 | tf_op jit(solution)/shard_map/ppermute | solution.py:582
  183.6 27.4 %collective-permute-start.15 = (bf16[128,2048]{1,0:T(8,128)(2,1)}, bf16[128,2048]{1,0:T(8,128)(2,1)}, u32[]{:S(2)}, u32[]{:S(2)}) collective-permute-start(bf16[128,2048]{1,0:T(8,128)(2,1)} %get-tuple-element.371), channel_id=1, source_target_pairs={{1,0},{2,1},{3,2},{5,4},{6,5},{7,6},{9,8},{10,9},{11,10},{13,12},{... | collective-permute-start | bytes 1572872 | tf_op jit(solution)/shard_map/ppermute | solution.py:582
  184.9 26.1 %collective-permute-start.16 = (bf16[128,2048]{1,0:T(8,128)(2,1)}, bf16[128,2048]{1,0:T(8,128)(2,1)}, u32[]{:S(2)}, u32[]{:S(2)}) collective-permute-start(bf16[128,2048]{1,0:T(8,128)(2,1)} %get-tuple-element.371), channel_id=1, source_target_pairs={{0,1},{1,2},{2,3},{4,5},{5,6},{6,7},{8,9},{9,10},{10,11},{12,13},{... | collective-permute-start | bytes 1572872 | tf_op jit(solution)/shard_map/ppermute | solution.py:582
  227.3 120.3 %all-gather.32.cloned.1.call-start = ((), (), s32[]{:S(2)}) async-start(), calls=%async_computation.22 | async-start | bytes 2621440 | tf_op jit(solution)/shard_map/all_gather | solution.py:640
  250.7 96.9 %all-gather.34.cloned.1.call-start = ((), (), s32[]{:S(2)}) async-start(), calls=%async_computation.23 | async-start | bytes 7208960 | tf_op jit(solution)/shard_map/all_gather | solution.py:640
  251.4 139.0 %all-gather.36.cloned.1.call-start = ((), (), s32[]{:S(2)}) async-start(), calls=%async_computation.24 | async-start | bytes 7208960 | tf_op jit(solution)/shard_map/all_gather | solution.py:640
  273.0 25.6 %collective-permute-start.18 = (bf16[128,2048]{1,0:T(8,128)(2,1)S(1)}, bf16[128,2048]{1,0:T(8,128)(2,1)S(1)}, u32[]{:S(2)}, u32[]{:S(2)}) collective-permute-start(bf16[128,2048]{1,0:T(8,128)(2,1)S(1)} %add_convert_fusion.9), channel_id=1, source_target_pairs={{0,2},{2,0},{1,3},{3,1},{4,6},{6,4},{5,7},{7,5},{8,10},{10,8},{9,1... | collective-permute-start | bytes 1572872 | tf_op jit(solution)/shard_map/ppermute | solution.py:598
  299.9 140.1 %all-gather.38.cloned.1.call-start = ((), (), s32[]{:S(2)}) async-start(), calls=%async_computation.25 | async-start | bytes 7208960 | tf_op jit(solution)/shard_map/all_gather | solution.py:640
  305.6 26.5 %collective-permute-start.21 = (bf16[128,2048]{1,0:T(8,128)(2,1)}, bf16[128,2048]{1,0:T(8,128)(2,1)}, u32[]{:S(2)}, u32[]{:S(2)}) collective-permute-start(bf16[128,2048]{1,0:T(8,128)(2,1)} %get-tuple-element.369), channel_id=1, source_target_pairs={{0,2},{2,0},{1,3},{3,1},{4,6},{6,4},{5,7},{7,5},{8,10},{10,8},{9,1... | collective-permute-start | bytes 1572872 | tf_op jit(solution)/shard_map/ppermute | solution.py:582
  305.6 29.0 %collective-permute-start.23 = (bf16[128,2048]{1,0:T(8,128)(2,1)}, bf16[128,2048]{1,0:T(8,128)(2,1)}, u32[]{:S(2)}, u32[]{:S(2)}) collective-permute-start(bf16[128,2048]{1,0:T(8,128)(2,1)} %get-tuple-element.369), channel_id=1, source_target_pairs={{1,0},{2,1},{3,2},{5,4},{6,5},{7,6},{9,8},{10,9},{11,10},{13,12},{... | collective-permute-start | bytes 1572872 | tf_op jit(solution)/shard_map/ppermute | solution.py:582
  306.9 27.7 %collective-permute-start.24 = (bf16[128,2048]{1,0:T(8,128)(2,1)}, bf16[128,2048]{1,0:T(8,128)(2,1)}, u32[]{:S(2)}, u32[]{:S(2)}) collective-permute-start(bf16[128,2048]{1,0:T(8,128)(2,1)} %get-tuple-element.369), channel_id=1, source_target_pairs={{0,1},{1,2},{2,3},{4,5},{5,6},{6,7},{8,9},{9,10},{10,11},{12,13},{... | collective-permute-start | bytes 1572872 | tf_op jit(solution)/shard_map/ppermute | solution.py:582
  347.6 359.0 %reduce-scatter.9.cloned.1.call-start = ((), (), s32[]{:S(2)}) async-start(), calls=%async_computation.9 | async-start | bytes 7208960 | tf_op jit(solution)/shard_map/reduce_scatter | solution.py:644
  410.0 28.6 %collective-permute-start.27 = (bf16[128,2048]{1,0:T(8,128)(2,1)S(1)}, bf16[128,2048]{1,0:T(8,128)(2,1)S(1)}, u32[]{:S(2)}, u32[]{:S(2)}) collective-permute-start(bf16[128,2048]{1,0:T(8,128)(2,1)S(1)} %add_convert_fusion.7), channel_id=1, source_target_pairs={{0,2},{2,0},{1,3},{3,1},{4,6},{6,4},{5,7},{7,5},{8,10},{10,8},{9,1... | collective-permute-start | bytes 1572872 | tf_op jit(solution)/shard_map/ppermute | solution.py:598
  445.3 25.8 %collective-permute-start.30 = (bf16[128,2048]{1,0:T(8,128)(2,1)S(1)}, bf16[128,2048]{1,0:T(8,128)(2,1)S(1)}, u32[]{:S(2)}, u32[]{:S(2)}) collective-permute-start(bf16[128,2048]{1,0:T(8,128)(2,1)S(1)} %get-tuple-element.367), channel_id=1, source_target_pairs={{0,2},{2,0},{1,3},{3,1},{4,6},{6,4},{5,7},{7,5},{8,10},{10,8},{9,1... | collective-permute-start | bytes 1572872 | tf_op jit(solution)/shard_map/ppermute | solution.py:582
  445.3 27.1 %collective-permute-start.32 = (bf16[128,2048]{1,0:T(8,128)(2,1)S(1)}, bf16[128,2048]{1,0:T(8,128)(2,1)S(1)}, u32[]{:S(2)}, u32[]{:S(2)}) collective-permute-start(bf16[128,2048]{1,0:T(8,128)(2,1)S(1)} %get-tuple-element.367), channel_id=1, source_target_pairs={{1,0},{2,1},{3,2},{5,4},{6,5},{7,6},{9,8},{10,9},{11,10},{13,12},{... | collective-permute-start | bytes 1572872 | tf_op jit(solution)/shard_map/ppermute | solution.py:582
  446.6 25.8 %collective-permute-start.33 = (bf16[128,2048]{1,0:T(8,128)(2,1)S(1)}, bf16[128,2048]{1,0:T(8,128)(2,1)S(1)}, u32[]{:S(2)}, u32[]{:S(2)}) collective-permute-start(bf16[128,2048]{1,0:T(8,128)(2,1)S(1)} %get-tuple-element.367), channel_id=1, source_target_pairs={{0,1},{1,2},{2,3},{4,5},{5,6},{6,7},{8,9},{9,10},{10,11},{12,13},{... | collective-permute-start | bytes 1572872 | tf_op jit(solution)/shard_map/ppermute | solution.py:582
  528.6 30.0 %collective-permute-start.35 = (bf16[128,2048]{1,0:T(8,128)(2,1)}, bf16[128,2048]{1,0:T(8,128)(2,1)}, u32[]{:S(2)}, u32[]{:S(2)}) collective-permute-start(bf16[128,2048]{1,0:T(8,128)(2,1)} %add_convert_fusion.5), channel_id=1, source_target_pairs={{0,2},{2,0},{1,3},{3,1},{4,6},{6,4},{5,7},{7,5},{8,10},{10,8},{9,1... | collective-permute-start | bytes 1572872 | tf_op jit(solution)/shard_map/ppermute | solution.py:598
  570.9 210.4 %reduce-scatter.11.cloned.1.call-start = ((), (), s32[]{:S(2)}) async-start(), calls=%async_computation.10 | async-start | bytes 7208960 | tf_op jit(solution)/shard_map/reduce_scatter | solution.py:644
  579.3 239.2 %reduce-scatter.15.cloned.1.call-start = ((), (), s32[]{:S(2)}) async-start(), calls=%async_computation.12 | async-start | bytes 2621440 | tf_op jit(solution)/shard_map/reduce_scatter | solution.py:644
  579.5 28.3 %collective-permute-start.40 = (bf16[128,2048]{1,0:T(8,128)(2,1)}, bf16[128,2048]{1,0:T(8,128)(2,1)S(1)}, u32[]{:S(2)}, u32[]{:S(2)}) collective-permute-start(bf16[128,2048]{1,0:T(8,128)(2,1)} %copy-done.40), channel_id=1, source_target_pairs={{1,0},{2,1},{3,2},{5,4},{6,5},{7,6},{9,8},{10,9},{11,10},{13,12},{... | collective-permute-start | bytes 1572872 | tf_op jit(solution)/shard_map/ppermute | solution.py:582
  580.8 27.0 %collective-permute-start.41 = (bf16[128,2048]{1,0:T(8,128)(2,1)}, bf16[128,2048]{1,0:T(8,128)(2,1)S(1)}, u32[]{:S(2)}, u32[]{:S(2)}) collective-permute-start(bf16[128,2048]{1,0:T(8,128)(2,1)} %copy-done.40), channel_id=1, source_target_pairs={{0,1},{1,2},{2,3},{4,5},{5,6},{6,7},{8,9},{9,10},{10,11},{12,13},{... | collective-permute-start | bytes 1572872 | tf_op jit(solution)/shard_map/ppermute | solution.py:582
  637.1 181.4 %reduce-scatter.13.cloned.1.call-start = ((), (), s32[]{:S(2)}) async-start(), calls=%async_computation.11 | async-start | bytes 7208960 | tf_op jit(solution)/shard_map/reduce_scatter | solution.py:644
  645.6 246.1 %reduce-scatter.17.cloned.1.call-start = ((), (), s32[]{:S(2)}) async-start(), calls=%async_computation.13 | async-start | bytes 7864320 | tf_op jit(solution)/shard_map/reduce_scatter | solution.py:644
  649.1 52.3 %collective-permute-start.42 = (bf16[1024,512]{1,0:T(8,128)(2,1)}, bf16[1024,512]{1,0:T(8,128)(2,1)S(1)}, u32[]{:S(2)}, u32[]{:S(2)}) collective-permute-start(bf16[1024,512]{1,0:T(8,128)(2,1)} %copy-done.62), channel_id=1, source_target_pairs={{4,0},{5,1},{6,2},{7,3},{12,8},{13,9},{14,10},{15,11},{20,16},{21,... | collective-permute-start | bytes 3145736 | tf_op jit(solution)/shard_map/ppermute | solution.py:633
  650.4 55.1 %collective-permute-start.46 = (bf16[128,2048]{1,0:T(8,128)(2,1)S(1)}, bf16[128,2048]{1,0:T(8,128)(2,1)S(1)}, u32[]{:S(2)}, u32[]{:S(2)}) collective-permute-start(bf16[128,2048]{1,0:T(8,128)(2,1)S(1)} %get-tuple-element.396), channel_id=1, source_target_pairs={{3,2},{2,1},{1,0},{7,6},{6,5},{5,4},{11,10},{10,9},{9,8},{15,14},{... | collective-permute-start | bytes 1572872 | tf_op jit(solution)/shard_map/ppermute | solution.py:598
  651.7 53.8 %collective-permute-start.45 = (bf16[128,2048]{1,0:T(8,128)(2,1)S(1)}, bf16[128,2048]{1,0:T(8,128)(2,1)S(1)}, u32[]{:S(2)}, u32[]{:S(2)}) collective-permute-start(bf16[128,2048]{1,0:T(8,128)(2,1)S(1)} %get-tuple-element.395), channel_id=1, source_target_pairs={{0,1},{1,2},{2,3},{4,5},{5,6},{6,7},{8,9},{9,10},{10,11},{12,13},{... | collective-permute-start | bytes 1572872 | tf_op jit(solution)/shard_map/ppermute | solution.py:598
  661.4 44.1 %collective-permute-start.44 = (bf16[128,2048]{1,0:T(8,128)(2,1)S(1)}, bf16[128,2048]{1,0:T(8,128)(2,1)S(1)}, u32[]{:S(2)}, u32[]{:S(2)}) collective-permute-start(bf16[128,2048]{1,0:T(8,128)(2,1)S(1)} %add_convert_fusion.4), channel_id=1, source_target_pairs={{0,2},{2,0},{1,3},{3,1},{4,6},{6,4},{5,7},{7,5},{8,10},{10,8},{9,1... | collective-permute-start | bytes 1572872 | tf_op jit(solution)/shard_map/ppermute | solution.py:598
  717.1 51.4 %collective-permute-start.51 = (bf16[1408,512]{1,0:T(8,128)(2,1)}, bf16[1408,512]{1,0:T(8,128)(2,1)}, u32[]{:S(2)}, u32[]{:S(2)}) collective-permute-start(bf16[1408,512]{1,0:T(8,128)(2,1)} %reduce-scatter.9.cloned.1.call-done.refs_0_), channel_id=1, source_target_pairs={{0,4},{4,0},{1,5},{5,1},{2,6},{6,2},{3,7},{7,3},{8,12},{12,8},{9,1... | collective-permute-start | bytes 4325384 | tf_op jit(solution)/shard_map/ppermute | solution.py:560
  733.2 35.3 %collective-permute-start.48 = (bf16[128,2048]{1,0:T(8,128)(2,1)}, bf16[128,2048]{1,0:T(8,128)(2,1)}, u32[]{:S(2)}, u32[]{:S(2)}) collective-permute-start(bf16[128,2048]{1,0:T(8,128)(2,1)} %add_convert_fusion.2), channel_id=1, source_target_pairs={{0,2},{2,0},{1,3},{3,1},{4,6},{6,4},{5,7},{7,5},{8,10},{10,8},{9,1... | collective-permute-start | bytes 1572872 | tf_op jit(solution)/shard_map/ppermute | solution.py:598
  781.2 171.5 %reduce-scatter.19.cloned.1.call-start = ((), (), s32[]{:S(2)}) async-start(), calls=%async_computation.14 | async-start | bytes 7208960 | tf_op jit(solution)/shard_map/reduce_scatter | solution.py:644
  781.4 37.2 %collective-permute-start.56 = (bf16[512,1408]{1,0:T(8,128)(2,1)}, bf16[512,1408]{1,0:T(8,128)(2,1)}, u32[]{:S(2)}, u32[]{:S(2)}) collective-permute-start(bf16[512,1408]{1,0:T(8,128)(2,1)} %reduce-scatter.11.cloned.1.call-done.refs_0_), channel_id=1, source_target_pairs={{0,4},{4,0},{1,5},{5,1},{2,6},{6,2},{3,7},{7,3},{8,12},{12,8},{9,1... | collective-permute-start | bytes 4325384 | tf_op jit(solution)/shard_map/ppermute | solution.py:560
  781.7 26.0 %collective-permute-start.54 = (bf16[128,2048]{1,0:T(8,128)(2,1)S(1)}, bf16[128,2048]{1,0:T(8,128)(2,1)S(1)}, u32[]{:S(2)}, u32[]{:S(2)}) collective-permute-start(bf16[128,2048]{1,0:T(8,128)(2,1)S(1)} %get-tuple-element.256), channel_id=1, source_target_pairs={{1,0},{2,1},{3,2},{5,4},{6,5},{7,6},{9,8},{10,9},{11,10},{13,12},{... | collective-permute-start | bytes 1572872 | tf_op jit(solution)/shard_map/ppermute | solution.py:582
  783.0 24.7 %collective-permute-start.55 = (bf16[128,2048]{1,0:T(8,128)(2,1)S(1)}, bf16[128,2048]{1,0:T(8,128)(2,1)S(1)}, u32[]{:S(2)}, u32[]{:S(2)}) collective-permute-start(bf16[128,2048]{1,0:T(8,128)(2,1)S(1)} %get-tuple-element.256), channel_id=1, source_target_pairs={{0,1},{1,2},{2,3},{4,5},{5,6},{6,7},{8,9},{9,10},{10,11},{12,13},{... | collective-permute-start | bytes 1572872 | tf_op jit(solution)/shard_map/ppermute | solution.py:582
  826.7 190.0 %reduce-scatter.21.cloned.1.call-start = ((), (), s32[]{:S(2)}) async-start(), calls=%async_computation.15 | async-start | bytes 7208960 | tf_op jit(solution)/shard_map/reduce_scatter | solution.py:644
  848.6 43.1 %collective-permute-start.61 = (bf16[512,1408]{1,0:T(8,128)(2,1)}, bf16[512,1408]{1,0:T(8,128)(2,1)}, u32[]{:S(2)}, u32[]{:S(2)}) collective-permute-start(bf16[512,1408]{1,0:T(8,128)(2,1)} %reduce-scatter.13.cloned.1.call-done.refs_2_), channel_id=1, source_target_pairs={{0,4},{4,0},{1,5},{5,1},{2,6},{6,2},{3,7},{7,3},{8,12},{12,8},{9,1... | collective-permute-start | bytes 4325384 | tf_op jit(solution)/shard_map/ppermute | solution.py:560
  853.7 38.1 %collective-permute-start.62 = (bf16[512,512]{1,0:T(8,128)(2,1)S(1)}, bf16[512,512]{1,0:T(8,128)(2,1)}, u32[]{:S(2)}, u32[]{:S(2)}) collective-permute-start(bf16[512,512]{1,0:T(8,128)(2,1)S(1)} %copy-done.63), channel_id=1, source_target_pairs={{0,4},{4,0},{1,5},{5,1},{2,6},{6,2},{3,7},{7,3},{8,12},{12,8},{9,1... | collective-permute-start | bytes 1572872 | tf_op jit(solution)/shard_map/ppermute | solution.py:560
  861.9 29.9 %collective-permute-start.58 = (bf16[128,2048]{1,0:T(8,128)(2,1)}, bf16[128,2048]{1,0:T(8,128)(2,1)}, u32[]{:S(2)}, u32[]{:S(2)}) collective-permute-start(bf16[128,2048]{1,0:T(8,128)(2,1)} %add_convert_fusion.1), channel_id=1, source_target_pairs={{0,2},{2,0},{1,3},{3,1},{4,6},{6,4},{5,7},{7,5},{8,10},{10,8},{9,1... | collective-permute-start | bytes 1572872 | tf_op jit(solution)/shard_map/ppermute | solution.py:598
  903.4 125.1 %reduce-scatter.23.cloned.1.call-start = ((), (), s32[]{:S(2)}) async-start(), calls=%async_computation.16 | async-start | bytes 7208960 | tf_op jit(solution)/shard_map/reduce_scatter | solution.py:644
  911.9 39.6 %collective-permute-start.67 = (bf16[512,1536]{1,0:T(8,128)(2,1)}, bf16[512,1536]{1,0:T(8,128)(2,1)S(1)}, u32[]{:S(2)}, u32[]{:S(2)}) collective-permute-start(bf16[512,1536]{1,0:T(8,128)(2,1)} %reduce-scatter.17.cloned.1.call-done.refs_0_), channel_id=1, source_target_pairs={{0,4},{4,0},{1,5},{5,1},{2,6},{6,2},{3,7},{7,3},{8,12},{12,8},{9,1... | collective-permute-start | bytes 4718600 | tf_op jit(solution)/shard_map/ppermute | solution.py:560
  913.8 24.0 %collective-permute-start.65 = (bf16[128,2048]{1,0:T(8,128)(2,1)S(1)}, bf16[128,2048]{1,0:T(8,128)(2,1)S(1)}, u32[]{:S(2)}, u32[]{:S(2)}) collective-permute-start(bf16[128,2048]{1,0:T(8,128)(2,1)S(1)} %get-tuple-element.277), channel_id=1, source_target_pairs={{1,0},{2,1},{3,2},{5,4},{6,5},{7,6},{9,8},{10,9},{11,10},{13,12},{... | collective-permute-start | bytes 1572872 | tf_op jit(solution)/shard_map/ppermute | solution.py:582
  952.7 59.1 %collective-permute-start.69 = (bf16[1408,512]{1,0:T(8,128)(2,1)}, bf16[1408,512]{1,0:T(8,128)(2,1)}, u32[]{:S(2)}, u32[]{:S(2)}) collective-permute-start(bf16[1408,512]{1,0:T(8,128)(2,1)} %reduce-scatter.19.cloned.1.call-done.refs_0_), channel_id=1, source_target_pairs={{0,4},{4,0},{1,5},{5,1},{2,6},{6,2},{3,7},{7,3},{8,12},{12,8},{9,1... | collective-permute-start | bytes 4325384 | tf_op jit(solution)/shard_map/ppermute | solution.py:560
  975.9 32.8 %collective-permute-start.68 = (bf16[1024,512]{1,0:T(8,128)(2,1)}, bf16[1024,512]{1,0:T(8,128)(2,1)}, u32[]{:S(2)}, u32[]{:S(2)}) collective-permute-start(bf16[1024,512]{1,0:T(8,128)(2,1)} %get-tuple-element.287), channel_id=1, source_target_pairs={{4,0},{5,1},{6,2},{7,3},{12,8},{13,9},{14,10},{15,11},{20,16},{21,... | collective-permute-start | bytes 3145736 | tf_op jit(solution)/shard_map/ppermute | solution.py:633
  1022.5 47.3 %collective-permute-start.76 = (bf16[512,1408]{1,0:T(8,128)(2,1)}, bf16[512,1408]{1,0:T(8,128)(2,1)}, u32[]{:S(2)}, u32[]{:S(2)}) collective-permute-start(bf16[512,1408]{1,0:T(8,128)(2,1)} %reduce-scatter.21.cloned.1.call-done.refs_0_), channel_id=1, source_target_pairs={{0,4},{4,0},{1,5},{5,1},{2,6},{6,2},{3,7},{7,3},{8,12},{12,8},{9,1... | collective-permute-start | bytes 4325384 | tf_op jit(solution)/shard_map/ppermute | solution.py:560
  1036.5 44.9 %collective-permute-start.77 = (bf16[512,1536]{1,0:T(8,128)(2,1)}, bf16[512,1536]{1,0:T(8,128)(2,1)}, u32[]{:S(2)}, u32[]{:S(2)}) collective-permute-start(bf16[512,1536]{1,0:T(8,128)(2,1)} %split.30), channel_id=1, source_target_pairs={{0,16},{8,24},{16,0},{24,8},{1,17},{9,25},{17,1},{25,9},{2,18},{10... | collective-permute-start | bytes 4718600 | tf_op jit(solution)/shard_map/ppermute | solution.py:560
  1040.1 31.6 %collective-permute-start.74 = (bf16[128,2048]{1,0:T(8,128)(2,1)}, bf16[128,2048]{1,0:T(8,128)(2,1)S(1)}, u32[]{:S(2)}, u32[]{:S(2)}) collective-permute-start(bf16[128,2048]{1,0:T(8,128)(2,1)} %get-tuple-element.387), channel_id=1, source_target_pairs={{0,1},{1,2},{2,3},{4,5},{5,6},{6,7},{8,9},{9,10},{10,11},{12,13},{... | collective-permute-start | bytes 1572872 | tf_op jit(solution)/shard_map/ppermute | solution.py:598
  1041.6 31.0 %collective-permute-start.75 = (bf16[128,2048]{1,0:T(8,128)(2,1)}, bf16[128,2048]{1,0:T(8,128)(2,1)}, u32[]{:S(2)}, u32[]{:S(2)}) collective-permute-start(bf16[128,2048]{1,0:T(8,128)(2,1)} %get-tuple-element.385), channel_id=1, source_target_pairs={{3,2},{2,1},{1,0},{7,6},{6,5},{5,4},{11,10},{10,9},{9,8},{15,14},{... | collective-permute-start | bytes 1572872 | tf_op jit(solution)/shard_map/ppermute | solution.py:598
  1045.5 36.0 %collective-permute-start.73 = (bf16[128,2048]{1,0:T(8,128)(2,1)}, bf16[128,2048]{1,0:T(8,128)(2,1)}, u32[]{:S(2)}, u32[]{:S(2)}) collective-permute-start(bf16[128,2048]{1,0:T(8,128)(2,1)} %add_convert_fusion), channel_id=1, source_target_pairs={{0,2},{2,0},{1,3},{3,1},{4,6},{6,4},{5,7},{7,5},{8,10},{10,8},{9,1... | collective-permute-start | bytes 1572872 | tf_op jit(solution)/shard_map/ppermute | solution.py:598
  1069.8 65.9 %collective-permute-start.86 = (bf16[512,1408]{1,0:T(8,128)(2,1)}, bf16[512,1408]{1,0:T(8,128)(2,1)}, u32[]{:S(2)}, u32[]{:S(2)}) collective-permute-start(bf16[512,1408]{1,0:T(8,128)(2,1)} %reduce-scatter.23.cloned.1.call-done.refs_2_), channel_id=1, source_target_pairs={{0,4},{4,0},{1,5},{5,1},{2,6},{6,2},{3,7},{7,3},{8,12},{12,8},{9,1... | collective-permute-start | bytes 4325384 | tf_op jit(solution)/shard_map/ppermute | solution.py:560
  1092.1 60.0 %collective-permute-start.83 = (bf16[512,1536]{1,0:T(8,128)(2,1)}, bf16[512,1536]{1,0:T(8,128)(2,1)}, u32[]{:S(2)}, u32[]{:S(2)}) collective-permute-start(bf16[512,1536]{1,0:T(8,128)(2,1)} %fusion.refs_0_), channel_id=1, source_target_pairs={{0,4},{4,0},{1,5},{5,1},{2,6},{6,2},{3,7},{7,3},{8,12},{12,8},{9,1... | collective-permute-start | bytes 4718600 | tf_op jit(solution)/shard_map/ppermute | solution.py:560
  1094.1 26.4 %collective-permute-start.84 = (bf16[512,512]{1,0:T(8,128)(2,1)S(1)}, bf16[512,512]{1,0:T(8,128)(2,1)S(1)}, u32[]{:S(2)}, u32[]{:S(2)}) collective-permute-start(bf16[512,512]{1,0:T(8,128)(2,1)S(1)} %split.31), channel_id=1, source_target_pairs={{0,16},{8,24},{16,0},{24,8},{1,17},{9,25},{17,1},{25,9},{2,18},{10... | collective-permute-start | bytes 1572872 | tf_op jit(solution)/shard_map/ppermute | solution.py:560
  1120.7 29.9 %collective-permute-start.85 = (bf16[512,512]{1,0:T(8,128)(2,1)S(1)}, bf16[512,512]{1,0:T(8,128)(2,1)S(1)}, u32[]{:S(2)}, u32[]{:S(2)}) collective-permute-start(bf16[512,512]{1,0:T(8,128)(2,1)S(1)} %fusion.6.refs_0_), channel_id=1, source_target_pairs={{0,4},{4,0},{1,5},{5,1},{2,6},{6,2},{3,7},{7,3},{8,12},{12,8},{9,1... | collective-permute-start | bytes 1572872 | tf_op jit(solution)/shard_map/ppermute | solution.py:560
  (172 other events, 2447.2 us)
Sparse Core Ops, SparseCore 0:
  10.2 49.0 all-gather.21
  61.4 22.6 all-gather.19
  86.2 43.3 all-gather.23
  131.6 43.3 all-gather.25
  176.5 43.3 all-gather.27
  227.5 46.9 all-gather.29
  276.6 22.5 all-gather.31
  300.8 43.3 all-gather.33
  345.8 43.3 all-gather.35
  391.2 43.3 all-gather.37
  571.0 67.6 reduce-scatter.8
  641.9 54.8 reduce-scatter.10
  699.3 31.4 reduce-scatter.14
  733.9 54.8 reduce-scatter.12
  791.8 58.3 reduce-scatter.16
  853.3 54.8 reduce-scatter.18
  911.2 54.8 reduce-scatter.20
  969.2 54.8 reduce-scatter.22

commit v4 on v3

--- a/solution.py
+++ b/solution.py
@@ -332,85 +332,97 @@
     return out, sums[:, 0]
 
 
-def attend_kernel(blocks, ctx_ref, qpos_ref, kpos_ref, q_ref, *refs):
-    keys, values = refs[: 2 * blocks : 2], refs[1 : 2 * blocks : 2]
-    out_ref, lse_ref, acc_ref, top_ref, total_ref = refs[2 * blocks :]
-    allowed = kpos_ref[...] <= qpos_ref[...]
+def attend_near_kernel(qpos_ref, kpos_ref, q_ref, key_ref, value_ref, acc_ref, top_ref, total_ref):
+    allowed = kpos_ref[0] <= qpos_ref[...]
     for half in range(PAIR // HD):
         lanes = slice(half * HD, (half + 1) * HD)
         q = q_ref[:, lanes] * jnp.asarray(HD**-0.5, LOW)
-        s = jnp.where(allowed, dot(q, keys[0][:, lanes], NT), MASKED)
+        s = jnp.where(allowed, dot(q, key_ref[:, lanes], NT), MASKED)
         top = jnp.max(s, axis=1, keepdims=True)
         p = jnp.exp(s - top)
         top_ref[half] = top
         total_ref[half] = jnp.sum(p, axis=1, keepdims=True)
-        acc_ref[half] = dot(p.astype(LOW), values[0][:, lanes], NN)
-        for b in range(1, blocks):
-
-            @pl.when(ctx_ref[0] >= b)
-            def _():
-                s = dot(q, keys[b][:, lanes], NT)
-                top = top_ref[half]
-                new_top = jnp.maximum(top, jnp.max(s, axis=1, keepdims=True))
-                p = jnp.exp(s - new_top)
-                factor = jnp.exp(top - new_top)
-                top_ref[half] = new_top
-                total_ref[half] = total_ref[half] * factor + jnp.sum(p, axis=1, keepdims=True)
-                acc_ref[half] = acc_ref[half] * factor + dot(
-                    p.astype(LOW), values[b][:, lanes], NN
-                )
-
-        out_ref[:, lanes] = acc_ref[half] / total_ref[half]
-        lse_ref[half] = top_ref[half] + jnp.log(total_ref[half])
-
-
-def attention_specs(rows, key_rows, blocks):
+        acc_ref[:, lanes] = dot(p.astype(LOW), value_ref[:, lanes], NN)
+
+
+def attend_far_kernel(blocks, qpos_ref, kpos_ref, q_ref, acc_in_ref, top_in_ref, total_in_ref, *refs):
+    keys, values = refs[: 2 * blocks : 2], refs[1 : 2 * blocks : 2]
+    out_ref, lse_ref = refs[2 * blocks :]
+    allowed = [kpos_ref[b] <= qpos_ref[...] for b in range(blocks)]
+    for half in range(PAIR // HD):
+        lanes = slice(half * HD, (half + 1) * HD)
+        q = q_ref[:, lanes] * jnp.asarray(HD**-0.5, LOW)
+        top, total, acc = top_in_ref[half], total_in_ref[half], acc_in_ref[:, lanes]
+        for b in range(blocks):
+            s = jnp.where(allowed[b], dot(q, keys[b][:, lanes], NT), MASKED)
+            new_top = jnp.maximum(top, jnp.max(s, axis=1, keepdims=True))
+            p = jnp.exp(s - new_top)
+            factor = jnp.exp(top - new_top)
+            total = total * factor + jnp.sum(p, axis=1, keepdims=True)
+            acc = acc * factor + dot(p.astype(LOW), values[b][:, lanes], NN)
+            top = new_top
+        out_ref[:, lanes] = acc / total
+        lse_ref[half] = top + jnp.log(total)
+
+
+def pair_call(kernel, name, rows, width, kpos, operands, stacked, outs, flops):
+    blocks, _, key_rows = kpos.shape
     column = lambda i: (0, i)
-    fixed = lambda i: (0, 0)
+    specs = {
+        "row": pl.BlockSpec((rows, PAIR), column),
+        "head": pl.BlockSpec((PAIR // HD, rows, 1), lambda i: (i, 0, 0)),
+        "keys": pl.BlockSpec((2 * key_rows, PAIR), column),
+    }
+    shapes = {"row": (rows, width), "head": (width // HD, rows, 1), "keys": (2 * key_rows, width)}
+    halves = [pl.BlockSpec((key_rows, PAIR), lambda i, c=c: (c, i)) for c in range(2)]
     common = [
-        pl.BlockSpec(memory_space=pltpu.SMEM),
-        pl.BlockSpec((rows, 1), fixed),
-        pl.BlockSpec((1, key_rows), fixed),
+        pl.BlockSpec((rows, 1), lambda i: (0, 0)),
+        pl.BlockSpec((blocks, 1, key_rows), lambda i: (0, 0, 0)),
     ]
-    row = pl.BlockSpec((rows, PAIR), column)
-    lse = pl.BlockSpec((PAIR // HD, rows, 1), lambda i: (i, 0, 0))
-    halves = [pl.BlockSpec((key_rows, PAIR), lambda i, c=c: (c, i)) for c in range(2)]
-    return common, row, lse, halves * blocks
-
-
-def attend(ctx, qpos, kpos, q, pairs_of_rows):
+    return pl.pallas_call(
+        kernel,
+        grid=(width // PAIR,),
+        in_specs=common + [specs[k] for k, _ in operands[1:]] + halves * len(stacked),
+        out_specs=[specs[k] for k, _ in outs],
+        out_shape=[jax.ShapeDtypeStruct(shapes[k], t) for k, t in outs],
+        compiler_params=pltpu.CompilerParams(vmem_limit_bytes=40 * 1024 * 1024),
+        cost_estimate=work(flops * rows * key_rows * blocks * width),
+        name=name,
+    )(operands[0], kpos, *[v for _, v in operands[1:]], *[s for s in stacked for c in range(2)])
+
+
+def attend_near(qpos, kpos, q, own):
     rows, width = q.shape
-    key_rows, blocks, heads = pairs_of_rows[0].shape[0] // 2, len(pairs_of_rows), width // HD
-    common, row, lse, keys = attention_specs(rows, key_rows, blocks)
-    per_pair = PAIR // HD
-    return pl.pallas_call(
-        functools.partial(attend_kernel, blocks),
-        grid=(width // PAIR,),
-        in_specs=common + [row] + keys,
-        out_specs=[row, lse],
-        out_shape=[
-            jax.ShapeDtypeStruct((rows, width), WIDE),
-            jax.ShapeDtypeStruct((heads, rows, 1), WIDE),
-        ],
-        scratch_shapes=[
-            pltpu.VMEM((per_pair, rows, HD), WIDE),
-            pltpu.VMEM((per_pair, rows, 1), WIDE),
-            pltpu.VMEM((per_pair, rows, 1), WIDE),
-        ],
-        compiler_params=pltpu.CompilerParams(vmem_limit_bytes=32 * 1024 * 1024),
-        cost_estimate=work(43 * rows * key_rows * blocks * width),
-        name="attend",
-    )(ctx, qpos, kpos, q, *[p for p in pairs_of_rows for c in range(2)])
-
-
-def attend_back_kernel(
-    blocks, ctx_ref, qpos_ref, kpos_ref, q_ref, grad_ref, out_ref, lse_ref, *refs
-):
+    outs = [("row", WIDE), ("head", WIDE), ("head", WIDE)]
+    return pair_call(
+        attend_near_kernel, "attend_near", rows, width, kpos, [qpos, ("row", q)], [own], outs, 43
+    )
+
+
+def attend_far(qpos, kpos, q, near, far):
+    rows, width = q.shape
+    kinds = ("row", "head", "head")
+    operands = [qpos, ("row", q), *zip(kinds, near)]
+    return pair_call(
+        functools.partial(attend_far_kernel, len(far)),
+        "attend_far",
+        rows,
+        width,
+        kpos,
+        operands,
+        far,
+        [("row", WIDE), ("head", WIDE)],
+        43,
+    )
+
+
+def attend_back_kernel(blocks, more, qpos_ref, kpos_ref, q_ref, grad_ref, out_ref, lse_ref, *refs):
+    before, refs = refs[:more], refs[more:]
     keys, values = refs[: 2 * blocks : 2], refs[1 : 2 * blocks : 2]
     dq_ref = refs[2 * blocks]
     dboth = refs[2 * blocks + 1 :]
     key_rows = keys[0].shape[0]
-    allowed = kpos_ref[...] <= qpos_ref[...]
+    allowed = [kpos_ref[b] <= qpos_ref[...] for b in range(blocks)]
     scale = HD**-0.5
     for half in range(PAIR // HD):
         lanes = slice(half * HD, (half + 1) * HD)
@@ -418,50 +430,35 @@
         grad = grad_ref[:, lanes]
         lse = lse_ref[half]
         delta = jnp.sum(grad.astype(WIDE) * out_ref[:, lanes], axis=1, keepdims=True)
-
-        def block(b):
+        dq = []
+        for b in range(blocks):
             k = keys[b][:, lanes]
-            s = dot(q, k, NT)
-            if b == 0:
-                s = jnp.where(allowed, s, MASKED)
+            s = jnp.where(allowed[b], dot(q, k, NT), MASKED)
             p = jnp.exp(s - lse)
             dp = dot(grad, values[b][:, lanes], NT)
             ds = (p * (dp - delta)).astype(LOW)
             kind = dboth[b].dtype
             dboth[b][key_rows:, lanes] = dot(p.astype(LOW), grad, TN).astype(kind)
             dboth[b][:key_rows, lanes] = dot(ds, q, TN).astype(kind)
-            return dot(ds, k, NN) * scale
-
-        dq_ref[:, lanes] = block(0)
-        for b in range(1, blocks):
-
-            @pl.when(ctx_ref[0] >= b)
-            def _():
-                dq_ref[:, lanes] += block(b)
-
-            @pl.when(ctx_ref[0] < b)
-            def _():
-                dboth[b][:, lanes] = jnp.zeros((2 * key_rows, HD), LOW)
-
-
-def attend_back(ctx, qpos, kpos, q, grad, out, lse, pairs_of_rows):
+            dq.append(dot(ds, k, NN))
+        dq_ref[:, lanes] = total_of([total_of(dq) * scale] + [r[:, lanes] for r in before])
+
+
+def attend_back(qpos, kpos, q, grad, out, lse, stacked, kind, before):
     rows, width = q.shape
-    key_rows, blocks = pairs_of_rows[0].shape[0] // 2, len(pairs_of_rows)
-    common, row, lse_spec, keys = attention_specs(rows, key_rows, blocks)
-    both = pl.BlockSpec((2 * key_rows, PAIR), lambda i: (0, i))
-    near = [jax.ShapeDtypeStruct((2 * key_rows, width), WIDE)]
-    far = [jax.ShapeDtypeStruct((2 * key_rows, width), LOW)] * (blocks - 1)
-    results = pl.pallas_call(
-        functools.partial(attend_back_kernel, blocks),
-        grid=(width // PAIR,),
-        in_specs=common + [row, row, row, lse_spec] + keys,
-        out_specs=[row] + [both] * blocks,
-        out_shape=[jax.ShapeDtypeStruct((rows, width), WIDE)] + near + far,
-        compiler_params=pltpu.CompilerParams(vmem_limit_bytes=40 * 1024 * 1024),
-        cost_estimate=work(75 * rows * key_rows * blocks * width),
-        name="attend_back",
-    )(ctx, qpos, kpos, q, grad, out, lse, *[p for p in pairs_of_rows for c in range(2)])
-    return results[0], results[1], results[2:]
+    rest = [("row", v) for v in (q, grad, out)] + [("head", lse)] + [("row", v) for v in before]
+    results = pair_call(
+        functools.partial(attend_back_kernel, len(stacked), len(before)),
+        "attend_back",
+        rows,
+        width,
+        kpos,
+        [qpos] + rest,
+        stacked,
+        [("row", WIDE)] + [("keys", kind)] * len(stacked),
+        75,
+    )
+    return results[0], results[1:]
 
 
 def norm_back_kernel(count, *refs):
@@ -566,7 +563,7 @@
 
 class Line:
     def __init__(self, own_rows):
-        n_tensor = lax.axis_size("tensor")
+        n_tensor, n_ctx = lax.axis_size("tensor"), lax.axis_size("ctx")
         tensor, ctx = lax.axis_index("tensor"), lax.axis_index("ctx")
         self.count, self.tensor = n_tensor, tensor
         row = jnp.arange(own_rows, dtype=jnp.int32)
@@ -574,7 +571,9 @@
         place = (chip[:, None] * own_rows + row[None, :]).reshape(-1)
         block = n_tensor * own_rows
         self.places = ctx * block + place
-        self.ctx = ctx.astype(jnp.int32).reshape(1)
+        self.far_places = [
+            jnp.where(ctx >= s, (ctx - s) * block + place, 1 << 30) for s in range(1, n_ctx)
+        ]
         self.own_rows = own_rows
 
     def gather_rows(self, low):
@@ -726,7 +725,8 @@
     tables = rotary_tables(plan.places)
     tables_back = (tables[0], -tables[1], -tables[2])
     qpos = plan.places[:, None]
-    kpos = plan.places[None, :]
+    near_places = plan.places[None, None, :]
+    far_places = jnp.stack(plan.far_places)[:, None, :]
     gains = (norm_gains)
     biases = (norm_biases)
     qkv_bias_own = lax.dynamic_slice_in_dim(qkv_bias, lax.axis_index("tensor") * heads_width, heads_width, 2)
@@ -766,23 +766,28 @@
             late_cotangent, queries = lax.optimization_barrier((cotangent[0], queries))
             grad_stream = late_cotangent.astype(WIDE)
             branch = plan.gather_rows(late_cotangent)
-        all_kv = [keys_values] + plan.far_keys(keys_values)
-        attended, lse = attend(plan.ctx, qpos, kpos, queries, all_kv)
+        prepared = {}
+        if not last:
+            prepared, queries = weight_jobs(layer + 1, queries)
+        far_kv = plan.far_keys(keys_values)
+        near = attend_near(qpos, near_places, queries, keys_values)
+        attended, lse = attend_far(qpos, far_places, queries, near, far_kv)
         attended_low = meanwhile(attended.astype(LOW), now["out"])
+        attended_low = held(attended_low, *map(prepared.get, ("gate", "up")))
         if layer == 0:
             attended_low, branch = lax.optimization_barrier((attended_low, branch))
         else:
             attended_low = meanwhile(attended_low, now["up"])
         out_full = now["out"].finish()
         mid = stream + plan.sum_of(plan.sum_rows(times_wide(attended_low, out_full, "out")))
-        mid = meanwhile(mid, now["gate"], now["up"])
+        mid = meanwhile(mid, now["gate"])
         if layer > 0:
             mid = meanwhile(mid, now["down"])
         else:
-            later, mid = weight_jobs(layer + 1, mid)
+            later = prepared
         normed_two, unit_two, inverse_two = layer_norm_rows(mid, gains[layer, 1], biases[layer, 1])
         rows_two = plan.gather_rows(normed_two.astype(LOW))
-        rows_two = meanwhile(rows_two, now["down"], later.get("qkv"))
+        rows_two = meanwhile(rows_two, now["up"], now["down"], later.get("qkv"))
         flat = lambda v: v.reshape(v.shape[0] * v.shape[1], v.shape[2])
         gate_full, up_full = flat(now["gate"].finish()), flat(now["up"].finish())
         gate, up, activated = gate_up_rows(rows_two, gate_full, up_full)
@@ -797,7 +802,7 @@
             (
                 (qkv_full, out_full, gate_full, up_full, down_full),
                 (rows_one, unit_one, inverse_one),
-                (queries, all_kv, attended, attended_low, lse),
+                (queries, keys_values, far_kv, attended, attended_low, lse),
                 (rows_two, unit_two, inverse_two),
                 (gate, up, activated),
             )
@@ -811,7 +816,7 @@
         (
             (qkv_full, out_full, gate_full, up_full, down_full),
             (rows_one, unit_one, inverse_one),
-            (queries, all_kv, attended, attended_low, lse),
+            (queries, keys_values, far_kv, attended, attended_low, lse),
             (rows_two, unit_two, inverse_two),
             (gate, up, activated),
         ) = saved[layer]
@@ -852,7 +857,8 @@
         if layer > 0:
             mine["down"] = out_job(activated, branch)
         mine["gate"] = in_job(rows_two, grad_gate)
-        mine["up"] = in_job(rows_two, grad_up)
+        if layer == 0:
+            mine["up"] = in_job(rows_two, grad_up)
         top = layer + 1 == LAYERS
         if top:
             late, hidden_low = lax.optimization_barrier((activated, hidden_low))
@@ -865,20 +871,29 @@
             attention, partial_out = lax.optimization_barrier((attention, partial_out))
             output = (mid + plan.sum_of(plan.sum_rows(partial_out))).astype(LOW)[None]
         grad_attended = out_back(attention, out_full)
-        grad_queries, grad_kv, far_grads = attend_back(
-            plan.ctx, qpos, kpos, queries, grad_attended, attended, lse, all_kv
+        shared = (queries, grad_attended, attended, lse)
+        far_queries, far_grads = attend_back(qpos, far_places, *shared, far_kv, LOW, [])
+        returned = plan.far_key_grads(far_grads)
+        grad_queries, grad_kv = attend_back(
+            qpos, near_places, *shared, [keys_values], WIDE, [far_queries]
         )
-        grad_queries, attention = lax.optimization_barrier((grad_queries, attention))
+        if top:
+            grad_queries, output = lax.optimization_barrier((grad_queries, output))
+        projected, qkv_bias_grads[layer] = project_back(
+            grad_queries, grad_kv[0], returned, tables_back
+        )
+        projected, (attention, grad_up) = lax.optimization_barrier(
+            (projected, (attention, grad_up))
+        )
+        if layer > 0:
+            mine["up"] = in_job(rows_two, grad_up)
         if layer == 0:
             mine["out"] = Job(
                 pair_stages(plan, lambda r, a=attention: (attended_low, own_part(a, r)), 1)
             )
         else:
             mine["out"] = out_job(attended_low, attention)
-        projected, qkv_bias_grads[layer] = project_back(
-            grad_queries, grad_kv, plan.far_key_grads(far_grads), tables_back
-        )
-        projected = meanwhile(projected, mine["down"], *old("qkv"))
+        projected = meanwhile(projected, mine["down"] if layer > 0 else None, *old("qkv"))
         if not top:
             above_done, projected = lax.optimization_barrier(
                 ({k: j.finish() for k, j in above.items()}, projected)
@@ -896,10 +911,9 @@
             )
             projected = meanwhile(projected, *map(mine.get, ("qkv", "out", "gate")))
         partial_in = project_in(projected, qkv_full)
-        if top:
-            partial_in, output = lax.optimization_barrier((partial_in, output))
         if layer == 0:
-            partial_in = held(meanwhile(partial_in, mine["up"], mine["qkv"]), mine["out"])
+            partial_in = meanwhile(partial_in, *map(mine.get, ("down", "up", "qkv")))
+            partial_in = held(partial_in, mine["out"])
         summed = plan.sum_rows(partial_in)
         if layer > 0:
             summed = meanwhile(summed, mine["down"])

time: 1180 us -> 1160 us (0.983)
  Pallas kernels: 246 us -> 290 us
  waiting for transfers between devices: 514 us -> 488 us
  starting transfers between devices: 211 us -> 192 us
  local copies, waits for them, and re-layouts: 108 us -> 90.6 us
    ppermute x2, waiting for transfers between devices: 60.4 us -> 15.2 us  [far_key_grads(): lax.ppermute(values[s - 1], 'ctx', [(i + s, i) for i in range(count - s)])]
    pallas_call x4 -> x8, Pallas kernels: 41.9 us -> 85.9 us  [pair_call(): pl.pallas_call(kernel, grid=(width // PAIR,), in_specs=common + [specs[k]...]
    ppermute x32, waiting for transfers between devices: 203 us -> 181 us  [gather_rows(): send = lambda v, *route: lax.ppermute(v, 'tensor', list(route))]
    ppermute x19, waiting for transfers between devices: 53.3 us -> 75.4 us  [swapped(): return lax.ppermute(value, axis, [(i, i ^ mask) for i in range(count)])]
    unnamed x263 -> x247, local copies, waits for them, and re-layouts: 75.6 us -> 56.9 us
    ppermute x32, waiting for transfers between devices: 168 us -> 185 us  [sum_rows(): send = lambda v, *route: lax.ppermute(v, 'tensor', list(route))]
    ppermute x32, starting transfers between devices: 95.2 us -> 83.3 us  [sum_rows(): send = lambda v, *route: lax.ppermute(v, 'tensor', list(route))]
  transfers between devices with their start and end apart: 105 -> 105, of which waited for: 48 -> 50; matrix products, arithmetic and copies ran while one was open for 8% -> 9% of each run, Pallas kernels for 18% -> 22%
where the time goes in v4:
time: 1160 us; the launch traced here: 1150 us
  waiting for transfers between devices  488 us (42%)
  Pallas kernels  290 us (25%)
  starting transfers between devices  192 us (17%)
  local copies, waits for them, and re-layouts  90.6 us (8%)
  other arithmetic  73.2 us (6%)
  between operations  17 us (1%)
    ppermute x32, waiting for transfers between devices, sum_rows(): send = lambda v, *route: lax.ppermute(v, 'tensor', list(route))  185 us
    ppermute x32, waiting for transfers between devices, gather_rows(): send = lambda v, *route: lax.ppermute(v, 'tensor', list(route))  181 us
    pallas_call x32, Pallas kernels, tiled(): pl.pallas_call(kernel, grid=(steps,), in_specs=[pl.BlockSpec(block, index...  160 us
    pallas_call x8, Pallas kernels, pair_call(): pl.pallas_call(kernel, grid=(width // PAIR,), in_specs=common + [specs[k]...  85.9 us
    ppermute x32, starting transfers between devices, sum_rows(): send = lambda v, *route: lax.ppermute(v, 'tensor', list(route))  83.3 us
    ppermute x32, starting transfers between devices, gather_rows(): send = lambda v, *route: lax.ppermute(v, 'tensor', list(route))  78.9 us
    ppermute x19, waiting for transfers between devices, swapped(): return lax.ppermute(value, axis, [(i, i ^ mask) for i in range(count)])  75.4 us
    unnamed x247, local copies, waits for them, and re-layouts  56.9 us
  transfers between devices with their start and end apart: 105, of which 50 were waited for; matrix products, arithmetic and copies ran while one was open for 9% of the time, Pallas kernels for 22%

profile of v4, /device:TPU:0, one launch (start us, length us, event | category | flops | bytes accessed | tf_op | source)
XLA Modules:
  0.0 1150.6 jit_solution(11754405145036952354)
XLA Ops:
  32.3 16.2 %collective-permute-done = bf16[128,2048]{1,0:T(8,128)(2,1)} collective-permute-done((bf16[128,2048]{1,0:T(8,128)(2,1)S(1)}, bf16[128,2048]{1,0:T(8,128)(2,1)}, u32[]{:S(2)}, u32[]{:S(2)}) %collective-permute-start) | collective-permute-done | bytes 524320 | tf_op jit(solution)/shard_map/ppermute | solution.py:581
  52.4 10.4 collective-permute-done.1
  64.2 7.4 project.2
  75.5 6.0 collective-permute-start.8
  87.5 9.8 attend_near.2
  105.7 13.9 %attend_far.2 = (f32[512,512]{1,0:T(8,128)S(1)}, f32[8,512,1]{2,1,0:T(8,128)S(1)}) custom-call(s32[512,1]{1,0:T(8,128)S(1)} %copy.70.qpos_ref, s32[1,1,512]{2,1,0:T(1,128)S(1)} %bitcast.103, bf16[512,512]{1,0:T(8,128)(2,1)S(1)} %get-tuple-element.196.q_ref, f32[512,512]{1,0:T(8,128)S(1)} %get-tuple-element.198.acc_in_ref, ...), custom_call_target="tpu_custom_call" | custom-call | flops 5771362304 | tf_op jit(solution)/shard_map/attend_far/pallas_call | solution.py:382
  137.4 6.4 collective-permute-done.9
  155.1 10.6 collective-permute-done.10
  174.9 8.8 collective-permute-start.16
  183.7 11.7 %collective-permute-done.13 = bf16[128,2048]{1,0:T(8,128)(2,1)} collective-permute-done((bf16[128,2048]{1,0:T(8,128)(2,1)}, bf16[128,2048]{1,0:T(8,128)(2,1)}, u32[]{:S(2)}, u32[]{:S(2)}) %collective-permute-start.13) | collective-permute-done | bytes 524320 | tf_op jit(solution)/shard_map/ppermute | solution.py:581
  198.0 9.6 collective-permute-done.14
  211.6 8.3 all-gather.28.cloned.1.call-done
  223.5 11.1 gate_up.2
  253.4 6.3 collective-permute-done.17
  263.4 9.3 collective-permute-done.20
  272.7 13.0 %collective-permute-done.18 = bf16[128,2048]{1,0:T(8,128)(2,1)S(1)} collective-permute-done((bf16[128,2048]{1,0:T(8,128)(2,1)S(1)}, bf16[128,2048]{1,0:T(8,128)(2,1)S(1)}, u32[]{:S(2)}, u32[]{:S(2)}) %collective-permute-start.18) | collective-permute-done | bytes 524320 | tf_op jit(solution)/shard_map/ppermute | solution.py:597
  294.0 8.3 collective-permute-start.24
  302.3 17.7 %collective-permute-done.21 = bf16[128,2048]{1,0:T(8,128)(2,1)} collective-permute-done((bf16[128,2048]{1,0:T(8,128)(2,1)}, bf16[128,2048]{1,0:T(8,128)(2,1)}, u32[]{:S(2)}, u32[]{:S(2)}) %collective-permute-start.21) | collective-permute-done | bytes 524320 | tf_op jit(solution)/shard_map/ppermute | solution.py:581
  322.5 8.9 collective-permute-done.22
  340.9 7.4 project.3
  351.6 9.8 attend_near.3
  361.5 12.9 %collective-permute-done.25.refs_0_.refs_1_ = bf16[1024,512]{1,0:T(8,128)(2,1)S(1)} collective-permute-done((bf16[1024,512]{1,0:T(8,128)(2,1)S(1)}, bf16[1024,512]{1,0:T(8,128)(2,1)S(1)}, u32[]{:S(2)}, u32[]{:S(2)}) %collective-permute-start.25) | collective-permute-done | bytes 1048608 | tf_op jit(solution)/shard_map/ppermute | solution.py:625
  374.4 13.9 %attend_far.3 = (f32[512,512]{1,0:T(8,128)S(1)}, f32[8,512,1]{2,1,0:T(8,128)S(1)}) custom-call(s32[512,1]{1,0:T(8,128)S(1)} %copy.70.qpos_ref, s32[1,1,512]{2,1,0:T(1,128)S(1)} %bitcast.104, bf16[512,512]{1,0:T(8,128)(2,1)S(1)} %get-tuple-element.229.q_ref, f32[512,512]{1,0:T(8,128)S(1)} %get-tuple-element.231.acc_in_ref, ...), custom_call_target="tpu_custom_call" | custom-call | flops 5771362304 | tf_op jit(solution)/shard_map/attend_far/pallas_call | solution.py:382
  404.1 6.4 collective-permute-done.26
  414.1 8.9 collective-permute-done.29
  423.0 11.5 %collective-permute-done.27 = bf16[128,2048]{1,0:T(8,128)(2,1)S(1)} collective-permute-done((bf16[128,2048]{1,0:T(8,128)(2,1)S(1)}, bf16[128,2048]{1,0:T(8,128)(2,1)S(1)}, u32[]{:S(2)}, u32[]{:S(2)}) %collective-permute-start.27) | collective-permute-done | bytes 524320 | tf_op jit(solution)/shard_map/ppermute | solution.py:597
  442.8 8.1 collective-permute-start.33
  450.9 17.2 %collective-permute-done.30 = bf16[128,2048]{1,0:T(8,128)(2,1)S(1)} collective-permute-done((bf16[128,2048]{1,0:T(8,128)(2,1)S(1)}, bf16[128,2048]{1,0:T(8,128)(2,1)S(1)}, u32[]{:S(2)}, u32[]{:S(2)}) %collective-permute-start.30) | collective-permute-done | bytes 524320 | tf_op jit(solution)/shard_map/ppermute | solution.py:581
  469.6 9.5 collective-permute-done.31
  479.5 11.5 %gate_up.3 = (f32[512,1408]{1,0:T(8,128)}, f32[512,1408]{1,0:T(8,128)}, bf16[512,1408]{1,0:T(8,128)(2,1)S(1)}) custom-call(bf16[512,2048]{1,0:T(8,128)(2,1)S(1)} %pad_maximum_fusion.4.rows_ref.a_ref, bf16[2048,1408]{1,0:T(8,128)(2,1)} %all-gather.34.cloned.1.call-done, bf16[2048,1408]{1,0:T(8,128)(2,1)} %all-gather.36.cloned.1.call-done), custom_call_target="tpu_custom_call" | custom-call | flops 14763950080 | tf_op jit(solution)/shard_map/gate_up/pallas_call | solution.py:77
  492.1 7.3 gate_up_back.2
  499.4 10.3 gate_up_in.2.refs_0_
  515.8 8.9 collective-permute-done.34
  525.7 7.7 collective-permute-start.35
  535.6 20.2 %collective-permute-done.35.refs_1_ = bf16[128,2048]{1,0:T(8,128)(2,1)} collective-permute-done((bf16[128,2048]{1,0:T(8,128)(2,1)}, bf16[128,2048]{1,0:T(8,128)(2,1)}, u32[]{:S(2)}, u32[]{:S(2)}) %collective-permute-start.35) | collective-permute-done | bytes 524320 | tf_op jit(solution)/shard_map/ppermute | solution.py:597
  583.8 12.2 %collective-permute-done.38 = bf16[128,2048]{1,0:T(8,128)(2,1)S(1)} collective-permute-done((bf16[128,2048]{1,0:T(8,128)(2,1)}, bf16[128,2048]{1,0:T(8,128)(2,1)S(1)}, u32[]{:S(2)}, u32[]{:S(2)}) %collective-permute-start.38) | collective-permute-done | bytes 524320 | tf_op jit(solution)/shard_map/ppermute | solution.py:581
  604.5 8.5 collective-permute-done.39
  625.4 10.0 attend_back.4
  643.8 9.3 attend_back.5
  653.1 13.7 %collective-permute-done.43 = bf16[128,2048]{1,0:T(8,128)(2,1)S(1)} collective-permute-done((bf16[128,2048]{1,0:T(8,128)(2,1)S(1)}, bf16[128,2048]{1,0:T(8,128)(2,1)S(1)}, u32[]{:S(2)}, u32[]{:S(2)}) %collective-permute-start.43) | collective-permute-done | bytes 524320 | tf_op jit(solution)/shard_map/ppermute | solution.py:597
  684.5 6.2 project_in.2.refs_0_
  699.1 6.6 collective-permute-done.47
  709.1 7.9 collective-permute-done.49.refs_2_
  717.8 18.8 %collective-permute-done.48.refs_1_ = bf16[128,2048]{1,0:T(8,128)(2,1)} collective-permute-done((bf16[128,2048]{1,0:T(8,128)(2,1)}, bf16[128,2048]{1,0:T(8,128)(2,1)}, u32[]{:S(2)}, u32[]{:S(2)}) %collective-permute-start.48) | collective-permute-done | bytes 524320 | tf_op jit(solution)/shard_map/ppermute | solution.py:597
  755.8 12.0 %collective-permute-done.52 = bf16[128,2048]{1,0:T(8,128)(2,1)S(1)} collective-permute-done((bf16[128,2048]{1,0:T(8,128)(2,1)S(1)}, bf16[128,2048]{1,0:T(8,128)(2,1)S(1)}, u32[]{:S(2)}, u32[]{:S(2)}) %collective-permute-start.52) | collective-permute-done | bytes 524320 | tf_op jit(solution)/shard_map/ppermute | solution.py:581
  769.1 8.7 collective-permute-done.54
  777.8 9.1 collective-permute-done.53
  798.6 7.3 gate_up_back.3
  805.9 10.3 gate_up_in.3.refs_0_
  825.0 6.8 collective-permute-done.57
  835.1 8.0 collective-permute-done.59.refs_2_
  843.1 20.0 %collective-permute-done.62.refs_1_ = bf16[512,512]{1,0:T(8,128)(2,1)} collective-permute-done((bf16[512,512]{1,0:T(8,128)(2,1)S(1)}, bf16[512,512]{1,0:T(8,128)(2,1)}, u32[]{:S(2)}, u32[]{:S(2)}) %collective-permute-start.62) | collective-permute-done | bytes 524320 | tf_op jit(solution)/shard_map/ppermute | solution.py:557
  891.8 14.7 %collective-permute-done.63 = bf16[128,2048]{1,0:T(8,128)(2,1)} collective-permute-done((bf16[128,2048]{1,0:T(8,128)(2,1)S(1)}, bf16[128,2048]{1,0:T(8,128)(2,1)}, u32[]{:S(2)}, u32[]{:S(2)}) %collective-permute-start.63) | collective-permute-done | bytes 524320 | tf_op jit(solution)/shard_map/ppermute | solution.py:581
  909.8 12.6 %collective-permute-done.64 = bf16[128,2048]{1,0:T(8,128)(2,1)} collective-permute-done((bf16[128,2048]{1,0:T(8,128)(2,1)}, bf16[128,2048]{1,0:T(8,128)(2,1)}, u32[]{:S(2)}, u32[]{:S(2)}) %collective-permute-start.64) | collective-permute-done | bytes 524320 | tf_op jit(solution)/shard_map/ppermute | solution.py:581
  928.9 10.0 attend_back.6
  940.5 9.3 attend_back.7
  949.8 15.2 %collective-permute-done.68.refs_0_ = bf16[1024,512]{1,0:T(8,128)(2,1)S(1)} collective-permute-done((bf16[1024,512]{1,0:T(8,128)(2,1)S(1)}, bf16[1024,512]{1,0:T(8,128)(2,1)S(1)}, u32[]{:S(2)}, u32[]{:S(2)}) %collective-permute-start.68) | collective-permute-done | bytes 1048608 | tf_op jit(solution)/shard_map/ppermute | solution.py:632
  981.3 6.0 project_in.3.refs_0_
  988.7 20.0 %collective-permute-done.69.refs_1_ = bf16[1408,512]{1,0:T(8,128)(2,1)} collective-permute-done((bf16[1408,512]{1,0:T(8,128)(2,1)}, bf16[1408,512]{1,0:T(8,128)(2,1)}, u32[]{:S(2)}, u32[]{:S(2)}) %collective-permute-start.69) | collective-permute-done | bytes 1441824 | tf_op jit(solution)/shard_map/ppermute | solution.py:557
  1046.4 9.2 finish_gate_up.2.refs_4_
  1057.2 7.3 collective-permute-done.73.refs_1_
  1075.6 17.7 %collective-permute-done.78 = f32[14,2048]{1,0:T(8,128)S(1)} collective-permute-done((f32[14,2048]{1,0:T(8,128)S(1)}, f32[14,2048]{1,0:T(8,128)S(1)}, u32[]{:S(2)}, u32[]{:S(2)}) %collective-permute-start.78) | collective-permute-done | bytes 114720 | tf_op jit(solution)/shard_map/ppermute | solution.py:557
  1107.4 6.3 collective-permute-done.82
  1125.0 8.8 finish_gate_up.3
  (592 shorter events, 455.6 us)
Async XLA Ops:
  7.2 56.9 %all-gather.22.cloned.1.call-start = ((), (), s32[]{:S(2)}) async-start(), calls=%async_computation.17 | async-start | bytes 7864320 | tf_op jit(solution)/shard_map/all_gather | solution.py:639
  10.0 112.1 %all-gather.20.cloned.1.call-start = ((), (), s32[]{:S(2)}) async-start(), calls=%async_computation.8 | async-start | bytes 2621440 | tf_op jit(solution)/shard_map/all_gather | solution.py:639
  10.9 156.2 %all-gather.24.cloned.1.call-start = ((), (), s32[]{:S(2)}) async-start(), calls=%async_computation.18 | async-start | bytes 7208960 | tf_op jit(solution)/shard_map/all_gather | solution.py:639
  16.1 195.5 %all-gather.26.cloned.1.call-start = ((), (), s32[]{:S(2)}) async-start(), calls=%async_computation.19 | async-start | bytes 7208960 | tf_op jit(solution)/shard_map/all_gather | solution.py:639
  16.7 203.3 %all-gather.28.cloned.1.call-start = ((), (), s32[]{:S(2)}) async-start(), calls=%async_computation.20 | async-start | bytes 7208960 | tf_op jit(solution)/shard_map/all_gather | solution.py:639
  20.2 28.2 %collective-permute-start = (bf16[128,2048]{1,0:T(8,128)(2,1)S(1)}, bf16[128,2048]{1,0:T(8,128)(2,1)}, u32[]{:S(2)}, u32[]{:S(2)}) collective-permute-start(bf16[128,2048]{1,0:T(8,128)(2,1)S(1)} %get-tuple-element.432), channel_id=1, source_target_pairs={{0,2},{2,0},{1,3},{3,1},{4,6},{6,4},{5,7},{7,5},{8,10},{10,8},{9,1... | collective-permute-start | bytes 1572872 | tf_op jit(solution)/shard_map/ppermute | solution.py:581
  24.3 28.1 %collective-permute-start.2 = (bf16[128,2048]{1,0:T(8,128)(2,1)S(1)}, bf16[128,2048]{1,0:T(8,128)(2,1)S(1)}, u32[]{:S(2)}, u32[]{:S(2)}) collective-permute-start(bf16[128,2048]{1,0:T(8,128)(2,1)S(1)} %get-tuple-element.432), channel_id=1, source_target_pairs={{1,0},{2,1},{3,2},{5,4},{6,5},{7,6},{9,8},{10,9},{11,10},{13,12},{... | collective-permute-start | bytes 1572872 | tf_op jit(solution)/shard_map/ppermute | solution.py:581
  25.6 26.8 %collective-permute-start.3 = (bf16[128,2048]{1,0:T(8,128)(2,1)S(1)}, bf16[128,2048]{1,0:T(8,128)(2,1)S(1)}, u32[]{:S(2)}, u32[]{:S(2)}) collective-permute-start(bf16[128,2048]{1,0:T(8,128)(2,1)S(1)} %get-tuple-element.432), channel_id=1, source_target_pairs={{0,1},{1,2},{2,3},{4,5},{5,6},{6,7},{8,9},{9,10},{10,11},{12,13},{... | collective-permute-start | bytes 1572872 | tf_op jit(solution)/shard_map/ppermute | solution.py:581
  64.1 222.9 %all-gather.30.cloned.1.call-start = ((), (), s32[]{:S(2)}) async-start(), calls=%async_computation.21 | async-start | bytes 7864320 | tf_op jit(solution)/shard_map/all_gather | solution.py:639
  71.7 27.3 %collective-permute-start.5 = (bf16[128,2048]{1,0:T(8,128)(2,1)}, bf16[128,2048]{1,0:T(8,128)(2,1)}, u32[]{:S(2)}, u32[]{:S(2)}) collective-permute-start(bf16[128,2048]{1,0:T(8,128)(2,1)} %bitcast.4), channel_id=1, source_target_pairs={{0,2},{2,0},{1,3},{3,1},{4,6},{6,4},{5,7},{7,5},{8,10},{10,8},{9,1... | collective-permute-start | bytes 1572872 | tf_op jit(solution)/shard_map/ppermute | solution.py:581
  74.2 47.9 %collective-permute-start.7 = (bf16[128,2048]{1,0:T(8,128)(2,1)}, bf16[128,2048]{1,0:T(8,128)(2,1)}, u32[]{:S(2)}, u32[]{:S(2)}) collective-permute-start(bf16[128,2048]{1,0:T(8,128)(2,1)} %bitcast.4), channel_id=1, source_target_pairs={{1,0},{2,1},{3,2},{5,4},{6,5},{7,6},{9,8},{10,9},{11,10},{13,12},{... | collective-permute-start | bytes 1572872 | tf_op jit(solution)/shard_map/ppermute | solution.py:581
  75.5 46.6 %collective-permute-start.8 = (bf16[128,2048]{1,0:T(8,128)(2,1)}, bf16[128,2048]{1,0:T(8,128)(2,1)}, u32[]{:S(2)}, u32[]{:S(2)}) collective-permute-start(bf16[128,2048]{1,0:T(8,128)(2,1)} %bitcast.4), channel_id=1, source_target_pairs={{0,1},{1,2},{2,3},{4,5},{5,6},{6,7},{8,9},{9,10},{10,11},{12,13},{... | collective-permute-start | bytes 1572872 | tf_op jit(solution)/shard_map/ppermute | solution.py:581
  220.0 115.5 %all-gather.32.cloned.1.call-start = ((), (), s32[]{:S(2)}) async-start(), calls=%async_computation.22 | async-start | bytes 2621440 | tf_op jit(solution)/shard_map/all_gather | solution.py:639
  235.8 102.3 %all-gather.34.cloned.1.call-start = ((), (), s32[]{:S(2)}) async-start(), calls=%async_computation.23 | async-start | bytes 7208960 | tf_op jit(solution)/shard_map/all_gather | solution.py:639
  236.5 154.2 %all-gather.36.cloned.1.call-start = ((), (), s32[]{:S(2)}) async-start(), calls=%async_computation.24 | async-start | bytes 7208960 | tf_op jit(solution)/shard_map/all_gather | solution.py:639
  247.5 25.1 %collective-permute-start.20 = (bf16[128,2048]{1,0:T(8,128)(2,1)S(1)}, bf16[128,2048]{1,0:T(8,128)(2,1)S(1)}, u32[]{:S(2)}, u32[]{:S(2)}) collective-permute-start(bf16[128,2048]{1,0:T(8,128)(2,1)S(1)} %get-tuple-element.427), channel_id=1, source_target_pairs={{3,2},{2,1},{1,0},{7,6},{6,5},{5,4},{11,10},{10,9},{9,8},{15,14},{... | collective-permute-start | bytes 1572872 | tf_op jit(solution)/shard_map/ppermute | solution.py:597
  259.9 25.8 %collective-permute-start.18 = (bf16[128,2048]{1,0:T(8,128)(2,1)S(1)}, bf16[128,2048]{1,0:T(8,128)(2,1)S(1)}, u32[]{:S(2)}, u32[]{:S(2)}) collective-permute-start(bf16[128,2048]{1,0:T(8,128)(2,1)S(1)} %add_convert_fusion.9), channel_id=1, source_target_pairs={{0,2},{2,0},{1,3},{3,1},{4,6},{6,4},{5,7},{7,5},{8,10},{10,8},{9,1... | collective-permute-start | bytes 1572872 | tf_op jit(solution)/shard_map/ppermute | solution.py:597
  287.0 148.9 %all-gather.38.cloned.1.call-start = ((), (), s32[]{:S(2)}) async-start(), calls=%async_computation.25 | async-start | bytes 7208960 | tf_op jit(solution)/shard_map/all_gather | solution.py:639
  292.7 27.3 %collective-permute-start.21 = (bf16[128,2048]{1,0:T(8,128)(2,1)}, bf16[128,2048]{1,0:T(8,128)(2,1)}, u32[]{:S(2)}, u32[]{:S(2)}) collective-permute-start(bf16[128,2048]{1,0:T(8,128)(2,1)} %get-tuple-element.391), channel_id=1, source_target_pairs={{0,2},{2,0},{1,3},{3,1},{4,6},{6,4},{5,7},{7,5},{8,10},{10,8},{9,1... | collective-permute-start | bytes 1572872 | tf_op jit(solution)/shard_map/ppermute | solution.py:581
  292.7 29.8 %collective-permute-start.23 = (bf16[128,2048]{1,0:T(8,128)(2,1)}, bf16[128,2048]{1,0:T(8,128)(2,1)}, u32[]{:S(2)}, u32[]{:S(2)}) collective-permute-start(bf16[128,2048]{1,0:T(8,128)(2,1)} %get-tuple-element.391), channel_id=1, source_target_pairs={{1,0},{2,1},{3,2},{5,4},{6,5},{7,6},{9,8},{10,9},{11,10},{13,12},{... | collective-permute-start | bytes 1572872 | tf_op jit(solution)/shard_map/ppermute | solution.py:581
  294.0 28.5 %collective-permute-start.24 = (bf16[128,2048]{1,0:T(8,128)(2,1)}, bf16[128,2048]{1,0:T(8,128)(2,1)}, u32[]{:S(2)}, u32[]{:S(2)}) collective-permute-start(bf16[128,2048]{1,0:T(8,128)(2,1)} %get-tuple-element.391), channel_id=1, source_target_pairs={{0,1},{1,2},{2,3},{4,5},{5,6},{6,7},{8,9},{9,10},{10,11},{12,13},{... | collective-permute-start | bytes 1572872 | tf_op jit(solution)/shard_map/ppermute | solution.py:581
  338.2 344.9 %reduce-scatter.9.cloned.1.call-start = ((), (), s32[]{:S(2)}) async-start(), calls=%async_computation.9 | async-start | bytes 7208960 | tf_op jit(solution)/shard_map/reduce_scatter | solution.py:643
  348.3 26.1 %collective-permute-start.25 = (bf16[1024,512]{1,0:T(8,128)(2,1)S(1)}, bf16[1024,512]{1,0:T(8,128)(2,1)S(1)}, u32[]{:S(2)}, u32[]{:S(2)}) collective-permute-start(bf16[1024,512]{1,0:T(8,128)(2,1)S(1)} %get-tuple-element.230.key_ref.value_ref.refs_1_.refs_2_), channel_id=1, source_target_pairs={{0,4},{1,5},{2,6},{3,7},{8,12},{9,13},{10,14},{11,15},{16,20},{17,... | collective-permute-start | bytes 3145736 | tf_op jit(solution)/shard_map/ppermute | solution.py:625
  398.2 24.8 %collective-permute-start.29 = (bf16[128,2048]{1,0:T(8,128)(2,1)S(1)}, bf16[128,2048]{1,0:T(8,128)(2,1)S(1)}, u32[]{:S(2)}, u32[]{:S(2)}) collective-permute-start(bf16[128,2048]{1,0:T(8,128)(2,1)S(1)} %get-tuple-element.424), channel_id=1, source_target_pairs={{3,2},{2,1},{1,0},{7,6},{6,5},{5,4},{11,10},{10,9},{9,8},{15,14},{... | collective-permute-start | bytes 1572872 | tf_op jit(solution)/shard_map/ppermute | solution.py:597
  441.3 26.8 %collective-permute-start.30 = (bf16[128,2048]{1,0:T(8,128)(2,1)S(1)}, bf16[128,2048]{1,0:T(8,128)(2,1)S(1)}, u32[]{:S(2)}, u32[]{:S(2)}) collective-permute-start(bf16[128,2048]{1,0:T(8,128)(2,1)S(1)} %get-tuple-element.389), channel_id=1, source_target_pairs={{0,2},{2,0},{1,3},{3,1},{4,6},{6,4},{5,7},{7,5},{8,10},{10,8},{9,1... | collective-permute-start | bytes 1572872 | tf_op jit(solution)/shard_map/ppermute | solution.py:581
  441.5 28.1 %collective-permute-start.32 = (bf16[128,2048]{1,0:T(8,128)(2,1)S(1)}, bf16[128,2048]{1,0:T(8,128)(2,1)S(1)}, u32[]{:S(2)}, u32[]{:S(2)}) collective-permute-start(bf16[128,2048]{1,0:T(8,128)(2,1)S(1)} %get-tuple-element.389), channel_id=1, source_target_pairs={{1,0},{2,1},{3,2},{5,4},{6,5},{7,6},{9,8},{10,9},{11,10},{13,12},{... | collective-permute-start | bytes 1572872 | tf_op jit(solution)/shard_map/ppermute | solution.py:581
  442.8 26.8 %collective-permute-start.33 = (bf16[128,2048]{1,0:T(8,128)(2,1)S(1)}, bf16[128,2048]{1,0:T(8,128)(2,1)S(1)}, u32[]{:S(2)}, u32[]{:S(2)}) collective-permute-start(bf16[128,2048]{1,0:T(8,128)(2,1)S(1)} %get-tuple-element.389), channel_id=1, source_target_pairs={{0,1},{1,2},{2,3},{4,5},{5,6},{6,7},{8,9},{9,10},{10,11},{12,13},{... | collective-permute-start | bytes 1572872 | tf_op jit(solution)/shard_map/ppermute | solution.py:581
  525.7 30.2 %collective-permute-start.35 = (bf16[128,2048]{1,0:T(8,128)(2,1)}, bf16[128,2048]{1,0:T(8,128)(2,1)}, u32[]{:S(2)}, u32[]{:S(2)}) collective-permute-start(bf16[128,2048]{1,0:T(8,128)(2,1)} %add_convert_fusion.5), channel_id=1, source_target_pairs={{0,2},{2,0},{1,3},{3,1},{4,6},{6,4},{5,7},{7,5},{8,10},{10,8},{9,1... | collective-permute-start | bytes 1572872 | tf_op jit(solution)/shard_map/ppermute | solution.py:597
  568.1 181.4 %reduce-scatter.11.cloned.1.call-start = ((), (), s32[]{:S(2)}) async-start(), calls=%async_computation.10 | async-start | bytes 7208960 | tf_op jit(solution)/shard_map/reduce_scatter | solution.py:643
  576.6 212.1 %reduce-scatter.15.cloned.1.call-start = ((), (), s32[]{:S(2)}) async-start(), calls=%async_computation.12 | async-start | bytes 2621440 | tf_op jit(solution)/shard_map/reduce_scatter | solution.py:643
  577.9 26.6 %collective-permute-start.40 = (bf16[128,2048]{1,0:T(8,128)(2,1)}, bf16[128,2048]{1,0:T(8,128)(2,1)S(1)}, u32[]{:S(2)}, u32[]{:S(2)}) collective-permute-start(bf16[128,2048]{1,0:T(8,128)(2,1)} %copy-done.35), channel_id=1, source_target_pairs={{1,0},{2,1},{3,2},{5,4},{6,5},{7,6},{9,8},{10,9},{11,10},{13,12},{... | collective-permute-start | bytes 1572872 | tf_op jit(solution)/shard_map/ppermute | solution.py:581
  579.2 25.3 %collective-permute-start.41 = (bf16[128,2048]{1,0:T(8,128)(2,1)}, bf16[128,2048]{1,0:T(8,128)(2,1)S(1)}, u32[]{:S(2)}, u32[]{:S(2)}) collective-permute-start(bf16[128,2048]{1,0:T(8,128)(2,1)} %copy-done.35), channel_id=1, source_target_pairs={{0,1},{1,2},{2,3},{4,5},{5,6},{6,7},{8,9},{9,10},{10,11},{12,13},{... | collective-permute-start | bytes 1572872 | tf_op jit(solution)/shard_map/ppermute | solution.py:581
  614.6 38.5 %collective-permute-start.45 = (bf16[128,2048]{1,0:T(8,128)(2,1)}, bf16[128,2048]{1,0:T(8,128)(2,1)S(1)}, u32[]{:S(2)}, u32[]{:S(2)}) collective-permute-start(bf16[128,2048]{1,0:T(8,128)(2,1)} %get-tuple-element.418), channel_id=1, source_target_pairs={{3,2},{2,1},{1,0},{7,6},{6,5},{5,4},{11,10},{10,9},{9,8},{15,14},{... | collective-permute-start | bytes 1572872 | tf_op jit(solution)/shard_map/ppermute | solution.py:597
  616.0 37.1 %collective-permute-start.44 = (bf16[128,2048]{1,0:T(8,128)(2,1)}, bf16[128,2048]{1,0:T(8,128)(2,1)}, u32[]{:S(2)}, u32[]{:S(2)}) collective-permute-start(bf16[128,2048]{1,0:T(8,128)(2,1)} %get-tuple-element.417), channel_id=1, source_target_pairs={{0,1},{1,2},{2,3},{4,5},{5,6},{6,7},{8,9},{9,10},{10,11},{12,13},{... | collective-permute-start | bytes 1572872 | tf_op jit(solution)/shard_map/ppermute | solution.py:597
  635.4 33.6 %collective-permute-start.46 = (bf16[1024,512]{1,0:T(8,128)(2,1)S(1)}, bf16[1024,512]{1,0:T(8,128)(2,1)S(1)}, u32[]{:S(2)}, u32[]{:S(2)}) collective-permute-start(bf16[1024,512]{1,0:T(8,128)(2,1)S(1)} %get-tuple-element.261), channel_id=1, source_target_pairs={{4,0},{5,1},{6,2},{7,3},{12,8},{13,9},{14,10},{15,11},{20,16},{21,... | collective-permute-start | bytes 3145736 | tf_op jit(solution)/shard_map/ppermute | solution.py:632
  674.6 114.0 %reduce-scatter.13.cloned.1.call-start = ((), (), s32[]{:S(2)}) async-start(), calls=%async_computation.11 | async-start | bytes 7208960 | tf_op jit(solution)/shard_map/reduce_scatter | solution.py:643
  683.0 180.1 %reduce-scatter.17.cloned.1.call-start = ((), (), s32[]{:S(2)}) async-start(), calls=%async_computation.13 | async-start | bytes 7864320 | tf_op jit(solution)/shard_map/reduce_scatter | solution.py:643
  693.3 43.2 %collective-permute-start.51 = (bf16[1408,512]{1,0:T(8,128)(2,1)}, bf16[1408,512]{1,0:T(8,128)(2,1)}, u32[]{:S(2)}, u32[]{:S(2)}) collective-permute-start(bf16[1408,512]{1,0:T(8,128)(2,1)} %reduce-scatter.9.cloned.1.call-done.refs_0_), channel_id=1, source_target_pairs={{0,4},{4,0},{1,5},{5,1},{2,6},{6,2},{3,7},{7,3},{8,12},{12,8},{9,1... | collective-permute-start | bytes 4325384 | tf_op jit(solution)/shard_map/ppermute | solution.py:557
  706.6 30.0 %collective-permute-start.48 = (bf16[128,2048]{1,0:T(8,128)(2,1)}, bf16[128,2048]{1,0:T(8,128)(2,1)}, u32[]{:S(2)}, u32[]{:S(2)}) collective-permute-start(bf16[128,2048]{1,0:T(8,128)(2,1)} %add_convert_fusion.2), channel_id=1, source_target_pairs={{0,2},{2,0},{1,3},{3,1},{4,6},{6,4},{5,7},{7,5},{8,10},{10,8},{9,1... | collective-permute-start | bytes 1572872 | tf_op jit(solution)/shard_map/ppermute | solution.py:597
  749.5 175.4 %reduce-scatter.19.cloned.1.call-start = ((), (), s32[]{:S(2)}) async-start(), calls=%async_computation.14 | async-start | bytes 7208960 | tf_op jit(solution)/shard_map/reduce_scatter | solution.py:643
  749.7 39.0 %collective-permute-start.56 = (bf16[512,1408]{1,0:T(8,128)(2,1)}, bf16[512,1408]{1,0:T(8,128)(2,1)}, u32[]{:S(2)}, u32[]{:S(2)}) collective-permute-start(bf16[512,1408]{1,0:T(8,128)(2,1)} %reduce-scatter.11.cloned.1.call-done.refs_0_), channel_id=1, source_target_pairs={{0,4},{4,0},{1,5},{5,1},{2,6},{6,2},{3,7},{7,3},{8,12},{12,8},{9,1... | collective-permute-start | bytes 4325384 | tf_op jit(solution)/shard_map/ppermute | solution.py:557
  750.0 27.9 %collective-permute-start.54 = (bf16[128,2048]{1,0:T(8,128)(2,1)S(1)}, bf16[128,2048]{1,0:T(8,128)(2,1)S(1)}, u32[]{:S(2)}, u32[]{:S(2)}) collective-permute-start(bf16[128,2048]{1,0:T(8,128)(2,1)S(1)} %get-tuple-element.278), channel_id=1, source_target_pairs={{1,0},{2,1},{3,2},{5,4},{6,5},{7,6},{9,8},{10,9},{11,10},{13,12},{... | collective-permute-start | bytes 1572872 | tf_op jit(solution)/shard_map/ppermute | solution.py:581
  751.2 26.6 %collective-permute-start.55 = (bf16[128,2048]{1,0:T(8,128)(2,1)S(1)}, bf16[128,2048]{1,0:T(8,128)(2,1)S(1)}, u32[]{:S(2)}, u32[]{:S(2)}) collective-permute-start(bf16[128,2048]{1,0:T(8,128)(2,1)S(1)} %get-tuple-element.278), channel_id=1, source_target_pairs={{0,1},{1,2},{2,3},{4,5},{5,6},{6,7},{8,9},{9,10},{10,11},{12,13},{... | collective-permute-start | bytes 1572872 | tf_op jit(solution)/shard_map/ppermute | solution.py:581
  796.8 177.1 %reduce-scatter.21.cloned.1.call-start = ((), (), s32[]{:S(2)}) async-start(), calls=%async_computation.15 | async-start | bytes 7208960 | tf_op jit(solution)/shard_map/reduce_scatter | solution.py:643
  819.4 43.7 %collective-permute-start.61 = (bf16[512,1408]{1,0:T(8,128)(2,1)}, bf16[512,1408]{1,0:T(8,128)(2,1)}, u32[]{:S(2)}, u32[]{:S(2)}) collective-permute-start(bf16[512,1408]{1,0:T(8,128)(2,1)} %reduce-scatter.13.cloned.1.call-done.refs_2_), channel_id=1, source_target_pairs={{0,4},{4,0},{1,5},{5,1},{2,6},{6,2},{3,7},{7,3},{8,12},{12,8},{9,1... | collective-permute-start | bytes 4325384 | tf_op jit(solution)/shard_map/ppermute | solution.py:557
  824.2 38.9 %collective-permute-start.62 = (bf16[512,512]{1,0:T(8,128)(2,1)S(1)}, bf16[512,512]{1,0:T(8,128)(2,1)}, u32[]{:S(2)}, u32[]{:S(2)}) collective-permute-start(bf16[512,512]{1,0:T(8,128)(2,1)S(1)} %copy-done.60), channel_id=1, source_target_pairs={{0,4},{4,0},{1,5},{5,1},{2,6},{6,2},{3,7},{7,3},{8,12},{12,8},{9,1... | collective-permute-start | bytes 1572872 | tf_op jit(solution)/shard_map/ppermute | solution.py:557
  832.7 30.4 %collective-permute-start.58 = (bf16[128,2048]{1,0:T(8,128)(2,1)}, bf16[128,2048]{1,0:T(8,128)(2,1)}, u32[]{:S(2)}, u32[]{:S(2)}) collective-permute-start(bf16[128,2048]{1,0:T(8,128)(2,1)} %add_convert_fusion.1), channel_id=1, source_target_pairs={{0,2},{2,0},{1,3},{3,1},{4,6},{6,4},{5,7},{7,5},{8,10},{10,8},{9,1... | collective-permute-start | bytes 1572872 | tf_op jit(solution)/shard_map/ppermute | solution.py:597
  874.8 133.9 %reduce-scatter.23.cloned.1.call-start = ((), (), s32[]{:S(2)}) async-start(), calls=%async_computation.16 | async-start | bytes 7208960 | tf_op jit(solution)/shard_map/reduce_scatter | solution.py:643
  883.4 41.5 %collective-permute-start.67 = (bf16[512,1536]{1,0:T(8,128)(2,1)}, bf16[512,1536]{1,0:T(8,128)(2,1)}, u32[]{:S(2)}, u32[]{:S(2)}) collective-permute-start(bf16[512,1536]{1,0:T(8,128)(2,1)} %reduce-scatter.17.cloned.1.call-done.refs_0_), channel_id=1, source_target_pairs={{0,4},{4,0},{1,5},{5,1},{2,6},{6,2},{3,7},{7,3},{8,12},{12,8},{9,1... | collective-permute-start | bytes 4718600 | tf_op jit(solution)/shard_map/ppermute | solution.py:557
  885.1 24.6 %collective-permute-start.65 = (bf16[128,2048]{1,0:T(8,128)(2,1)S(1)}, bf16[128,2048]{1,0:T(8,128)(2,1)}, u32[]{:S(2)}, u32[]{:S(2)}) collective-permute-start(bf16[128,2048]{1,0:T(8,128)(2,1)S(1)} %get-tuple-element.299), channel_id=1, source_target_pairs={{1,0},{2,1},{3,2},{5,4},{6,5},{7,6},{9,8},{10,9},{11,10},{13,12},{... | collective-permute-start | bytes 1572872 | tf_op jit(solution)/shard_map/ppermute | solution.py:581
  938.9 26.1 %collective-permute-start.68 = (bf16[1024,512]{1,0:T(8,128)(2,1)S(1)}, bf16[1024,512]{1,0:T(8,128)(2,1)S(1)}, u32[]{:S(2)}, u32[]{:S(2)}) collective-permute-start(bf16[1024,512]{1,0:T(8,128)(2,1)S(1)} %get-tuple-element.309), channel_id=1, source_target_pairs={{4,0},{5,1},{6,2},{7,3},{12,8},{13,9},{14,10},{15,11},{20,16},{21,... | collective-permute-start | bytes 3145736 | tf_op jit(solution)/shard_map/ppermute | solution.py:632
  974.0 34.7 %collective-permute-start.70 = (bf16[1024,1536]{1,0:T(8,128)(2,1)}, bf16[1024,1536]{1,0:T(8,128)(2,1)}, u32[]{:S(2)}, u32[]{:S(2)}) collective-permute-start(bf16[1024,1536]{1,0:T(8,128)(2,1)} %copy-done.47), channel_id=1, source_target_pairs={{0,8},{8,0},{16,24},{24,16},{1,9},{9,1},{17,25},{25,17},{2,10},{10... | collective-permute-start | bytes 9437192 | tf_op jit(solution)/shard_map/ppermute | solution.py:557
  974.0 34.7 %collective-permute-start.69 = (bf16[1408,512]{1,0:T(8,128)(2,1)}, bf16[1408,512]{1,0:T(8,128)(2,1)}, u32[]{:S(2)}, u32[]{:S(2)}) collective-permute-start(bf16[1408,512]{1,0:T(8,128)(2,1)} %reduce-scatter.19.cloned.1.call-done.refs_0_), channel_id=1, source_target_pairs={{0,4},{4,0},{1,5},{5,1},{2,6},{6,2},{3,7},{7,3},{8,12},{12,8},{9,1... | collective-permute-start | bytes 4325384 | tf_op jit(solution)/shard_map/ppermute | solution.py:557
  974.3 34.4 %collective-permute-start.71 = (bf16[512,1024]{1,0:T(8,128)(2,1)}, bf16[512,1024]{1,0:T(8,128)(2,1)}, u32[]{:S(2)}, u32[]{:S(2)}) collective-permute-start(bf16[512,1024]{1,0:T(8,128)(2,1)} %outer.19), channel_id=1, source_target_pairs={{0,8},{8,0},{16,24},{24,16},{1,9},{9,1},{17,25},{25,17},{2,10},{10... | collective-permute-start | bytes 3145736 | tf_op jit(solution)/shard_map/ppermute | solution.py:557
  979.3 76.3 %collective-permute-start.76 = (bf16[512,1408]{1,0:T(8,128)(2,1)S(1)}, bf16[512,1408]{1,0:T(8,128)(2,1)S(1)}, u32[]{:S(2)}, u32[]{:S(2)}) collective-permute-start(bf16[512,1408]{1,0:T(8,128)(2,1)S(1)} %copy-done.17), channel_id=1, source_target_pairs={{0,4},{4,0},{1,5},{5,1},{2,6},{6,2},{3,7},{7,3},{8,12},{12,8},{9,1... | collective-permute-start | bytes 4325384 | tf_op jit(solution)/shard_map/ppermute | solution.py:557
  1019.4 45.1 %collective-permute-start.77 = (bf16[512,1536]{1,0:T(8,128)(2,1)}, bf16[512,1536]{1,0:T(8,128)(2,1)}, u32[]{:S(2)}, u32[]{:S(2)}) collective-permute-start(bf16[512,1536]{1,0:T(8,128)(2,1)} %split.30), channel_id=1, source_target_pairs={{0,16},{8,24},{16,0},{24,8},{1,17},{9,25},{17,1},{25,9},{2,18},{10... | collective-permute-start | bytes 4718600 | tf_op jit(solution)/shard_map/ppermute | solution.py:557
  1023.8 33.4 %collective-permute-start.74 = (bf16[128,2048]{1,0:T(8,128)(2,1)}, bf16[128,2048]{1,0:T(8,128)(2,1)S(1)}, u32[]{:S(2)}, u32[]{:S(2)}) collective-permute-start(bf16[128,2048]{1,0:T(8,128)(2,1)} %get-tuple-element.409), channel_id=1, source_target_pairs={{0,1},{1,2},{2,3},{4,5},{5,6},{6,7},{8,9},{9,10},{10,11},{12,13},{... | collective-permute-start | bytes 1572872 | tf_op jit(solution)/shard_map/ppermute | solution.py:597
  1025.1 32.1 %collective-permute-start.75 = (bf16[128,2048]{1,0:T(8,128)(2,1)}, bf16[128,2048]{1,0:T(8,128)(2,1)S(1)}, u32[]{:S(2)}, u32[]{:S(2)}) collective-permute-start(bf16[128,2048]{1,0:T(8,128)(2,1)} %get-tuple-element.407), channel_id=1, source_target_pairs={{3,2},{2,1},{1,0},{7,6},{6,5},{5,4},{11,10},{10,9},{9,8},{15,14},{... | collective-permute-start | bytes 1572872 | tf_op jit(solution)/shard_map/ppermute | solution.py:597
  1027.7 36.8 %collective-permute-start.73 = (bf16[128,2048]{1,0:T(8,128)(2,1)S(1)}, bf16[128,2048]{1,0:T(8,128)(2,1)S(1)}, u32[]{:S(2)}, u32[]{:S(2)}) collective-permute-start(bf16[128,2048]{1,0:T(8,128)(2,1)S(1)} %add_convert_fusion), channel_id=1, source_target_pairs={{0,2},{2,0},{1,3},{3,1},{4,6},{6,4},{5,7},{7,5},{8,10},{10,8},{9,1... | collective-permute-start | bytes 1572872 | tf_op jit(solution)/shard_map/ppermute | solution.py:597
  1055.7 69.3 %collective-permute-start.86 = (bf16[512,1408]{1,0:T(8,128)(2,1)}, bf16[512,1408]{1,0:T(8,128)(2,1)}, u32[]{:S(2)}, u32[]{:S(2)}) collective-permute-start(bf16[512,1408]{1,0:T(8,128)(2,1)} %reduce-scatter.23.cloned.1.call-done.refs_2_), channel_id=1, source_target_pairs={{0,4},{4,0},{1,5},{5,1},{2,6},{6,2},{3,7},{7,3},{8,12},{12,8},{9,1... | collective-permute-start | bytes 4325384 | tf_op jit(solution)/shard_map/ppermute | solution.py:557
  1068.1 25.2 %collective-permute-start.78 = (f32[14,2048]{1,0:T(8,128)S(1)}, f32[14,2048]{1,0:T(8,128)S(1)}, u32[]{:S(2)}, u32[]{:S(2)}) collective-permute-start(f32[14,2048]{1,0:T(8,128)S(1)} %pad_maximum_fusion.12), channel_id=1, source_target_pairs={{0,4},{4,0},{1,5},{5,1},{2,6},{6,2},{3,7},{7,3},{8,12},{12,8},{9,1... | collective-permute-start | bytes 344072 | tf_op jit(solution)/shard_map/ppermute | solution.py:557
  1072.4 67.1 %collective-permute-start.83 = (bf16[512,1536]{1,0:T(8,128)(2,1)S(1)}, bf16[512,1536]{1,0:T(8,128)(2,1)}, u32[]{:S(2)}, u32[]{:S(2)}) collective-permute-start(bf16[512,1536]{1,0:T(8,128)(2,1)S(1)} %fusion.refs_0_), channel_id=1, source_target_pairs={{0,4},{4,0},{1,5},{5,1},{2,6},{6,2},{3,7},{7,3},{8,12},{12,8},{9,1... | collective-permute-start | bytes 4718600 | tf_op jit(solution)/shard_map/ppermute | solution.py:557
  1074.7 31.0 %collective-permute-start.84 = (bf16[512,512]{1,0:T(8,128)(2,1)S(1)}, bf16[512,512]{1,0:T(8,128)(2,1)S(1)}, u32[]{:S(2)}, u32[]{:S(2)}) collective-permute-start(bf16[512,512]{1,0:T(8,128)(2,1)S(1)} %split.31), channel_id=1, source_target_pairs={{0,16},{8,24},{16,0},{24,8},{1,17},{9,25},{17,1},{25,9},{2,18},{10... | collective-permute-start | bytes 1572872 | tf_op jit(solution)/shard_map/ppermute | solution.py:557
  1105.9 30.4 %collective-permute-start.85 = (bf16[512,512]{1,0:T(8,128)(2,1)S(1)}, bf16[512,512]{1,0:T(8,128)(2,1)}, u32[]{:S(2)}, u32[]{:S(2)}) collective-permute-start(bf16[512,512]{1,0:T(8,128)(2,1)S(1)} %fusion.6.refs_0_), channel_id=1, source_target_pairs={{0,4},{4,0},{1,5},{5,1},{2,6},{6,2},{3,7},{7,3},{8,12},{12,8},{9,1... | collective-permute-start | bytes 1572872 | tf_op jit(solution)/shard_map/ppermute | solution.py:557
  (164 other events, 2548.2 us)
Sparse Core Ops, SparseCore 0:
  10.2 49.0 all-gather.21
  61.4 22.5 all-gather.19
  86.2 43.4 all-gather.23
  131.7 43.3 all-gather.25
  176.5 43.3 all-gather.27
  222.0 46.3 all-gather.29
  270.5 22.5 all-gather.31
  294.7 43.3 all-gather.33
  339.7 43.3 all-gather.35
  385.1 43.3 all-gather.37
  568.3 53.6 reduce-scatter.8
  625.1 54.8 reduce-scatter.10
  682.5 31.4 reduce-scatter.14
  717.1 54.8 reduce-scatter.12
  775.0 58.3 reduce-scatter.16
  836.5 54.8 reduce-scatter.18
  894.3 54.8 reduce-scatter.20
  952.4 54.8 reduce-scatter.22

commit v5 on v4

--- a/solution.py
+++ b/solution.py
@@ -340,8 +340,9 @@
         s = jnp.where(allowed, dot(q, key_ref[:, lanes], NT), MASKED)
         top = jnp.max(s, axis=1, keepdims=True)
         p = jnp.exp(s - top)
-        top_ref[half] = top
-        total_ref[half] = jnp.sum(p, axis=1, keepdims=True)
+        spread = (top.shape[0], HD)
+        top_ref[:, lanes] = jnp.broadcast_to(top, spread)
+        total_ref[:, lanes] = jnp.broadcast_to(jnp.sum(p, axis=1, keepdims=True), spread)
         acc_ref[:, lanes] = dot(p.astype(LOW), value_ref[:, lanes], NN)
 
 
@@ -352,7 +353,8 @@
     for half in range(PAIR // HD):
         lanes = slice(half * HD, (half + 1) * HD)
         q = q_ref[:, lanes] * jnp.asarray(HD**-0.5, LOW)
-        top, total, acc = top_in_ref[half], total_in_ref[half], acc_in_ref[:, lanes]
+        first = slice(half * HD, half * HD + 1)
+        top, total, acc = top_in_ref[:, first], total_in_ref[:, first], acc_in_ref[:, lanes]
         for b in range(blocks):
             s = jnp.where(allowed[b], dot(q, keys[b][:, lanes], NT), MASKED)
             new_top = jnp.maximum(top, jnp.max(s, axis=1, keepdims=True))
@@ -362,7 +364,7 @@
             acc = acc * factor + dot(p.astype(LOW), values[b][:, lanes], NN)
             top = new_top
         out_ref[:, lanes] = acc / total
-        lse_ref[half] = top + jnp.log(total)
+        lse_ref[:, lanes] = jnp.broadcast_to(top + jnp.log(total), acc.shape)
 
 
 def pair_call(kernel, name, rows, width, kpos, operands, stacked, outs, flops):
@@ -370,10 +372,9 @@
     column = lambda i: (0, i)
     specs = {
         "row": pl.BlockSpec((rows, PAIR), column),
-        "head": pl.BlockSpec((PAIR // HD, rows, 1), lambda i: (i, 0, 0)),
         "keys": pl.BlockSpec((2 * key_rows, PAIR), column),
     }
-    shapes = {"row": (rows, width), "head": (width // HD, rows, 1), "keys": (2 * key_rows, width)}
+    shapes = {"row": (rows, width), "keys": (2 * key_rows, width)}
     halves = [pl.BlockSpec((key_rows, PAIR), lambda i, c=c: (c, i)) for c in range(2)]
     common = [
         pl.BlockSpec((rows, 1), lambda i: (0, 0)),
@@ -382,36 +383,32 @@
     return pl.pallas_call(
         kernel,
         grid=(width // PAIR,),
-        in_specs=common + [specs[k] for k, _ in operands[1:]] + halves * len(stacked),
+        in_specs=common + [specs["row"]] * (len(operands) - 1) + halves * len(stacked),
         out_specs=[specs[k] for k, _ in outs],
         out_shape=[jax.ShapeDtypeStruct(shapes[k], t) for k, t in outs],
         compiler_params=pltpu.CompilerParams(vmem_limit_bytes=40 * 1024 * 1024),
         cost_estimate=work(flops * rows * key_rows * blocks * width),
         name=name,
-    )(operands[0], kpos, *[v for _, v in operands[1:]], *[s for s in stacked for c in range(2)])
+    )(operands[0], kpos, *operands[1:], *[s for s in stacked for c in range(2)])
 
 
 def attend_near(qpos, kpos, q, own):
     rows, width = q.shape
-    outs = [("row", WIDE), ("head", WIDE), ("head", WIDE)]
-    return pair_call(
-        attend_near_kernel, "attend_near", rows, width, kpos, [qpos, ("row", q)], [own], outs, 43
-    )
+    outs = [("row", WIDE)] * 3
+    return pair_call(attend_near_kernel, "attend_near", rows, width, kpos, [qpos, q], [own], outs, 43)
 
 
 def attend_far(qpos, kpos, q, near, far):
     rows, width = q.shape
-    kinds = ("row", "head", "head")
-    operands = [qpos, ("row", q), *zip(kinds, near)]
     return pair_call(
         functools.partial(attend_far_kernel, len(far)),
         "attend_far",
         rows,
         width,
         kpos,
-        operands,
+        [qpos, q, *near],
         far,
-        [("row", WIDE), ("head", WIDE)],
+        [("row", WIDE)] * 2,
         43,
     )
 
@@ -428,7 +425,7 @@
         lanes = slice(half * HD, (half + 1) * HD)
         q = q_ref[:, lanes] * jnp.asarray(scale, LOW)
         grad = grad_ref[:, lanes]
-        lse = lse_ref[half]
+        lse = lse_ref[:, half * HD : half * HD + 1]
         delta = jnp.sum(grad.astype(WIDE) * out_ref[:, lanes], axis=1, keepdims=True)
         dq = []
         for b in range(blocks):
@@ -446,14 +443,13 @@
 
 def attend_back(qpos, kpos, q, grad, out, lse, stacked, kind, before):
     rows, width = q.shape
-    rest = [("row", v) for v in (q, grad, out)] + [("head", lse)] + [("row", v) for v in before]
     results = pair_call(
         functools.partial(attend_back_kernel, len(stacked), len(before)),
         "attend_back",
         rows,
         width,
         kpos,
-        [qpos] + rest,
+        [qpos, q, grad, out, lse, *before],
         stacked,
         [("row", WIDE)] + [("keys", kind)] * len(stacked),
         75,
@@ -591,7 +587,7 @@
             ]
         return jnp.concatenate(found, axis=0)
 
-    def sum_rows(self, low):
+    def sum_rows(self, low, *jobs):
         rows, count, t = self.own_rows, self.count, self.tensor
         terms = [low[d * rows : (d + 1) * rows] for d in range(count)]
         send = lambda v, *route: lax.ppermute(v, "tensor", list(route))
@@ -600,7 +596,7 @@
             end = send(jnp.where(t == 0, terms[3], terms[1]), (0, 1), (3, 2))
             above = send(terms[1], (0, 1), (1, 2), (2, 3))
             below = send(terms[3], (3, 2), (2, 1), (1, 0))
-            far = (wide(terms[2]) + wide(end)).astype(LOW)
+            far = meanwhile((wide(terms[2]) + wide(end)).astype(LOW), *jobs)
             got = [send(far, (0, 2), (2, 0), (1, 3), (3, 1)), above, below]
         else:
             got = [
@@ -838,7 +834,7 @@
 
         if layer + 1 < LAYERS:
             branch = plan.gather_rows(grad_low)
-        branch = meanwhile(branch, *old("gate", "up", "out"))
+        branch = held(meanwhile(branch, *old("gate", "up", "qkv")), *old("out"))
         if layer == 0:
             down_grad, branch = lax.optimization_barrier(
                 (outer(activated, branch), branch)
@@ -864,7 +860,7 @@
             late, hidden_low = lax.optimization_barrier((activated, hidden_low))
             partial_out = times_wide(late, down_full, "down")
         attention = plan.gather_rows(hidden_low)
-        attention = meanwhile(attention, *old("qkv"))
+        attention = meanwhile(attention, *old("out", "qkv"))
         if layer == 0:
             attention = meanwhile(attention, mine["down"])
         if top:
@@ -873,6 +869,8 @@
         grad_attended = out_back(attention, out_full)
         shared = (queries, grad_attended, attended, lse)
         far_queries, far_grads = attend_back(qpos, far_places, *shared, far_kv, LOW, [])
+        if layer == 0:
+            far_queries = meanwhile(far_queries, mine["down"])
         returned = plan.far_key_grads(far_grads)
         grad_queries, grad_kv = attend_back(
             qpos, near_places, *shared, [keys_values], WIDE, [far_queries]
@@ -887,12 +885,12 @@
         )
         if layer > 0:
             mine["up"] = in_job(rows_two, grad_up)
-        if layer == 0:
-            mine["out"] = Job(
-                pair_stages(plan, lambda r, a=attention: (attended_low, own_part(a, r)), 1)
-            )
-        else:
-            mine["out"] = out_job(attended_low, attention)
+        mine["out"] = Job(
+            pair_stages(plan, lambda r, a=attention: (attended_low, own_part(a, r)), 1)
+        )
+        if layer > 0:
+            mine["up"] = in_job(rows_two, grad_up)
+        projected = meanwhile(projected, mine["out"])
         projected = meanwhile(projected, mine["down"] if layer > 0 else None, *old("qkv"))
         if not top:
             above_done, projected = lax.optimization_barrier(
@@ -909,14 +907,15 @@
             mine["qkv"] = Job(
                 pair_stages(plan, lambda r, b=projected: (own_part(rows_one, r), b), 0)
             )
-            projected = meanwhile(projected, *map(mine.get, ("qkv", "out", "gate")))
+            projected = meanwhile(projected, mine["qkv"], mine["gate"])
         partial_in = project_in(projected, qkv_full)
         if layer == 0:
-            partial_in = meanwhile(partial_in, *map(mine.get, ("down", "up", "qkv")))
-            partial_in = held(partial_in, mine["out"])
-        summed = plan.sum_rows(partial_in)
+            partial_in = held(meanwhile(partial_in, mine["qkv"]), mine["out"])
+            summed = plan.sum_rows(partial_in, mine["up"])
+        else:
+            summed = plan.sum_rows(partial_in)
         if layer > 0:
-            summed = meanwhile(summed, mine["down"])
+            summed = meanwhile(summed, mine["down"], mine["out"])
         else:
             summed = meanwhile(summed, *map(mine.get, ("gate", "out", "qkv")))
         grad_stream, grad_low, gain_one, bias_one = norm_back(
@@ -924,8 +923,10 @@
         )
         if layer > 0:
             grad_low, projected = lax.optimization_barrier((grad_low, projected))
-            mine["qkv"] = in_job(rows_one, projected)
-            grad_low = meanwhile(grad_low, mine["gate"])
+            mine["qkv"] = Job(
+                pair_stages(plan, lambda r, a=rows_one, b=projected: (own_part(a, r), b), 0)
+            )
+            grad_low = meanwhile(grad_low, mine["gate"], mine["qkv"])
         gain_grads[layer] = jnp.stack([gain_one, gain_two])
         bias_grads[layer] = jnp.stack([bias_one, bias_two])
 

time: 1160 us -> 1160 us (level)
  waiting for transfers between devices: 488 us -> 474 us
    ppermute x32, waiting for transfers between devices: 185 us -> 204 us  [sum_rows(): send = lambda v, *route: lax.ppermute(v, 'tensor', list(route))]
    ppermute x19 -> x23, waiting for transfers between devices: 75.4 us -> 57.6 us  [swapped(): return lax.ppermute(value, axis, [(i, i ^ mask) for i in range(count)])]
    unnamed x247 -> x253, local copies, waits for them, and re-layouts: 56.9 us -> 54.7 us
    pallas_call x32 -> x34, Pallas kernels: 160 us -> 162 us  [tiled(): pl.pallas_call(kernel, grid=(steps,), in_specs=[pl.BlockSpec(block, index...]
  transfers between devices with their start and end apart: 105 -> 107, of which waited for: 50 -> 53; matrix products, arithmetic and copies ran while one was open for 9% -> 10% of each run, Pallas kernels for 22% -> 21%
where the time goes in v5:
time: 1160 us; the launch traced here: 1150 us
  waiting for transfers between devices  474 us (41%)
  Pallas kernels  289 us (25%)
  starting transfers between devices  200 us (17%)
  local copies, waits for them, and re-layouts  90.8 us (8%)
  other arithmetic  83.4 us (7%)
  between operations  16.7 us (1%)
    ppermute x32, waiting for transfers between devices, sum_rows(): send = lambda v, *route: lax.ppermute(v, 'tensor', list(route))  204 us
    ppermute x32, waiting for transfers between devices, gather_rows(): send = lambda v, *route: lax.ppermute(v, 'tensor', list(route))  174 us
    pallas_call x34, Pallas kernels, tiled(): pl.pallas_call(kernel, grid=(steps,), in_specs=[pl.BlockSpec(block, index...  162 us
    pallas_call x8, Pallas kernels, pair_call(): pl.pallas_call(kernel, grid=(width // PAIR,), in_specs=common + [specs['r...  89.1 us
    ppermute x32, starting transfers between devices, sum_rows(): send = lambda v, *route: lax.ppermute(v, 'tensor', list(route))  88.6 us
    ppermute x32, starting transfers between devices, gather_rows(): send = lambda v, *route: lax.ppermute(v, 'tensor', list(route))  77.8 us
    ppermute x23, waiting for transfers between devices, swapped(): return lax.ppermute(value, axis, [(i, i ^ mask) for i in range(count)])  57.6 us
    unnamed x253, local copies, waits for them, and re-layouts  54.7 us
  transfers between devices with their start and end apart: 107, of which 53 were waited for; matrix products, arithmetic and copies ran while one was open for 10% of the time, Pallas kernels for 21%

profile of v5, /device:TPU:0, one launch (start us, length us, event | category | flops | bytes accessed | tf_op | source)
XLA Modules:
  0.0 1153.2 jit_solution(7406225948206797680)
XLA Ops:
  32.3 15.4 %collective-permute-done = bf16[128,2048]{1,0:T(8,128)(2,1)} collective-permute-done((bf16[128,2048]{1,0:T(8,128)(2,1)S(1)}, bf16[128,2048]{1,0:T(8,128)(2,1)}, u32[]{:S(2)}, u32[]{:S(2)}) %collective-permute-start) | collective-permute-done | bytes 524320 | tf_op jit(solution)/shard_map/ppermute | solution.py:577
  51.7 10.4 collective-permute-done.1
  64.6 7.4 project.2
  90.2 10.1 attend_near.2
  105.9 14.7 %attend_far.2 = (f32[512,512]{1,0:T(8,128)S(1)}, f32[512,512]{1,0:T(8,128)S(1)}) custom-call(s32[512,1]{1,0:T(8,128)S(1)} %copy.70.qpos_ref, s32[1,1,512]{2,1,0:T(1,128)S(1)} %bitcast.103, bf16[512,512]{1,0:T(8,128)(2,1)S(1)} %get-tuple-element.206.q_ref, f32[512,512]{1,0:T(8,128)S(1)} %get-tuple-element.208.acc_in_ref, ...), custom_call_target="tpu_custom_call" | custom-call | flops 5771362304 | tf_op jit(solution)/shard_map/attend_far/pallas_call | solution.py:383
  138.1 6.4 collective-permute-done.9
  155.7 10.6 collective-permute-done.10
  175.4 8.9 collective-permute-start.16
  184.3 11.9 %collective-permute-done.13 = bf16[128,2048]{1,0:T(8,128)(2,1)} collective-permute-done((bf16[128,2048]{1,0:T(8,128)(2,1)}, bf16[128,2048]{1,0:T(8,128)(2,1)}, u32[]{:S(2)}, u32[]{:S(2)}) %collective-permute-start.13) | collective-permute-done | bytes 524320 | tf_op jit(solution)/shard_map/ppermute | solution.py:577
  198.8 9.2 collective-permute-done.14
  212.0 8.0 all-gather.28.cloned.1.call-done
  223.6 11.2 gate_up.2
  253.5 6.3 collective-permute-done.17
  263.4 7.6 collective-permute-done.19
  271.1 14.7 %collective-permute-done.18 = bf16[128,2048]{1,0:T(8,128)(2,1)S(1)} collective-permute-done((bf16[128,2048]{1,0:T(8,128)(2,1)S(1)}, bf16[128,2048]{1,0:T(8,128)(2,1)S(1)}, u32[]{:S(2)}, u32[]{:S(2)}) %collective-permute-start.18) | collective-permute-done | bytes 524320 | tf_op jit(solution)/shard_map/ppermute | solution.py:593
  294.1 8.2 collective-permute-start.24
  302.4 17.8 %collective-permute-done.21 = bf16[128,2048]{1,0:T(8,128)(2,1)} collective-permute-done((bf16[128,2048]{1,0:T(8,128)(2,1)}, bf16[128,2048]{1,0:T(8,128)(2,1)}, u32[]{:S(2)}, u32[]{:S(2)}) %collective-permute-start.21) | collective-permute-done | bytes 524320 | tf_op jit(solution)/shard_map/ppermute | solution.py:577
  322.6 8.9 collective-permute-done.22
  341.0 7.4 project.3
  351.7 10.1 attend_near.3
  361.9 12.6 %collective-permute-done.25.refs_0_.refs_1_ = bf16[1024,512]{1,0:T(8,128)(2,1)S(1)} collective-permute-done((bf16[1024,512]{1,0:T(8,128)(2,1)S(1)}, bf16[1024,512]{1,0:T(8,128)(2,1)S(1)}, u32[]{:S(2)}, u32[]{:S(2)}) %collective-permute-start.25) | collective-permute-done | bytes 1048608 | tf_op jit(solution)/shard_map/ppermute | solution.py:621
  374.5 14.7 %attend_far.3 = (f32[512,512]{1,0:T(8,128)S(1)}, f32[512,512]{1,0:T(8,128)S(1)}) custom-call(s32[512,1]{1,0:T(8,128)S(1)} %copy.70.qpos_ref, s32[1,1,512]{2,1,0:T(1,128)S(1)} %bitcast.104, bf16[512,512]{1,0:T(8,128)(2,1)S(1)} %get-tuple-element.239.q_ref, f32[512,512]{1,0:T(8,128)S(1)} %get-tuple-element.241.acc_in_ref, ...), custom_call_target="tpu_custom_call" | custom-call | flops 5771362304 | tf_op jit(solution)/shard_map/attend_far/pallas_call | solution.py:383
  404.6 6.4 collective-permute-done.26
  414.7 9.1 collective-permute-done.29
  423.8 11.5 collective-permute-done.27
  443.4 8.1 collective-permute-start.33
  451.5 17.3 %collective-permute-done.30 = bf16[128,2048]{1,0:T(8,128)(2,1)S(1)} collective-permute-done((bf16[128,2048]{1,0:T(8,128)(2,1)S(1)}, bf16[128,2048]{1,0:T(8,128)(2,1)S(1)}, u32[]{:S(2)}, u32[]{:S(2)}) %collective-permute-start.30) | collective-permute-done | bytes 524320 | tf_op jit(solution)/shard_map/ppermute | solution.py:577
  470.3 9.5 collective-permute-done.31
  480.2 11.5 gate_up.3
  492.9 7.3 gate_up_back.2
  500.3 10.2 gate_up_in.2.refs_0_
  516.6 8.9 collective-permute-done.34
  526.4 7.7 collective-permute-start.35
  536.4 20.3 %collective-permute-done.35.refs_1_ = bf16[128,2048]{1,0:T(8,128)(2,1)} collective-permute-done((bf16[128,2048]{1,0:T(8,128)(2,1)}, bf16[128,2048]{1,0:T(8,128)(2,1)}, u32[]{:S(2)}, u32[]{:S(2)}) %collective-permute-start.35) | collective-permute-done | bytes 524320 | tf_op jit(solution)/shard_map/ppermute | solution.py:593
  584.5 12.3 %collective-permute-done.38 = bf16[128,2048]{1,0:T(8,128)(2,1)S(1)} collective-permute-done((bf16[128,2048]{1,0:T(8,128)(2,1)}, bf16[128,2048]{1,0:T(8,128)(2,1)S(1)}, u32[]{:S(2)}, u32[]{:S(2)}) %collective-permute-start.38) | collective-permute-done | bytes 524320 | tf_op jit(solution)/shard_map/ppermute | solution.py:577
  605.3 8.5 collective-permute-done.39
  627.3 10.3 attend_back.4
  644.7 9.4 attend_back.5
  654.1 13.9 %collective-permute-done.43 = bf16[128,2048]{1,0:T(8,128)(2,1)S(1)} collective-permute-done((bf16[128,2048]{1,0:T(8,128)(2,1)S(1)}, bf16[128,2048]{1,0:T(8,128)(2,1)S(1)}, u32[]{:S(2)}, u32[]{:S(2)}) %collective-permute-start.43) | collective-permute-done | bytes 524320 | tf_op jit(solution)/shard_map/ppermute | solution.py:593
  684.7 6.5 project_in.2.refs_0_
  699.7 6.4 collective-permute-done.47
  718.3 18.6 %collective-permute-done.48.refs_1_ = bf16[128,2048]{1,0:T(8,128)(2,1)} collective-permute-done((bf16[128,2048]{1,0:T(8,128)(2,1)}, bf16[128,2048]{1,0:T(8,128)(2,1)}, u32[]{:S(2)}, u32[]{:S(2)}) %collective-permute-start.48) | collective-permute-done | bytes 524320 | tf_op jit(solution)/shard_map/ppermute | solution.py:593
  751.3 16.3 %collective-permute-done.53 = bf16[128,2048]{1,0:T(8,128)(2,1)S(1)} collective-permute-done((bf16[128,2048]{1,0:T(8,128)(2,1)}, bf16[128,2048]{1,0:T(8,128)(2,1)S(1)}, u32[]{:S(2)}, u32[]{:S(2)}) %collective-permute-start.53) | collective-permute-done | bytes 524320 | tf_op jit(solution)/shard_map/ppermute | solution.py:577
  774.6 9.5 collective-permute-done.54
  807.8 7.5 gate_up_back.3
  815.4 10.6 gate_up_in.3.refs_0_
  827.3 6.3 collective-permute-start.60
  837.8 8.2 collective-permute-done.60
  849.4 7.9 collective-permute-done.62.refs_2_
  858.0 15.3 %collective-permute-done.61.refs_1_ = bf16[128,2048]{1,0:T(8,128)(2,1)} collective-permute-done((bf16[128,2048]{1,0:T(8,128)(2,1)}, bf16[128,2048]{1,0:T(8,128)(2,1)}, u32[]{:S(2)}, u32[]{:S(2)}) %collective-permute-start.61) | collective-permute-done | bytes 524320 | tf_op jit(solution)/shard_map/ppermute | solution.py:593
  905.1 9.6 collective-permute-done.66
  918.5 7.5 collective-permute-done.68
  926.0 9.8 collective-permute-done.67
  952.1 10.3 attend_back.6
  964.3 16.0 %collective-permute-done.72.refs_1_ = bf16[1408,512]{1,0:T(8,128)(2,1)S(1)} collective-permute-done((bf16[1408,512]{1,0:T(8,128)(2,1)}, bf16[1408,512]{1,0:T(8,128)(2,1)S(1)}, u32[]{:S(2)}, u32[]{:S(2)}) %collective-permute-start.72) | collective-permute-done | bytes 1441824 | tf_op jit(solution)/shard_map/ppermute | solution.py:553
  980.3 9.4 attend_back.7
  989.7 9.6 collective-permute-done.73.refs_0_
  1012.5 6.0 project_in.3.refs_0_
  1050.7 9.2 finish_gate_up.2.refs_4_
  1061.7 9.6 collective-permute-done.77.refs_1_
  1083.8 13.6 %collective-permute-done.82 = f32[14,2048]{1,0:T(8,128)S(1)} collective-permute-done((f32[14,2048]{1,0:T(8,128)S(1)}, f32[14,2048]{1,0:T(8,128)S(1)}, u32[]{:S(2)}, u32[]{:S(2)}) %collective-permute-start.82) | collective-permute-done | bytes 114720 | tf_op jit(solution)/shard_map/ppermute | solution.py:553
  1112.1 6.0 collective-permute-done.86
  1124.9 9.1 finish_gate_up.3
  1134.0 6.3 collective-permute-done.89.refs_1_
  (613 shorter events, 476.2 us)
Async XLA Ops:
  7.2 56.4 %all-gather.22.cloned.1.call-start = ((), (), s32[]{:S(2)}) async-start(), calls=%async_computation.13 | async-start | bytes 7864320 | tf_op jit(solution)/shard_map/all_gather | solution.py:635
  10.0 112.7 %all-gather.20.cloned.1.call-start = ((), (), s32[]{:S(2)}) async-start(), calls=%async_computation.6 | async-start | bytes 2621440 | tf_op jit(solution)/shard_map/all_gather | solution.py:635
  10.9 156.9 %all-gather.24.cloned.1.call-start = ((), (), s32[]{:S(2)}) async-start(), calls=%async_computation.14 | async-start | bytes 7208960 | tf_op jit(solution)/shard_map/all_gather | solution.py:635
  16.1 195.9 %all-gather.26.cloned.1.call-start = ((), (), s32[]{:S(2)}) async-start(), calls=%async_computation.15 | async-start | bytes 7208960 | tf_op jit(solution)/shard_map/all_gather | solution.py:635
  16.7 203.3 %all-gather.28.cloned.1.call-start = ((), (), s32[]{:S(2)}) async-start(), calls=%async_computation.16 | async-start | bytes 7208960 | tf_op jit(solution)/shard_map/all_gather | solution.py:635
  19.6 28.2 %collective-permute-start = (bf16[128,2048]{1,0:T(8,128)(2,1)S(1)}, bf16[128,2048]{1,0:T(8,128)(2,1)}, u32[]{:S(2)}, u32[]{:S(2)}) collective-permute-start(bf16[128,2048]{1,0:T(8,128)(2,1)S(1)} %get-tuple-element.460), channel_id=1, source_target_pairs={{0,2},{2,0},{1,3},{3,1},{4,6},{6,4},{5,7},{7,5},{8,10},{10,8},{9,1... | collective-permute-start | bytes 1572872 | tf_op jit(solution)/shard_map/ppermute | solution.py:577
  23.6 28.1 %collective-permute-start.2 = (bf16[128,2048]{1,0:T(8,128)(2,1)S(1)}, bf16[128,2048]{1,0:T(8,128)(2,1)S(1)}, u32[]{:S(2)}, u32[]{:S(2)}) collective-permute-start(bf16[128,2048]{1,0:T(8,128)(2,1)S(1)} %get-tuple-element.460), channel_id=1, source_target_pairs={{1,0},{2,1},{3,2},{5,4},{6,5},{7,6},{9,8},{10,9},{11,10},{13,12},{... | collective-permute-start | bytes 1572872 | tf_op jit(solution)/shard_map/ppermute | solution.py:577
  24.9 26.8 %collective-permute-start.3 = (bf16[128,2048]{1,0:T(8,128)(2,1)S(1)}, bf16[128,2048]{1,0:T(8,128)(2,1)S(1)}, u32[]{:S(2)}, u32[]{:S(2)}) collective-permute-start(bf16[128,2048]{1,0:T(8,128)(2,1)S(1)} %get-tuple-element.460), channel_id=1, source_target_pairs={{0,1},{1,2},{2,3},{4,5},{5,6},{6,7},{8,9},{9,10},{10,11},{12,13},{... | collective-permute-start | bytes 1572872 | tf_op jit(solution)/shard_map/ppermute | solution.py:577
  63.6 223.5 %all-gather.30.cloned.1.call-start = ((), (), s32[]{:S(2)}) async-start(), calls=%async_computation.17 | async-start | bytes 7864320 | tf_op jit(solution)/shard_map/all_gather | solution.py:635
  72.0 28.4 %collective-permute-start.5 = (bf16[128,2048]{1,0:T(8,128)(2,1)}, bf16[128,2048]{1,0:T(8,128)(2,1)}, u32[]{:S(2)}, u32[]{:S(2)}) collective-permute-start(bf16[128,2048]{1,0:T(8,128)(2,1)} %bitcast.4), channel_id=1, source_target_pairs={{0,2},{2,0},{1,3},{3,1},{4,6},{6,4},{5,7},{7,5},{8,10},{10,8},{9,1... | collective-permute-start | bytes 1572872 | tf_op jit(solution)/shard_map/ppermute | solution.py:577
  74.4 48.3 %collective-permute-start.7 = (bf16[128,2048]{1,0:T(8,128)(2,1)}, bf16[128,2048]{1,0:T(8,128)(2,1)}, u32[]{:S(2)}, u32[]{:S(2)}) collective-permute-start(bf16[128,2048]{1,0:T(8,128)(2,1)} %bitcast.4), channel_id=1, source_target_pairs={{1,0},{2,1},{3,2},{5,4},{6,5},{7,6},{9,8},{10,9},{11,10},{13,12},{... | collective-permute-start | bytes 1572872 | tf_op jit(solution)/shard_map/ppermute | solution.py:577
  75.7 47.1 %collective-permute-start.8 = (bf16[128,2048]{1,0:T(8,128)(2,1)}, bf16[128,2048]{1,0:T(8,128)(2,1)}, u32[]{:S(2)}, u32[]{:S(2)}) collective-permute-start(bf16[128,2048]{1,0:T(8,128)(2,1)} %bitcast.4), channel_id=1, source_target_pairs={{0,1},{1,2},{2,3},{4,5},{5,6},{6,7},{8,9},{9,10},{10,11},{12,13},{... | collective-permute-start | bytes 1572872 | tf_op jit(solution)/shard_map/ppermute | solution.py:577
  81.6 24.3 %collective-permute-start.4 = (bf16[1024,512]{1,0:T(8,128)(2,1)S(1)}, bf16[1024,512]{1,0:T(8,128)(2,1)S(1)}, u32[]{:S(2)}, u32[]{:S(2)}) collective-permute-start(bf16[1024,512]{1,0:T(8,128)(2,1)S(1)} %get-tuple-element.207.key_ref.value_ref.refs_1_.refs_2_), channel_id=1, source_target_pairs={{0,4},{1,5},{2,6},{3,7},{8,12},{9,13},{10,14},{11,15},{16,20},{17,... | collective-permute-start | bytes 3145736 | tf_op jit(solution)/shard_map/ppermute | solution.py:621
  174.1 24.6 %collective-permute-start.15 = (bf16[128,2048]{1,0:T(8,128)(2,1)}, bf16[128,2048]{1,0:T(8,128)(2,1)}, u32[]{:S(2)}, u32[]{:S(2)}) collective-permute-start(bf16[128,2048]{1,0:T(8,128)(2,1)} %get-tuple-element.413), channel_id=1, source_target_pairs={{1,0},{2,1},{3,2},{5,4},{6,5},{7,6},{9,8},{10,9},{11,10},{13,12},{... | collective-permute-start | bytes 1572872 | tf_op jit(solution)/shard_map/ppermute | solution.py:577
  220.1 115.6 %all-gather.32.cloned.1.call-start = ((), (), s32[]{:S(2)}) async-start(), calls=%async_computation.18 | async-start | bytes 2621440 | tf_op jit(solution)/shard_map/all_gather | solution.py:635
  235.9 102.3 %all-gather.34.cloned.1.call-start = ((), (), s32[]{:S(2)}) async-start(), calls=%async_computation.19 | async-start | bytes 7208960 | tf_op jit(solution)/shard_map/all_gather | solution.py:635
  236.6 154.7 %all-gather.36.cloned.1.call-start = ((), (), s32[]{:S(2)}) async-start(), calls=%async_computation.20 | async-start | bytes 7208960 | tf_op jit(solution)/shard_map/all_gather | solution.py:635
  260.0 25.8 %collective-permute-start.18 = (bf16[128,2048]{1,0:T(8,128)(2,1)S(1)}, bf16[128,2048]{1,0:T(8,128)(2,1)S(1)}, u32[]{:S(2)}, u32[]{:S(2)}) collective-permute-start(bf16[128,2048]{1,0:T(8,128)(2,1)S(1)} %add_convert_fusion.9), channel_id=1, source_target_pairs={{0,2},{2,0},{1,3},{3,1},{4,6},{6,4},{5,7},{7,5},{8,10},{10,8},{9,1... | collective-permute-start | bytes 1572872 | tf_op jit(solution)/shard_map/ppermute | solution.py:593
  287.1 149.5 %all-gather.38.cloned.1.call-start = ((), (), s32[]{:S(2)}) async-start(), calls=%async_computation.21 | async-start | bytes 7208960 | tf_op jit(solution)/shard_map/all_gather | solution.py:635
  292.8 27.3 %collective-permute-start.21 = (bf16[128,2048]{1,0:T(8,128)(2,1)}, bf16[128,2048]{1,0:T(8,128)(2,1)}, u32[]{:S(2)}, u32[]{:S(2)}) collective-permute-start(bf16[128,2048]{1,0:T(8,128)(2,1)} %get-tuple-element.411), channel_id=1, source_target_pairs={{0,2},{2,0},{1,3},{3,1},{4,6},{6,4},{5,7},{7,5},{8,10},{10,8},{9,1... | collective-permute-start | bytes 1572872 | tf_op jit(solution)/shard_map/ppermute | solution.py:577
  292.8 29.8 %collective-permute-start.23 = (bf16[128,2048]{1,0:T(8,128)(2,1)}, bf16[128,2048]{1,0:T(8,128)(2,1)}, u32[]{:S(2)}, u32[]{:S(2)}) collective-permute-start(bf16[128,2048]{1,0:T(8,128)(2,1)} %get-tuple-element.411), channel_id=1, source_target_pairs={{1,0},{2,1},{3,2},{5,4},{6,5},{7,6},{9,8},{10,9},{11,10},{13,12},{... | collective-permute-start | bytes 1572872 | tf_op jit(solution)/shard_map/ppermute | solution.py:577
  294.1 28.5 %collective-permute-start.24 = (bf16[128,2048]{1,0:T(8,128)(2,1)}, bf16[128,2048]{1,0:T(8,128)(2,1)}, u32[]{:S(2)}, u32[]{:S(2)}) collective-permute-start(bf16[128,2048]{1,0:T(8,128)(2,1)} %get-tuple-element.411), channel_id=1, source_target_pairs={{0,1},{1,2},{2,3},{4,5},{5,6},{6,7},{8,9},{9,10},{10,11},{12,13},{... | collective-permute-start | bytes 1572872 | tf_op jit(solution)/shard_map/ppermute | solution.py:577
  338.2 345.1 %reduce-scatter.7.cloned.1.call-start = ((), (), s32[]{:S(2)}) async-start(), calls=%async_computation.7 | async-start | bytes 7208960 | tf_op jit(solution)/shard_map/reduce_scatter | solution.py:639
  348.4 26.1 %collective-permute-start.25 = (bf16[1024,512]{1,0:T(8,128)(2,1)S(1)}, bf16[1024,512]{1,0:T(8,128)(2,1)S(1)}, u32[]{:S(2)}, u32[]{:S(2)}) collective-permute-start(bf16[1024,512]{1,0:T(8,128)(2,1)S(1)} %get-tuple-element.240.key_ref.value_ref.refs_1_.refs_2_), channel_id=1, source_target_pairs={{0,4},{1,5},{2,6},{3,7},{8,12},{9,13},{10,14},{11,15},{16,20},{17,... | collective-permute-start | bytes 3145736 | tf_op jit(solution)/shard_map/ppermute | solution.py:621
  398.7 25.0 %collective-permute-start.29 = (bf16[128,2048]{1,0:T(8,128)(2,1)S(1)}, bf16[128,2048]{1,0:T(8,128)(2,1)S(1)}, u32[]{:S(2)}, u32[]{:S(2)}) collective-permute-start(bf16[128,2048]{1,0:T(8,128)(2,1)S(1)} %get-tuple-element.452), channel_id=1, source_target_pairs={{3,2},{2,1},{1,0},{7,6},{6,5},{5,4},{11,10},{10,9},{9,8},{15,14},{... | collective-permute-start | bytes 1572872 | tf_op jit(solution)/shard_map/ppermute | solution.py:593
  411.2 24.0 %collective-permute-start.27 = (bf16[128,2048]{1,0:T(8,128)(2,1)S(1)}, bf16[128,2048]{1,0:T(8,128)(2,1)S(1)}, u32[]{:S(2)}, u32[]{:S(2)}) collective-permute-start(bf16[128,2048]{1,0:T(8,128)(2,1)S(1)} %add_convert_fusion.7), channel_id=1, source_target_pairs={{0,2},{2,0},{1,3},{3,1},{4,6},{6,4},{5,7},{7,5},{8,10},{10,8},{9,1... | collective-permute-start | bytes 1572872 | tf_op jit(solution)/shard_map/ppermute | solution.py:593
  441.9 26.9 %collective-permute-start.30 = (bf16[128,2048]{1,0:T(8,128)(2,1)S(1)}, bf16[128,2048]{1,0:T(8,128)(2,1)S(1)}, u32[]{:S(2)}, u32[]{:S(2)}) collective-permute-start(bf16[128,2048]{1,0:T(8,128)(2,1)S(1)} %get-tuple-element.409), channel_id=1, source_target_pairs={{0,2},{2,0},{1,3},{3,1},{4,6},{6,4},{5,7},{7,5},{8,10},{10,8},{9,1... | collective-permute-start | bytes 1572872 | tf_op jit(solution)/shard_map/ppermute | solution.py:577
  442.1 28.2 %collective-permute-start.32 = (bf16[128,2048]{1,0:T(8,128)(2,1)S(1)}, bf16[128,2048]{1,0:T(8,128)(2,1)S(1)}, u32[]{:S(2)}, u32[]{:S(2)}) collective-permute-start(bf16[128,2048]{1,0:T(8,128)(2,1)S(1)} %get-tuple-element.409), channel_id=1, source_target_pairs={{1,0},{2,1},{3,2},{5,4},{6,5},{7,6},{9,8},{10,9},{11,10},{13,12},{... | collective-permute-start | bytes 1572872 | tf_op jit(solution)/shard_map/ppermute | solution.py:577
  443.4 26.9 %collective-permute-start.33 = (bf16[128,2048]{1,0:T(8,128)(2,1)S(1)}, bf16[128,2048]{1,0:T(8,128)(2,1)S(1)}, u32[]{:S(2)}, u32[]{:S(2)}) collective-permute-start(bf16[128,2048]{1,0:T(8,128)(2,1)S(1)} %get-tuple-element.409), channel_id=1, source_target_pairs={{0,1},{1,2},{2,3},{4,5},{5,6},{6,7},{8,9},{9,10},{10,11},{12,13},{... | collective-permute-start | bytes 1572872 | tf_op jit(solution)/shard_map/ppermute | solution.py:577
  526.4 30.2 %collective-permute-start.35 = (bf16[128,2048]{1,0:T(8,128)(2,1)}, bf16[128,2048]{1,0:T(8,128)(2,1)}, u32[]{:S(2)}, u32[]{:S(2)}) collective-permute-start(bf16[128,2048]{1,0:T(8,128)(2,1)} %add_convert_fusion.5), channel_id=1, source_target_pairs={{0,2},{2,0},{1,3},{3,1},{4,6},{6,4},{5,7},{7,5},{8,10},{10,8},{9,1... | collective-permute-start | bytes 1572872 | tf_op jit(solution)/shard_map/ppermute | solution.py:593
  569.0 176.3 %reduce-scatter.9.cloned.1.call-start = ((), (), s32[]{:S(2)}) async-start(), calls=%async_computation.8 | async-start | bytes 7208960 | tf_op jit(solution)/shard_map/reduce_scatter | solution.py:639
  577.4 208.4 %reduce-scatter.11.cloned.1.call-start = ((), (), s32[]{:S(2)}) async-start(), calls=%async_computation.9 | async-start | bytes 7208960 | tf_op jit(solution)/shard_map/reduce_scatter | solution.py:639
  578.6 26.7 %collective-permute-start.40 = (bf16[128,2048]{1,0:T(8,128)(2,1)}, bf16[128,2048]{1,0:T(8,128)(2,1)S(1)}, u32[]{:S(2)}, u32[]{:S(2)}) collective-permute-start(bf16[128,2048]{1,0:T(8,128)(2,1)} %copy-done.38), channel_id=1, source_target_pairs={{1,0},{2,1},{3,2},{5,4},{6,5},{7,6},{9,8},{10,9},{11,10},{13,12},{... | collective-permute-start | bytes 1572872 | tf_op jit(solution)/shard_map/ppermute | solution.py:577
  579.9 25.4 %collective-permute-start.41 = (bf16[128,2048]{1,0:T(8,128)(2,1)}, bf16[128,2048]{1,0:T(8,128)(2,1)S(1)}, u32[]{:S(2)}, u32[]{:S(2)}) collective-permute-start(bf16[128,2048]{1,0:T(8,128)(2,1)} %copy-done.38), channel_id=1, source_target_pairs={{0,1},{1,2},{2,3},{4,5},{5,6},{6,7},{8,9},{9,10},{10,11},{12,13},{... | collective-permute-start | bytes 1572872 | tf_op jit(solution)/shard_map/ppermute | solution.py:577
  615.4 38.6 %collective-permute-start.45 = (bf16[128,2048]{1,0:T(8,128)(2,1)}, bf16[128,2048]{1,0:T(8,128)(2,1)}, u32[]{:S(2)}, u32[]{:S(2)}) collective-permute-start(bf16[128,2048]{1,0:T(8,128)(2,1)} %get-tuple-element.446), channel_id=1, source_target_pairs={{3,2},{2,1},{1,0},{7,6},{6,5},{5,4},{11,10},{10,9},{9,8},{15,14},{... | collective-permute-start | bytes 1572872 | tf_op jit(solution)/shard_map/ppermute | solution.py:593
  616.8 37.2 %collective-permute-start.44 = (bf16[128,2048]{1,0:T(8,128)(2,1)}, bf16[128,2048]{1,0:T(8,128)(2,1)}, u32[]{:S(2)}, u32[]{:S(2)}) collective-permute-start(bf16[128,2048]{1,0:T(8,128)(2,1)} %get-tuple-element.445), channel_id=1, source_target_pairs={{0,1},{1,2},{2,3},{4,5},{5,6},{6,7},{8,9},{9,10},{10,11},{12,13},{... | collective-permute-start | bytes 1572872 | tf_op jit(solution)/shard_map/ppermute | solution.py:593
  637.7 32.7 %collective-permute-start.46 = (bf16[1024,512]{1,0:T(8,128)(2,1)S(1)}, bf16[1024,512]{1,0:T(8,128)(2,1)S(1)}, u32[]{:S(2)}, u32[]{:S(2)}) collective-permute-start(bf16[1024,512]{1,0:T(8,128)(2,1)S(1)} %get-tuple-element.271), channel_id=1, source_target_pairs={{4,0},{5,1},{6,2},{7,3},{12,8},{13,9},{14,10},{15,11},{20,16},{21,... | collective-permute-start | bytes 3145736 | tf_op jit(solution)/shard_map/ppermute | solution.py:628
  678.7 266.9 %reduce-scatter.13.cloned.1.call-start = ((), (), s32[]{:S(2)}) async-start(), calls=%async_computation.10 | async-start | bytes 7208960 | tf_op jit(solution)/shard_map/reduce_scatter | solution.py:639
  693.8 43.2 %collective-permute-start.51 = (bf16[1408,512]{1,0:T(8,128)(2,1)}, bf16[1408,512]{1,0:T(8,128)(2,1)}, u32[]{:S(2)}, u32[]{:S(2)}) collective-permute-start(bf16[1408,512]{1,0:T(8,128)(2,1)} %reduce-scatter.7.cloned.1.call-done.refs_0_), channel_id=1, source_target_pairs={{0,4},{4,0},{1,5},{5,1},{2,6},{6,2},{3,7},{7,3},{8,12},{12,8},{9,1... | collective-permute-start | bytes 4325384 | tf_op jit(solution)/shard_map/ppermute | solution.py:553
  707.0 29.9 %collective-permute-start.48 = (bf16[128,2048]{1,0:T(8,128)(2,1)}, bf16[128,2048]{1,0:T(8,128)(2,1)}, u32[]{:S(2)}, u32[]{:S(2)}) collective-permute-start(bf16[128,2048]{1,0:T(8,128)(2,1)} %add_convert_fusion.2), channel_id=1, source_target_pairs={{0,2},{2,0},{1,3},{3,1},{4,6},{6,4},{5,7},{7,5},{8,10},{10,8},{9,1... | collective-permute-start | bytes 1572872 | tf_op jit(solution)/shard_map/ppermute | solution.py:593
  745.3 40.5 %collective-permute-start.58 = (bf16[1024,1536]{1,0:T(8,128)(2,1)}, bf16[1024,1536]{1,0:T(8,128)(2,1)}, u32[]{:S(2)}, u32[]{:S(2)}) collective-permute-start(bf16[1024,1536]{1,0:T(8,128)(2,1)} %copy-done.52), channel_id=1, source_target_pairs={{0,8},{8,0},{16,24},{24,16},{1,9},{9,1},{17,25},{25,17},{2,10},{10... | collective-permute-start | bytes 9437192 | tf_op jit(solution)/shard_map/ppermute | solution.py:553
  745.3 40.5 %collective-permute-start.57 = (bf16[512,1408]{1,0:T(8,128)(2,1)}, bf16[512,1408]{1,0:T(8,128)(2,1)}, u32[]{:S(2)}, u32[]{:S(2)}) collective-permute-start(bf16[512,1408]{1,0:T(8,128)(2,1)} %reduce-scatter.9.cloned.1.call-done.refs_0_), channel_id=1, source_target_pairs={{0,4},{4,0},{1,5},{5,1},{2,6},{6,2},{3,7},{7,3},{8,12},{12,8},{9,1... | collective-permute-start | bytes 4325384 | tf_op jit(solution)/shard_map/ppermute | solution.py:553
  745.5 28.6 %collective-permute-start.55 = (bf16[128,2048]{1,0:T(8,128)(2,1)}, bf16[128,2048]{1,0:T(8,128)(2,1)S(1)}, u32[]{:S(2)}, u32[]{:S(2)}) collective-permute-start(bf16[128,2048]{1,0:T(8,128)(2,1)} %copy-done.40), channel_id=1, source_target_pairs={{1,0},{2,1},{3,2},{5,4},{6,5},{7,6},{9,8},{10,9},{11,10},{13,12},{... | collective-permute-start | bytes 1572872 | tf_op jit(solution)/shard_map/ppermute | solution.py:577
  746.7 27.8 %collective-permute-start.56 = (bf16[128,2048]{1,0:T(8,128)(2,1)}, bf16[128,2048]{1,0:T(8,128)(2,1)S(1)}, u32[]{:S(2)}, u32[]{:S(2)}) collective-permute-start(bf16[128,2048]{1,0:T(8,128)(2,1)} %copy-done.40), channel_id=1, source_target_pairs={{0,1},{1,2},{2,3},{4,5},{5,6},{6,7},{8,9},{9,10},{10,11},{12,13},{... | collective-permute-start | bytes 1572872 | tf_op jit(solution)/shard_map/ppermute | solution.py:577
  796.3 212.1 %reduce-scatter.15.cloned.1.call-start = ((), (), s32[]{:S(2)}) async-start(), calls=%async_computation.11 | async-start | bytes 7208960 | tf_op jit(solution)/shard_map/reduce_scatter | solution.py:639
  804.7 68.6 %collective-permute-start.65 = (bf16[512,1536]{1,0:T(8,128)(2,1)}, bf16[512,1536]{1,0:T(8,128)(2,1)}, u32[]{:S(2)}, u32[]{:S(2)}) collective-permute-start(bf16[512,1536]{1,0:T(8,128)(2,1)} %split.61), channel_id=1, source_target_pairs={{0,16},{8,24},{16,0},{24,8},{1,17},{9,25},{17,1},{25,9},{2,18},{10... | collective-permute-start | bytes 4718600 | tf_op jit(solution)/shard_map/ppermute | solution.py:553
  833.6 39.7 %collective-permute-start.64 = (bf16[512,1408]{1,0:T(8,128)(2,1)}, bf16[512,1408]{1,0:T(8,128)(2,1)}, u32[]{:S(2)}, u32[]{:S(2)}) collective-permute-start(bf16[512,1408]{1,0:T(8,128)(2,1)} %reduce-scatter.11.cloned.1.call-done.refs_2_), channel_id=1, source_target_pairs={{0,4},{4,0},{1,5},{5,1},{2,6},{6,2},{3,7},{7,3},{8,12},{12,8},{9,1... | collective-permute-start | bytes 4325384 | tf_op jit(solution)/shard_map/ppermute | solution.py:553
  846.9 26.5 %collective-permute-start.61 = (bf16[128,2048]{1,0:T(8,128)(2,1)}, bf16[128,2048]{1,0:T(8,128)(2,1)}, u32[]{:S(2)}, u32[]{:S(2)}) collective-permute-start(bf16[128,2048]{1,0:T(8,128)(2,1)} %add_convert_fusion.1), channel_id=1, source_target_pairs={{0,2},{2,0},{1,3},{3,1},{4,6},{6,4},{5,7},{7,5},{8,10},{10,8},{9,1... | collective-permute-start | bytes 1572872 | tf_op jit(solution)/shard_map/ppermute | solution.py:593
  885.7 150.2 %reduce-scatter.17.cloned.1.call-start = ((), (), s32[]{:S(2)}) async-start(), calls=%async_computation.12 | async-start | bytes 7208960 | tf_op jit(solution)/shard_map/reduce_scatter | solution.py:639
  897.6 46.7 %collective-permute-start.71 = (bf16[512,1536]{1,0:T(8,128)(2,1)S(1)}, bf16[512,1536]{1,0:T(8,128)(2,1)S(1)}, u32[]{:S(2)}, u32[]{:S(2)}) collective-permute-start(bf16[512,1536]{1,0:T(8,128)(2,1)S(1)} %fusion.1.refs_0_), channel_id=1, source_target_pairs={{0,4},{4,0},{1,5},{5,1},{2,6},{6,2},{3,7},{7,3},{8,12},{12,8},{9,1... | collective-permute-start | bytes 4718600 | tf_op jit(solution)/shard_map/ppermute | solution.py:553
  899.2 26.8 %collective-permute-start.68 = (bf16[128,2048]{1,0:T(8,128)(2,1)}, bf16[128,2048]{1,0:T(8,128)(2,1)S(1)}, u32[]{:S(2)}, u32[]{:S(2)}) collective-permute-start(bf16[128,2048]{1,0:T(8,128)(2,1)} %get-tuple-element.314), channel_id=1, source_target_pairs={{1,0},{2,1},{3,2},{5,4},{6,5},{7,6},{9,8},{10,9},{11,10},{13,12},{... | collective-permute-start | bytes 1572872 | tf_op jit(solution)/shard_map/ppermute | solution.py:577
  900.5 25.5 %collective-permute-start.69 = (bf16[128,2048]{1,0:T(8,128)(2,1)}, bf16[128,2048]{1,0:T(8,128)(2,1)S(1)}, u32[]{:S(2)}, u32[]{:S(2)}) collective-permute-start(bf16[128,2048]{1,0:T(8,128)(2,1)} %get-tuple-element.314), channel_id=1, source_target_pairs={{0,1},{1,2},{2,3},{4,5},{5,6},{6,7},{8,9},{9,10},{10,11},{12,13},{... | collective-permute-start | bytes 1572872 | tf_op jit(solution)/shard_map/ppermute | solution.py:577
  917.3 26.3 %collective-permute-start.70 = (bf16[512,512]{1,0:T(8,128)(2,1)S(1)}, bf16[512,512]{1,0:T(8,128)(2,1)S(1)}, u32[]{:S(2)}, u32[]{:S(2)}) collective-permute-start(bf16[512,512]{1,0:T(8,128)(2,1)S(1)} %fusion.8.refs_0_), channel_id=1, source_target_pairs={{0,4},{4,0},{1,5},{5,1},{2,6},{6,2},{3,7},{7,3},{8,12},{12,8},{9,1... | collective-permute-start | bytes 1572872 | tf_op jit(solution)/shard_map/ppermute | solution.py:553
  945.6 34.7 %collective-permute-start.72 = (bf16[1408,512]{1,0:T(8,128)(2,1)}, bf16[1408,512]{1,0:T(8,128)(2,1)S(1)}, u32[]{:S(2)}, u32[]{:S(2)}) collective-permute-start(bf16[1408,512]{1,0:T(8,128)(2,1)} %reduce-scatter.13.cloned.1.call-done.refs_0_), channel_id=1, source_target_pairs={{0,4},{4,0},{1,5},{5,1},{2,6},{6,2},{3,7},{7,3},{8,12},{12,8},{9,1... | collective-permute-start | bytes 4325384 | tf_op jit(solution)/shard_map/ppermute | solution.py:553
  962.4 36.9 %collective-permute-start.73 = (bf16[1024,512]{1,0:T(8,128)(2,1)S(1)}, bf16[1024,512]{1,0:T(8,128)(2,1)S(1)}, u32[]{:S(2)}, u32[]{:S(2)}) collective-permute-start(bf16[1024,512]{1,0:T(8,128)(2,1)S(1)} %get-tuple-element.328), channel_id=1, source_target_pairs={{4,0},{5,1},{6,2},{7,3},{12,8},{13,9},{14,10},{15,11},{20,16},{21,... | collective-permute-start | bytes 3145736 | tf_op jit(solution)/shard_map/ppermute | solution.py:628
  1012.4 47.6 %collective-permute-start.80 = (bf16[512,1408]{1,0:T(8,128)(2,1)}, bf16[512,1408]{1,0:T(8,128)(2,1)}, u32[]{:S(2)}, u32[]{:S(2)}) collective-permute-start(bf16[512,1408]{1,0:T(8,128)(2,1)} %reduce-scatter.15.cloned.1.call-done.refs_0_), channel_id=1, source_target_pairs={{0,4},{4,0},{1,5},{5,1},{2,6},{6,2},{3,7},{7,3},{8,12},{12,8},{9,1... | collective-permute-start | bytes 4325384 | tf_op jit(solution)/shard_map/ppermute | solution.py:553
  1026.5 44.8 %collective-permute-start.81 = (bf16[512,1536]{1,0:T(8,128)(2,1)}, bf16[512,1536]{1,0:T(8,128)(2,1)}, u32[]{:S(2)}, u32[]{:S(2)}) collective-permute-start(bf16[512,1536]{1,0:T(8,128)(2,1)} %split.60), channel_id=1, source_target_pairs={{0,16},{8,24},{16,0},{24,8},{1,17},{9,25},{17,1},{25,9},{2,18},{10... | collective-permute-start | bytes 4718600 | tf_op jit(solution)/shard_map/ppermute | solution.py:553
  1028.5 33.2 %collective-permute-start.78 = (bf16[128,2048]{1,0:T(8,128)(2,1)}, bf16[128,2048]{1,0:T(8,128)(2,1)}, u32[]{:S(2)}, u32[]{:S(2)}) collective-permute-start(bf16[128,2048]{1,0:T(8,128)(2,1)} %get-tuple-element.429), channel_id=1, source_target_pairs={{0,1},{1,2},{2,3},{4,5},{5,6},{6,7},{8,9},{9,10},{10,11},{12,13},{... | collective-permute-start | bytes 1572872 | tf_op jit(solution)/shard_map/ppermute | solution.py:593
  1030.6 31.1 %collective-permute-start.79 = (bf16[128,2048]{1,0:T(8,128)(2,1)}, bf16[128,2048]{1,0:T(8,128)(2,1)}, u32[]{:S(2)}, u32[]{:S(2)}) collective-permute-start(bf16[128,2048]{1,0:T(8,128)(2,1)} %get-tuple-element.427), channel_id=1, source_target_pairs={{3,2},{2,1},{1,0},{7,6},{6,5},{5,4},{11,10},{10,9},{9,8},{15,14},{... | collective-permute-start | bytes 1572872 | tf_op jit(solution)/shard_map/ppermute | solution.py:593
  1035.9 35.4 %collective-permute-start.77 = (bf16[128,2048]{1,0:T(8,128)(2,1)}, bf16[128,2048]{1,0:T(8,128)(2,1)S(1)}, u32[]{:S(2)}, u32[]{:S(2)}) collective-permute-start(bf16[128,2048]{1,0:T(8,128)(2,1)} %add_convert_fusion), channel_id=1, source_target_pairs={{0,2},{2,0},{1,3},{3,1},{4,6},{6,4},{5,7},{7,5},{8,10},{10,8},{9,1... | collective-permute-start | bytes 1572872 | tf_op jit(solution)/shard_map/ppermute | solution.py:593
  1059.9 64.9 %collective-permute-start.90 = (bf16[512,1408]{1,0:T(8,128)(2,1)S(1)}, bf16[512,1408]{1,0:T(8,128)(2,1)}, u32[]{:S(2)}, u32[]{:S(2)}) collective-permute-start(bf16[512,1408]{1,0:T(8,128)(2,1)S(1)} %copy-done.19), channel_id=1, source_target_pairs={{0,4},{4,0},{1,5},{5,1},{2,6},{6,2},{3,7},{7,3},{8,12},{12,8},{9,1... | collective-permute-start | bytes 4325384 | tf_op jit(solution)/shard_map/ppermute | solution.py:553
  1080.9 60.9 %collective-permute-start.87 = (bf16[512,1536]{1,0:T(8,128)(2,1)}, bf16[512,1536]{1,0:T(8,128)(2,1)}, u32[]{:S(2)}, u32[]{:S(2)}) collective-permute-start(bf16[512,1536]{1,0:T(8,128)(2,1)} %fusion.refs_0_), channel_id=1, source_target_pairs={{0,4},{4,0},{1,5},{5,1},{2,6},{6,2},{3,7},{7,3},{8,12},{12,8},{9,1... | collective-permute-start | bytes 4718600 | tf_op jit(solution)/shard_map/ppermute | solution.py:553
  1081.9 28.1 %collective-permute-start.88 = (bf16[512,512]{1,0:T(8,128)(2,1)S(1)}, bf16[512,512]{1,0:T(8,128)(2,1)S(1)}, u32[]{:S(2)}, u32[]{:S(2)}) collective-permute-start(bf16[512,512]{1,0:T(8,128)(2,1)S(1)} %split.62), channel_id=1, source_target_pairs={{0,16},{8,24},{16,0},{24,8},{1,17},{9,25},{17,1},{25,9},{2,18},{10... | collective-permute-start | bytes 1572872 | tf_op jit(solution)/shard_map/ppermute | solution.py:553
  1110.2 30.0 %collective-permute-start.89 = (bf16[512,512]{1,0:T(8,128)(2,1)S(1)}, bf16[512,512]{1,0:T(8,128)(2,1)S(1)}, u32[]{:S(2)}, u32[]{:S(2)}) collective-permute-start(bf16[512,512]{1,0:T(8,128)(2,1)S(1)} %fusion.7.refs_0_), channel_id=1, source_target_pairs={{0,4},{4,0},{1,5},{5,1},{2,6},{6,2},{3,7},{7,3},{8,12},{12,8},{9,1... | collective-permute-start | bytes 1572872 | tf_op jit(solution)/shard_map/ppermute | solution.py:553
  (169 other events, 2609.5 us)
Sparse Core Ops, SparseCore 0:
  10.2 49.0 all-gather.21
  61.4 22.5 all-gather.19
  86.2 43.4 all-gather.23
  131.7 43.4 all-gather.25
  176.6 43.3 all-gather.27
  222.0 46.3 all-gather.29
  270.6 22.5 all-gather.31
  294.8 43.3 all-gather.33
  339.8 43.3 all-gather.35
  385.2 43.3 all-gather.37
  569.1 53.3 reduce-scatter.6
  625.6 54.8 reduce-scatter.8
  683.5 55.4 reduce-scatter.10
  796.4 76.5 reduce-scatter.12
  885.8 52.2 reduce-scatter.14
  941.3 54.8 reduce-scatter.16

commit v6 on v5

--- a/solution.py
+++ b/solution.py
@@ -510,7 +510,7 @@
         out_shape=jax.ShapeDtypeStruct(shape, WIDE),
         input_output_aliases={} if buffer is None else {len(terms): 0},
         compiler_params=pltpu.CompilerParams(vmem_limit_bytes=48 * 1024 * 1024),
-        cost_estimate=work(1e9),
+        cost_estimate=work(len(terms) * terms[0].size * 3.5e3),
         name=name,
     )(*operands)
 
@@ -854,15 +854,13 @@
             mine["down"] = out_job(activated, branch)
         mine["gate"] = in_job(rows_two, grad_gate)
         if layer == 0:
-            mine["up"] = in_job(rows_two, grad_up)
+            hidden_low = meanwhile(hidden_low, mine["down"])
         top = layer + 1 == LAYERS
         if top:
             late, hidden_low = lax.optimization_barrier((activated, hidden_low))
             partial_out = times_wide(late, down_full, "down")
         attention = plan.gather_rows(hidden_low)
         attention = meanwhile(attention, *old("out", "qkv"))
-        if layer == 0:
-            attention = meanwhile(attention, mine["down"])
         if top:
             attention, partial_out = lax.optimization_barrier((attention, partial_out))
             output = (mid + plan.sum_of(plan.sum_rows(partial_out))).astype(LOW)[None]
@@ -870,6 +868,8 @@
         shared = (queries, grad_attended, attended, lse)
         far_queries, far_grads = attend_back(qpos, far_places, *shared, far_kv, LOW, [])
         if layer == 0:
+            far_queries, grad_up = lax.optimization_barrier((far_queries, grad_up))
+            mine["up"] = in_job(rows_two, grad_up)
             far_queries = meanwhile(far_queries, mine["down"])
         returned = plan.far_key_grads(far_grads)
         grad_queries, grad_kv = attend_back(
@@ -896,13 +896,6 @@
             above_done, projected = lax.optimization_barrier(
                 ({k: j.finish() for k, j in above.items()}, projected)
             )
-            sums = above_done
-            results = [
-                finish_projections(None, layer + 1, sums["qkv"]),
-                finish_matrix(None, layer + 1, sums["out"], "finish_out"),
-                finish_gate_up(None, layer + 1, sums["gate"], sums["up"]),
-                finish_matrix(None, layer + 1, sums["down"], "finish_down"),
-            ]
         if layer == 0:
             mine["qkv"] = Job(
                 pair_stages(plan, lambda r, b=projected: (own_part(rows_one, r), b), 0)
@@ -921,7 +914,9 @@
         grad_stream, grad_low, gain_one, bias_one = norm_back(
             summed, unit_one, inverse_one, gains[layer, 0], hidden_grad
         )
-        if layer > 0:
+        if layer == 0:
+            gain_one = meanwhile(gain_one, mine["up"])
+        else:
             grad_low, projected = lax.optimization_barrier((grad_low, projected))
             mine["qkv"] = Job(
                 pair_stages(plan, lambda r, a=rows_one, b=projected: (own_part(a, r), b), 0)
@@ -945,17 +940,23 @@
         ],
         axis=0,
     )
-    for axis in ("ctx", "dp", "tensor"):
+    above_done, down_done, small = lax.optimization_barrier(
+        (above_done, grad_jobs[0]["down"].finish(), small)
+    )
+    for axis in ("dp", "tensor", "ctx"):
         for bit in bits_of(lax.axis_size(axis)):
             small = small + swapped(small, axis, bit)
-        small, results = lax.optimization_barrier((small, results))
-    sums = {k: j.finish() for k, j in grad_jobs[0].items()}
-    results = [
-        finish_projections(results[0], 0, sums["qkv"]),
-        finish_matrix(results[1], 0, sums["out"], "finish_out"),
-        finish_gate_up(results[2], 0, sums["gate"], sums["up"]),
-        finish_matrix(results[3], 0, sums["down"], "finish_down"),
-    ]
+    results = [None] * 4
+    for layer, sums in ((1, above_done), (0, grad_jobs[0])):
+        if layer == 0:
+            sums = {k: j.finish() for k, j in sums.items()}
+            sums["down"] = down_done
+        results = [
+            finish_projections(results[0], layer, sums["qkv"]),
+            finish_matrix(results[1], layer, sums["out"], "finish_out"),
+            finish_gate_up(results[2], layer, sums["gate"], sums["up"]),
+            finish_matrix(results[3], layer, sums["down"], "finish_down"),
+        ]
     return (
         output,
         tokens_grad,

time: 1160 us -> 1170 us (level)
  waiting for transfers between devices: 474 us -> 500 us
    ppermute x23, waiting for transfers between devices: 57.6 us -> 76.2 us  [swapped(): return lax.ppermute(value, axis, [(i, i ^ mask) for i in range(count)])]
    unnamed x253 -> x273, local copies, waits for them, and re-layouts: 54.7 us -> 48.6 us
  transfers between devices with their start and end apart: 107 -> 107, of which waited for: 53 -> 54; matrix products, arithmetic and copies ran while one was open for 10% -> 9% of each run, Pallas kernels for 21% -> 21%
where the time goes in v6:
time: 1170 us; the launch traced here: 1160 us
  waiting for transfers between devices  500 us (43%)
  Pallas kernels  290 us (25%)
  starting transfers between devices  193 us (16%)
  local copies, waits for them, and re-layouts  82.8 us (7%)
  other arithmetic  79.6 us (7%)
  between operations  17 us (1%)
    ppermute x32, waiting for transfers between devices, sum_rows(): send = lambda v, *route: lax.ppermute(v, 'tensor', list(route))  211 us
    ppermute x32, waiting for transfers between devices, gather_rows(): send = lambda v, *route: lax.ppermute(v, 'tensor', list(route))  174 us
    pallas_call x34, Pallas kernels, tiled(): pl.pallas_call(kernel, grid=(steps,), in_specs=[pl.BlockSpec(block, index...  162 us
    pallas_call x8, Pallas kernels, pair_call(): pl.pallas_call(kernel, grid=(width // PAIR,), in_specs=common + [specs['r...  89.1 us
    ppermute x32, starting transfers between devices, sum_rows(): send = lambda v, *route: lax.ppermute(v, 'tensor', list(route))  87.9 us
    ppermute x32, starting transfers between devices, gather_rows(): send = lambda v, *route: lax.ppermute(v, 'tensor', list(route))  77.9 us
    ppermute x23, waiting for transfers between devices, swapped(): return lax.ppermute(value, axis, [(i, i ^ mask) for i in range(count)])  76.2 us
    unnamed x273, local copies, waits for them, and re-layouts  48.6 us
  transfers between devices with their start and end apart: 107, of which 54 were waited for; matrix products, arithmetic and copies ran while one was open for 9% of the time, Pallas kernels for 21%

profile of v6, /device:TPU:0, one launch (start us, length us, event | category | flops | bytes accessed | tf_op | source)
XLA Modules:
  0.0 1162.9 jit_solution(9210173781239011285)
XLA Ops:
  32.2 16.2 %collective-permute-done = bf16[128,2048]{1,0:T(8,128)(2,1)} collective-permute-done((bf16[128,2048]{1,0:T(8,128)(2,1)S(1)}, bf16[128,2048]{1,0:T(8,128)(2,1)}, u32[]{:S(2)}, u32[]{:S(2)}) %collective-permute-start) | collective-permute-done | bytes 524320 | tf_op jit(solution)/shard_map/ppermute | solution.py:577
  52.4 10.4 collective-permute-done.1
  64.2 7.4 project.2
  87.4 10.1 attend_near.2
  105.7 14.7 %attend_far.2 = (f32[512,512]{1,0:T(8,128)S(1)}, f32[512,512]{1,0:T(8,128)S(1)}) custom-call(s32[512,1]{1,0:T(8,128)S(1)} %copy.70.qpos_ref, s32[1,1,512]{2,1,0:T(1,128)S(1)} %bitcast.105, bf16[512,512]{1,0:T(8,128)(2,1)S(1)} %get-tuple-element.208.q_ref, f32[512,512]{1,0:T(8,128)S(1)} %get-tuple-element.210.acc_in_ref, ...), custom_call_target="tpu_custom_call" | custom-call | flops 5771362304 | tf_op jit(solution)/shard_map/attend_far/pallas_call | solution.py:383
  137.8 6.4 collective-permute-done.9
  155.5 10.6 collective-permute-done.10
  175.2 8.9 collective-permute-start.16
  184.0 11.9 %collective-permute-done.13 = bf16[128,2048]{1,0:T(8,128)(2,1)} collective-permute-done((bf16[128,2048]{1,0:T(8,128)(2,1)}, bf16[128,2048]{1,0:T(8,128)(2,1)}, u32[]{:S(2)}, u32[]{:S(2)}) %collective-permute-start.13) | collective-permute-done | bytes 524320 | tf_op jit(solution)/shard_map/ppermute | solution.py:577
  198.5 9.2 collective-permute-done.14
  211.8 8.2 all-gather.28.cloned.1.call-done
  223.5 11.1 gate_up.2
  253.4 6.3 collective-permute-done.17
  263.3 9.3 collective-permute-done.20
  272.7 13.0 %collective-permute-done.18 = bf16[128,2048]{1,0:T(8,128)(2,1)S(1)} collective-permute-done((bf16[128,2048]{1,0:T(8,128)(2,1)S(1)}, bf16[128,2048]{1,0:T(8,128)(2,1)S(1)}, u32[]{:S(2)}, u32[]{:S(2)}) %collective-permute-start.18) | collective-permute-done | bytes 524320 | tf_op jit(solution)/shard_map/ppermute | solution.py:593
  294.5 8.2 collective-permute-start.24
  302.7 17.8 %collective-permute-done.21 = bf16[128,2048]{1,0:T(8,128)(2,1)} collective-permute-done((bf16[128,2048]{1,0:T(8,128)(2,1)}, bf16[128,2048]{1,0:T(8,128)(2,1)}, u32[]{:S(2)}, u32[]{:S(2)}) %collective-permute-start.21) | collective-permute-done | bytes 524320 | tf_op jit(solution)/shard_map/ppermute | solution.py:577
  323.0 8.9 collective-permute-done.22
  340.9 7.4 project.3
  351.6 10.1 attend_near.3
  361.8 12.6 %collective-permute-done.25.refs_0_.refs_1_ = bf16[1024,512]{1,0:T(8,128)(2,1)S(1)} collective-permute-done((bf16[1024,512]{1,0:T(8,128)(2,1)S(1)}, bf16[1024,512]{1,0:T(8,128)(2,1)S(1)}, u32[]{:S(2)}, u32[]{:S(2)}) %collective-permute-start.25) | collective-permute-done | bytes 1048608 | tf_op jit(solution)/shard_map/ppermute | solution.py:621
  374.4 14.7 %attend_far.3 = (f32[512,512]{1,0:T(8,128)S(1)}, f32[512,512]{1,0:T(8,128)S(1)}) custom-call(s32[512,1]{1,0:T(8,128)S(1)} %copy.70.qpos_ref, s32[1,1,512]{2,1,0:T(1,128)S(1)} %bitcast.106, bf16[512,512]{1,0:T(8,128)(2,1)S(1)} %get-tuple-element.241.q_ref, f32[512,512]{1,0:T(8,128)S(1)} %get-tuple-element.243.acc_in_ref, ...), custom_call_target="tpu_custom_call" | custom-call | flops 5771362304 | tf_op jit(solution)/shard_map/attend_far/pallas_call | solution.py:383
  404.6 6.4 collective-permute-done.26
  414.6 9.1 collective-permute-done.29
  423.7 11.5 collective-permute-done.27
  443.4 8.1 collective-permute-start.33
  451.5 17.3 %collective-permute-done.30 = bf16[128,2048]{1,0:T(8,128)(2,1)S(1)} collective-permute-done((bf16[128,2048]{1,0:T(8,128)(2,1)S(1)}, bf16[128,2048]{1,0:T(8,128)(2,1)S(1)}, u32[]{:S(2)}, u32[]{:S(2)}) %collective-permute-start.30) | collective-permute-done | bytes 524320 | tf_op jit(solution)/shard_map/ppermute | solution.py:577
  470.4 9.5 collective-permute-done.31
  480.3 11.5 gate_up.3
  492.9 7.3 gate_up_back.2
  500.3 10.2 gate_up_in.2.refs_0_
  516.6 8.9 collective-permute-done.34
  526.5 7.7 collective-permute-start.35
  536.4 20.3 %collective-permute-done.35.refs_1_ = bf16[128,2048]{1,0:T(8,128)(2,1)} collective-permute-done((bf16[128,2048]{1,0:T(8,128)(2,1)}, bf16[128,2048]{1,0:T(8,128)(2,1)}, u32[]{:S(2)}, u32[]{:S(2)}) %collective-permute-start.35) | collective-permute-done | bytes 524320 | tf_op jit(solution)/shard_map/ppermute | solution.py:593
  584.6 12.3 %collective-permute-done.38 = bf16[128,2048]{1,0:T(8,128)(2,1)S(1)} collective-permute-done((bf16[128,2048]{1,0:T(8,128)(2,1)}, bf16[128,2048]{1,0:T(8,128)(2,1)S(1)}, u32[]{:S(2)}, u32[]{:S(2)}) %collective-permute-start.38) | collective-permute-done | bytes 524320 | tf_op jit(solution)/shard_map/ppermute | solution.py:577
  605.4 8.5 collective-permute-done.39
  626.4 10.3 attend_back.4
  644.7 9.4 attend_back.5
  654.1 13.9 %collective-permute-done.43 = bf16[128,2048]{1,0:T(8,128)(2,1)S(1)} collective-permute-done((bf16[128,2048]{1,0:T(8,128)(2,1)S(1)}, bf16[128,2048]{1,0:T(8,128)(2,1)S(1)}, u32[]{:S(2)}, u32[]{:S(2)}) %collective-permute-start.43) | collective-permute-done | bytes 524320 | tf_op jit(solution)/shard_map/ppermute | solution.py:593
  684.7 6.5 project_in.2.refs_0_
  699.6 6.5 collective-permute-done.47
  718.4 18.5 %collective-permute-done.48.refs_1_ = bf16[128,2048]{1,0:T(8,128)(2,1)} collective-permute-done((bf16[128,2048]{1,0:T(8,128)(2,1)}, bf16[128,2048]{1,0:T(8,128)(2,1)}, u32[]{:S(2)}, u32[]{:S(2)}) %collective-permute-start.48) | collective-permute-done | bytes 524320 | tf_op jit(solution)/shard_map/ppermute | solution.py:593
  751.3 16.3 %collective-permute-done.53 = bf16[128,2048]{1,0:T(8,128)(2,1)S(1)} collective-permute-done((bf16[128,2048]{1,0:T(8,128)(2,1)}, bf16[128,2048]{1,0:T(8,128)(2,1)S(1)}, u32[]{:S(2)}, u32[]{:S(2)}) %collective-permute-start.53) | collective-permute-done | bytes 524320 | tf_op jit(solution)/shard_map/ppermute | solution.py:577
  775.4 8.7 collective-permute-done.54
  808.8 7.6 gate_up_back.3
  816.4 10.7 gate_up_in.3.refs_0_
  837.1 8.9 collective-permute-done.60
  849.5 7.9 collective-permute-done.62.refs_2_
  857.4 16.0 %collective-permute-done.61.refs_1_ = bf16[128,2048]{1,0:T(8,128)(2,1)} collective-permute-done((bf16[128,2048]{1,0:T(8,128)(2,1)}, bf16[128,2048]{1,0:T(8,128)(2,1)}, u32[]{:S(2)}, u32[]{:S(2)}) %collective-permute-start.61) | collective-permute-done | bytes 524320 | tf_op jit(solution)/shard_map/ppermute | solution.py:593
  895.7 10.7 collective-permute-done.66
  910.2 6.7 collective-permute-done.68
  916.9 8.5 collective-permute-done.67
  927.0 7.2 collective-permute-done.70.refs_1_
  937.6 10.3 attend_back.6
  959.5 30.6 %collective-permute-done.72.refs_1_ = bf16[1408,512]{1,0:T(8,128)(2,1)S(1)} collective-permute-done((bf16[1408,512]{1,0:T(8,128)(2,1)}, bf16[1408,512]{1,0:T(8,128)(2,1)S(1)}, u32[]{:S(2)}, u32[]{:S(2)}) %collective-permute-start.72) | collective-permute-done | bytes 1441824 | tf_op jit(solution)/shard_map/ppermute | solution.py:553
  990.2 9.4 attend_back.7
  999.6 9.0 collective-permute-done.73.refs_0_
  1038.7 7.9 collective-permute-done.76
  1056.3 11.5 collective-permute-done.80.refs_1_
  1068.1 9.0 collective-permute-done.77.refs_1_
  1087.3 6.8 collective-permute-done.89
  1095.8 6.8 collective-permute-done.82.refs_3_
  1104.2 9.2 finish_gate_up.2.refs_4_
  1113.4 9.2 finish_gate_up.3
  (634 shorter events, 469.8 us)
Async XLA Ops:
  7.2 56.9 %all-gather.22.cloned.1.call-start = ((), (), s32[]{:S(2)}) async-start(), calls=%async_computation.13 | async-start | bytes 7864320 | tf_op jit(solution)/shard_map/all_gather | solution.py:635
  10.0 112.5 %all-gather.20.cloned.1.call-start = ((), (), s32[]{:S(2)}) async-start(), calls=%async_computation.6 | async-start | bytes 2621440 | tf_op jit(solution)/shard_map/all_gather | solution.py:635
  10.9 156.6 %all-gather.24.cloned.1.call-start = ((), (), s32[]{:S(2)}) async-start(), calls=%async_computation.14 | async-start | bytes 7208960 | tf_op jit(solution)/shard_map/all_gather | solution.py:635
  16.1 195.6 %all-gather.26.cloned.1.call-start = ((), (), s32[]{:S(2)}) async-start(), calls=%async_computation.15 | async-start | bytes 7208960 | tf_op jit(solution)/shard_map/all_gather | solution.py:635
  16.7 203.3 %all-gather.28.cloned.1.call-start = ((), (), s32[]{:S(2)}) async-start(), calls=%async_computation.16 | async-start | bytes 7208960 | tf_op jit(solution)/shard_map/all_gather | solution.py:635
  20.2 28.2 %collective-permute-start = (bf16[128,2048]{1,0:T(8,128)(2,1)S(1)}, bf16[128,2048]{1,0:T(8,128)(2,1)}, u32[]{:S(2)}, u32[]{:S(2)}) collective-permute-start(bf16[128,2048]{1,0:T(8,128)(2,1)S(1)} %get-tuple-element.464), channel_id=1, source_target_pairs={{0,2},{2,0},{1,3},{3,1},{4,6},{6,4},{5,7},{7,5},{8,10},{10,8},{9,1... | collective-permute-start | bytes 1572872 | tf_op jit(solution)/shard_map/ppermute | solution.py:577
  24.2 28.1 %collective-permute-start.2 = (bf16[128,2048]{1,0:T(8,128)(2,1)S(1)}, bf16[128,2048]{1,0:T(8,128)(2,1)S(1)}, u32[]{:S(2)}, u32[]{:S(2)}) collective-permute-start(bf16[128,2048]{1,0:T(8,128)(2,1)S(1)} %get-tuple-element.464), channel_id=1, source_target_pairs={{1,0},{2,1},{3,2},{5,4},{6,5},{7,6},{9,8},{10,9},{11,10},{13,12},{... | collective-permute-start | bytes 1572872 | tf_op jit(solution)/shard_map/ppermute | solution.py:577
  25.5 26.8 %collective-permute-start.3 = (bf16[128,2048]{1,0:T(8,128)(2,1)S(1)}, bf16[128,2048]{1,0:T(8,128)(2,1)S(1)}, u32[]{:S(2)}, u32[]{:S(2)}) collective-permute-start(bf16[128,2048]{1,0:T(8,128)(2,1)S(1)} %get-tuple-element.464), channel_id=1, source_target_pairs={{0,1},{1,2},{2,3},{4,5},{5,6},{6,7},{8,9},{9,10},{10,11},{12,13},{... | collective-permute-start | bytes 1572872 | tf_op jit(solution)/shard_map/ppermute | solution.py:577
  64.1 222.9 %all-gather.30.cloned.1.call-start = ((), (), s32[]{:S(2)}) async-start(), calls=%async_computation.17 | async-start | bytes 7864320 | tf_op jit(solution)/shard_map/all_gather | solution.py:635
  71.6 27.3 %collective-permute-start.5 = (bf16[128,2048]{1,0:T(8,128)(2,1)}, bf16[128,2048]{1,0:T(8,128)(2,1)}, u32[]{:S(2)}, u32[]{:S(2)}) collective-permute-start(bf16[128,2048]{1,0:T(8,128)(2,1)} %bitcast.4), channel_id=1, source_target_pairs={{0,2},{2,0},{1,3},{3,1},{4,6},{6,4},{5,7},{7,5},{8,10},{10,8},{9,1... | collective-permute-start | bytes 1572872 | tf_op jit(solution)/shard_map/ppermute | solution.py:577
  74.2 48.3 %collective-permute-start.7 = (bf16[128,2048]{1,0:T(8,128)(2,1)}, bf16[128,2048]{1,0:T(8,128)(2,1)}, u32[]{:S(2)}, u32[]{:S(2)}) collective-permute-start(bf16[128,2048]{1,0:T(8,128)(2,1)} %bitcast.4), channel_id=1, source_target_pairs={{1,0},{2,1},{3,2},{5,4},{6,5},{7,6},{9,8},{10,9},{11,10},{13,12},{... | collective-permute-start | bytes 1572872 | tf_op jit(solution)/shard_map/ppermute | solution.py:577
  75.5 47.0 %collective-permute-start.8 = (bf16[128,2048]{1,0:T(8,128)(2,1)}, bf16[128,2048]{1,0:T(8,128)(2,1)}, u32[]{:S(2)}, u32[]{:S(2)}) collective-permute-start(bf16[128,2048]{1,0:T(8,128)(2,1)} %bitcast.4), channel_id=1, source_target_pairs={{0,1},{1,2},{2,3},{4,5},{5,6},{6,7},{8,9},{9,10},{10,11},{12,13},{... | collective-permute-start | bytes 1572872 | tf_op jit(solution)/shard_map/ppermute | solution.py:577
  81.4 24.3 %collective-permute-start.4 = (bf16[1024,512]{1,0:T(8,128)(2,1)S(1)}, bf16[1024,512]{1,0:T(8,128)(2,1)S(1)}, u32[]{:S(2)}, u32[]{:S(2)}) collective-permute-start(bf16[1024,512]{1,0:T(8,128)(2,1)S(1)} %get-tuple-element.209.key_ref.value_ref.refs_1_.refs_2_), channel_id=1, source_target_pairs={{0,4},{1,5},{2,6},{3,7},{8,12},{9,13},{10,14},{11,15},{16,20},{17,... | collective-permute-start | bytes 3145736 | tf_op jit(solution)/shard_map/ppermute | solution.py:621
  173.9 24.6 %collective-permute-start.15 = (bf16[128,2048]{1,0:T(8,128)(2,1)}, bf16[128,2048]{1,0:T(8,128)(2,1)}, u32[]{:S(2)}, u32[]{:S(2)}) collective-permute-start(bf16[128,2048]{1,0:T(8,128)(2,1)} %get-tuple-element.417), channel_id=1, source_target_pairs={{1,0},{2,1},{3,2},{5,4},{6,5},{7,6},{9,8},{10,9},{11,10},{13,12},{... | collective-permute-start | bytes 1572872 | tf_op jit(solution)/shard_map/ppermute | solution.py:577
  220.0 116.1 %all-gather.32.cloned.1.call-start = ((), (), s32[]{:S(2)}) async-start(), calls=%async_computation.18 | async-start | bytes 2621440 | tf_op jit(solution)/shard_map/all_gather | solution.py:635
  235.8 102.4 %all-gather.34.cloned.1.call-start = ((), (), s32[]{:S(2)}) async-start(), calls=%async_computation.19 | async-start | bytes 7208960 | tf_op jit(solution)/shard_map/all_gather | solution.py:635
  236.5 154.8 %all-gather.36.cloned.1.call-start = ((), (), s32[]{:S(2)}) async-start(), calls=%async_computation.20 | async-start | bytes 7208960 | tf_op jit(solution)/shard_map/all_gather | solution.py:635
  247.5 25.1 %collective-permute-start.20 = (bf16[128,2048]{1,0:T(8,128)(2,1)S(1)}, bf16[128,2048]{1,0:T(8,128)(2,1)S(1)}, u32[]{:S(2)}, u32[]{:S(2)}) collective-permute-start(bf16[128,2048]{1,0:T(8,128)(2,1)S(1)} %get-tuple-element.459), channel_id=1, source_target_pairs={{3,2},{2,1},{1,0},{7,6},{6,5},{5,4},{11,10},{10,9},{9,8},{15,14},{... | collective-permute-start | bytes 1572872 | tf_op jit(solution)/shard_map/ppermute | solution.py:593
  259.9 25.8 %collective-permute-start.18 = (bf16[128,2048]{1,0:T(8,128)(2,1)S(1)}, bf16[128,2048]{1,0:T(8,128)(2,1)S(1)}, u32[]{:S(2)}, u32[]{:S(2)}) collective-permute-start(bf16[128,2048]{1,0:T(8,128)(2,1)S(1)} %add_convert_fusion.9), channel_id=1, source_target_pairs={{0,2},{2,0},{1,3},{3,1},{4,6},{6,4},{5,7},{7,5},{8,10},{10,8},{9,1... | collective-permute-start | bytes 1572872 | tf_op jit(solution)/shard_map/ppermute | solution.py:593
  287.0 149.6 %all-gather.38.cloned.1.call-start = ((), (), s32[]{:S(2)}) async-start(), calls=%async_computation.21 | async-start | bytes 7208960 | tf_op jit(solution)/shard_map/all_gather | solution.py:635
  293.2 27.3 %collective-permute-start.21 = (bf16[128,2048]{1,0:T(8,128)(2,1)}, bf16[128,2048]{1,0:T(8,128)(2,1)}, u32[]{:S(2)}, u32[]{:S(2)}) collective-permute-start(bf16[128,2048]{1,0:T(8,128)(2,1)} %get-tuple-element.415), channel_id=1, source_target_pairs={{0,2},{2,0},{1,3},{3,1},{4,6},{6,4},{5,7},{7,5},{8,10},{10,8},{9,1... | collective-permute-start | bytes 1572872 | tf_op jit(solution)/shard_map/ppermute | solution.py:577
  293.2 29.8 %collective-permute-start.23 = (bf16[128,2048]{1,0:T(8,128)(2,1)}, bf16[128,2048]{1,0:T(8,128)(2,1)}, u32[]{:S(2)}, u32[]{:S(2)}) collective-permute-start(bf16[128,2048]{1,0:T(8,128)(2,1)} %get-tuple-element.415), channel_id=1, source_target_pairs={{1,0},{2,1},{3,2},{5,4},{6,5},{7,6},{9,8},{10,9},{11,10},{13,12},{... | collective-permute-start | bytes 1572872 | tf_op jit(solution)/shard_map/ppermute | solution.py:577
  294.5 28.5 %collective-permute-start.24 = (bf16[128,2048]{1,0:T(8,128)(2,1)}, bf16[128,2048]{1,0:T(8,128)(2,1)}, u32[]{:S(2)}, u32[]{:S(2)}) collective-permute-start(bf16[128,2048]{1,0:T(8,128)(2,1)} %get-tuple-element.415), channel_id=1, source_target_pairs={{0,1},{1,2},{2,3},{4,5},{5,6},{6,7},{8,9},{9,10},{10,11},{12,13},{... | collective-permute-start | bytes 1572872 | tf_op jit(solution)/shard_map/ppermute | solution.py:577
  338.2 345.1 %reduce-scatter.7.cloned.1.call-start = ((), (), s32[]{:S(2)}) async-start(), calls=%async_computation.7 | async-start | bytes 7208960 | tf_op jit(solution)/shard_map/reduce_scatter | solution.py:639
  348.3 26.1 %collective-permute-start.25 = (bf16[1024,512]{1,0:T(8,128)(2,1)S(1)}, bf16[1024,512]{1,0:T(8,128)(2,1)S(1)}, u32[]{:S(2)}, u32[]{:S(2)}) collective-permute-start(bf16[1024,512]{1,0:T(8,128)(2,1)S(1)} %get-tuple-element.242.key_ref.value_ref.refs_1_.refs_2_), channel_id=1, source_target_pairs={{0,4},{1,5},{2,6},{3,7},{8,12},{9,13},{10,14},{11,15},{16,20},{17,... | collective-permute-start | bytes 3145736 | tf_op jit(solution)/shard_map/ppermute | solution.py:621
  398.7 25.0 %collective-permute-start.29 = (bf16[128,2048]{1,0:T(8,128)(2,1)S(1)}, bf16[128,2048]{1,0:T(8,128)(2,1)S(1)}, u32[]{:S(2)}, u32[]{:S(2)}) collective-permute-start(bf16[128,2048]{1,0:T(8,128)(2,1)S(1)} %get-tuple-element.456), channel_id=1, source_target_pairs={{3,2},{2,1},{1,0},{7,6},{6,5},{5,4},{11,10},{10,9},{9,8},{15,14},{... | collective-permute-start | bytes 1572872 | tf_op jit(solution)/shard_map/ppermute | solution.py:593
  411.1 24.0 %collective-permute-start.27 = (bf16[128,2048]{1,0:T(8,128)(2,1)S(1)}, bf16[128,2048]{1,0:T(8,128)(2,1)S(1)}, u32[]{:S(2)}, u32[]{:S(2)}) collective-permute-start(bf16[128,2048]{1,0:T(8,128)(2,1)S(1)} %add_convert_fusion.7), channel_id=1, source_target_pairs={{0,2},{2,0},{1,3},{3,1},{4,6},{6,4},{5,7},{7,5},{8,10},{10,8},{9,1... | collective-permute-start | bytes 1572872 | tf_op jit(solution)/shard_map/ppermute | solution.py:593
  441.9 26.9 %collective-permute-start.30 = (bf16[128,2048]{1,0:T(8,128)(2,1)S(1)}, bf16[128,2048]{1,0:T(8,128)(2,1)S(1)}, u32[]{:S(2)}, u32[]{:S(2)}) collective-permute-start(bf16[128,2048]{1,0:T(8,128)(2,1)S(1)} %get-tuple-element.413), channel_id=1, source_target_pairs={{0,2},{2,0},{1,3},{3,1},{4,6},{6,4},{5,7},{7,5},{8,10},{10,8},{9,1... | collective-permute-start | bytes 1572872 | tf_op jit(solution)/shard_map/ppermute | solution.py:577
  442.1 28.2 %collective-permute-start.32 = (bf16[128,2048]{1,0:T(8,128)(2,1)S(1)}, bf16[128,2048]{1,0:T(8,128)(2,1)S(1)}, u32[]{:S(2)}, u32[]{:S(2)}) collective-permute-start(bf16[128,2048]{1,0:T(8,128)(2,1)S(1)} %get-tuple-element.413), channel_id=1, source_target_pairs={{1,0},{2,1},{3,2},{5,4},{6,5},{7,6},{9,8},{10,9},{11,10},{13,12},{... | collective-permute-start | bytes 1572872 | tf_op jit(solution)/shard_map/ppermute | solution.py:577
  443.4 26.9 %collective-permute-start.33 = (bf16[128,2048]{1,0:T(8,128)(2,1)S(1)}, bf16[128,2048]{1,0:T(8,128)(2,1)S(1)}, u32[]{:S(2)}, u32[]{:S(2)}) collective-permute-start(bf16[128,2048]{1,0:T(8,128)(2,1)S(1)} %get-tuple-element.413), channel_id=1, source_target_pairs={{0,1},{1,2},{2,3},{4,5},{5,6},{6,7},{8,9},{9,10},{10,11},{12,13},{... | collective-permute-start | bytes 1572872 | tf_op jit(solution)/shard_map/ppermute | solution.py:577
  526.5 30.2 %collective-permute-start.35 = (bf16[128,2048]{1,0:T(8,128)(2,1)}, bf16[128,2048]{1,0:T(8,128)(2,1)}, u32[]{:S(2)}, u32[]{:S(2)}) collective-permute-start(bf16[128,2048]{1,0:T(8,128)(2,1)} %add_convert_fusion.5), channel_id=1, source_target_pairs={{0,2},{2,0},{1,3},{3,1},{4,6},{6,4},{5,7},{7,5},{8,10},{10,8},{9,1... | collective-permute-start | bytes 1572872 | tf_op jit(solution)/shard_map/ppermute | solution.py:593
  569.0 176.3 %reduce-scatter.9.cloned.1.call-start = ((), (), s32[]{:S(2)}) async-start(), calls=%async_computation.8 | async-start | bytes 7208960 | tf_op jit(solution)/shard_map/reduce_scatter | solution.py:639
  577.4 208.3 %reduce-scatter.11.cloned.1.call-start = ((), (), s32[]{:S(2)}) async-start(), calls=%async_computation.9 | async-start | bytes 7208960 | tf_op jit(solution)/shard_map/reduce_scatter | solution.py:639
  578.7 26.7 %collective-permute-start.40 = (bf16[128,2048]{1,0:T(8,128)(2,1)}, bf16[128,2048]{1,0:T(8,128)(2,1)S(1)}, u32[]{:S(2)}, u32[]{:S(2)}) collective-permute-start(bf16[128,2048]{1,0:T(8,128)(2,1)} %copy-done.31), channel_id=1, source_target_pairs={{1,0},{2,1},{3,2},{5,4},{6,5},{7,6},{9,8},{10,9},{11,10},{13,12},{... | collective-permute-start | bytes 1572872 | tf_op jit(solution)/shard_map/ppermute | solution.py:577
  580.0 25.4 %collective-permute-start.41 = (bf16[128,2048]{1,0:T(8,128)(2,1)}, bf16[128,2048]{1,0:T(8,128)(2,1)S(1)}, u32[]{:S(2)}, u32[]{:S(2)}) collective-permute-start(bf16[128,2048]{1,0:T(8,128)(2,1)} %copy-done.31), channel_id=1, source_target_pairs={{0,1},{1,2},{2,3},{4,5},{5,6},{6,7},{8,9},{9,10},{10,11},{12,13},{... | collective-permute-start | bytes 1572872 | tf_op jit(solution)/shard_map/ppermute | solution.py:577
  615.5 38.6 %collective-permute-start.45 = (bf16[128,2048]{1,0:T(8,128)(2,1)}, bf16[128,2048]{1,0:T(8,128)(2,1)S(1)}, u32[]{:S(2)}, u32[]{:S(2)}) collective-permute-start(bf16[128,2048]{1,0:T(8,128)(2,1)} %get-tuple-element.450), channel_id=1, source_target_pairs={{3,2},{2,1},{1,0},{7,6},{6,5},{5,4},{11,10},{10,9},{9,8},{15,14},{... | collective-permute-start | bytes 1572872 | tf_op jit(solution)/shard_map/ppermute | solution.py:593
  616.9 37.2 %collective-permute-start.44 = (bf16[128,2048]{1,0:T(8,128)(2,1)}, bf16[128,2048]{1,0:T(8,128)(2,1)}, u32[]{:S(2)}, u32[]{:S(2)}) collective-permute-start(bf16[128,2048]{1,0:T(8,128)(2,1)} %get-tuple-element.449), channel_id=1, source_target_pairs={{0,1},{1,2},{2,3},{4,5},{5,6},{6,7},{8,9},{9,10},{10,11},{12,13},{... | collective-permute-start | bytes 1572872 | tf_op jit(solution)/shard_map/ppermute | solution.py:593
  636.7 33.5 %collective-permute-start.46 = (bf16[1024,512]{1,0:T(8,128)(2,1)S(1)}, bf16[1024,512]{1,0:T(8,128)(2,1)S(1)}, u32[]{:S(2)}, u32[]{:S(2)}) collective-permute-start(bf16[1024,512]{1,0:T(8,128)(2,1)S(1)} %get-tuple-element.273), channel_id=1, source_target_pairs={{4,0},{5,1},{6,2},{7,3},{12,8},{13,9},{14,10},{15,11},{20,16},{21,... | collective-permute-start | bytes 3145736 | tf_op jit(solution)/shard_map/ppermute | solution.py:628
  678.7 207.0 %reduce-scatter.13.cloned.1.call-start = ((), (), s32[]{:S(2)}) async-start(), calls=%async_computation.10 | async-start | bytes 7208960 | tf_op jit(solution)/shard_map/reduce_scatter | solution.py:639
  693.8 43.1 %collective-permute-start.51 = (bf16[1408,512]{1,0:T(8,128)(2,1)}, bf16[1408,512]{1,0:T(8,128)(2,1)}, u32[]{:S(2)}, u32[]{:S(2)}) collective-permute-start(bf16[1408,512]{1,0:T(8,128)(2,1)} %reduce-scatter.7.cloned.1.call-done.refs_0_), channel_id=1, source_target_pairs={{0,4},{4,0},{1,5},{5,1},{2,6},{6,2},{3,7},{7,3},{8,12},{12,8},{9,1... | collective-permute-start | bytes 4325384 | tf_op jit(solution)/shard_map/ppermute | solution.py:553
  707.1 29.8 %collective-permute-start.48 = (bf16[128,2048]{1,0:T(8,128)(2,1)}, bf16[128,2048]{1,0:T(8,128)(2,1)}, u32[]{:S(2)}, u32[]{:S(2)}) collective-permute-start(bf16[128,2048]{1,0:T(8,128)(2,1)} %add_convert_fusion.2), channel_id=1, source_target_pairs={{0,2},{2,0},{1,3},{3,1},{4,6},{6,4},{5,7},{7,5},{8,10},{10,8},{9,1... | collective-permute-start | bytes 1572872 | tf_op jit(solution)/shard_map/ppermute | solution.py:593
  745.3 40.5 %collective-permute-start.58 = (bf16[1024,1536]{1,0:T(8,128)(2,1)}, bf16[1024,1536]{1,0:T(8,128)(2,1)}, u32[]{:S(2)}, u32[]{:S(2)}) collective-permute-start(bf16[1024,1536]{1,0:T(8,128)(2,1)} %copy-done.46), channel_id=1, source_target_pairs={{0,8},{8,0},{16,24},{24,16},{1,9},{9,1},{17,25},{25,17},{2,10},{10... | collective-permute-start | bytes 9437192 | tf_op jit(solution)/shard_map/ppermute | solution.py:553
  745.3 40.4 %collective-permute-start.57 = (bf16[512,1408]{1,0:T(8,128)(2,1)}, bf16[512,1408]{1,0:T(8,128)(2,1)}, u32[]{:S(2)}, u32[]{:S(2)}) collective-permute-start(bf16[512,1408]{1,0:T(8,128)(2,1)} %reduce-scatter.9.cloned.1.call-done.refs_0_), channel_id=1, source_target_pairs={{0,4},{4,0},{1,5},{5,1},{2,6},{6,2},{3,7},{7,3},{8,12},{12,8},{9,1... | collective-permute-start | bytes 4325384 | tf_op jit(solution)/shard_map/ppermute | solution.py:553
  745.4 29.4 %collective-permute-start.55 = (bf16[128,2048]{1,0:T(8,128)(2,1)}, bf16[128,2048]{1,0:T(8,128)(2,1)S(1)}, u32[]{:S(2)}, u32[]{:S(2)}) collective-permute-start(bf16[128,2048]{1,0:T(8,128)(2,1)} %copy-done.33), channel_id=1, source_target_pairs={{1,0},{2,1},{3,2},{5,4},{6,5},{7,6},{9,8},{10,9},{11,10},{13,12},{... | collective-permute-start | bytes 1572872 | tf_op jit(solution)/shard_map/ppermute | solution.py:577
  746.7 28.6 %collective-permute-start.56 = (bf16[128,2048]{1,0:T(8,128)(2,1)}, bf16[128,2048]{1,0:T(8,128)(2,1)S(1)}, u32[]{:S(2)}, u32[]{:S(2)}) collective-permute-start(bf16[128,2048]{1,0:T(8,128)(2,1)} %copy-done.33), channel_id=1, source_target_pairs={{0,1},{1,2},{2,3},{4,5},{5,6},{6,7},{8,9},{9,10},{10,11},{12,13},{... | collective-permute-start | bytes 1572872 | tf_op jit(solution)/shard_map/ppermute | solution.py:577
  797.2 220.4 %reduce-scatter.15.cloned.1.call-start = ((), (), s32[]{:S(2)}) async-start(), calls=%async_computation.11 | async-start | bytes 7208960 | tf_op jit(solution)/shard_map/reduce_scatter | solution.py:639
  806.1 67.3 %collective-permute-start.65 = (bf16[512,1536]{1,0:T(8,128)(2,1)}, bf16[512,1536]{1,0:T(8,128)(2,1)}, u32[]{:S(2)}, u32[]{:S(2)}) collective-permute-start(bf16[512,1536]{1,0:T(8,128)(2,1)} %split.61), channel_id=1, source_target_pairs={{0,16},{8,24},{16,0},{24,8},{1,17},{9,25},{17,1},{25,9},{2,18},{10... | collective-permute-start | bytes 4718600 | tf_op jit(solution)/shard_map/ppermute | solution.py:553
  833.8 39.6 %collective-permute-start.64 = (bf16[512,1408]{1,0:T(8,128)(2,1)}, bf16[512,1408]{1,0:T(8,128)(2,1)}, u32[]{:S(2)}, u32[]{:S(2)}) collective-permute-start(bf16[512,1408]{1,0:T(8,128)(2,1)} %reduce-scatter.11.cloned.1.call-done.refs_2_), channel_id=1, source_target_pairs={{0,4},{4,0},{1,5},{5,1},{2,6},{6,2},{3,7},{7,3},{8,12},{12,8},{9,1... | collective-permute-start | bytes 4325384 | tf_op jit(solution)/shard_map/ppermute | solution.py:553
  847.0 26.4 %collective-permute-start.61 = (bf16[128,2048]{1,0:T(8,128)(2,1)}, bf16[128,2048]{1,0:T(8,128)(2,1)}, u32[]{:S(2)}, u32[]{:S(2)}) collective-permute-start(bf16[128,2048]{1,0:T(8,128)(2,1)} %add_convert_fusion.1), channel_id=1, source_target_pairs={{0,2},{2,0},{1,3},{3,1},{4,6},{6,4},{5,7},{7,5},{8,10},{10,8},{9,1... | collective-permute-start | bytes 1572872 | tf_op jit(solution)/shard_map/ppermute | solution.py:593
  885.6 163.0 %reduce-scatter.17.cloned.1.call-start = ((), (), s32[]{:S(2)}) async-start(), calls=%async_computation.12 | async-start | bytes 7208960 | tf_op jit(solution)/shard_map/reduce_scatter | solution.py:639
  888.8 46.2 %collective-permute-start.71 = (bf16[512,1536]{1,0:T(8,128)(2,1)S(1)}, bf16[512,1536]{1,0:T(8,128)(2,1)S(1)}, u32[]{:S(2)}, u32[]{:S(2)}) collective-permute-start(bf16[512,1536]{1,0:T(8,128)(2,1)S(1)} %fusion.1.refs_0_), channel_id=1, source_target_pairs={{0,4},{4,0},{1,5},{5,1},{2,6},{6,2},{3,7},{7,3},{8,12},{12,8},{9,1... | collective-permute-start | bytes 4718600 | tf_op jit(solution)/shard_map/ppermute | solution.py:553
  889.8 27.1 %collective-permute-start.68 = (bf16[128,2048]{1,0:T(8,128)(2,1)}, bf16[128,2048]{1,0:T(8,128)(2,1)S(1)}, u32[]{:S(2)}, u32[]{:S(2)}) collective-permute-start(bf16[128,2048]{1,0:T(8,128)(2,1)} %get-tuple-element.318), channel_id=1, source_target_pairs={{1,0},{2,1},{3,2},{5,4},{6,5},{7,6},{9,8},{10,9},{11,10},{13,12},{... | collective-permute-start | bytes 1572872 | tf_op jit(solution)/shard_map/ppermute | solution.py:577
  891.1 25.8 %collective-permute-start.69 = (bf16[128,2048]{1,0:T(8,128)(2,1)}, bf16[128,2048]{1,0:T(8,128)(2,1)S(1)}, u32[]{:S(2)}, u32[]{:S(2)}) collective-permute-start(bf16[128,2048]{1,0:T(8,128)(2,1)} %get-tuple-element.318), channel_id=1, source_target_pairs={{0,1},{1,2},{2,3},{4,5},{5,6},{6,7},{8,9},{9,10},{10,11},{12,13},{... | collective-permute-start | bytes 1572872 | tf_op jit(solution)/shard_map/ppermute | solution.py:577
  908.9 25.3 %collective-permute-start.70 = (bf16[512,512]{1,0:T(8,128)(2,1)S(1)}, bf16[512,512]{1,0:T(8,128)(2,1)S(1)}, u32[]{:S(2)}, u32[]{:S(2)}) collective-permute-start(bf16[512,512]{1,0:T(8,128)(2,1)S(1)} %fusion.8.refs_0_), channel_id=1, source_target_pairs={{0,4},{4,0},{1,5},{5,1},{2,6},{6,2},{3,7},{7,3},{8,12},{12,8},{9,1... | collective-permute-start | bytes 1572872 | tf_op jit(solution)/shard_map/ppermute | solution.py:553
  955.3 34.8 %collective-permute-start.72 = (bf16[1408,512]{1,0:T(8,128)(2,1)}, bf16[1408,512]{1,0:T(8,128)(2,1)S(1)}, u32[]{:S(2)}, u32[]{:S(2)}) collective-permute-start(bf16[1408,512]{1,0:T(8,128)(2,1)} %reduce-scatter.13.cloned.1.call-done.refs_0_), channel_id=1, source_target_pairs={{0,4},{4,0},{1,5},{5,1},{2,6},{6,2},{3,7},{7,3},{8,12},{12,8},{9,1... | collective-permute-start | bytes 4325384 | tf_op jit(solution)/shard_map/ppermute | solution.py:553
  957.7 50.9 %collective-permute-start.73 = (bf16[1024,512]{1,0:T(8,128)(2,1)S(1)}, bf16[1024,512]{1,0:T(8,128)(2,1)S(1)}, u32[]{:S(2)}, u32[]{:S(2)}) collective-permute-start(bf16[1024,512]{1,0:T(8,128)(2,1)S(1)} %copy-done.68), channel_id=1, source_target_pairs={{4,0},{5,1},{6,2},{7,3},{12,8},{13,9},{14,10},{15,11},{20,16},{21,... | collective-permute-start | bytes 3145736 | tf_op jit(solution)/shard_map/ppermute | solution.py:628
  1029.7 38.4 %collective-permute-start.81 = (bf16[512,1536]{1,0:T(8,128)(2,1)}, bf16[512,1536]{1,0:T(8,128)(2,1)}, u32[]{:S(2)}, u32[]{:S(2)}) collective-permute-start(bf16[512,1536]{1,0:T(8,128)(2,1)} %split.60), channel_id=1, source_target_pairs={{0,16},{8,24},{16,0},{24,8},{1,17},{9,25},{17,1},{25,9},{2,18},{10... | collective-permute-start | bytes 4718600 | tf_op jit(solution)/shard_map/ppermute | solution.py:553
  1034.9 32.9 %collective-permute-start.80 = (bf16[512,1408]{1,0:T(8,128)(2,1)}, bf16[512,1408]{1,0:T(8,128)(2,1)}, u32[]{:S(2)}, u32[]{:S(2)}) collective-permute-start(bf16[512,1408]{1,0:T(8,128)(2,1)} %reduce-scatter.15.cloned.1.call-done.refs_0_), channel_id=1, source_target_pairs={{0,4},{4,0},{1,5},{5,1},{2,6},{6,2},{3,7},{7,3},{8,12},{12,8},{9,1... | collective-permute-start | bytes 4325384 | tf_op jit(solution)/shard_map/ppermute | solution.py:553
  1035.0 33.0 %collective-permute-start.78 = (bf16[128,2048]{1,0:T(8,128)(2,1)}, bf16[128,2048]{1,0:T(8,128)(2,1)}, u32[]{:S(2)}, u32[]{:S(2)}) collective-permute-start(bf16[128,2048]{1,0:T(8,128)(2,1)} %get-tuple-element.433), channel_id=1, source_target_pairs={{0,1},{1,2},{2,3},{4,5},{5,6},{6,7},{8,9},{9,10},{10,11},{12,13},{... | collective-permute-start | bytes 1572872 | tf_op jit(solution)/shard_map/ppermute | solution.py:593
  1037.1 30.9 %collective-permute-start.79 = (bf16[128,2048]{1,0:T(8,128)(2,1)}, bf16[128,2048]{1,0:T(8,128)(2,1)}, u32[]{:S(2)}, u32[]{:S(2)}) collective-permute-start(bf16[128,2048]{1,0:T(8,128)(2,1)} %get-tuple-element.431), channel_id=1, source_target_pairs={{3,2},{2,1},{1,0},{7,6},{6,5},{5,4},{11,10},{10,9},{9,8},{15,14},{... | collective-permute-start | bytes 1572872 | tf_op jit(solution)/shard_map/ppermute | solution.py:593
  1048.6 28.4 %collective-permute-start.77 = (bf16[128,2048]{1,0:T(8,128)(2,1)}, bf16[128,2048]{1,0:T(8,128)(2,1)}, u32[]{:S(2)}, u32[]{:S(2)}) collective-permute-start(bf16[128,2048]{1,0:T(8,128)(2,1)} %add_convert_fusion), channel_id=1, source_target_pairs={{0,2},{2,0},{1,3},{3,1},{4,6},{6,4},{5,7},{7,5},{8,10},{10,8},{9,1... | collective-permute-start | bytes 1572872 | tf_op jit(solution)/shard_map/ppermute | solution.py:593
  1067.8 34.8 %collective-permute-start.82 = (bf16[512,1408]{1,0:T(8,128)(2,1)}, bf16[512,1408]{1,0:T(8,128)(2,1)}, u32[]{:S(2)}, u32[]{:S(2)}) collective-permute-start(bf16[512,1408]{1,0:T(8,128)(2,1)} %reduce-scatter.17.cloned.1.call-done.refs_2_), channel_id=1, source_target_pairs={{0,4},{4,0},{1,5},{5,1},{2,6},{6,2},{3,7},{7,3},{8,12},{12,8},{9,1... | collective-permute-start | bytes 4325384 | tf_op jit(solution)/shard_map/ppermute | solution.py:553
  1085.6 66.5 %collective-permute-start.88 = (bf16[512,1536]{1,0:T(8,128)(2,1)S(1)}, bf16[512,1536]{1,0:T(8,128)(2,1)}, u32[]{:S(2)}, u32[]{:S(2)}) collective-permute-start(bf16[512,1536]{1,0:T(8,128)(2,1)S(1)} %fusion.refs_0_), channel_id=1, source_target_pairs={{0,4},{4,0},{1,5},{5,1},{2,6},{6,2},{3,7},{7,3},{8,12},{12,8},{9,1... | collective-permute-start | bytes 4718600 | tf_op jit(solution)/shard_map/ppermute | solution.py:553
  1094.3 51.1 %collective-permute-start.90 = (bf16[512,512]{1,0:T(8,128)(2,1)S(1)}, bf16[512,512]{1,0:T(8,128)(2,1)}, u32[]{:S(2)}, u32[]{:S(2)}) collective-permute-start(bf16[512,512]{1,0:T(8,128)(2,1)S(1)} %fusion.7.refs_0_), channel_id=1, source_target_pairs={{0,4},{4,0},{1,5},{5,1},{2,6},{6,2},{3,7},{7,3},{8,12},{12,8},{9,1... | collective-permute-start | bytes 1572872 | tf_op jit(solution)/shard_map/ppermute | solution.py:553
  (179 other events, 3103.0 us)
Sparse Core Ops, SparseCore 0:
  10.2 49.0 all-gather.21
  61.4 22.5 all-gather.19
  86.2 43.4 all-gather.23
  131.7 43.3 all-gather.25
  176.5 43.3 all-gather.27
  222.0 46.3 all-gather.29
  270.5 22.5 all-gather.31
  294.7 43.3 all-gather.33
  339.7 43.3 all-gather.35
  385.1 43.3 all-gather.37
  569.1 53.3 reduce-scatter.6
  625.6 54.8 reduce-scatter.8
  683.6 55.4 reduce-scatter.10
  797.3 76.5 reduce-scatter.12
  885.8 52.0 reduce-scatter.14
  955.4 53.6 reduce-scatter.16

commit v7 on v4

--- a/solution.py
+++ b/solution.py
@@ -332,88 +332,66 @@
     return out, sums[:, 0]
 
 
-def attend_near_kernel(qpos_ref, kpos_ref, q_ref, key_ref, value_ref, acc_ref, top_ref, total_ref):
-    allowed = kpos_ref[0] <= qpos_ref[...]
-    for half in range(PAIR // HD):
-        lanes = slice(half * HD, (half + 1) * HD)
-        q = q_ref[:, lanes] * jnp.asarray(HD**-0.5, LOW)
-        s = jnp.where(allowed, dot(q, key_ref[:, lanes], NT), MASKED)
-        top = jnp.max(s, axis=1, keepdims=True)
-        p = jnp.exp(s - top)
-        top_ref[half] = top
-        total_ref[half] = jnp.sum(p, axis=1, keepdims=True)
-        acc_ref[:, lanes] = dot(p.astype(LOW), value_ref[:, lanes], NN)
-
-
-def attend_far_kernel(blocks, qpos_ref, kpos_ref, q_ref, acc_in_ref, top_in_ref, total_in_ref, *refs):
+GROUP = 256
+
+
+def attend_kernel(blocks, qpos_ref, kpos_ref, q_ref, *refs):
     keys, values = refs[: 2 * blocks : 2], refs[1 : 2 * blocks : 2]
     out_ref, lse_ref = refs[2 * blocks :]
     allowed = [kpos_ref[b] <= qpos_ref[...] for b in range(blocks)]
-    for half in range(PAIR // HD):
+    for half in range(q_ref.shape[1] // HD):
         lanes = slice(half * HD, (half + 1) * HD)
         q = q_ref[:, lanes] * jnp.asarray(HD**-0.5, LOW)
-        top, total, acc = top_in_ref[half], total_in_ref[half], acc_in_ref[:, lanes]
+        top, total, acc = None, None, None
         for b in range(blocks):
             s = jnp.where(allowed[b], dot(q, keys[b][:, lanes], NT), MASKED)
-            new_top = jnp.maximum(top, jnp.max(s, axis=1, keepdims=True))
+            block_top = jnp.max(s, axis=1, keepdims=True)
+            new_top = block_top if b == 0 else jnp.maximum(top, block_top)
             p = jnp.exp(s - new_top)
-            factor = jnp.exp(top - new_top)
-            total = total * factor + jnp.sum(p, axis=1, keepdims=True)
-            acc = acc * factor + dot(p.astype(LOW), values[b][:, lanes], NN)
+            block_total = jnp.sum(p, axis=1, keepdims=True)
+            block_acc = dot(p.astype(LOW), values[b][:, lanes], NN)
+            if b == 0:
+                total, acc = block_total, block_acc
+            else:
+                factor = jnp.exp(top - new_top)
+                total = total * factor + block_total
+                acc = acc * factor + block_acc
             top = new_top
         out_ref[:, lanes] = acc / total
-        lse_ref[half] = top + jnp.log(total)
-
-
-def pair_call(kernel, name, rows, width, kpos, operands, stacked, outs, flops):
+        lse_ref[:, lanes] = jnp.broadcast_to(top + jnp.log(total), acc.shape)
+
+
+def group_call(kernel, name, rows, width, kpos, operands, stacked, outs, flops):
     blocks, _, key_rows = kpos.shape
+    group = GROUP if blocks <= 2 else PAIR
     column = lambda i: (0, i)
     specs = {
-        "row": pl.BlockSpec((rows, PAIR), column),
-        "head": pl.BlockSpec((PAIR // HD, rows, 1), lambda i: (i, 0, 0)),
-        "keys": pl.BlockSpec((2 * key_rows, PAIR), column),
+        "row": pl.BlockSpec((rows, group), column),
+        "keys": pl.BlockSpec((2 * key_rows, group), column),
     }
-    shapes = {"row": (rows, width), "head": (width // HD, rows, 1), "keys": (2 * key_rows, width)}
-    halves = [pl.BlockSpec((key_rows, PAIR), lambda i, c=c: (c, i)) for c in range(2)]
+    shapes = {"row": (rows, width), "keys": (2 * key_rows, width)}
+    halves = [pl.BlockSpec((key_rows, group), lambda i, c=c: (c, i)) for c in range(2)]
     common = [
         pl.BlockSpec((rows, 1), lambda i: (0, 0)),
         pl.BlockSpec((blocks, 1, key_rows), lambda i: (0, 0, 0)),
     ]
     return pl.pallas_call(
         kernel,
-        grid=(width // PAIR,),
-        in_specs=common + [specs[k] for k, _ in operands[1:]] + halves * len(stacked),
+        grid=(width // group,),
+        in_specs=common + [specs["row"]] * (len(operands) - 1) + halves * len(stacked),
         out_specs=[specs[k] for k, _ in outs],
         out_shape=[jax.ShapeDtypeStruct(shapes[k], t) for k, t in outs],
         compiler_params=pltpu.CompilerParams(vmem_limit_bytes=40 * 1024 * 1024),
         cost_estimate=work(flops * rows * key_rows * blocks * width),
         name=name,
-    )(operands[0], kpos, *[v for _, v in operands[1:]], *[s for s in stacked for c in range(2)])
-
-
-def attend_near(qpos, kpos, q, own):
+    )(operands[0], kpos, *operands[1:], *[s for s in stacked for c in range(2)])
+
+
+def attend(qpos, kpos, q, stacked):
     rows, width = q.shape
-    outs = [("row", WIDE), ("head", WIDE), ("head", WIDE)]
-    return pair_call(
-        attend_near_kernel, "attend_near", rows, width, kpos, [qpos, ("row", q)], [own], outs, 43
-    )
-
-
-def attend_far(qpos, kpos, q, near, far):
-    rows, width = q.shape
-    kinds = ("row", "head", "head")
-    operands = [qpos, ("row", q), *zip(kinds, near)]
-    return pair_call(
-        functools.partial(attend_far_kernel, len(far)),
-        "attend_far",
-        rows,
-        width,
-        kpos,
-        operands,
-        far,
-        [("row", WIDE), ("head", WIDE)],
-        43,
-    )
+    kernel = functools.partial(attend_kernel, len(stacked))
+    outs = [("row", WIDE)] * 2
+    return group_call(kernel, "attend", rows, width, kpos, [qpos, q], stacked, outs, 43)
 
 
 def attend_back_kernel(blocks, more, qpos_ref, kpos_ref, q_ref, grad_ref, out_ref, lse_ref, *refs):
@@ -424,11 +402,11 @@
     key_rows = keys[0].shape[0]
     allowed = [kpos_ref[b] <= qpos_ref[...] for b in range(blocks)]
     scale = HD**-0.5
-    for half in range(PAIR // HD):
+    for half in range(q_ref.shape[1] // HD):
         lanes = slice(half * HD, (half + 1) * HD)
         q = q_ref[:, lanes] * jnp.asarray(scale, LOW)
         grad = grad_ref[:, lanes]
-        lse = lse_ref[half]
+        lse = lse_ref[:, half * HD : half * HD + 1]
         delta = jnp.sum(grad.astype(WIDE) * out_ref[:, lanes], axis=1, keepdims=True)
         dq = []
         for b in range(blocks):
@@ -446,14 +424,13 @@
 
 def attend_back(qpos, kpos, q, grad, out, lse, stacked, kind, before):
     rows, width = q.shape
-    rest = [("row", v) for v in (q, grad, out)] + [("head", lse)] + [("row", v) for v in before]
-    results = pair_call(
+    results = group_call(
         functools.partial(attend_back_kernel, len(stacked), len(before)),
         "attend_back",
         rows,
         width,
         kpos,
-        [qpos] + rest,
+        [qpos, q, grad, out, lse, *before],
         stacked,
         [("row", WIDE)] + [("keys", kind)] * len(stacked),
         75,
@@ -727,6 +704,7 @@
     qpos = plan.places[:, None]
     near_places = plan.places[None, None, :]
     far_places = jnp.stack(plan.far_places)[:, None, :]
+    all_places = jnp.concatenate([near_places, far_places])
     gains = (norm_gains)
     biases = (norm_biases)
     qkv_bias_own = lax.dynamic_slice_in_dim(qkv_bias, lax.axis_index("tensor") * heads_width, heads_width, 2)
@@ -770,8 +748,7 @@
         if not last:
             prepared, queries = weight_jobs(layer + 1, queries)
         far_kv = plan.far_keys(keys_values)
-        near = attend_near(qpos, near_places, queries, keys_values)
-        attended, lse = attend_far(qpos, far_places, queries, near, far_kv)
+        attended, lse = attend(qpos, all_places, queries, [keys_values, *far_kv])
         attended_low = meanwhile(attended.astype(LOW), now["out"])
         attended_low = held(attended_low, *map(prepared.get, ("gate", "up")))
         if layer == 0:

time: 1160 us -> 1150 us (level)
  Pallas kernels: 290 us -> 261 us
  waiting for transfers between devices: 488 us -> 517 us
    pallas_call x8 -> x6, Pallas kernels: 85.9 us -> 56.9 us  [group_call(): pl.pallas_call(kernel, grid=(width // group,), in_specs=common + [specs['...]
    ppermute x32, waiting for transfers between devices: 181 us -> 197 us  [gather_rows(): send = lambda v, *route: lax.ppermute(v, 'tensor', list(route))]
    unnamed x247 -> x239, local copies, waits for them, and re-layouts: 56.9 us -> 57.5 us
  transfers between devices with their start and end apart: 105 -> 105, of which waited for: 50 -> 49; matrix products, arithmetic and copies ran while one was open for 9% -> 8% of each run, Pallas kernels for 22% -> 19%
where the time goes in v7:
time: 1150 us; the launch traced here: 1140 us
  waiting for transfers between devices  517 us (45%)
  Pallas kernels  261 us (23%)
  starting transfers between devices  187 us (16%)
  local copies, waits for them, and re-layouts  87 us (8%)
  other arithmetic  72.1 us (6%)
  between operations  16.8 us (1%)
    ppermute x32, waiting for transfers between devices, gather_rows(): send = lambda v, *route: lax.ppermute(v, 'tensor', list(route))  197 us
    ppermute x32, waiting for transfers between devices, sum_rows(): send = lambda v, *route: lax.ppermute(v, 'tensor', list(route))  193 us
    pallas_call x32, Pallas kernels, tiled(): pl.pallas_call(kernel, grid=(steps,), in_specs=[pl.BlockSpec(block, index...  161 us
    ppermute x32, starting transfers between devices, sum_rows(): send = lambda v, *route: lax.ppermute(v, 'tensor', list(route))  82 us
    ppermute x19, waiting for transfers between devices, swapped(): return lax.ppermute(value, axis, [(i, i ^ mask) for i in range(count)])  80.6 us
    ppermute x32, starting transfers between devices, gather_rows(): send = lambda v, *route: lax.ppermute(v, 'tensor', list(route))  78.1 us
    unnamed x239, local copies, waits for them, and re-layouts  57.5 us
    pallas_call x6, Pallas kernels, group_call(): pl.pallas_call(kernel, grid=(width // group,), in_specs=common + [specs['...  56.9 us
  transfers between devices with their start and end apart: 105, of which 49 were waited for; matrix products, arithmetic and copies ran while one was open for 8% of the time, Pallas kernels for 19%

profile of v7, /device:TPU:0, one launch (start us, length us, event | category | flops | bytes accessed | tf_op | source)
XLA Modules:
  0.0 1140.5 jit_solution(3000081465183772910)
XLA Ops:
  31.4 16.3 %collective-permute-done = bf16[128,2048]{1,0:T(8,128)(2,1)} collective-permute-done((bf16[128,2048]{1,0:T(8,128)(2,1)S(1)}, bf16[128,2048]{1,0:T(8,128)(2,1)}, u32[]{:S(2)}, u32[]{:S(2)}) %collective-permute-start) | collective-permute-done | bytes 524320 | tf_op jit(solution)/shard_map/ppermute | solution.py:558
  51.7 10.5 collective-permute-done.1
  63.6 8.3 project.2
  91.8 12.3 %collective-permute-done.5 = bf16[128,2048]{1,0:T(8,128)(2,1)} collective-permute-done((bf16[128,2048]{1,0:T(8,128)(2,1)}, bf16[128,2048]{1,0:T(8,128)(2,1)}, u32[]{:S(2)}, u32[]{:S(2)}) %collective-permute-start.5) | collective-permute-done | bytes 524320 | tf_op jit(solution)/shard_map/ppermute | solution.py:558
  105.6 10.8 attend.2
  136.3 6.4 collective-permute-done.9
  145.4 8.5 collective-permute-done.11
  154.0 12.2 %collective-permute-done.10 = bf16[128,2048]{1,0:T(8,128)(2,1)S(1)} collective-permute-done((bf16[128,2048]{1,0:T(8,128)(2,1)S(1)}, bf16[128,2048]{1,0:T(8,128)(2,1)S(1)}, u32[]{:S(2)}, u32[]{:S(2)}) %collective-permute-start.10) | collective-permute-done | bytes 524320 | tf_op jit(solution)/shard_map/ppermute | solution.py:574
  175.0 8.3 collective-permute-start.16
  183.3 15.9 %collective-permute-done.13 = bf16[128,2048]{1,0:T(8,128)(2,1)} collective-permute-done((bf16[128,2048]{1,0:T(8,128)(2,1)}, bf16[128,2048]{1,0:T(8,128)(2,1)}, u32[]{:S(2)}, u32[]{:S(2)}) %collective-permute-start.13) | collective-permute-done | bytes 524320 | tf_op jit(solution)/shard_map/ppermute | solution.py:558
  201.7 8.8 collective-permute-done.14
  223.4 11.2 gate_up.2
  238.0 5.9 down.2
  253.4 6.3 collective-permute-done.17
  263.3 7.6 collective-permute-done.19
  271.0 14.7 %collective-permute-done.18 = bf16[128,2048]{1,0:T(8,128)(2,1)S(1)} collective-permute-done((bf16[128,2048]{1,0:T(8,128)(2,1)S(1)}, bf16[128,2048]{1,0:T(8,128)(2,1)S(1)}, u32[]{:S(2)}, u32[]{:S(2)}) %collective-permute-start.18) | collective-permute-done | bytes 524320 | tf_op jit(solution)/shard_map/ppermute | solution.py:574
  294.5 8.2 collective-permute-start.24
  302.8 17.8 %collective-permute-done.21 = bf16[128,2048]{1,0:T(8,128)(2,1)} collective-permute-done((bf16[128,2048]{1,0:T(8,128)(2,1)}, bf16[128,2048]{1,0:T(8,128)(2,1)}, u32[]{:S(2)}, u32[]{:S(2)}) %collective-permute-start.21) | collective-permute-done | bytes 524320 | tf_op jit(solution)/shard_map/ppermute | solution.py:558
  323.5 8.4 collective-permute-done.22
  339.8 7.2 project.3
  350.4 22.8 %collective-permute-done.25.refs_2_.refs_3_.refs_0_.refs_1_ = bf16[1024,512]{1,0:T(8,128)(2,1)S(1)} collective-permute-done((bf16[1024,512]{1,0:T(8,128)(2,1)S(1)}, bf16[1024,512]{1,0:T(8,128)(2,1)S(1)}, u32[]{:S(2)}, u32[]{:S(2)}) %collective-permute-start.25) | collective-permute-done | bytes 1048608 | tf_op jit(solution)/shard_map/ppermute | solution.py:602
  373.2 9.8 attend.3
  398.1 6.4 collective-permute-done.26
  408.1 8.7 collective-permute-done.29
  416.9 11.8 %collective-permute-done.27 = bf16[128,2048]{1,0:T(8,128)(2,1)S(1)} collective-permute-done((bf16[128,2048]{1,0:T(8,128)(2,1)S(1)}, bf16[128,2048]{1,0:T(8,128)(2,1)S(1)}, u32[]{:S(2)}, u32[]{:S(2)}) %collective-permute-start.27) | collective-permute-done | bytes 524320 | tf_op jit(solution)/shard_map/ppermute | solution.py:574
  437.5 7.5 collective-permute-start.33
  445.0 17.3 %collective-permute-done.30 = bf16[128,2048]{1,0:T(8,128)(2,1)S(1)} collective-permute-done((bf16[128,2048]{1,0:T(8,128)(2,1)S(1)}, bf16[128,2048]{1,0:T(8,128)(2,1)S(1)}, u32[]{:S(2)}, u32[]{:S(2)}) %collective-permute-start.30) | collective-permute-done | bytes 524320 | tf_op jit(solution)/shard_map/ppermute | solution.py:558
  463.8 10.1 collective-permute-done.31
  474.3 11.5 %gate_up.3 = (f32[512,1408]{1,0:T(8,128)}, f32[512,1408]{1,0:T(8,128)}, bf16[512,1408]{1,0:T(8,128)(2,1)S(1)}) custom-call(bf16[512,2048]{1,0:T(8,128)(2,1)S(1)} %pad_maximum_fusion.4.rows_ref.a_ref, bf16[2048,1408]{1,0:T(8,128)(2,1)} %all-gather.34.cloned.1.call-done, bf16[2048,1408]{1,0:T(8,128)(2,1)} %all-gather.36.cloned.1.call-done), custom_call_target="tpu_custom_call" | custom-call | flops 14763950080 | tf_op jit(solution)/shard_map/gate_up/pallas_call | solution.py:77
  486.9 7.3 gate_up_back.2
  494.3 10.3 gate_up_in.2.refs_0_
  510.5 8.9 collective-permute-done.34
  520.4 7.1 collective-permute-start.35
  530.8 20.5 %collective-permute-done.35.refs_1_ = bf16[128,2048]{1,0:T(8,128)(2,1)} collective-permute-done((bf16[128,2048]{1,0:T(8,128)(2,1)}, bf16[128,2048]{1,0:T(8,128)(2,1)}, u32[]{:S(2)}, u32[]{:S(2)}) %collective-permute-start.35) | collective-permute-done | bytes 524320 | tf_op jit(solution)/shard_map/ppermute | solution.py:574
  579.5 13.1 %collective-permute-done.38 = bf16[128,2048]{1,0:T(8,128)(2,1)S(1)} collective-permute-done((bf16[128,2048]{1,0:T(8,128)(2,1)}, bf16[128,2048]{1,0:T(8,128)(2,1)S(1)}, u32[]{:S(2)}, u32[]{:S(2)}) %collective-permute-start.38) | collective-permute-done | bytes 524320 | tf_op jit(solution)/shard_map/ppermute | solution.py:558
  595.3 5.8 down.3
  601.2 8.7 collective-permute-done.39
  623.2 8.9 attend_back.4
  640.8 8.4 attend_back.5
  649.2 14.2 %collective-permute-done.43 = bf16[128,2048]{1,0:T(8,128)(2,1)S(1)} collective-permute-done((bf16[128,2048]{1,0:T(8,128)(2,1)S(1)}, bf16[128,2048]{1,0:T(8,128)(2,1)S(1)}, u32[]{:S(2)}, u32[]{:S(2)}) %collective-permute-start.43) | collective-permute-done | bytes 524320 | tf_op jit(solution)/shard_map/ppermute | solution.py:574
  681.2 6.2 project_in.2.refs_0_
  692.8 9.5 collective-permute-done.47
  705.9 7.7 collective-permute-done.49.refs_2_
  714.5 16.0 %collective-permute-done.48.refs_1_ = bf16[128,2048]{1,0:T(8,128)(2,1)} collective-permute-done((bf16[128,2048]{1,0:T(8,128)(2,1)}, bf16[128,2048]{1,0:T(8,128)(2,1)}, u32[]{:S(2)}, u32[]{:S(2)}) %collective-permute-start.48) | collective-permute-done | bytes 524320 | tf_op jit(solution)/shard_map/ppermute | solution.py:574
  751.2 12.8 %collective-permute-done.52 = bf16[128,2048]{1,0:T(8,128)(2,1)S(1)} collective-permute-done((bf16[128,2048]{1,0:T(8,128)(2,1)S(1)}, bf16[128,2048]{1,0:T(8,128)(2,1)S(1)}, u32[]{:S(2)}, u32[]{:S(2)}) %collective-permute-start.52) | collective-permute-done | bytes 524320 | tf_op jit(solution)/shard_map/ppermute | solution.py:558
  765.2 6.9 collective-permute-done.54
  772.1 9.4 collective-permute-done.53
  793.0 7.3 gate_up_back.3
  800.3 10.3 gate_up_in.3.refs_0_
  819.5 6.8 collective-permute-done.57
  829.2 8.3 collective-permute-done.59.refs_2_
  837.6 20.0 %collective-permute-done.62.refs_1_ = bf16[512,512]{1,0:T(8,128)(2,1)} collective-permute-done((bf16[512,512]{1,0:T(8,128)(2,1)S(1)}, bf16[512,512]{1,0:T(8,128)(2,1)}, u32[]{:S(2)}, u32[]{:S(2)}) %collective-permute-start.62) | collective-permute-done | bytes 524320 | tf_op jit(solution)/shard_map/ppermute | solution.py:534
  885.6 15.3 %collective-permute-done.63 = bf16[128,2048]{1,0:T(8,128)(2,1)} collective-permute-done((bf16[128,2048]{1,0:T(8,128)(2,1)S(1)}, bf16[128,2048]{1,0:T(8,128)(2,1)}, u32[]{:S(2)}, u32[]{:S(2)}) %collective-permute-start.63) | collective-permute-done | bytes 524320 | tf_op jit(solution)/shard_map/ppermute | solution.py:558
  903.6 13.2 %collective-permute-done.64 = bf16[128,2048]{1,0:T(8,128)(2,1)} collective-permute-done((bf16[128,2048]{1,0:T(8,128)(2,1)}, bf16[128,2048]{1,0:T(8,128)(2,1)}, u32[]{:S(2)}, u32[]{:S(2)}) %collective-permute-start.64) | collective-permute-done | bytes 524320 | tf_op jit(solution)/shard_map/ppermute | solution.py:558
  925.7 9.9 attend_back.6
  937.3 9.2 attend_back.7
  946.6 15.1 %collective-permute-done.68.refs_0_ = bf16[1024,512]{1,0:T(8,128)(2,1)S(1)} collective-permute-done((bf16[1024,512]{1,0:T(8,128)(2,1)S(1)}, bf16[1024,512]{1,0:T(8,128)(2,1)S(1)}, u32[]{:S(2)}, u32[]{:S(2)}) %collective-permute-start.68) | collective-permute-done | bytes 1048608 | tf_op jit(solution)/shard_map/ppermute | solution.py:609
  977.0 6.1 project_in.3.refs_0_
  983.1 22.1 %collective-permute-done.69.refs_1_ = bf16[1408,512]{1,0:T(8,128)(2,1)} collective-permute-done((bf16[1408,512]{1,0:T(8,128)(2,1)}, bf16[1408,512]{1,0:T(8,128)(2,1)}, u32[]{:S(2)}, u32[]{:S(2)}) %collective-permute-start.69) | collective-permute-done | bytes 1441824 | tf_op jit(solution)/shard_map/ppermute | solution.py:534
  1038.1 9.2 finish_gate_up.2.refs_4_
  1047.4 8.2 collective-permute-done.73.refs_1_
  1067.1 17.8 %collective-permute-done.78 = f32[14,2048]{1,0:T(8,128)S(1)} collective-permute-done((f32[14,2048]{1,0:T(8,128)S(1)}, f32[14,2048]{1,0:T(8,128)S(1)}, u32[]{:S(2)}, u32[]{:S(2)}) %collective-permute-start.78) | collective-permute-done | bytes 114720 | tf_op jit(solution)/shard_map/ppermute | solution.py:534
  1099.4 5.9 collective-permute-done.82
  1112.5 9.4 finish_gate_up.3
  (582 shorter events, 436.3 us)
Async XLA Ops:
  7.2 56.4 %all-gather.22.cloned.1.call-start = ((), (), s32[]{:S(2)}) async-start(), calls=%async_computation.17 | async-start | bytes 7864320 | tf_op jit(solution)/shard_map/all_gather | solution.py:616
  10.0 108.6 %all-gather.20.cloned.1.call-start = ((), (), s32[]{:S(2)}) async-start(), calls=%async_computation.8 | async-start | bytes 2621440 | tf_op jit(solution)/shard_map/all_gather | solution.py:616
  10.9 156.7 %all-gather.24.cloned.1.call-start = ((), (), s32[]{:S(2)}) async-start(), calls=%async_computation.18 | async-start | bytes 7208960 | tf_op jit(solution)/shard_map/all_gather | solution.py:616
  16.1 198.5 %all-gather.26.cloned.1.call-start = ((), (), s32[]{:S(2)}) async-start(), calls=%async_computation.19 | async-start | bytes 7208960 | tf_op jit(solution)/shard_map/all_gather | solution.py:616
  16.7 203.2 %all-gather.28.cloned.1.call-start = ((), (), s32[]{:S(2)}) async-start(), calls=%async_computation.20 | async-start | bytes 7208960 | tf_op jit(solution)/shard_map/all_gather | solution.py:616
  19.6 28.2 %collective-permute-start = (bf16[128,2048]{1,0:T(8,128)(2,1)S(1)}, bf16[128,2048]{1,0:T(8,128)(2,1)}, u32[]{:S(2)}, u32[]{:S(2)}) collective-permute-start(bf16[128,2048]{1,0:T(8,128)(2,1)S(1)} %get-tuple-element.420), channel_id=1, source_target_pairs={{0,2},{2,0},{1,3},{3,1},{4,6},{6,4},{5,7},{7,5},{8,10},{10,8},{9,1... | collective-permute-start | bytes 1572872 | tf_op jit(solution)/shard_map/ppermute | solution.py:558
  23.6 28.0 %collective-permute-start.2 = (bf16[128,2048]{1,0:T(8,128)(2,1)S(1)}, bf16[128,2048]{1,0:T(8,128)(2,1)S(1)}, u32[]{:S(2)}, u32[]{:S(2)}) collective-permute-start(bf16[128,2048]{1,0:T(8,128)(2,1)S(1)} %get-tuple-element.420), channel_id=1, source_target_pairs={{1,0},{2,1},{3,2},{5,4},{6,5},{7,6},{9,8},{10,9},{11,10},{13,12},{... | collective-permute-start | bytes 1572872 | tf_op jit(solution)/shard_map/ppermute | solution.py:558
  24.9 26.8 %collective-permute-start.3 = (bf16[128,2048]{1,0:T(8,128)(2,1)S(1)}, bf16[128,2048]{1,0:T(8,128)(2,1)S(1)}, u32[]{:S(2)}, u32[]{:S(2)}) collective-permute-start(bf16[128,2048]{1,0:T(8,128)(2,1)S(1)} %get-tuple-element.420), channel_id=1, source_target_pairs={{0,1},{1,2},{2,3},{4,5},{5,6},{6,7},{8,9},{9,10},{10,11},{12,13},{... | collective-permute-start | bytes 1572872 | tf_op jit(solution)/shard_map/ppermute | solution.py:558
  71.8 33.8 %collective-permute-start.4 = (bf16[1024,512]{1,0:T(8,128)(2,1)}, bf16[1024,512]{1,0:T(8,128)(2,1)}, u32[]{:S(2)}, u32[]{:S(2)}) collective-permute-start(bf16[1024,512]{1,0:T(8,128)(2,1)} %get-tuple-element.191.refs_0_.refs_1_.refs_2_), channel_id=1, source_target_pairs={{0,4},{1,5},{2,6},{3,7},{8,12},{9,13},{10,14},{11,15},{16,20},{17,... | collective-permute-start | bytes 3145736 | tf_op jit(solution)/shard_map/ppermute | solution.py:602
  76.0 211.1 %all-gather.30.cloned.1.call-start = ((), (), s32[]{:S(2)}) async-start(), calls=%async_computation.21 | async-start | bytes 7864320 | tf_op jit(solution)/shard_map/all_gather | solution.py:616
  76.9 27.2 %collective-permute-start.5 = (bf16[128,2048]{1,0:T(8,128)(2,1)}, bf16[128,2048]{1,0:T(8,128)(2,1)}, u32[]{:S(2)}, u32[]{:S(2)}) collective-permute-start(bf16[128,2048]{1,0:T(8,128)(2,1)} %bitcast.108), channel_id=1, source_target_pairs={{0,2},{2,0},{1,3},{3,1},{4,6},{6,4},{5,7},{7,5},{8,10},{10,8},{9,1... | collective-permute-start | bytes 1572872 | tf_op jit(solution)/shard_map/ppermute | solution.py:558
  79.7 38.9 %collective-permute-start.7 = (bf16[128,2048]{1,0:T(8,128)(2,1)}, bf16[128,2048]{1,0:T(8,128)(2,1)}, u32[]{:S(2)}, u32[]{:S(2)}) collective-permute-start(bf16[128,2048]{1,0:T(8,128)(2,1)} %bitcast.109), channel_id=1, source_target_pairs={{1,0},{2,1},{3,2},{5,4},{6,5},{7,6},{9,8},{10,9},{11,10},{13,12},{... | collective-permute-start | bytes 1572872 | tf_op jit(solution)/shard_map/ppermute | solution.py:558
  80.9 37.6 %collective-permute-start.8 = (bf16[128,2048]{1,0:T(8,128)(2,1)}, bf16[128,2048]{1,0:T(8,128)(2,1)}, u32[]{:S(2)}, u32[]{:S(2)}) collective-permute-start(bf16[128,2048]{1,0:T(8,128)(2,1)} %bitcast.110), channel_id=1, source_target_pairs={{0,1},{1,2},{2,3},{4,5},{5,6},{6,7},{8,9},{9,10},{10,11},{12,13},{... | collective-permute-start | bytes 1572872 | tf_op jit(solution)/shard_map/ppermute | solution.py:558
  173.7 28.0 %collective-permute-start.15 = (bf16[128,2048]{1,0:T(8,128)(2,1)}, bf16[128,2048]{1,0:T(8,128)(2,1)}, u32[]{:S(2)}, u32[]{:S(2)}) collective-permute-start(bf16[128,2048]{1,0:T(8,128)(2,1)} %get-tuple-element.381), channel_id=1, source_target_pairs={{1,0},{2,1},{3,2},{5,4},{6,5},{7,6},{9,8},{10,9},{11,10},{13,12},{... | collective-permute-start | bytes 1572872 | tf_op jit(solution)/shard_map/ppermute | solution.py:558
  175.0 26.7 %collective-permute-start.16 = (bf16[128,2048]{1,0:T(8,128)(2,1)}, bf16[128,2048]{1,0:T(8,128)(2,1)}, u32[]{:S(2)}, u32[]{:S(2)}) collective-permute-start(bf16[128,2048]{1,0:T(8,128)(2,1)} %get-tuple-element.381), channel_id=1, source_target_pairs={{0,1},{1,2},{2,3},{4,5},{5,6},{6,7},{8,9},{9,10},{10,11},{12,13},{... | collective-permute-start | bytes 1572872 | tf_op jit(solution)/shard_map/ppermute | solution.py:558
  219.9 116.1 %all-gather.32.cloned.1.call-start = ((), (), s32[]{:S(2)}) async-start(), calls=%async_computation.22 | async-start | bytes 2621440 | tf_op jit(solution)/shard_map/all_gather | solution.py:616
  235.8 102.3 %all-gather.34.cloned.1.call-start = ((), (), s32[]{:S(2)}) async-start(), calls=%async_computation.23 | async-start | bytes 7208960 | tf_op jit(solution)/shard_map/all_gather | solution.py:616
  236.6 148.5 %all-gather.36.cloned.1.call-start = ((), (), s32[]{:S(2)}) async-start(), calls=%async_computation.24 | async-start | bytes 7208960 | tf_op jit(solution)/shard_map/all_gather | solution.py:616
  259.9 25.8 %collective-permute-start.18 = (bf16[128,2048]{1,0:T(8,128)(2,1)S(1)}, bf16[128,2048]{1,0:T(8,128)(2,1)S(1)}, u32[]{:S(2)}, u32[]{:S(2)}) collective-permute-start(bf16[128,2048]{1,0:T(8,128)(2,1)S(1)} %add_convert_fusion.9), channel_id=1, source_target_pairs={{0,2},{2,0},{1,3},{3,1},{4,6},{6,4},{5,7},{7,5},{8,10},{10,8},{9,1... | collective-permute-start | bytes 1572872 | tf_op jit(solution)/shard_map/ppermute | solution.py:574
  287.0 143.0 %all-gather.38.cloned.1.call-start = ((), (), s32[]{:S(2)}) async-start(), calls=%async_computation.25 | async-start | bytes 7208960 | tf_op jit(solution)/shard_map/all_gather | solution.py:616
  293.2 27.3 %collective-permute-start.21 = (bf16[128,2048]{1,0:T(8,128)(2,1)}, bf16[128,2048]{1,0:T(8,128)(2,1)}, u32[]{:S(2)}, u32[]{:S(2)}) collective-permute-start(bf16[128,2048]{1,0:T(8,128)(2,1)} %get-tuple-element.379), channel_id=1, source_target_pairs={{0,2},{2,0},{1,3},{3,1},{4,6},{6,4},{5,7},{7,5},{8,10},{10,8},{9,1... | collective-permute-start | bytes 1572872 | tf_op jit(solution)/shard_map/ppermute | solution.py:558
  293.2 30.3 %collective-permute-start.23 = (bf16[128,2048]{1,0:T(8,128)(2,1)}, bf16[128,2048]{1,0:T(8,128)(2,1)}, u32[]{:S(2)}, u32[]{:S(2)}) collective-permute-start(bf16[128,2048]{1,0:T(8,128)(2,1)} %get-tuple-element.379), channel_id=1, source_target_pairs={{1,0},{2,1},{3,2},{5,4},{6,5},{7,6},{9,8},{10,9},{11,10},{13,12},{... | collective-permute-start | bytes 1572872 | tf_op jit(solution)/shard_map/ppermute | solution.py:558
  294.5 29.0 %collective-permute-start.24 = (bf16[128,2048]{1,0:T(8,128)(2,1)}, bf16[128,2048]{1,0:T(8,128)(2,1)}, u32[]{:S(2)}, u32[]{:S(2)}) collective-permute-start(bf16[128,2048]{1,0:T(8,128)(2,1)} %get-tuple-element.379), channel_id=1, source_target_pairs={{0,1},{1,2},{2,3},{4,5},{5,6},{6,7},{8,9},{9,10},{10,11},{12,13},{... | collective-permute-start | bytes 1572872 | tf_op jit(solution)/shard_map/ppermute | solution.py:558
  338.1 341.7 %reduce-scatter.9.cloned.1.call-start = ((), (), s32[]{:S(2)}) async-start(), calls=%async_computation.9 | async-start | bytes 7208960 | tf_op jit(solution)/shard_map/reduce_scatter | solution.py:620
  347.0 26.2 %collective-permute-start.25 = (bf16[1024,512]{1,0:T(8,128)(2,1)S(1)}, bf16[1024,512]{1,0:T(8,128)(2,1)S(1)}, u32[]{:S(2)}, u32[]{:S(2)}) collective-permute-start(bf16[1024,512]{1,0:T(8,128)(2,1)S(1)} %get-tuple-element.221.refs_0_.refs_1_.refs_2_), channel_id=1, source_target_pairs={{0,4},{1,5},{2,6},{3,7},{8,12},{9,13},{10,14},{11,15},{16,20},{17,... | collective-permute-start | bytes 3145736 | tf_op jit(solution)/shard_map/ppermute | solution.py:602
  435.4 26.9 %collective-permute-start.30 = (bf16[128,2048]{1,0:T(8,128)(2,1)S(1)}, bf16[128,2048]{1,0:T(8,128)(2,1)S(1)}, u32[]{:S(2)}, u32[]{:S(2)}) collective-permute-start(bf16[128,2048]{1,0:T(8,128)(2,1)S(1)} %get-tuple-element.377), channel_id=1, source_target_pairs={{0,2},{2,0},{1,3},{3,1},{4,6},{6,4},{5,7},{7,5},{8,10},{10,8},{9,1... | collective-permute-start | bytes 1572872 | tf_op jit(solution)/shard_map/ppermute | solution.py:558
  436.2 27.6 %collective-permute-start.32 = (bf16[128,2048]{1,0:T(8,128)(2,1)S(1)}, bf16[128,2048]{1,0:T(8,128)(2,1)S(1)}, u32[]{:S(2)}, u32[]{:S(2)}) collective-permute-start(bf16[128,2048]{1,0:T(8,128)(2,1)S(1)} %get-tuple-element.377), channel_id=1, source_target_pairs={{1,0},{2,1},{3,2},{5,4},{6,5},{7,6},{9,8},{10,9},{11,10},{13,12},{... | collective-permute-start | bytes 1572872 | tf_op jit(solution)/shard_map/ppermute | solution.py:558
  437.5 26.3 %collective-permute-start.33 = (bf16[128,2048]{1,0:T(8,128)(2,1)S(1)}, bf16[128,2048]{1,0:T(8,128)(2,1)S(1)}, u32[]{:S(2)}, u32[]{:S(2)}) collective-permute-start(bf16[128,2048]{1,0:T(8,128)(2,1)S(1)} %get-tuple-element.377), channel_id=1, source_target_pairs={{0,1},{1,2},{2,3},{4,5},{5,6},{6,7},{8,9},{9,10},{10,11},{12,13},{... | collective-permute-start | bytes 1572872 | tf_op jit(solution)/shard_map/ppermute | solution.py:558
  520.4 30.9 %collective-permute-start.35 = (bf16[128,2048]{1,0:T(8,128)(2,1)}, bf16[128,2048]{1,0:T(8,128)(2,1)}, u32[]{:S(2)}, u32[]{:S(2)}) collective-permute-start(bf16[128,2048]{1,0:T(8,128)(2,1)} %add_convert_fusion.5), channel_id=1, source_target_pairs={{0,2},{2,0},{1,3},{3,1},{4,6},{6,4},{5,7},{7,5},{8,10},{10,8},{9,1... | collective-permute-start | bytes 1572872 | tf_op jit(solution)/shard_map/ppermute | solution.py:574
  563.6 179.9 %reduce-scatter.11.cloned.1.call-start = ((), (), s32[]{:S(2)}) async-start(), calls=%async_computation.10 | async-start | bytes 7208960 | tf_op jit(solution)/shard_map/reduce_scatter | solution.py:620
  572.4 210.8 %reduce-scatter.15.cloned.1.call-start = ((), (), s32[]{:S(2)}) async-start(), calls=%async_computation.12 | async-start | bytes 2621440 | tf_op jit(solution)/shard_map/reduce_scatter | solution.py:620
  573.6 27.5 %collective-permute-start.40 = (bf16[128,2048]{1,0:T(8,128)(2,1)}, bf16[128,2048]{1,0:T(8,128)(2,1)S(1)}, u32[]{:S(2)}, u32[]{:S(2)}) collective-permute-start(bf16[128,2048]{1,0:T(8,128)(2,1)} %copy-done.34), channel_id=1, source_target_pairs={{1,0},{2,1},{3,2},{5,4},{6,5},{7,6},{9,8},{10,9},{11,10},{13,12},{... | collective-permute-start | bytes 1572872 | tf_op jit(solution)/shard_map/ppermute | solution.py:558
  574.9 26.3 %collective-permute-start.41 = (bf16[128,2048]{1,0:T(8,128)(2,1)}, bf16[128,2048]{1,0:T(8,128)(2,1)S(1)}, u32[]{:S(2)}, u32[]{:S(2)}) collective-permute-start(bf16[128,2048]{1,0:T(8,128)(2,1)} %copy-done.34), channel_id=1, source_target_pairs={{0,1},{1,2},{2,3},{4,5},{5,6},{6,7},{8,9},{9,10},{10,11},{12,13},{... | collective-permute-start | bytes 1572872 | tf_op jit(solution)/shard_map/ppermute | solution.py:558
  611.4 37.8 %collective-permute-start.45 = (bf16[128,2048]{1,0:T(8,128)(2,1)}, bf16[128,2048]{1,0:T(8,128)(2,1)S(1)}, u32[]{:S(2)}, u32[]{:S(2)}) collective-permute-start(bf16[128,2048]{1,0:T(8,128)(2,1)} %get-tuple-element.406), channel_id=1, source_target_pairs={{3,2},{2,1},{1,0},{7,6},{6,5},{5,4},{11,10},{10,9},{9,8},{15,14},{... | collective-permute-start | bytes 1572872 | tf_op jit(solution)/shard_map/ppermute | solution.py:574
  612.8 36.4 %collective-permute-start.44 = (bf16[128,2048]{1,0:T(8,128)(2,1)}, bf16[128,2048]{1,0:T(8,128)(2,1)}, u32[]{:S(2)}, u32[]{:S(2)}) collective-permute-start(bf16[128,2048]{1,0:T(8,128)(2,1)} %get-tuple-element.405), channel_id=1, source_target_pairs={{0,1},{1,2},{2,3},{4,5},{5,6},{6,7},{8,9},{9,10},{10,11},{12,13},{... | collective-permute-start | bytes 1572872 | tf_op jit(solution)/shard_map/ppermute | solution.py:574
  632.0 33.6 %collective-permute-start.46 = (bf16[1024,512]{1,0:T(8,128)(2,1)S(1)}, bf16[1024,512]{1,0:T(8,128)(2,1)S(1)}, u32[]{:S(2)}, u32[]{:S(2)}) collective-permute-start(bf16[1024,512]{1,0:T(8,128)(2,1)S(1)} %get-tuple-element.249), channel_id=1, source_target_pairs={{4,0},{5,1},{6,2},{7,3},{12,8},{13,9},{14,10},{15,11},{20,16},{21,... | collective-permute-start | bytes 3145736 | tf_op jit(solution)/shard_map/ppermute | solution.py:609
  671.2 111.9 %reduce-scatter.13.cloned.1.call-start = ((), (), s32[]{:S(2)}) async-start(), calls=%async_computation.11 | async-start | bytes 7208960 | tf_op jit(solution)/shard_map/reduce_scatter | solution.py:620
  679.7 177.9 %reduce-scatter.17.cloned.1.call-start = ((), (), s32[]{:S(2)}) async-start(), calls=%async_computation.13 | async-start | bytes 7864320 | tf_op jit(solution)/shard_map/reduce_scatter | solution.py:620
  690.0 40.4 %collective-permute-start.51 = (bf16[1408,512]{1,0:T(8,128)(2,1)}, bf16[1408,512]{1,0:T(8,128)(2,1)}, u32[]{:S(2)}, u32[]{:S(2)}) collective-permute-start(bf16[1408,512]{1,0:T(8,128)(2,1)} %reduce-scatter.9.cloned.1.call-done.refs_0_), channel_id=1, source_target_pairs={{0,4},{4,0},{1,5},{5,1},{2,6},{6,2},{3,7},{7,3},{8,12},{12,8},{9,1... | collective-permute-start | bytes 4325384 | tf_op jit(solution)/shard_map/ppermute | solution.py:534
  703.3 27.2 %collective-permute-start.48 = (bf16[128,2048]{1,0:T(8,128)(2,1)}, bf16[128,2048]{1,0:T(8,128)(2,1)}, u32[]{:S(2)}, u32[]{:S(2)}) collective-permute-start(bf16[128,2048]{1,0:T(8,128)(2,1)} %add_convert_fusion.2), channel_id=1, source_target_pairs={{0,2},{2,0},{1,3},{3,1},{4,6},{6,4},{5,7},{7,5},{8,10},{10,8},{9,1... | collective-permute-start | bytes 1572872 | tf_op jit(solution)/shard_map/ppermute | solution.py:574
  743.4 177.3 %reduce-scatter.19.cloned.1.call-start = ((), (), s32[]{:S(2)}) async-start(), calls=%async_computation.14 | async-start | bytes 7208960 | tf_op jit(solution)/shard_map/reduce_scatter | solution.py:620
  743.6 39.6 %collective-permute-start.56 = (bf16[512,1408]{1,0:T(8,128)(2,1)}, bf16[512,1408]{1,0:T(8,128)(2,1)}, u32[]{:S(2)}, u32[]{:S(2)}) collective-permute-start(bf16[512,1408]{1,0:T(8,128)(2,1)} %reduce-scatter.11.cloned.1.call-done.refs_0_), channel_id=1, source_target_pairs={{0,4},{4,0},{1,5},{5,1},{2,6},{6,2},{3,7},{7,3},{8,12},{12,8},{9,1... | collective-permute-start | bytes 4325384 | tf_op jit(solution)/shard_map/ppermute | solution.py:534
  745.1 27.0 %collective-permute-start.54 = (bf16[128,2048]{1,0:T(8,128)(2,1)S(1)}, bf16[128,2048]{1,0:T(8,128)(2,1)S(1)}, u32[]{:S(2)}, u32[]{:S(2)}) collective-permute-start(bf16[128,2048]{1,0:T(8,128)(2,1)S(1)} %get-tuple-element.266), channel_id=1, source_target_pairs={{1,0},{2,1},{3,2},{5,4},{6,5},{7,6},{9,8},{10,9},{11,10},{13,12},{... | collective-permute-start | bytes 1572872 | tf_op jit(solution)/shard_map/ppermute | solution.py:558
  746.4 25.7 %collective-permute-start.55 = (bf16[128,2048]{1,0:T(8,128)(2,1)S(1)}, bf16[128,2048]{1,0:T(8,128)(2,1)S(1)}, u32[]{:S(2)}, u32[]{:S(2)}) collective-permute-start(bf16[128,2048]{1,0:T(8,128)(2,1)S(1)} %get-tuple-element.266), channel_id=1, source_target_pairs={{0,1},{1,2},{2,3},{4,5},{5,6},{6,7},{8,9},{9,10},{10,11},{12,13},{... | collective-permute-start | bytes 1572872 | tf_op jit(solution)/shard_map/ppermute | solution.py:558
  791.4 179.2 %reduce-scatter.21.cloned.1.call-start = ((), (), s32[]{:S(2)}) async-start(), calls=%async_computation.15 | async-start | bytes 7208960 | tf_op jit(solution)/shard_map/reduce_scatter | solution.py:620
  813.9 43.7 %collective-permute-start.61 = (bf16[512,1408]{1,0:T(8,128)(2,1)}, bf16[512,1408]{1,0:T(8,128)(2,1)}, u32[]{:S(2)}, u32[]{:S(2)}) collective-permute-start(bf16[512,1408]{1,0:T(8,128)(2,1)} %reduce-scatter.13.cloned.1.call-done.refs_2_), channel_id=1, source_target_pairs={{0,4},{4,0},{1,5},{5,1},{2,6},{6,2},{3,7},{7,3},{8,12},{12,8},{9,1... | collective-permute-start | bytes 4325384 | tf_op jit(solution)/shard_map/ppermute | solution.py:534
  818.1 39.5 %collective-permute-start.62 = (bf16[512,512]{1,0:T(8,128)(2,1)S(1)}, bf16[512,512]{1,0:T(8,128)(2,1)}, u32[]{:S(2)}, u32[]{:S(2)}) collective-permute-start(bf16[512,512]{1,0:T(8,128)(2,1)S(1)} %copy-done.59), channel_id=1, source_target_pairs={{0,4},{4,0},{1,5},{5,1},{2,6},{6,2},{3,7},{7,3},{8,12},{12,8},{9,1... | collective-permute-start | bytes 1572872 | tf_op jit(solution)/shard_map/ppermute | solution.py:534
  827.1 30.4 %collective-permute-start.58 = (bf16[128,2048]{1,0:T(8,128)(2,1)}, bf16[128,2048]{1,0:T(8,128)(2,1)}, u32[]{:S(2)}, u32[]{:S(2)}) collective-permute-start(bf16[128,2048]{1,0:T(8,128)(2,1)} %add_convert_fusion.1), channel_id=1, source_target_pairs={{0,2},{2,0},{1,3},{3,1},{4,6},{6,4},{5,7},{7,5},{8,10},{10,8},{9,1... | collective-permute-start | bytes 1572872 | tf_op jit(solution)/shard_map/ppermute | solution.py:574
  869.2 136.0 %reduce-scatter.23.cloned.1.call-start = ((), (), s32[]{:S(2)}) async-start(), calls=%async_computation.16 | async-start | bytes 7208960 | tf_op jit(solution)/shard_map/reduce_scatter | solution.py:620
  877.8 42.9 %collective-permute-start.67 = (bf16[512,1536]{1,0:T(8,128)(2,1)}, bf16[512,1536]{1,0:T(8,128)(2,1)}, u32[]{:S(2)}, u32[]{:S(2)}) collective-permute-start(bf16[512,1536]{1,0:T(8,128)(2,1)} %reduce-scatter.17.cloned.1.call-done.refs_0_), channel_id=1, source_target_pairs={{0,4},{4,0},{1,5},{5,1},{2,6},{6,2},{3,7},{7,3},{8,12},{12,8},{9,1... | collective-permute-start | bytes 4718600 | tf_op jit(solution)/shard_map/ppermute | solution.py:534
  935.6 26.0 %collective-permute-start.68 = (bf16[1024,512]{1,0:T(8,128)(2,1)S(1)}, bf16[1024,512]{1,0:T(8,128)(2,1)S(1)}, u32[]{:S(2)}, u32[]{:S(2)}) collective-permute-start(bf16[1024,512]{1,0:T(8,128)(2,1)S(1)} %get-tuple-element.297), channel_id=1, source_target_pairs={{4,0},{5,1},{6,2},{7,3},{12,8},{13,9},{14,10},{15,11},{20,16},{21,... | collective-permute-start | bytes 3145736 | tf_op jit(solution)/shard_map/ppermute | solution.py:609
  970.6 34.7 %collective-permute-start.70 = (bf16[1024,1536]{1,0:T(8,128)(2,1)}, bf16[1024,1536]{1,0:T(8,128)(2,1)}, u32[]{:S(2)}, u32[]{:S(2)}) collective-permute-start(bf16[1024,1536]{1,0:T(8,128)(2,1)} %copy-done.50), channel_id=1, source_target_pairs={{0,8},{8,0},{16,24},{24,16},{1,9},{9,1},{17,25},{25,17},{2,10},{10... | collective-permute-start | bytes 9437192 | tf_op jit(solution)/shard_map/ppermute | solution.py:534
  970.6 34.7 %collective-permute-start.69 = (bf16[1408,512]{1,0:T(8,128)(2,1)}, bf16[1408,512]{1,0:T(8,128)(2,1)}, u32[]{:S(2)}, u32[]{:S(2)}) collective-permute-start(bf16[1408,512]{1,0:T(8,128)(2,1)} %reduce-scatter.19.cloned.1.call-done.refs_0_), channel_id=1, source_target_pairs={{0,4},{4,0},{1,5},{5,1},{2,6},{6,2},{3,7},{7,3},{8,12},{12,8},{9,1... | collective-permute-start | bytes 4325384 | tf_op jit(solution)/shard_map/ppermute | solution.py:534
  970.9 34.4 %collective-permute-start.71 = (bf16[512,1024]{1,0:T(8,128)(2,1)}, bf16[512,1024]{1,0:T(8,128)(2,1)}, u32[]{:S(2)}, u32[]{:S(2)}) collective-permute-start(bf16[512,1024]{1,0:T(8,128)(2,1)} %outer.19), channel_id=1, source_target_pairs={{0,8},{8,0},{16,24},{24,16},{1,9},{9,1},{17,25},{25,17},{2,10},{10... | collective-permute-start | bytes 3145736 | tf_op jit(solution)/shard_map/ppermute | solution.py:534
  975.8 71.5 %collective-permute-start.76 = (bf16[512,1408]{1,0:T(8,128)(2,1)}, bf16[512,1408]{1,0:T(8,128)(2,1)}, u32[]{:S(2)}, u32[]{:S(2)}) collective-permute-start(bf16[512,1408]{1,0:T(8,128)(2,1)} %reduce-scatter.21.cloned.1.call-done.refs_0_), channel_id=1, source_target_pairs={{0,4},{4,0},{1,5},{5,1},{2,6},{6,2},{3,7},{7,3},{8,12},{12,8},{9,1... | collective-permute-start | bytes 4325384 | tf_op jit(solution)/shard_map/ppermute | solution.py:534
  1014.2 41.3 %collective-permute-start.77 = (bf16[512,1536]{1,0:T(8,128)(2,1)}, bf16[512,1536]{1,0:T(8,128)(2,1)}, u32[]{:S(2)}, u32[]{:S(2)}) collective-permute-start(bf16[512,1536]{1,0:T(8,128)(2,1)} %split.30), channel_id=1, source_target_pairs={{0,16},{8,24},{16,0},{24,8},{1,17},{9,25},{17,1},{25,9},{2,18},{10... | collective-permute-start | bytes 4718600 | tf_op jit(solution)/shard_map/ppermute | solution.py:534
  1015.8 31.5 %collective-permute-start.74 = (bf16[128,2048]{1,0:T(8,128)(2,1)}, bf16[128,2048]{1,0:T(8,128)(2,1)S(1)}, u32[]{:S(2)}, u32[]{:S(2)}) collective-permute-start(bf16[128,2048]{1,0:T(8,128)(2,1)} %get-tuple-element.397), channel_id=1, source_target_pairs={{0,1},{1,2},{2,3},{4,5},{5,6},{6,7},{8,9},{9,10},{10,11},{12,13},{... | collective-permute-start | bytes 1572872 | tf_op jit(solution)/shard_map/ppermute | solution.py:574
  1017.2 30.2 %collective-permute-start.75 = (bf16[128,2048]{1,0:T(8,128)(2,1)}, bf16[128,2048]{1,0:T(8,128)(2,1)S(1)}, u32[]{:S(2)}, u32[]{:S(2)}) collective-permute-start(bf16[128,2048]{1,0:T(8,128)(2,1)} %get-tuple-element.395), channel_id=1, source_target_pairs={{3,2},{2,1},{1,0},{7,6},{6,5},{5,4},{11,10},{10,9},{9,8},{15,14},{... | collective-permute-start | bytes 1572872 | tf_op jit(solution)/shard_map/ppermute | solution.py:574
  1021.9 33.6 %collective-permute-start.73 = (bf16[128,2048]{1,0:T(8,128)(2,1)S(1)}, bf16[128,2048]{1,0:T(8,128)(2,1)S(1)}, u32[]{:S(2)}, u32[]{:S(2)}) collective-permute-start(bf16[128,2048]{1,0:T(8,128)(2,1)S(1)} %add_convert_fusion), channel_id=1, source_target_pairs={{0,2},{2,0},{1,3},{3,1},{4,6},{6,4},{5,7},{7,5},{8,10},{10,8},{9,1... | collective-permute-start | bytes 1572872 | tf_op jit(solution)/shard_map/ppermute | solution.py:574
  1047.3 65.2 %collective-permute-start.86 = (bf16[512,1408]{1,0:T(8,128)(2,1)}, bf16[512,1408]{1,0:T(8,128)(2,1)}, u32[]{:S(2)}, u32[]{:S(2)}) collective-permute-start(bf16[512,1408]{1,0:T(8,128)(2,1)} %reduce-scatter.23.cloned.1.call-done.refs_2_), channel_id=1, source_target_pairs={{0,4},{4,0},{1,5},{5,1},{2,6},{6,2},{3,7},{7,3},{8,12},{12,8},{9,1... | collective-permute-start | bytes 4325384 | tf_op jit(solution)/shard_map/ppermute | solution.py:534
  1058.9 25.9 %collective-permute-start.78 = (f32[14,2048]{1,0:T(8,128)S(1)}, f32[14,2048]{1,0:T(8,128)S(1)}, u32[]{:S(2)}, u32[]{:S(2)}) collective-permute-start(f32[14,2048]{1,0:T(8,128)S(1)} %pad_maximum_fusion.12), channel_id=1, source_target_pairs={{0,4},{4,0},{1,5},{5,1},{2,6},{6,2},{3,7},{7,3},{8,12},{12,8},{9,1... | collective-permute-start | bytes 344072 | tf_op jit(solution)/shard_map/ppermute | solution.py:534
  1063.5 65.3 %collective-permute-start.83 = (bf16[512,1536]{1,0:T(8,128)(2,1)}, bf16[512,1536]{1,0:T(8,128)(2,1)}, u32[]{:S(2)}, u32[]{:S(2)}) collective-permute-start(bf16[512,1536]{1,0:T(8,128)(2,1)} %fusion.refs_0_), channel_id=1, source_target_pairs={{0,4},{4,0},{1,5},{5,1},{2,6},{6,2},{3,7},{7,3},{8,12},{12,8},{9,1... | collective-permute-start | bytes 4718600 | tf_op jit(solution)/shard_map/ppermute | solution.py:534
  1066.8 32.3 %collective-permute-start.84 = (bf16[512,512]{1,0:T(8,128)(2,1)S(1)}, bf16[512,512]{1,0:T(8,128)(2,1)S(1)}, u32[]{:S(2)}, u32[]{:S(2)}) collective-permute-start(bf16[512,512]{1,0:T(8,128)(2,1)S(1)} %split.31), channel_id=1, source_target_pairs={{0,16},{8,24},{16,0},{24,8},{1,17},{9,25},{17,1},{25,9},{2,18},{10... | collective-permute-start | bytes 1572872 | tf_op jit(solution)/shard_map/ppermute | solution.py:534
  1099.2 28.0 %collective-permute-start.85 = (bf16[512,512]{1,0:T(8,128)(2,1)S(1)}, bf16[512,512]{1,0:T(8,128)(2,1)S(1)}, u32[]{:S(2)}, u32[]{:S(2)}) collective-permute-start(bf16[512,512]{1,0:T(8,128)(2,1)S(1)} %fusion.6.refs_0_), channel_id=1, source_target_pairs={{0,4},{4,0},{1,5},{5,1},{2,6},{6,2},{3,7},{7,3},{8,12},{12,8},{9,1... | collective-permute-start | bytes 1572872 | tf_op jit(solution)/shard_map/ppermute | solution.py:534
  (160 other events, 2594.2 us)
Sparse Core Ops, SparseCore 0:
  10.2 49.0 all-gather.21
  61.4 22.5 all-gather.19
  86.2 43.3 all-gather.23
  131.6 43.3 all-gather.25
  176.5 43.3 all-gather.27
  221.9 46.3 all-gather.29
  270.5 22.5 all-gather.31
  294.6 43.3 all-gather.33
  339.6 43.3 all-gather.35
  385.1 43.3 all-gather.37
  563.7 52.0 reduce-scatter.8
  619.0 54.8 reduce-scatter.10
  676.4 31.4 reduce-scatter.14
  711.0 54.8 reduce-scatter.12
  768.9 58.3 reduce-scatter.16
  830.4 54.8 reduce-scatter.18
  888.3 54.8 reduce-scatter.20
  946.3 54.8 reduce-scatter.22

commit v8 on v7

--- a/solution.py
+++ b/solution.py
@@ -850,6 +850,8 @@
         grad_attended = out_back(attention, out_full)
         shared = (queries, grad_attended, attended, lse)
         far_queries, far_grads = attend_back(qpos, far_places, *shared, far_kv, LOW, [])
+        if layer == 0:
+            far_queries = meanwhile(far_queries, mine["down"])
         returned = plan.far_key_grads(far_grads)
         grad_queries, grad_kv = attend_back(
             qpos, near_places, *shared, [keys_values], WIDE, [far_queries]
@@ -889,7 +891,7 @@
             projected = meanwhile(projected, *map(mine.get, ("qkv", "out", "gate")))
         partial_in = project_in(projected, qkv_full)
         if layer == 0:
-            partial_in = meanwhile(partial_in, *map(mine.get, ("down", "up", "qkv")))
+            partial_in = meanwhile(partial_in, mine["up"], mine["qkv"])
             partial_in = held(partial_in, mine["out"])
         summed = plan.sum_rows(partial_in)
         if layer > 0:
@@ -921,16 +923,22 @@
         ],
         axis=0,
     )
-    for axis in ("ctx", "dp", "tensor"):
+    sums = {k: j.finish() for k, j in grad_jobs[0].items()}
+    for axis in ("dp", "tensor", "ctx"):
+        if axis == "ctx":
+            large = [
+                finish_gate_up(results[2], 0, sums["gate"], sums["up"]),
+                finish_matrix(results[3], 0, sums["down"], "finish_down"),
+            ]
+            small, large = lax.optimization_barrier((small, large))
         for bit in bits_of(lax.axis_size(axis)):
             small = small + swapped(small, axis, bit)
-        small, results = lax.optimization_barrier((small, results))
-    sums = {k: j.finish() for k, j in grad_jobs[0].items()}
+        if axis == "dp":
+            small, results = lax.optimization_barrier((small, results))
     results = [
         finish_projections(results[0], 0, sums["qkv"]),
         finish_matrix(results[1], 0, sums["out"], "finish_out"),
-        finish_gate_up(results[2], 0, sums["gate"], sums["up"]),
-        finish_matrix(results[3], 0, sums["down"], "finish_down"),
+        *large,
     ]
     return (
         output,

time: 1150 us -> 1140 us (level)
    ppermute x19, waiting for transfers between devices: 80.6 us -> 56.2 us  [swapped(): return lax.ppermute(value, axis, [(i, i ^ mask) for i in range(count)])]
    ppermute x32, waiting for transfers between devices: 193 us -> 205 us  [sum_rows(): send = lambda v, *route: lax.ppermute(v, 'tensor', list(route))]
    unnamed x239 -> x241, local copies, waits for them, and re-layouts: 57.5 us -> 53.7 us
where the time goes in v8:
time: 1140 us; the launch traced here: 1130 us
  waiting for transfers between devices  507 us (44%)
  Pallas kernels  259 us (23%)
  starting transfers between devices  188 us (16%)
  local copies, waits for them, and re-layouts  83 us (7%)
  other arithmetic  71.9 us (6%)
  between operations  16.9 us (1%)
    ppermute x32, waiting for transfers between devices, sum_rows(): send = lambda v, *route: lax.ppermute(v, 'tensor', list(route))  205 us
    ppermute x32, waiting for transfers between devices, gather_rows(): send = lambda v, *route: lax.ppermute(v, 'tensor', list(route))  198 us
    pallas_call x32, Pallas kernels, tiled(): pl.pallas_call(kernel, grid=(steps,), in_specs=[pl.BlockSpec(block, index...  160 us
    ppermute x32, starting transfers between devices, sum_rows(): send = lambda v, *route: lax.ppermute(v, 'tensor', list(route))  83.6 us
    ppermute x32, starting transfers between devices, gather_rows(): send = lambda v, *route: lax.ppermute(v, 'tensor', list(route))  78.2 us
    pallas_call x6, Pallas kernels, group_call(): pl.pallas_call(kernel, grid=(width // group,), in_specs=common + [specs['...  57.4 us
    ppermute x19, waiting for transfers between devices, swapped(): return lax.ppermute(value, axis, [(i, i ^ mask) for i in range(count)])  56.2 us
    unnamed x241, local copies, waits for them, and re-layouts  53.7 us
  transfers between devices with their start and end apart: 105, of which 49 were waited for; matrix products, arithmetic and copies ran while one was open for 8% of the time, Pallas kernels for 19%

profile of v8, /device:TPU:0, one launch (start us, length us, event | category | flops | bytes accessed | tf_op | source)
XLA Modules:
  0.0 1125.3 jit_solution(7821804362758741705)
XLA Ops:
  31.4 16.3 %collective-permute-done = bf16[128,2048]{1,0:T(8,128)(2,1)} collective-permute-done((bf16[128,2048]{1,0:T(8,128)(2,1)S(1)}, bf16[128,2048]{1,0:T(8,128)(2,1)}, u32[]{:S(2)}, u32[]{:S(2)}) %collective-permute-start) | collective-permute-done | bytes 524320 | tf_op jit(solution)/shard_map/ppermute | solution.py:558
  51.7 10.5 collective-permute-done.1
  63.6 8.3 project.2
  91.9 12.3 %collective-permute-done.5 = bf16[128,2048]{1,0:T(8,128)(2,1)} collective-permute-done((bf16[128,2048]{1,0:T(8,128)(2,1)}, bf16[128,2048]{1,0:T(8,128)(2,1)}, u32[]{:S(2)}, u32[]{:S(2)}) %collective-permute-start.5) | collective-permute-done | bytes 524320 | tf_op jit(solution)/shard_map/ppermute | solution.py:558
  105.7 10.8 attend.2
  124.8 5.7 collective-permute-start.9
  136.3 6.4 collective-permute-done.9
  145.5 8.5 collective-permute-done.11
  154.0 12.2 %collective-permute-done.10 = bf16[128,2048]{1,0:T(8,128)(2,1)S(1)} collective-permute-done((bf16[128,2048]{1,0:T(8,128)(2,1)S(1)}, bf16[128,2048]{1,0:T(8,128)(2,1)S(1)}, u32[]{:S(2)}, u32[]{:S(2)}) %collective-permute-start.10) | collective-permute-done | bytes 524320 | tf_op jit(solution)/shard_map/ppermute | solution.py:574
  175.1 8.3 collective-permute-start.16
  183.3 15.8 %collective-permute-done.13 = bf16[128,2048]{1,0:T(8,128)(2,1)} collective-permute-done((bf16[128,2048]{1,0:T(8,128)(2,1)}, bf16[128,2048]{1,0:T(8,128)(2,1)}, u32[]{:S(2)}, u32[]{:S(2)}) %collective-permute-start.13) | collective-permute-done | bytes 524320 | tf_op jit(solution)/shard_map/ppermute | solution.py:558
  201.7 8.8 collective-permute-done.14
  223.4 11.2 gate_up.2
  238.0 5.9 down.2
  253.4 6.3 collective-permute-done.17
  263.3 7.6 collective-permute-done.19
  271.0 14.7 %collective-permute-done.18 = bf16[128,2048]{1,0:T(8,128)(2,1)S(1)} collective-permute-done((bf16[128,2048]{1,0:T(8,128)(2,1)S(1)}, bf16[128,2048]{1,0:T(8,128)(2,1)S(1)}, u32[]{:S(2)}, u32[]{:S(2)}) %collective-permute-start.18) | collective-permute-done | bytes 524320 | tf_op jit(solution)/shard_map/ppermute | solution.py:574
  294.6 8.2 collective-permute-start.24
  302.8 17.8 %collective-permute-done.21 = bf16[128,2048]{1,0:T(8,128)(2,1)} collective-permute-done((bf16[128,2048]{1,0:T(8,128)(2,1)}, bf16[128,2048]{1,0:T(8,128)(2,1)}, u32[]{:S(2)}, u32[]{:S(2)}) %collective-permute-start.21) | collective-permute-done | bytes 524320 | tf_op jit(solution)/shard_map/ppermute | solution.py:558
  323.5 8.4 collective-permute-done.22
  339.8 7.2 project.3
  350.4 22.8 %collective-permute-done.25.refs_2_.refs_3_.refs_0_.refs_1_ = bf16[1024,512]{1,0:T(8,128)(2,1)S(1)} collective-permute-done((bf16[1024,512]{1,0:T(8,128)(2,1)S(1)}, bf16[1024,512]{1,0:T(8,128)(2,1)S(1)}, u32[]{:S(2)}, u32[]{:S(2)}) %collective-permute-start.25) | collective-permute-done | bytes 1048608 | tf_op jit(solution)/shard_map/ppermute | solution.py:602
  373.2 9.8 attend.3
  398.1 6.4 collective-permute-done.26
  408.1 8.7 collective-permute-done.29
  416.8 11.9 %collective-permute-done.27 = bf16[128,2048]{1,0:T(8,128)(2,1)S(1)} collective-permute-done((bf16[128,2048]{1,0:T(8,128)(2,1)S(1)}, bf16[128,2048]{1,0:T(8,128)(2,1)S(1)}, u32[]{:S(2)}, u32[]{:S(2)}) %collective-permute-start.27) | collective-permute-done | bytes 524320 | tf_op jit(solution)/shard_map/ppermute | solution.py:574
  437.5 7.5 collective-permute-start.33
  445.0 17.3 %collective-permute-done.30 = bf16[128,2048]{1,0:T(8,128)(2,1)S(1)} collective-permute-done((bf16[128,2048]{1,0:T(8,128)(2,1)S(1)}, bf16[128,2048]{1,0:T(8,128)(2,1)S(1)}, u32[]{:S(2)}, u32[]{:S(2)}) %collective-permute-start.30) | collective-permute-done | bytes 524320 | tf_op jit(solution)/shard_map/ppermute | solution.py:558
  463.8 10.1 collective-permute-done.31
  474.3 11.5 %gate_up.3 = (f32[512,1408]{1,0:T(8,128)}, f32[512,1408]{1,0:T(8,128)}, bf16[512,1408]{1,0:T(8,128)(2,1)S(1)}) custom-call(bf16[512,2048]{1,0:T(8,128)(2,1)S(1)} %pad_maximum_fusion.4.rows_ref.a_ref, bf16[2048,1408]{1,0:T(8,128)(2,1)} %all-gather.34.cloned.1.call-done, bf16[2048,1408]{1,0:T(8,128)(2,1)} %all-gather.36.cloned.1.call-done), custom_call_target="tpu_custom_call" | custom-call | flops 14763950080 | tf_op jit(solution)/shard_map/gate_up/pallas_call | solution.py:77
  486.9 7.3 gate_up_back.2
  494.3 10.2 gate_up_in.2.refs_0_
  510.5 8.9 collective-permute-done.34
  520.4 7.1 collective-permute-start.35
  530.8 20.5 %collective-permute-done.35.refs_1_ = bf16[128,2048]{1,0:T(8,128)(2,1)} collective-permute-done((bf16[128,2048]{1,0:T(8,128)(2,1)}, bf16[128,2048]{1,0:T(8,128)(2,1)}, u32[]{:S(2)}, u32[]{:S(2)}) %collective-permute-start.35) | collective-permute-done | bytes 524320 | tf_op jit(solution)/shard_map/ppermute | solution.py:574
  579.5 13.1 %collective-permute-done.38 = bf16[128,2048]{1,0:T(8,128)(2,1)S(1)} collective-permute-done((bf16[128,2048]{1,0:T(8,128)(2,1)}, bf16[128,2048]{1,0:T(8,128)(2,1)S(1)}, u32[]{:S(2)}, u32[]{:S(2)}) %collective-permute-start.38) | collective-permute-done | bytes 524320 | tf_op jit(solution)/shard_map/ppermute | solution.py:558
  595.3 5.8 down.3
  601.2 8.7 collective-permute-done.39
  623.1 8.9 attend_back.4
  640.8 8.4 attend_back.5
  649.2 14.2 %collective-permute-done.43 = bf16[128,2048]{1,0:T(8,128)(2,1)S(1)} collective-permute-done((bf16[128,2048]{1,0:T(8,128)(2,1)S(1)}, bf16[128,2048]{1,0:T(8,128)(2,1)S(1)}, u32[]{:S(2)}, u32[]{:S(2)}) %collective-permute-start.43) | collective-permute-done | bytes 524320 | tf_op jit(solution)/shard_map/ppermute | solution.py:574
  681.2 6.3 project_in.2.refs_0_
  692.8 9.5 collective-permute-done.47
  705.9 7.7 collective-permute-done.49.refs_2_
  714.5 16.0 %collective-permute-done.48.refs_1_ = bf16[128,2048]{1,0:T(8,128)(2,1)} collective-permute-done((bf16[128,2048]{1,0:T(8,128)(2,1)}, bf16[128,2048]{1,0:T(8,128)(2,1)}, u32[]{:S(2)}, u32[]{:S(2)}) %collective-permute-start.48) | collective-permute-done | bytes 524320 | tf_op jit(solution)/shard_map/ppermute | solution.py:574
  751.1 12.8 %collective-permute-done.52 = bf16[128,2048]{1,0:T(8,128)(2,1)S(1)} collective-permute-done((bf16[128,2048]{1,0:T(8,128)(2,1)S(1)}, bf16[128,2048]{1,0:T(8,128)(2,1)S(1)}, u32[]{:S(2)}, u32[]{:S(2)}) %collective-permute-start.52) | collective-permute-done | bytes 524320 | tf_op jit(solution)/shard_map/ppermute | solution.py:558
  765.2 6.9 collective-permute-done.54
  772.1 9.4 collective-permute-done.53
  793.0 7.3 gate_up_back.3
  800.3 10.3 gate_up_in.3.refs_0_
  819.5 6.8 collective-permute-done.57
  829.3 8.3 collective-permute-done.59.refs_2_
  837.6 20.0 %collective-permute-done.62.refs_1_ = bf16[512,512]{1,0:T(8,128)(2,1)} collective-permute-done((bf16[512,512]{1,0:T(8,128)(2,1)S(1)}, bf16[512,512]{1,0:T(8,128)(2,1)}, u32[]{:S(2)}, u32[]{:S(2)}) %collective-permute-start.62) | collective-permute-done | bytes 524320 | tf_op jit(solution)/shard_map/ppermute | solution.py:534
  885.7 15.3 %collective-permute-done.63 = bf16[128,2048]{1,0:T(8,128)(2,1)} collective-permute-done((bf16[128,2048]{1,0:T(8,128)(2,1)S(1)}, bf16[128,2048]{1,0:T(8,128)(2,1)}, u32[]{:S(2)}, u32[]{:S(2)}) %collective-permute-start.63) | collective-permute-done | bytes 524320 | tf_op jit(solution)/shard_map/ppermute | solution.py:558
  903.6 13.2 %collective-permute-done.64 = bf16[128,2048]{1,0:T(8,128)(2,1)} collective-permute-done((bf16[128,2048]{1,0:T(8,128)(2,1)}, bf16[128,2048]{1,0:T(8,128)(2,1)}, u32[]{:S(2)}, u32[]{:S(2)}) %collective-permute-start.64) | collective-permute-done | bytes 524320 | tf_op jit(solution)/shard_map/ppermute | solution.py:558
  925.3 9.7 attend_back.6
  936.7 18.9 %collective-permute-done.68.refs_1_ = bf16[1408,512]{1,0:T(8,128)(2,1)S(1)} collective-permute-done((bf16[1408,512]{1,0:T(8,128)(2,1)}, bf16[1408,512]{1,0:T(8,128)(2,1)S(1)}, u32[]{:S(2)}, u32[]{:S(2)}) %collective-permute-start.68) | collective-permute-done | bytes 1441824 | tf_op jit(solution)/shard_map/ppermute | solution.py:534
  955.6 9.9 attend_back.7
  965.5 10.6 collective-permute-done.69.refs_0_
  990.2 6.0 project_in.3.refs_0_
  1033.2 19.0 %collective-permute-done.73.refs_1_ = bf16[128,2048]{1,0:T(8,128)(2,1)S(1)} collective-permute-done((bf16[128,2048]{1,0:T(8,128)(2,1)}, bf16[128,2048]{1,0:T(8,128)(2,1)S(1)}, u32[]{:S(2)}, u32[]{:S(2)}) %collective-permute-start.73) | collective-permute-done | bytes 524320 | tf_op jit(solution)/shard_map/ppermute | solution.py:574
  1069.3 9.2 finish_gate_up.2.refs_4_
  1087.2 9.4 finish_gate_up.3
  1105.2 6.9 collective-permute-done.86.refs_1_
  (584 shorter events, 428.7 us)
Async XLA Ops:
  7.2 56.4 %all-gather.22.cloned.1.call-start = ((), (), s32[]{:S(2)}) async-start(), calls=%async_computation.17 | async-start | bytes 7864320 | tf_op jit(solution)/shard_map/all_gather | solution.py:616
  10.0 108.6 %all-gather.20.cloned.1.call-start = ((), (), s32[]{:S(2)}) async-start(), calls=%async_computation.8 | async-start | bytes 2621440 | tf_op jit(solution)/shard_map/all_gather | solution.py:616
  10.9 156.7 %all-gather.24.cloned.1.call-start = ((), (), s32[]{:S(2)}) async-start(), calls=%async_computation.18 | async-start | bytes 7208960 | tf_op jit(solution)/shard_map/all_gather | solution.py:616
  16.1 198.5 %all-gather.26.cloned.1.call-start = ((), (), s32[]{:S(2)}) async-start(), calls=%async_computation.19 | async-start | bytes 7208960 | tf_op jit(solution)/shard_map/all_gather | solution.py:616
  16.7 203.2 %all-gather.28.cloned.1.call-start = ((), (), s32[]{:S(2)}) async-start(), calls=%async_computation.20 | async-start | bytes 7208960 | tf_op jit(solution)/shard_map/all_gather | solution.py:616
  19.6 28.2 %collective-permute-start = (bf16[128,2048]{1,0:T(8,128)(2,1)S(1)}, bf16[128,2048]{1,0:T(8,128)(2,1)}, u32[]{:S(2)}, u32[]{:S(2)}) collective-permute-start(bf16[128,2048]{1,0:T(8,128)(2,1)S(1)} %get-tuple-element.408), channel_id=1, source_target_pairs={{0,2},{2,0},{1,3},{3,1},{4,6},{6,4},{5,7},{7,5},{8,10},{10,8},{9,1... | collective-permute-start | bytes 1572872 | tf_op jit(solution)/shard_map/ppermute | solution.py:558
  23.6 28.0 %collective-permute-start.2 = (bf16[128,2048]{1,0:T(8,128)(2,1)S(1)}, bf16[128,2048]{1,0:T(8,128)(2,1)S(1)}, u32[]{:S(2)}, u32[]{:S(2)}) collective-permute-start(bf16[128,2048]{1,0:T(8,128)(2,1)S(1)} %get-tuple-element.408), channel_id=1, source_target_pairs={{1,0},{2,1},{3,2},{5,4},{6,5},{7,6},{9,8},{10,9},{11,10},{13,12},{... | collective-permute-start | bytes 1572872 | tf_op jit(solution)/shard_map/ppermute | solution.py:558
  24.9 26.7 %collective-permute-start.3 = (bf16[128,2048]{1,0:T(8,128)(2,1)S(1)}, bf16[128,2048]{1,0:T(8,128)(2,1)S(1)}, u32[]{:S(2)}, u32[]{:S(2)}) collective-permute-start(bf16[128,2048]{1,0:T(8,128)(2,1)S(1)} %get-tuple-element.408), channel_id=1, source_target_pairs={{0,1},{1,2},{2,3},{4,5},{5,6},{6,7},{8,9},{9,10},{10,11},{12,13},{... | collective-permute-start | bytes 1572872 | tf_op jit(solution)/shard_map/ppermute | solution.py:558
  71.9 33.8 %collective-permute-start.4 = (bf16[1024,512]{1,0:T(8,128)(2,1)}, bf16[1024,512]{1,0:T(8,128)(2,1)}, u32[]{:S(2)}, u32[]{:S(2)}) collective-permute-start(bf16[1024,512]{1,0:T(8,128)(2,1)} %get-tuple-element.185.refs_0_.refs_1_.refs_2_), channel_id=1, source_target_pairs={{0,4},{1,5},{2,6},{3,7},{8,12},{9,13},{10,14},{11,15},{16,20},{17,... | collective-permute-start | bytes 3145736 | tf_op jit(solution)/shard_map/ppermute | solution.py:602
  76.0 211.0 %all-gather.30.cloned.1.call-start = ((), (), s32[]{:S(2)}) async-start(), calls=%async_computation.21 | async-start | bytes 7864320 | tf_op jit(solution)/shard_map/all_gather | solution.py:616
  76.9 27.2 %collective-permute-start.5 = (bf16[128,2048]{1,0:T(8,128)(2,1)}, bf16[128,2048]{1,0:T(8,128)(2,1)}, u32[]{:S(2)}, u32[]{:S(2)}) collective-permute-start(bf16[128,2048]{1,0:T(8,128)(2,1)} %bitcast.108), channel_id=1, source_target_pairs={{0,2},{2,0},{1,3},{3,1},{4,6},{6,4},{5,7},{7,5},{8,10},{10,8},{9,1... | collective-permute-start | bytes 1572872 | tf_op jit(solution)/shard_map/ppermute | solution.py:558
  79.7 38.9 %collective-permute-start.7 = (bf16[128,2048]{1,0:T(8,128)(2,1)}, bf16[128,2048]{1,0:T(8,128)(2,1)}, u32[]{:S(2)}, u32[]{:S(2)}) collective-permute-start(bf16[128,2048]{1,0:T(8,128)(2,1)} %bitcast.109), channel_id=1, source_target_pairs={{1,0},{2,1},{3,2},{5,4},{6,5},{7,6},{9,8},{10,9},{11,10},{13,12},{... | collective-permute-start | bytes 1572872 | tf_op jit(solution)/shard_map/ppermute | solution.py:558
  81.0 37.6 %collective-permute-start.8 = (bf16[128,2048]{1,0:T(8,128)(2,1)}, bf16[128,2048]{1,0:T(8,128)(2,1)}, u32[]{:S(2)}, u32[]{:S(2)}) collective-permute-start(bf16[128,2048]{1,0:T(8,128)(2,1)} %bitcast.110), channel_id=1, source_target_pairs={{0,1},{1,2},{2,3},{4,5},{5,6},{6,7},{8,9},{9,10},{10,11},{12,13},{... | collective-permute-start | bytes 1572872 | tf_op jit(solution)/shard_map/ppermute | solution.py:558
  173.8 25.4 %collective-permute-start.13 = (bf16[128,2048]{1,0:T(8,128)(2,1)}, bf16[128,2048]{1,0:T(8,128)(2,1)}, u32[]{:S(2)}, u32[]{:S(2)}) collective-permute-start(bf16[128,2048]{1,0:T(8,128)(2,1)} %get-tuple-element.369), channel_id=1, source_target_pairs={{0,2},{2,0},{1,3},{3,1},{4,6},{6,4},{5,7},{7,5},{8,10},{10,8},{9,1... | collective-permute-start | bytes 1572872 | tf_op jit(solution)/shard_map/ppermute | solution.py:558
  173.8 28.0 %collective-permute-start.15 = (bf16[128,2048]{1,0:T(8,128)(2,1)}, bf16[128,2048]{1,0:T(8,128)(2,1)}, u32[]{:S(2)}, u32[]{:S(2)}) collective-permute-start(bf16[128,2048]{1,0:T(8,128)(2,1)} %get-tuple-element.369), channel_id=1, source_target_pairs={{1,0},{2,1},{3,2},{5,4},{6,5},{7,6},{9,8},{10,9},{11,10},{13,12},{... | collective-permute-start | bytes 1572872 | tf_op jit(solution)/shard_map/ppermute | solution.py:558
  175.1 26.7 %collective-permute-start.16 = (bf16[128,2048]{1,0:T(8,128)(2,1)}, bf16[128,2048]{1,0:T(8,128)(2,1)}, u32[]{:S(2)}, u32[]{:S(2)}) collective-permute-start(bf16[128,2048]{1,0:T(8,128)(2,1)} %get-tuple-element.369), channel_id=1, source_target_pairs={{0,1},{1,2},{2,3},{4,5},{5,6},{6,7},{8,9},{9,10},{10,11},{12,13},{... | collective-permute-start | bytes 1572872 | tf_op jit(solution)/shard_map/ppermute | solution.py:558
  219.9 116.2 %all-gather.32.cloned.1.call-start = ((), (), s32[]{:S(2)}) async-start(), calls=%async_computation.22 | async-start | bytes 2621440 | tf_op jit(solution)/shard_map/all_gather | solution.py:616
  235.8 102.3 %all-gather.34.cloned.1.call-start = ((), (), s32[]{:S(2)}) async-start(), calls=%async_computation.23 | async-start | bytes 7208960 | tf_op jit(solution)/shard_map/all_gather | solution.py:616
  236.5 148.5 %all-gather.36.cloned.1.call-start = ((), (), s32[]{:S(2)}) async-start(), calls=%async_computation.24 | async-start | bytes 7208960 | tf_op jit(solution)/shard_map/all_gather | solution.py:616
  259.9 25.8 %collective-permute-start.18 = (bf16[128,2048]{1,0:T(8,128)(2,1)S(1)}, bf16[128,2048]{1,0:T(8,128)(2,1)S(1)}, u32[]{:S(2)}, u32[]{:S(2)}) collective-permute-start(bf16[128,2048]{1,0:T(8,128)(2,1)S(1)} %add_convert_fusion.9), channel_id=1, source_target_pairs={{0,2},{2,0},{1,3},{3,1},{4,6},{6,4},{5,7},{7,5},{8,10},{10,8},{9,1... | collective-permute-start | bytes 1572872 | tf_op jit(solution)/shard_map/ppermute | solution.py:574
  287.0 143.0 %all-gather.38.cloned.1.call-start = ((), (), s32[]{:S(2)}) async-start(), calls=%async_computation.25 | async-start | bytes 7208960 | tf_op jit(solution)/shard_map/all_gather | solution.py:616
  293.3 27.3 %collective-permute-start.21 = (bf16[128,2048]{1,0:T(8,128)(2,1)}, bf16[128,2048]{1,0:T(8,128)(2,1)}, u32[]{:S(2)}, u32[]{:S(2)}) collective-permute-start(bf16[128,2048]{1,0:T(8,128)(2,1)} %get-tuple-element.367), channel_id=1, source_target_pairs={{0,2},{2,0},{1,3},{3,1},{4,6},{6,4},{5,7},{7,5},{8,10},{10,8},{9,1... | collective-permute-start | bytes 1572872 | tf_op jit(solution)/shard_map/ppermute | solution.py:558
  293.3 30.3 %collective-permute-start.23 = (bf16[128,2048]{1,0:T(8,128)(2,1)}, bf16[128,2048]{1,0:T(8,128)(2,1)}, u32[]{:S(2)}, u32[]{:S(2)}) collective-permute-start(bf16[128,2048]{1,0:T(8,128)(2,1)} %get-tuple-element.367), channel_id=1, source_target_pairs={{1,0},{2,1},{3,2},{5,4},{6,5},{7,6},{9,8},{10,9},{11,10},{13,12},{... | collective-permute-start | bytes 1572872 | tf_op jit(solution)/shard_map/ppermute | solution.py:558
  294.6 29.0 %collective-permute-start.24 = (bf16[128,2048]{1,0:T(8,128)(2,1)}, bf16[128,2048]{1,0:T(8,128)(2,1)}, u32[]{:S(2)}, u32[]{:S(2)}) collective-permute-start(bf16[128,2048]{1,0:T(8,128)(2,1)} %get-tuple-element.367), channel_id=1, source_target_pairs={{0,1},{1,2},{2,3},{4,5},{5,6},{6,7},{8,9},{9,10},{10,11},{12,13},{... | collective-permute-start | bytes 1572872 | tf_op jit(solution)/shard_map/ppermute | solution.py:558
  338.1 341.6 %reduce-scatter.9.cloned.1.call-start = ((), (), s32[]{:S(2)}) async-start(), calls=%async_computation.9 | async-start | bytes 7208960 | tf_op jit(solution)/shard_map/reduce_scatter | solution.py:620
  347.0 26.2 %collective-permute-start.25 = (bf16[1024,512]{1,0:T(8,128)(2,1)S(1)}, bf16[1024,512]{1,0:T(8,128)(2,1)S(1)}, u32[]{:S(2)}, u32[]{:S(2)}) collective-permute-start(bf16[1024,512]{1,0:T(8,128)(2,1)S(1)} %get-tuple-element.215.refs_0_.refs_1_.refs_2_), channel_id=1, source_target_pairs={{0,4},{1,5},{2,6},{3,7},{8,12},{9,13},{10,14},{11,15},{16,20},{17,... | collective-permute-start | bytes 3145736 | tf_op jit(solution)/shard_map/ppermute | solution.py:602
  392.2 24.6 %collective-permute-start.29 = (bf16[128,2048]{1,0:T(8,128)(2,1)S(1)}, bf16[128,2048]{1,0:T(8,128)(2,1)S(1)}, u32[]{:S(2)}, u32[]{:S(2)}) collective-permute-start(bf16[128,2048]{1,0:T(8,128)(2,1)S(1)} %get-tuple-element.400), channel_id=1, source_target_pairs={{3,2},{2,1},{1,0},{7,6},{6,5},{5,4},{11,10},{10,9},{9,8},{15,14},{... | collective-permute-start | bytes 1572872 | tf_op jit(solution)/shard_map/ppermute | solution.py:574
  404.6 24.0 %collective-permute-start.27 = (bf16[128,2048]{1,0:T(8,128)(2,1)S(1)}, bf16[128,2048]{1,0:T(8,128)(2,1)S(1)}, u32[]{:S(2)}, u32[]{:S(2)}) collective-permute-start(bf16[128,2048]{1,0:T(8,128)(2,1)S(1)} %add_convert_fusion.7), channel_id=1, source_target_pairs={{0,2},{2,0},{1,3},{3,1},{4,6},{6,4},{5,7},{7,5},{8,10},{10,8},{9,1... | collective-permute-start | bytes 1572872 | tf_op jit(solution)/shard_map/ppermute | solution.py:574
  435.4 26.9 %collective-permute-start.30 = (bf16[128,2048]{1,0:T(8,128)(2,1)S(1)}, bf16[128,2048]{1,0:T(8,128)(2,1)S(1)}, u32[]{:S(2)}, u32[]{:S(2)}) collective-permute-start(bf16[128,2048]{1,0:T(8,128)(2,1)S(1)} %get-tuple-element.365), channel_id=1, source_target_pairs={{0,2},{2,0},{1,3},{3,1},{4,6},{6,4},{5,7},{7,5},{8,10},{10,8},{9,1... | collective-permute-start | bytes 1572872 | tf_op jit(solution)/shard_map/ppermute | solution.py:558
  436.2 27.6 %collective-permute-start.32 = (bf16[128,2048]{1,0:T(8,128)(2,1)S(1)}, bf16[128,2048]{1,0:T(8,128)(2,1)S(1)}, u32[]{:S(2)}, u32[]{:S(2)}) collective-permute-start(bf16[128,2048]{1,0:T(8,128)(2,1)S(1)} %get-tuple-element.365), channel_id=1, source_target_pairs={{1,0},{2,1},{3,2},{5,4},{6,5},{7,6},{9,8},{10,9},{11,10},{13,12},{... | collective-permute-start | bytes 1572872 | tf_op jit(solution)/shard_map/ppermute | solution.py:558
  437.5 26.3 %collective-permute-start.33 = (bf16[128,2048]{1,0:T(8,128)(2,1)S(1)}, bf16[128,2048]{1,0:T(8,128)(2,1)S(1)}, u32[]{:S(2)}, u32[]{:S(2)}) collective-permute-start(bf16[128,2048]{1,0:T(8,128)(2,1)S(1)} %get-tuple-element.365), channel_id=1, source_target_pairs={{0,1},{1,2},{2,3},{4,5},{5,6},{6,7},{8,9},{9,10},{10,11},{12,13},{... | collective-permute-start | bytes 1572872 | tf_op jit(solution)/shard_map/ppermute | solution.py:558
  507.1 23.7 %collective-permute-start.36 = (bf16[128,2048]{1,0:T(8,128)(2,1)}, bf16[128,2048]{1,0:T(8,128)(2,1)}, u32[]{:S(2)}, u32[]{:S(2)}) collective-permute-start(bf16[128,2048]{1,0:T(8,128)(2,1)} %get-tuple-element.397), channel_id=1, source_target_pairs={{0,1},{1,2},{2,3},{4,5},{5,6},{6,7},{8,9},{9,10},{10,11},{12,13},{... | collective-permute-start | bytes 1572872 | tf_op jit(solution)/shard_map/ppermute | solution.py:574
  520.4 30.9 %collective-permute-start.35 = (bf16[128,2048]{1,0:T(8,128)(2,1)}, bf16[128,2048]{1,0:T(8,128)(2,1)}, u32[]{:S(2)}, u32[]{:S(2)}) collective-permute-start(bf16[128,2048]{1,0:T(8,128)(2,1)} %add_convert_fusion.5), channel_id=1, source_target_pairs={{0,2},{2,0},{1,3},{3,1},{4,6},{6,4},{5,7},{7,5},{8,10},{10,8},{9,1... | collective-permute-start | bytes 1572872 | tf_op jit(solution)/shard_map/ppermute | solution.py:574
  563.6 179.9 %reduce-scatter.11.cloned.1.call-start = ((), (), s32[]{:S(2)}) async-start(), calls=%async_computation.10 | async-start | bytes 7208960 | tf_op jit(solution)/shard_map/reduce_scatter | solution.py:620
  572.4 210.8 %reduce-scatter.15.cloned.1.call-start = ((), (), s32[]{:S(2)}) async-start(), calls=%async_computation.12 | async-start | bytes 2621440 | tf_op jit(solution)/shard_map/reduce_scatter | solution.py:620
  573.6 27.5 %collective-permute-start.40 = (bf16[128,2048]{1,0:T(8,128)(2,1)}, bf16[128,2048]{1,0:T(8,128)(2,1)S(1)}, u32[]{:S(2)}, u32[]{:S(2)}) collective-permute-start(bf16[128,2048]{1,0:T(8,128)(2,1)} %copy-done.37), channel_id=1, source_target_pairs={{1,0},{2,1},{3,2},{5,4},{6,5},{7,6},{9,8},{10,9},{11,10},{13,12},{... | collective-permute-start | bytes 1572872 | tf_op jit(solution)/shard_map/ppermute | solution.py:558
  574.9 26.2 %collective-permute-start.41 = (bf16[128,2048]{1,0:T(8,128)(2,1)}, bf16[128,2048]{1,0:T(8,128)(2,1)S(1)}, u32[]{:S(2)}, u32[]{:S(2)}) collective-permute-start(bf16[128,2048]{1,0:T(8,128)(2,1)} %copy-done.37), channel_id=1, source_target_pairs={{0,1},{1,2},{2,3},{4,5},{5,6},{6,7},{8,9},{9,10},{10,11},{12,13},{... | collective-permute-start | bytes 1572872 | tf_op jit(solution)/shard_map/ppermute | solution.py:558
  611.4 37.8 %collective-permute-start.45 = (bf16[128,2048]{1,0:T(8,128)(2,1)}, bf16[128,2048]{1,0:T(8,128)(2,1)S(1)}, u32[]{:S(2)}, u32[]{:S(2)}) collective-permute-start(bf16[128,2048]{1,0:T(8,128)(2,1)} %get-tuple-element.394), channel_id=1, source_target_pairs={{3,2},{2,1},{1,0},{7,6},{6,5},{5,4},{11,10},{10,9},{9,8},{15,14},{... | collective-permute-start | bytes 1572872 | tf_op jit(solution)/shard_map/ppermute | solution.py:574
  612.8 36.4 %collective-permute-start.44 = (bf16[128,2048]{1,0:T(8,128)(2,1)}, bf16[128,2048]{1,0:T(8,128)(2,1)}, u32[]{:S(2)}, u32[]{:S(2)}) collective-permute-start(bf16[128,2048]{1,0:T(8,128)(2,1)} %get-tuple-element.393), channel_id=1, source_target_pairs={{0,1},{1,2},{2,3},{4,5},{5,6},{6,7},{8,9},{9,10},{10,11},{12,13},{... | collective-permute-start | bytes 1572872 | tf_op jit(solution)/shard_map/ppermute | solution.py:574
  632.0 33.6 %collective-permute-start.46 = (bf16[1024,512]{1,0:T(8,128)(2,1)S(1)}, bf16[1024,512]{1,0:T(8,128)(2,1)S(1)}, u32[]{:S(2)}, u32[]{:S(2)}) collective-permute-start(bf16[1024,512]{1,0:T(8,128)(2,1)S(1)} %get-tuple-element.243), channel_id=1, source_target_pairs={{4,0},{5,1},{6,2},{7,3},{12,8},{13,9},{14,10},{15,11},{20,16},{21,... | collective-permute-start | bytes 3145736 | tf_op jit(solution)/shard_map/ppermute | solution.py:609
  671.2 112.0 %reduce-scatter.13.cloned.1.call-start = ((), (), s32[]{:S(2)}) async-start(), calls=%async_computation.11 | async-start | bytes 7208960 | tf_op jit(solution)/shard_map/reduce_scatter | solution.py:620
  679.7 177.9 %reduce-scatter.17.cloned.1.call-start = ((), (), s32[]{:S(2)}) async-start(), calls=%async_computation.13 | async-start | bytes 7864320 | tf_op jit(solution)/shard_map/reduce_scatter | solution.py:620
  690.0 40.4 %collective-permute-start.51 = (bf16[1408,512]{1,0:T(8,128)(2,1)}, bf16[1408,512]{1,0:T(8,128)(2,1)}, u32[]{:S(2)}, u32[]{:S(2)}) collective-permute-start(bf16[1408,512]{1,0:T(8,128)(2,1)} %reduce-scatter.9.cloned.1.call-done.refs_0_), channel_id=1, source_target_pairs={{0,4},{4,0},{1,5},{5,1},{2,6},{6,2},{3,7},{7,3},{8,12},{12,8},{9,1... | collective-permute-start | bytes 4325384 | tf_op jit(solution)/shard_map/ppermute | solution.py:534
  690.2 23.5 %collective-permute-start.49 = (bf16[128,2048]{1,0:T(8,128)(2,1)}, bf16[128,2048]{1,0:T(8,128)(2,1)S(1)}, u32[]{:S(2)}, u32[]{:S(2)}) collective-permute-start(bf16[128,2048]{1,0:T(8,128)(2,1)} %get-tuple-element.391), channel_id=1, source_target_pairs={{0,1},{1,2},{2,3},{4,5},{5,6},{6,7},{8,9},{9,10},{10,11},{12,13},{... | collective-permute-start | bytes 1572872 | tf_op jit(solution)/shard_map/ppermute | solution.py:574
  703.3 27.2 %collective-permute-start.48 = (bf16[128,2048]{1,0:T(8,128)(2,1)}, bf16[128,2048]{1,0:T(8,128)(2,1)}, u32[]{:S(2)}, u32[]{:S(2)}) collective-permute-start(bf16[128,2048]{1,0:T(8,128)(2,1)} %add_convert_fusion.2), channel_id=1, source_target_pairs={{0,2},{2,0},{1,3},{3,1},{4,6},{6,4},{5,7},{7,5},{8,10},{10,8},{9,1... | collective-permute-start | bytes 1572872 | tf_op jit(solution)/shard_map/ppermute | solution.py:574
  743.4 177.3 %reduce-scatter.19.cloned.1.call-start = ((), (), s32[]{:S(2)}) async-start(), calls=%async_computation.14 | async-start | bytes 7208960 | tf_op jit(solution)/shard_map/reduce_scatter | solution.py:620
  743.6 39.6 %collective-permute-start.56 = (bf16[512,1408]{1,0:T(8,128)(2,1)}, bf16[512,1408]{1,0:T(8,128)(2,1)}, u32[]{:S(2)}, u32[]{:S(2)}) collective-permute-start(bf16[512,1408]{1,0:T(8,128)(2,1)} %reduce-scatter.11.cloned.1.call-done.refs_0_), channel_id=1, source_target_pairs={{0,4},{4,0},{1,5},{5,1},{2,6},{6,2},{3,7},{7,3},{8,12},{12,8},{9,1... | collective-permute-start | bytes 4325384 | tf_op jit(solution)/shard_map/ppermute | solution.py:534
  745.1 27.1 %collective-permute-start.54 = (bf16[128,2048]{1,0:T(8,128)(2,1)S(1)}, bf16[128,2048]{1,0:T(8,128)(2,1)S(1)}, u32[]{:S(2)}, u32[]{:S(2)}) collective-permute-start(bf16[128,2048]{1,0:T(8,128)(2,1)S(1)} %get-tuple-element.260), channel_id=1, source_target_pairs={{1,0},{2,1},{3,2},{5,4},{6,5},{7,6},{9,8},{10,9},{11,10},{13,12},{... | collective-permute-start | bytes 1572872 | tf_op jit(solution)/shard_map/ppermute | solution.py:558
  746.4 25.8 %collective-permute-start.55 = (bf16[128,2048]{1,0:T(8,128)(2,1)S(1)}, bf16[128,2048]{1,0:T(8,128)(2,1)S(1)}, u32[]{:S(2)}, u32[]{:S(2)}) collective-permute-start(bf16[128,2048]{1,0:T(8,128)(2,1)S(1)} %get-tuple-element.260), channel_id=1, source_target_pairs={{0,1},{1,2},{2,3},{4,5},{5,6},{6,7},{8,9},{9,10},{10,11},{12,13},{... | collective-permute-start | bytes 1572872 | tf_op jit(solution)/shard_map/ppermute | solution.py:558
  791.4 193.6 %reduce-scatter.21.cloned.1.call-start = ((), (), s32[]{:S(2)}) async-start(), calls=%async_computation.15 | async-start | bytes 7208960 | tf_op jit(solution)/shard_map/reduce_scatter | solution.py:620
  814.0 43.6 %collective-permute-start.61 = (bf16[512,1408]{1,0:T(8,128)(2,1)}, bf16[512,1408]{1,0:T(8,128)(2,1)}, u32[]{:S(2)}, u32[]{:S(2)}) collective-permute-start(bf16[512,1408]{1,0:T(8,128)(2,1)} %reduce-scatter.13.cloned.1.call-done.refs_2_), channel_id=1, source_target_pairs={{0,4},{4,0},{1,5},{5,1},{2,6},{6,2},{3,7},{7,3},{8,12},{12,8},{9,1... | collective-permute-start | bytes 4325384 | tf_op jit(solution)/shard_map/ppermute | solution.py:534
  818.1 39.5 %collective-permute-start.62 = (bf16[512,512]{1,0:T(8,128)(2,1)S(1)}, bf16[512,512]{1,0:T(8,128)(2,1)}, u32[]{:S(2)}, u32[]{:S(2)}) collective-permute-start(bf16[512,512]{1,0:T(8,128)(2,1)S(1)} %copy-done.62), channel_id=1, source_target_pairs={{0,4},{4,0},{1,5},{5,1},{2,6},{6,2},{3,7},{7,3},{8,12},{12,8},{9,1... | collective-permute-start | bytes 1572872 | tf_op jit(solution)/shard_map/ppermute | solution.py:534
  827.2 30.4 %collective-permute-start.58 = (bf16[128,2048]{1,0:T(8,128)(2,1)}, bf16[128,2048]{1,0:T(8,128)(2,1)}, u32[]{:S(2)}, u32[]{:S(2)}) collective-permute-start(bf16[128,2048]{1,0:T(8,128)(2,1)} %add_convert_fusion.1), channel_id=1, source_target_pairs={{0,2},{2,0},{1,3},{3,1},{4,6},{6,4},{5,7},{7,5},{8,10},{10,8},{9,1... | collective-permute-start | bytes 1572872 | tf_op jit(solution)/shard_map/ppermute | solution.py:574
  869.3 132.0 %reduce-scatter.23.cloned.1.call-start = ((), (), s32[]{:S(2)}) async-start(), calls=%async_computation.16 | async-start | bytes 7208960 | tf_op jit(solution)/shard_map/reduce_scatter | solution.py:620
  877.8 42.9 %collective-permute-start.67 = (bf16[512,1536]{1,0:T(8,128)(2,1)}, bf16[512,1536]{1,0:T(8,128)(2,1)}, u32[]{:S(2)}, u32[]{:S(2)}) collective-permute-start(bf16[512,1536]{1,0:T(8,128)(2,1)} %reduce-scatter.17.cloned.1.call-done.refs_0_), channel_id=1, source_target_pairs={{0,4},{4,0},{1,5},{5,1},{2,6},{6,2},{3,7},{7,3},{8,12},{12,8},{9,1... | collective-permute-start | bytes 4718600 | tf_op jit(solution)/shard_map/ppermute | solution.py:534
  879.0 24.6 %collective-permute-start.65 = (bf16[128,2048]{1,0:T(8,128)(2,1)S(1)}, bf16[128,2048]{1,0:T(8,128)(2,1)}, u32[]{:S(2)}, u32[]{:S(2)}) collective-permute-start(bf16[128,2048]{1,0:T(8,128)(2,1)S(1)} %get-tuple-element.281), channel_id=1, source_target_pairs={{1,0},{2,1},{3,2},{5,4},{6,5},{7,6},{9,8},{10,9},{11,10},{13,12},{... | collective-permute-start | bytes 1572872 | tf_op jit(solution)/shard_map/ppermute | solution.py:558
  920.8 34.8 %collective-permute-start.68 = (bf16[1408,512]{1,0:T(8,128)(2,1)}, bf16[1408,512]{1,0:T(8,128)(2,1)S(1)}, u32[]{:S(2)}, u32[]{:S(2)}) collective-permute-start(bf16[1408,512]{1,0:T(8,128)(2,1)} %reduce-scatter.19.cloned.1.call-done.refs_0_), channel_id=1, source_target_pairs={{0,4},{4,0},{1,5},{5,1},{2,6},{6,2},{3,7},{7,3},{8,12},{12,8},{9,1... | collective-permute-start | bytes 4325384 | tf_op jit(solution)/shard_map/ppermute | solution.py:534
  935.0 41.1 %collective-permute-start.69 = (bf16[1024,512]{1,0:T(8,128)(2,1)S(1)}, bf16[1024,512]{1,0:T(8,128)(2,1)S(1)}, u32[]{:S(2)}, u32[]{:S(2)}) collective-permute-start(bf16[1024,512]{1,0:T(8,128)(2,1)S(1)} %get-tuple-element.293), channel_id=1, source_target_pairs={{4,0},{5,1},{6,2},{7,3},{12,8},{13,9},{14,10},{15,11},{20,16},{21,... | collective-permute-start | bytes 3145736 | tf_op jit(solution)/shard_map/ppermute | solution.py:609
  990.2 41.5 %collective-permute-start.76 = (bf16[512,1408]{1,0:T(8,128)(2,1)}, bf16[512,1408]{1,0:T(8,128)(2,1)}, u32[]{:S(2)}, u32[]{:S(2)}) collective-permute-start(bf16[512,1408]{1,0:T(8,128)(2,1)} %reduce-scatter.21.cloned.1.call-done.refs_0_), channel_id=1, source_target_pairs={{0,4},{4,0},{1,5},{5,1},{2,6},{6,2},{3,7},{7,3},{8,12},{12,8},{9,1... | collective-permute-start | bytes 4325384 | tf_op jit(solution)/shard_map/ppermute | solution.py:534
  1011.1 41.1 %collective-permute-start.77 = (bf16[512,1536]{1,0:T(8,128)(2,1)}, bf16[512,1536]{1,0:T(8,128)(2,1)}, u32[]{:S(2)}, u32[]{:S(2)}) collective-permute-start(bf16[512,1536]{1,0:T(8,128)(2,1)} %split.30), channel_id=1, source_target_pairs={{0,16},{8,24},{16,0},{24,8},{1,17},{9,25},{17,1},{25,9},{2,18},{10... | collective-permute-start | bytes 4718600 | tf_op jit(solution)/shard_map/ppermute | solution.py:534
  1019.0 33.2 %collective-permute-start.73 = (bf16[128,2048]{1,0:T(8,128)(2,1)}, bf16[128,2048]{1,0:T(8,128)(2,1)S(1)}, u32[]{:S(2)}, u32[]{:S(2)}) collective-permute-start(bf16[128,2048]{1,0:T(8,128)(2,1)} %add_convert_fusion), channel_id=1, source_target_pairs={{0,2},{2,0},{1,3},{3,1},{4,6},{6,4},{5,7},{7,5},{8,10},{10,8},{9,1... | collective-permute-start | bytes 1572872 | tf_op jit(solution)/shard_map/ppermute | solution.py:574
  1031.7 55.5 %collective-permute-start.82 = (bf16[512,1408]{1,0:T(8,128)(2,1)}, bf16[512,1408]{1,0:T(8,128)(2,1)}, u32[]{:S(2)}, u32[]{:S(2)}) collective-permute-start(bf16[512,1408]{1,0:T(8,128)(2,1)} %reduce-scatter.23.cloned.1.call-done.refs_2_), channel_id=1, source_target_pairs={{0,4},{4,0},{1,5},{5,1},{2,6},{6,2},{3,7},{7,3},{8,12},{12,8},{9,1... | collective-permute-start | bytes 4325384 | tf_op jit(solution)/shard_map/ppermute | solution.py:534
  1059.9 53.7 %collective-permute-start.84 = (bf16[512,1536]{1,0:T(8,128)(2,1)}, bf16[512,1536]{1,0:T(8,128)(2,1)}, u32[]{:S(2)}, u32[]{:S(2)}) collective-permute-start(bf16[512,1536]{1,0:T(8,128)(2,1)} %fusion.refs_0_), channel_id=1, source_target_pairs={{0,4},{4,0},{1,5},{5,1},{2,6},{6,2},{3,7},{7,3},{8,12},{12,8},{9,1... | collective-permute-start | bytes 4718600 | tf_op jit(solution)/shard_map/ppermute | solution.py:534
  1063.0 34.2 %collective-permute-start.85 = (bf16[512,512]{1,0:T(8,128)(2,1)S(1)}, bf16[512,512]{1,0:T(8,128)(2,1)S(1)}, u32[]{:S(2)}, u32[]{:S(2)}) collective-permute-start(bf16[512,512]{1,0:T(8,128)(2,1)S(1)} %split.31), channel_id=1, source_target_pairs={{0,16},{8,24},{16,0},{24,8},{1,17},{9,25},{17,1},{25,9},{2,18},{10... | collective-permute-start | bytes 1572872 | tf_op jit(solution)/shard_map/ppermute | solution.py:534
  (161 other events, 2581.1 us)
Sparse Core Ops, SparseCore 0:
  10.2 49.0 all-gather.21
  61.4 22.5 all-gather.19
  86.2 43.3 all-gather.23
  131.6 43.3 all-gather.25
  176.5 43.3 all-gather.27
  221.9 46.3 all-gather.29
  270.5 22.5 all-gather.31
  294.6 43.3 all-gather.33
  339.6 43.3 all-gather.35
  385.1 43.3 all-gather.37
  563.7 52.0 reduce-scatter.8
  619.0 54.8 reduce-scatter.10
  676.4 31.4 reduce-scatter.14
  711.0 54.8 reduce-scatter.12
  768.9 58.3 reduce-scatter.16
  830.4 54.8 reduce-scatter.18
  888.3 54.8 reduce-scatter.20
  946.3 54.8 reduce-scatter.22

commit v9 on v8

--- a/solution.py
+++ b/solution.py
@@ -834,8 +834,6 @@
         if layer > 0:
             mine["down"] = out_job(activated, branch)
         mine["gate"] = in_job(rows_two, grad_gate)
-        if layer == 0:
-            mine["up"] = in_job(rows_two, grad_up)
         top = layer + 1 == LAYERS
         if top:
             late, hidden_low = lax.optimization_barrier((activated, hidden_low))
@@ -851,6 +849,8 @@
         shared = (queries, grad_attended, attended, lse)
         far_queries, far_grads = attend_back(qpos, far_places, *shared, far_kv, LOW, [])
         if layer == 0:
+            far_queries, grad_up = lax.optimization_barrier((far_queries, grad_up))
+            mine["up"] = in_job(rows_two, grad_up)
             far_queries = meanwhile(far_queries, mine["down"])
         returned = plan.far_key_grads(far_grads)
         grad_queries, grad_kv = attend_back(

time: 1140 us -> 1140 us (level)
    ppermute x19, waiting for transfers between devices: 56.2 us -> 69.8 us  [swapped(): return lax.ppermute(value, axis, [(i, i ^ mask) for i in range(count)])]
    unnamed x241 -> x261, local copies, waits for them, and re-layouts: 53.7 us -> 57 us
where the time goes in v9:
time: 1140 us; the launch traced here: 1130 us
  waiting for transfers between devices  517 us (45%)
  Pallas kernels  258 us (23%)
  starting transfers between devices  183 us (16%)
  local copies, waits for them, and re-layouts  86.5 us (8%)
  other arithmetic  70 us (6%)
  between operations  16.9 us (1%)
    ppermute x32, waiting for transfers between devices, sum_rows(): send = lambda v, *route: lax.ppermute(v, 'tensor', list(route))  206 us
    ppermute x32, waiting for transfers between devices, gather_rows(): send = lambda v, *route: lax.ppermute(v, 'tensor', list(route))  199 us
    pallas_call x32, Pallas kernels, tiled(): pl.pallas_call(kernel, grid=(steps,), in_specs=[pl.BlockSpec(block, index...  160 us
    ppermute x32, starting transfers between devices, sum_rows(): send = lambda v, *route: lax.ppermute(v, 'tensor', list(route))  79.9 us
    ppermute x32, starting transfers between devices, gather_rows(): send = lambda v, *route: lax.ppermute(v, 'tensor', list(route))  77.4 us
    ppermute x19, waiting for transfers between devices, swapped(): return lax.ppermute(value, axis, [(i, i ^ mask) for i in range(count)])  69.8 us
    unnamed x261, local copies, waits for them, and re-layouts  57 us
    pallas_call x6, Pallas kernels, group_call(): pl.pallas_call(kernel, grid=(width // group,), in_specs=common + [specs['...  56.9 us
  transfers between devices with their start and end apart: 105, of which 49 were waited for; matrix products, arithmetic and copies ran while one was open for 8% of the time, Pallas kernels for 19%

profile of v9, /device:TPU:0, one launch (start us, length us, event | category | flops | bytes accessed | tf_op | source)
XLA Modules:
  0.0 1131.9 jit_solution(12315327804985876501)
XLA Ops:
  31.4 16.3 %collective-permute-done = bf16[128,2048]{1,0:T(8,128)(2,1)} collective-permute-done((bf16[128,2048]{1,0:T(8,128)(2,1)S(1)}, bf16[128,2048]{1,0:T(8,128)(2,1)}, u32[]{:S(2)}, u32[]{:S(2)}) %collective-permute-start) | collective-permute-done | bytes 524320 | tf_op jit(solution)/shard_map/ppermute | solution.py:558
  51.7 10.4 collective-permute-done.1
  63.6 8.3 project.2
  91.9 12.3 %collective-permute-done.5 = bf16[128,2048]{1,0:T(8,128)(2,1)} collective-permute-done((bf16[128,2048]{1,0:T(8,128)(2,1)}, bf16[128,2048]{1,0:T(8,128)(2,1)}, u32[]{:S(2)}, u32[]{:S(2)}) %collective-permute-start.5) | collective-permute-done | bytes 524320 | tf_op jit(solution)/shard_map/ppermute | solution.py:558
  105.7 10.8 attend.2
  124.8 5.7 collective-permute-start.9
  136.4 6.4 collective-permute-done.9
  145.5 8.5 collective-permute-done.11
  154.0 12.2 %collective-permute-done.10 = bf16[128,2048]{1,0:T(8,128)(2,1)S(1)} collective-permute-done((bf16[128,2048]{1,0:T(8,128)(2,1)S(1)}, bf16[128,2048]{1,0:T(8,128)(2,1)S(1)}, u32[]{:S(2)}, u32[]{:S(2)}) %collective-permute-start.10) | collective-permute-done | bytes 524320 | tf_op jit(solution)/shard_map/ppermute | solution.py:574
  175.1 8.3 collective-permute-start.16
  183.4 15.8 %collective-permute-done.13 = bf16[128,2048]{1,0:T(8,128)(2,1)} collective-permute-done((bf16[128,2048]{1,0:T(8,128)(2,1)}, bf16[128,2048]{1,0:T(8,128)(2,1)}, u32[]{:S(2)}, u32[]{:S(2)}) %collective-permute-start.13) | collective-permute-done | bytes 524320 | tf_op jit(solution)/shard_map/ppermute | solution.py:558
  201.8 8.8 collective-permute-done.14
  223.4 11.2 gate_up.2
  237.9 5.9 down.2
  253.4 6.3 collective-permute-done.17
  263.3 7.6 collective-permute-done.19
  271.0 14.7 %collective-permute-done.18 = bf16[128,2048]{1,0:T(8,128)(2,1)S(1)} collective-permute-done((bf16[128,2048]{1,0:T(8,128)(2,1)S(1)}, bf16[128,2048]{1,0:T(8,128)(2,1)S(1)}, u32[]{:S(2)}, u32[]{:S(2)}) %collective-permute-start.18) | collective-permute-done | bytes 524320 | tf_op jit(solution)/shard_map/ppermute | solution.py:574
  294.6 8.3 collective-permute-start.24
  302.8 17.8 %collective-permute-done.21 = bf16[128,2048]{1,0:T(8,128)(2,1)} collective-permute-done((bf16[128,2048]{1,0:T(8,128)(2,1)}, bf16[128,2048]{1,0:T(8,128)(2,1)}, u32[]{:S(2)}, u32[]{:S(2)}) %collective-permute-start.21) | collective-permute-done | bytes 524320 | tf_op jit(solution)/shard_map/ppermute | solution.py:558
  323.6 8.4 collective-permute-done.22
  339.8 7.2 project.3
  350.4 22.8 %collective-permute-done.25.refs_2_.refs_3_.refs_0_.refs_1_ = bf16[1024,512]{1,0:T(8,128)(2,1)S(1)} collective-permute-done((bf16[1024,512]{1,0:T(8,128)(2,1)S(1)}, bf16[1024,512]{1,0:T(8,128)(2,1)S(1)}, u32[]{:S(2)}, u32[]{:S(2)}) %collective-permute-start.25) | collective-permute-done | bytes 1048608 | tf_op jit(solution)/shard_map/ppermute | solution.py:602
  373.2 9.8 attend.3
  398.1 6.4 collective-permute-done.26
  408.2 8.7 collective-permute-done.29
  416.9 11.8 %collective-permute-done.27 = bf16[128,2048]{1,0:T(8,128)(2,1)S(1)} collective-permute-done((bf16[128,2048]{1,0:T(8,128)(2,1)S(1)}, bf16[128,2048]{1,0:T(8,128)(2,1)S(1)}, u32[]{:S(2)}, u32[]{:S(2)}) %collective-permute-start.27) | collective-permute-done | bytes 524320 | tf_op jit(solution)/shard_map/ppermute | solution.py:574
  437.5 7.5 collective-permute-start.33
  445.1 17.3 %collective-permute-done.30 = bf16[128,2048]{1,0:T(8,128)(2,1)S(1)} collective-permute-done((bf16[128,2048]{1,0:T(8,128)(2,1)S(1)}, bf16[128,2048]{1,0:T(8,128)(2,1)S(1)}, u32[]{:S(2)}, u32[]{:S(2)}) %collective-permute-start.30) | collective-permute-done | bytes 524320 | tf_op jit(solution)/shard_map/ppermute | solution.py:558
  463.9 10.1 collective-permute-done.31
  474.3 11.5 %gate_up.3 = (f32[512,1408]{1,0:T(8,128)}, f32[512,1408]{1,0:T(8,128)}, bf16[512,1408]{1,0:T(8,128)(2,1)S(1)}) custom-call(bf16[512,2048]{1,0:T(8,128)(2,1)S(1)} %pad_maximum_fusion.4.rows_ref.a_ref, bf16[2048,1408]{1,0:T(8,128)(2,1)} %all-gather.34.cloned.1.call-done, bf16[2048,1408]{1,0:T(8,128)(2,1)} %all-gather.36.cloned.1.call-done), custom_call_target="tpu_custom_call" | custom-call | flops 14763950080 | tf_op jit(solution)/shard_map/gate_up/pallas_call | solution.py:77
  487.0 7.3 gate_up_back.2
  494.3 10.3 gate_up_in.2.refs_0_
  510.6 8.9 collective-permute-done.34
  520.5 7.1 collective-permute-start.35
  530.9 20.5 %collective-permute-done.35.refs_1_ = bf16[128,2048]{1,0:T(8,128)(2,1)} collective-permute-done((bf16[128,2048]{1,0:T(8,128)(2,1)}, bf16[128,2048]{1,0:T(8,128)(2,1)}, u32[]{:S(2)}, u32[]{:S(2)}) %collective-permute-start.35) | collective-permute-done | bytes 524320 | tf_op jit(solution)/shard_map/ppermute | solution.py:574
  579.6 13.1 %collective-permute-done.38 = bf16[128,2048]{1,0:T(8,128)(2,1)S(1)} collective-permute-done((bf16[128,2048]{1,0:T(8,128)(2,1)}, bf16[128,2048]{1,0:T(8,128)(2,1)S(1)}, u32[]{:S(2)}, u32[]{:S(2)}) %collective-permute-start.38) | collective-permute-done | bytes 524320 | tf_op jit(solution)/shard_map/ppermute | solution.py:558
  595.3 5.8 down.3
  601.2 8.7 collective-permute-done.39
  623.1 8.9 attend_back.4
  640.8 8.4 attend_back.5
  649.2 14.2 %collective-permute-done.43 = bf16[128,2048]{1,0:T(8,128)(2,1)S(1)} collective-permute-done((bf16[128,2048]{1,0:T(8,128)(2,1)S(1)}, bf16[128,2048]{1,0:T(8,128)(2,1)S(1)}, u32[]{:S(2)}, u32[]{:S(2)}) %collective-permute-start.43) | collective-permute-done | bytes 524320 | tf_op jit(solution)/shard_map/ppermute | solution.py:574
  681.1 6.4 project_in.2.refs_0_
  692.8 9.6 collective-permute-done.47
  705.9 7.9 collective-permute-done.49.refs_2_
  714.5 15.8 %collective-permute-done.48.refs_1_ = bf16[128,2048]{1,0:T(8,128)(2,1)} collective-permute-done((bf16[128,2048]{1,0:T(8,128)(2,1)}, bf16[128,2048]{1,0:T(8,128)(2,1)}, u32[]{:S(2)}, u32[]{:S(2)}) %collective-permute-start.48) | collective-permute-done | bytes 524320 | tf_op jit(solution)/shard_map/ppermute | solution.py:574
  751.2 12.9 %collective-permute-done.52 = bf16[128,2048]{1,0:T(8,128)(2,1)S(1)} collective-permute-done((bf16[128,2048]{1,0:T(8,128)(2,1)S(1)}, bf16[128,2048]{1,0:T(8,128)(2,1)S(1)}, u32[]{:S(2)}, u32[]{:S(2)}) %collective-permute-start.52) | collective-permute-done | bytes 524320 | tf_op jit(solution)/shard_map/ppermute | solution.py:558
  765.3 6.8 collective-permute-done.54
  772.2 9.4 collective-permute-done.53
  793.1 7.3 gate_up_back.3
  800.4 10.3 gate_up_in.3.refs_0_
  819.5 6.8 collective-permute-done.57
  829.4 8.3 collective-permute-done.59.refs_2_
  837.7 20.0 %collective-permute-done.62.refs_1_ = bf16[512,512]{1,0:T(8,128)(2,1)} collective-permute-done((bf16[512,512]{1,0:T(8,128)(2,1)S(1)}, bf16[512,512]{1,0:T(8,128)(2,1)}, u32[]{:S(2)}, u32[]{:S(2)}) %collective-permute-start.62) | collective-permute-done | bytes 524320 | tf_op jit(solution)/shard_map/ppermute | solution.py:534
  876.1 16.4 %collective-permute-done.63 = bf16[128,2048]{1,0:T(8,128)(2,1)S(1)} collective-permute-done((bf16[128,2048]{1,0:T(8,128)(2,1)S(1)}, bf16[128,2048]{1,0:T(8,128)(2,1)S(1)}, u32[]{:S(2)}, u32[]{:S(2)}) %collective-permute-start.63) | collective-permute-done | bytes 524320 | tf_op jit(solution)/shard_map/ppermute | solution.py:558
  894.6 13.5 %collective-permute-done.64 = bf16[128,2048]{1,0:T(8,128)(2,1)S(1)} collective-permute-done((bf16[128,2048]{1,0:T(8,128)(2,1)S(1)}, bf16[128,2048]{1,0:T(8,128)(2,1)S(1)}, u32[]{:S(2)}, u32[]{:S(2)}) %collective-permute-start.64) | collective-permute-done | bytes 524320 | tf_op jit(solution)/shard_map/ppermute | solution.py:558
  915.9 9.9 attend_back.6
  937.3 30.8 %collective-permute-done.68.refs_1_ = bf16[1408,512]{1,0:T(8,128)(2,1)} collective-permute-done((bf16[1408,512]{1,0:T(8,128)(2,1)}, bf16[1408,512]{1,0:T(8,128)(2,1)}, u32[]{:S(2)}, u32[]{:S(2)}) %collective-permute-start.68) | collective-permute-done | bytes 1441824 | tf_op jit(solution)/shard_map/ppermute | solution.py:534
  968.1 9.2 attend_back.7
  977.4 11.2 collective-permute-done.69.refs_0_
  1002.7 6.0 project_in.3.refs_0_
  1036.3 20.5 %collective-permute-done.73.refs_1_ = bf16[128,2048]{1,0:T(8,128)(2,1)S(1)} collective-permute-done((bf16[128,2048]{1,0:T(8,128)(2,1)}, bf16[128,2048]{1,0:T(8,128)(2,1)S(1)}, u32[]{:S(2)}, u32[]{:S(2)}) %collective-permute-start.73) | collective-permute-done | bytes 524320 | tf_op jit(solution)/shard_map/ppermute | solution.py:574
  1074.2 9.2 finish_gate_up.2.refs_4_
  1093.8 9.4 finish_gate_up.3
  1111.8 6.9 collective-permute-done.86.refs_1_
  (604 shorter events, 420.3 us)
Async XLA Ops:
  7.2 56.4 %all-gather.22.cloned.1.call-start = ((), (), s32[]{:S(2)}) async-start(), calls=%async_computation.17 | async-start | bytes 7864320 | tf_op jit(solution)/shard_map/all_gather | solution.py:616
  10.0 108.6 %all-gather.20.cloned.1.call-start = ((), (), s32[]{:S(2)}) async-start(), calls=%async_computation.8 | async-start | bytes 2621440 | tf_op jit(solution)/shard_map/all_gather | solution.py:616
  10.9 156.7 %all-gather.24.cloned.1.call-start = ((), (), s32[]{:S(2)}) async-start(), calls=%async_computation.18 | async-start | bytes 7208960 | tf_op jit(solution)/shard_map/all_gather | solution.py:616
  16.1 198.6 %all-gather.26.cloned.1.call-start = ((), (), s32[]{:S(2)}) async-start(), calls=%async_computation.19 | async-start | bytes 7208960 | tf_op jit(solution)/shard_map/all_gather | solution.py:616
  16.7 203.2 %all-gather.28.cloned.1.call-start = ((), (), s32[]{:S(2)}) async-start(), calls=%async_computation.20 | async-start | bytes 7208960 | tf_op jit(solution)/shard_map/all_gather | solution.py:616
  19.6 28.2 %collective-permute-start = (bf16[128,2048]{1,0:T(8,128)(2,1)S(1)}, bf16[128,2048]{1,0:T(8,128)(2,1)}, u32[]{:S(2)}, u32[]{:S(2)}) collective-permute-start(bf16[128,2048]{1,0:T(8,128)(2,1)S(1)} %get-tuple-element.412), channel_id=1, source_target_pairs={{0,2},{2,0},{1,3},{3,1},{4,6},{6,4},{5,7},{7,5},{8,10},{10,8},{9,1... | collective-permute-start | bytes 1572872 | tf_op jit(solution)/shard_map/ppermute | solution.py:558
  23.7 28.1 %collective-permute-start.2 = (bf16[128,2048]{1,0:T(8,128)(2,1)S(1)}, bf16[128,2048]{1,0:T(8,128)(2,1)S(1)}, u32[]{:S(2)}, u32[]{:S(2)}) collective-permute-start(bf16[128,2048]{1,0:T(8,128)(2,1)S(1)} %get-tuple-element.412), channel_id=1, source_target_pairs={{1,0},{2,1},{3,2},{5,4},{6,5},{7,6},{9,8},{10,9},{11,10},{13,12},{... | collective-permute-start | bytes 1572872 | tf_op jit(solution)/shard_map/ppermute | solution.py:558
  24.9 26.8 %collective-permute-start.3 = (bf16[128,2048]{1,0:T(8,128)(2,1)S(1)}, bf16[128,2048]{1,0:T(8,128)(2,1)S(1)}, u32[]{:S(2)}, u32[]{:S(2)}) collective-permute-start(bf16[128,2048]{1,0:T(8,128)(2,1)S(1)} %get-tuple-element.412), channel_id=1, source_target_pairs={{0,1},{1,2},{2,3},{4,5},{5,6},{6,7},{8,9},{9,10},{10,11},{12,13},{... | collective-permute-start | bytes 1572872 | tf_op jit(solution)/shard_map/ppermute | solution.py:558
  71.9 33.8 %collective-permute-start.4 = (bf16[1024,512]{1,0:T(8,128)(2,1)}, bf16[1024,512]{1,0:T(8,128)(2,1)}, u32[]{:S(2)}, u32[]{:S(2)}) collective-permute-start(bf16[1024,512]{1,0:T(8,128)(2,1)} %get-tuple-element.187.refs_0_.refs_1_.refs_2_), channel_id=1, source_target_pairs={{0,4},{1,5},{2,6},{3,7},{8,12},{9,13},{10,14},{11,15},{16,20},{17,... | collective-permute-start | bytes 3145736 | tf_op jit(solution)/shard_map/ppermute | solution.py:602
  76.0 211.0 %all-gather.30.cloned.1.call-start = ((), (), s32[]{:S(2)}) async-start(), calls=%async_computation.21 | async-start | bytes 7864320 | tf_op jit(solution)/shard_map/all_gather | solution.py:616
  77.0 27.2 %collective-permute-start.5 = (bf16[128,2048]{1,0:T(8,128)(2,1)}, bf16[128,2048]{1,0:T(8,128)(2,1)}, u32[]{:S(2)}, u32[]{:S(2)}) collective-permute-start(bf16[128,2048]{1,0:T(8,128)(2,1)} %bitcast.108), channel_id=1, source_target_pairs={{0,2},{2,0},{1,3},{3,1},{4,6},{6,4},{5,7},{7,5},{8,10},{10,8},{9,1... | collective-permute-start | bytes 1572872 | tf_op jit(solution)/shard_map/ppermute | solution.py:558
  79.7 38.9 %collective-permute-start.7 = (bf16[128,2048]{1,0:T(8,128)(2,1)}, bf16[128,2048]{1,0:T(8,128)(2,1)}, u32[]{:S(2)}, u32[]{:S(2)}) collective-permute-start(bf16[128,2048]{1,0:T(8,128)(2,1)} %bitcast.109), channel_id=1, source_target_pairs={{1,0},{2,1},{3,2},{5,4},{6,5},{7,6},{9,8},{10,9},{11,10},{13,12},{... | collective-permute-start | bytes 1572872 | tf_op jit(solution)/shard_map/ppermute | solution.py:558
  81.0 37.6 %collective-permute-start.8 = (bf16[128,2048]{1,0:T(8,128)(2,1)}, bf16[128,2048]{1,0:T(8,128)(2,1)}, u32[]{:S(2)}, u32[]{:S(2)}) collective-permute-start(bf16[128,2048]{1,0:T(8,128)(2,1)} %bitcast.110), channel_id=1, source_target_pairs={{0,1},{1,2},{2,3},{4,5},{5,6},{6,7},{8,9},{9,10},{10,11},{12,13},{... | collective-permute-start | bytes 1572872 | tf_op jit(solution)/shard_map/ppermute | solution.py:558
  173.8 25.4 %collective-permute-start.13 = (bf16[128,2048]{1,0:T(8,128)(2,1)}, bf16[128,2048]{1,0:T(8,128)(2,1)}, u32[]{:S(2)}, u32[]{:S(2)}) collective-permute-start(bf16[128,2048]{1,0:T(8,128)(2,1)} %get-tuple-element.373), channel_id=1, source_target_pairs={{0,2},{2,0},{1,3},{3,1},{4,6},{6,4},{5,7},{7,5},{8,10},{10,8},{9,1... | collective-permute-start | bytes 1572872 | tf_op jit(solution)/shard_map/ppermute | solution.py:558
  173.8 28.0 %collective-permute-start.15 = (bf16[128,2048]{1,0:T(8,128)(2,1)}, bf16[128,2048]{1,0:T(8,128)(2,1)}, u32[]{:S(2)}, u32[]{:S(2)}) collective-permute-start(bf16[128,2048]{1,0:T(8,128)(2,1)} %get-tuple-element.373), channel_id=1, source_target_pairs={{1,0},{2,1},{3,2},{5,4},{6,5},{7,6},{9,8},{10,9},{11,10},{13,12},{... | collective-permute-start | bytes 1572872 | tf_op jit(solution)/shard_map/ppermute | solution.py:558
  175.1 26.7 %collective-permute-start.16 = (bf16[128,2048]{1,0:T(8,128)(2,1)}, bf16[128,2048]{1,0:T(8,128)(2,1)}, u32[]{:S(2)}, u32[]{:S(2)}) collective-permute-start(bf16[128,2048]{1,0:T(8,128)(2,1)} %get-tuple-element.373), channel_id=1, source_target_pairs={{0,1},{1,2},{2,3},{4,5},{5,6},{6,7},{8,9},{9,10},{10,11},{12,13},{... | collective-permute-start | bytes 1572872 | tf_op jit(solution)/shard_map/ppermute | solution.py:558
  219.9 116.2 %all-gather.32.cloned.1.call-start = ((), (), s32[]{:S(2)}) async-start(), calls=%async_computation.22 | async-start | bytes 2621440 | tf_op jit(solution)/shard_map/all_gather | solution.py:616
  235.8 102.3 %all-gather.34.cloned.1.call-start = ((), (), s32[]{:S(2)}) async-start(), calls=%async_computation.23 | async-start | bytes 7208960 | tf_op jit(solution)/shard_map/all_gather | solution.py:616
  236.5 148.6 %all-gather.36.cloned.1.call-start = ((), (), s32[]{:S(2)}) async-start(), calls=%async_computation.24 | async-start | bytes 7208960 | tf_op jit(solution)/shard_map/all_gather | solution.py:616
  259.9 25.8 %collective-permute-start.18 = (bf16[128,2048]{1,0:T(8,128)(2,1)S(1)}, bf16[128,2048]{1,0:T(8,128)(2,1)S(1)}, u32[]{:S(2)}, u32[]{:S(2)}) collective-permute-start(bf16[128,2048]{1,0:T(8,128)(2,1)S(1)} %add_convert_fusion.9), channel_id=1, source_target_pairs={{0,2},{2,0},{1,3},{3,1},{4,6},{6,4},{5,7},{7,5},{8,10},{10,8},{9,1... | collective-permute-start | bytes 1572872 | tf_op jit(solution)/shard_map/ppermute | solution.py:574
  287.0 143.1 %all-gather.38.cloned.1.call-start = ((), (), s32[]{:S(2)}) async-start(), calls=%async_computation.25 | async-start | bytes 7208960 | tf_op jit(solution)/shard_map/all_gather | solution.py:616
  293.3 27.3 %collective-permute-start.21 = (bf16[128,2048]{1,0:T(8,128)(2,1)}, bf16[128,2048]{1,0:T(8,128)(2,1)}, u32[]{:S(2)}, u32[]{:S(2)}) collective-permute-start(bf16[128,2048]{1,0:T(8,128)(2,1)} %get-tuple-element.371), channel_id=1, source_target_pairs={{0,2},{2,0},{1,3},{3,1},{4,6},{6,4},{5,7},{7,5},{8,10},{10,8},{9,1... | collective-permute-start | bytes 1572872 | tf_op jit(solution)/shard_map/ppermute | solution.py:558
  293.3 30.3 %collective-permute-start.23 = (bf16[128,2048]{1,0:T(8,128)(2,1)}, bf16[128,2048]{1,0:T(8,128)(2,1)}, u32[]{:S(2)}, u32[]{:S(2)}) collective-permute-start(bf16[128,2048]{1,0:T(8,128)(2,1)} %get-tuple-element.371), channel_id=1, source_target_pairs={{1,0},{2,1},{3,2},{5,4},{6,5},{7,6},{9,8},{10,9},{11,10},{13,12},{... | collective-permute-start | bytes 1572872 | tf_op jit(solution)/shard_map/ppermute | solution.py:558
  294.6 29.0 %collective-permute-start.24 = (bf16[128,2048]{1,0:T(8,128)(2,1)}, bf16[128,2048]{1,0:T(8,128)(2,1)}, u32[]{:S(2)}, u32[]{:S(2)}) collective-permute-start(bf16[128,2048]{1,0:T(8,128)(2,1)} %get-tuple-element.371), channel_id=1, source_target_pairs={{0,1},{1,2},{2,3},{4,5},{5,6},{6,7},{8,9},{9,10},{10,11},{12,13},{... | collective-permute-start | bytes 1572872 | tf_op jit(solution)/shard_map/ppermute | solution.py:558
  338.1 341.6 %reduce-scatter.9.cloned.1.call-start = ((), (), s32[]{:S(2)}) async-start(), calls=%async_computation.9 | async-start | bytes 7208960 | tf_op jit(solution)/shard_map/reduce_scatter | solution.py:620
  347.0 26.2 %collective-permute-start.25 = (bf16[1024,512]{1,0:T(8,128)(2,1)S(1)}, bf16[1024,512]{1,0:T(8,128)(2,1)S(1)}, u32[]{:S(2)}, u32[]{:S(2)}) collective-permute-start(bf16[1024,512]{1,0:T(8,128)(2,1)S(1)} %get-tuple-element.217.refs_0_.refs_1_.refs_2_), channel_id=1, source_target_pairs={{0,4},{1,5},{2,6},{3,7},{8,12},{9,13},{10,14},{11,15},{16,20},{17,... | collective-permute-start | bytes 3145736 | tf_op jit(solution)/shard_map/ppermute | solution.py:602
  392.2 24.6 %collective-permute-start.29 = (bf16[128,2048]{1,0:T(8,128)(2,1)S(1)}, bf16[128,2048]{1,0:T(8,128)(2,1)S(1)}, u32[]{:S(2)}, u32[]{:S(2)}) collective-permute-start(bf16[128,2048]{1,0:T(8,128)(2,1)S(1)} %get-tuple-element.404), channel_id=1, source_target_pairs={{3,2},{2,1},{1,0},{7,6},{6,5},{5,4},{11,10},{10,9},{9,8},{15,14},{... | collective-permute-start | bytes 1572872 | tf_op jit(solution)/shard_map/ppermute | solution.py:574
  404.7 24.0 %collective-permute-start.27 = (bf16[128,2048]{1,0:T(8,128)(2,1)S(1)}, bf16[128,2048]{1,0:T(8,128)(2,1)S(1)}, u32[]{:S(2)}, u32[]{:S(2)}) collective-permute-start(bf16[128,2048]{1,0:T(8,128)(2,1)S(1)} %add_convert_fusion.7), channel_id=1, source_target_pairs={{0,2},{2,0},{1,3},{3,1},{4,6},{6,4},{5,7},{7,5},{8,10},{10,8},{9,1... | collective-permute-start | bytes 1572872 | tf_op jit(solution)/shard_map/ppermute | solution.py:574
  435.5 26.9 %collective-permute-start.30 = (bf16[128,2048]{1,0:T(8,128)(2,1)S(1)}, bf16[128,2048]{1,0:T(8,128)(2,1)S(1)}, u32[]{:S(2)}, u32[]{:S(2)}) collective-permute-start(bf16[128,2048]{1,0:T(8,128)(2,1)S(1)} %get-tuple-element.369), channel_id=1, source_target_pairs={{0,2},{2,0},{1,3},{3,1},{4,6},{6,4},{5,7},{7,5},{8,10},{10,8},{9,1... | collective-permute-start | bytes 1572872 | tf_op jit(solution)/shard_map/ppermute | solution.py:558
  436.2 27.6 %collective-permute-start.32 = (bf16[128,2048]{1,0:T(8,128)(2,1)S(1)}, bf16[128,2048]{1,0:T(8,128)(2,1)S(1)}, u32[]{:S(2)}, u32[]{:S(2)}) collective-permute-start(bf16[128,2048]{1,0:T(8,128)(2,1)S(1)} %get-tuple-element.369), channel_id=1, source_target_pairs={{1,0},{2,1},{3,2},{5,4},{6,5},{7,6},{9,8},{10,9},{11,10},{13,12},{... | collective-permute-start | bytes 1572872 | tf_op jit(solution)/shard_map/ppermute | solution.py:558
  437.5 26.4 %collective-permute-start.33 = (bf16[128,2048]{1,0:T(8,128)(2,1)S(1)}, bf16[128,2048]{1,0:T(8,128)(2,1)S(1)}, u32[]{:S(2)}, u32[]{:S(2)}) collective-permute-start(bf16[128,2048]{1,0:T(8,128)(2,1)S(1)} %get-tuple-element.369), channel_id=1, source_target_pairs={{0,1},{1,2},{2,3},{4,5},{5,6},{6,7},{8,9},{9,10},{10,11},{12,13},{... | collective-permute-start | bytes 1572872 | tf_op jit(solution)/shard_map/ppermute | solution.py:558
  507.2 23.7 %collective-permute-start.36 = (bf16[128,2048]{1,0:T(8,128)(2,1)}, bf16[128,2048]{1,0:T(8,128)(2,1)}, u32[]{:S(2)}, u32[]{:S(2)}) collective-permute-start(bf16[128,2048]{1,0:T(8,128)(2,1)} %get-tuple-element.401), channel_id=1, source_target_pairs={{0,1},{1,2},{2,3},{4,5},{5,6},{6,7},{8,9},{9,10},{10,11},{12,13},{... | collective-permute-start | bytes 1572872 | tf_op jit(solution)/shard_map/ppermute | solution.py:574
  520.5 30.9 %collective-permute-start.35 = (bf16[128,2048]{1,0:T(8,128)(2,1)}, bf16[128,2048]{1,0:T(8,128)(2,1)}, u32[]{:S(2)}, u32[]{:S(2)}) collective-permute-start(bf16[128,2048]{1,0:T(8,128)(2,1)} %add_convert_fusion.5), channel_id=1, source_target_pairs={{0,2},{2,0},{1,3},{3,1},{4,6},{6,4},{5,7},{7,5},{8,10},{10,8},{9,1... | collective-permute-start | bytes 1572872 | tf_op jit(solution)/shard_map/ppermute | solution.py:574
  563.7 179.7 %reduce-scatter.11.cloned.1.call-start = ((), (), s32[]{:S(2)}) async-start(), calls=%async_computation.10 | async-start | bytes 7208960 | tf_op jit(solution)/shard_map/reduce_scatter | solution.py:620
  572.4 210.8 %reduce-scatter.15.cloned.1.call-start = ((), (), s32[]{:S(2)}) async-start(), calls=%async_computation.12 | async-start | bytes 2621440 | tf_op jit(solution)/shard_map/reduce_scatter | solution.py:620
  573.7 27.5 %collective-permute-start.40 = (bf16[128,2048]{1,0:T(8,128)(2,1)}, bf16[128,2048]{1,0:T(8,128)(2,1)S(1)}, u32[]{:S(2)}, u32[]{:S(2)}) collective-permute-start(bf16[128,2048]{1,0:T(8,128)(2,1)} %copy-done.39), channel_id=1, source_target_pairs={{1,0},{2,1},{3,2},{5,4},{6,5},{7,6},{9,8},{10,9},{11,10},{13,12},{... | collective-permute-start | bytes 1572872 | tf_op jit(solution)/shard_map/ppermute | solution.py:558
  575.0 26.2 %collective-permute-start.41 = (bf16[128,2048]{1,0:T(8,128)(2,1)}, bf16[128,2048]{1,0:T(8,128)(2,1)S(1)}, u32[]{:S(2)}, u32[]{:S(2)}) collective-permute-start(bf16[128,2048]{1,0:T(8,128)(2,1)} %copy-done.39), channel_id=1, source_target_pairs={{0,1},{1,2},{2,3},{4,5},{5,6},{6,7},{8,9},{9,10},{10,11},{12,13},{... | collective-permute-start | bytes 1572872 | tf_op jit(solution)/shard_map/ppermute | solution.py:558
  611.4 37.8 %collective-permute-start.45 = (bf16[128,2048]{1,0:T(8,128)(2,1)}, bf16[128,2048]{1,0:T(8,128)(2,1)S(1)}, u32[]{:S(2)}, u32[]{:S(2)}) collective-permute-start(bf16[128,2048]{1,0:T(8,128)(2,1)} %get-tuple-element.398), channel_id=1, source_target_pairs={{3,2},{2,1},{1,0},{7,6},{6,5},{5,4},{11,10},{10,9},{9,8},{15,14},{... | collective-permute-start | bytes 1572872 | tf_op jit(solution)/shard_map/ppermute | solution.py:574
  612.8 36.4 %collective-permute-start.44 = (bf16[128,2048]{1,0:T(8,128)(2,1)}, bf16[128,2048]{1,0:T(8,128)(2,1)}, u32[]{:S(2)}, u32[]{:S(2)}) collective-permute-start(bf16[128,2048]{1,0:T(8,128)(2,1)} %get-tuple-element.397), channel_id=1, source_target_pairs={{0,1},{1,2},{2,3},{4,5},{5,6},{6,7},{8,9},{9,10},{10,11},{12,13},{... | collective-permute-start | bytes 1572872 | tf_op jit(solution)/shard_map/ppermute | solution.py:574
  632.0 33.6 %collective-permute-start.46 = (bf16[1024,512]{1,0:T(8,128)(2,1)S(1)}, bf16[1024,512]{1,0:T(8,128)(2,1)S(1)}, u32[]{:S(2)}, u32[]{:S(2)}) collective-permute-start(bf16[1024,512]{1,0:T(8,128)(2,1)S(1)} %get-tuple-element.245), channel_id=1, source_target_pairs={{4,0},{5,1},{6,2},{7,3},{12,8},{13,9},{14,10},{15,11},{20,16},{21,... | collective-permute-start | bytes 3145736 | tf_op jit(solution)/shard_map/ppermute | solution.py:609
  671.2 112.0 %reduce-scatter.13.cloned.1.call-start = ((), (), s32[]{:S(2)}) async-start(), calls=%async_computation.11 | async-start | bytes 7208960 | tf_op jit(solution)/shard_map/reduce_scatter | solution.py:620
  679.6 178.0 %reduce-scatter.17.cloned.1.call-start = ((), (), s32[]{:S(2)}) async-start(), calls=%async_computation.13 | async-start | bytes 7864320 | tf_op jit(solution)/shard_map/reduce_scatter | solution.py:620
  690.1 40.3 %collective-permute-start.51 = (bf16[1408,512]{1,0:T(8,128)(2,1)}, bf16[1408,512]{1,0:T(8,128)(2,1)}, u32[]{:S(2)}, u32[]{:S(2)}) collective-permute-start(bf16[1408,512]{1,0:T(8,128)(2,1)} %reduce-scatter.9.cloned.1.call-done.refs_0_), channel_id=1, source_target_pairs={{0,4},{4,0},{1,5},{5,1},{2,6},{6,2},{3,7},{7,3},{8,12},{12,8},{9,1... | collective-permute-start | bytes 4325384 | tf_op jit(solution)/shard_map/ppermute | solution.py:534
  690.2 23.6 %collective-permute-start.49 = (bf16[128,2048]{1,0:T(8,128)(2,1)}, bf16[128,2048]{1,0:T(8,128)(2,1)S(1)}, u32[]{:S(2)}, u32[]{:S(2)}) collective-permute-start(bf16[128,2048]{1,0:T(8,128)(2,1)} %get-tuple-element.395), channel_id=1, source_target_pairs={{0,1},{1,2},{2,3},{4,5},{5,6},{6,7},{8,9},{9,10},{10,11},{12,13},{... | collective-permute-start | bytes 1572872 | tf_op jit(solution)/shard_map/ppermute | solution.py:574
  703.3 27.0 %collective-permute-start.48 = (bf16[128,2048]{1,0:T(8,128)(2,1)}, bf16[128,2048]{1,0:T(8,128)(2,1)}, u32[]{:S(2)}, u32[]{:S(2)}) collective-permute-start(bf16[128,2048]{1,0:T(8,128)(2,1)} %add_convert_fusion.2), channel_id=1, source_target_pairs={{0,2},{2,0},{1,3},{3,1},{4,6},{6,4},{5,7},{7,5},{8,10},{10,8},{9,1... | collective-permute-start | bytes 1572872 | tf_op jit(solution)/shard_map/ppermute | solution.py:574
  743.3 167.7 %reduce-scatter.19.cloned.1.call-start = ((), (), s32[]{:S(2)}) async-start(), calls=%async_computation.14 | async-start | bytes 7208960 | tf_op jit(solution)/shard_map/reduce_scatter | solution.py:620
  743.4 39.8 %collective-permute-start.56 = (bf16[512,1408]{1,0:T(8,128)(2,1)}, bf16[512,1408]{1,0:T(8,128)(2,1)}, u32[]{:S(2)}, u32[]{:S(2)}) collective-permute-start(bf16[512,1408]{1,0:T(8,128)(2,1)} %reduce-scatter.11.cloned.1.call-done.refs_0_), channel_id=1, source_target_pairs={{0,4},{4,0},{1,5},{5,1},{2,6},{6,2},{3,7},{7,3},{8,12},{12,8},{9,1... | collective-permute-start | bytes 4325384 | tf_op jit(solution)/shard_map/ppermute | solution.py:534
  745.1 27.0 %collective-permute-start.54 = (bf16[128,2048]{1,0:T(8,128)(2,1)S(1)}, bf16[128,2048]{1,0:T(8,128)(2,1)S(1)}, u32[]{:S(2)}, u32[]{:S(2)}) collective-permute-start(bf16[128,2048]{1,0:T(8,128)(2,1)S(1)} %get-tuple-element.262), channel_id=1, source_target_pairs={{1,0},{2,1},{3,2},{5,4},{6,5},{7,6},{9,8},{10,9},{11,10},{13,12},{... | collective-permute-start | bytes 1572872 | tf_op jit(solution)/shard_map/ppermute | solution.py:558
  746.4 25.8 %collective-permute-start.55 = (bf16[128,2048]{1,0:T(8,128)(2,1)S(1)}, bf16[128,2048]{1,0:T(8,128)(2,1)S(1)}, u32[]{:S(2)}, u32[]{:S(2)}) collective-permute-start(bf16[128,2048]{1,0:T(8,128)(2,1)S(1)} %get-tuple-element.262), channel_id=1, source_target_pairs={{0,1},{1,2},{2,3},{4,5},{5,6},{6,7},{8,9},{9,10},{10,11},{12,13},{... | collective-permute-start | bytes 1572872 | tf_op jit(solution)/shard_map/ppermute | solution.py:558
  791.4 206.1 %reduce-scatter.21.cloned.1.call-start = ((), (), s32[]{:S(2)}) async-start(), calls=%async_computation.15 | async-start | bytes 7208960 | tf_op jit(solution)/shard_map/reduce_scatter | solution.py:620
  814.0 43.7 %collective-permute-start.61 = (bf16[512,1408]{1,0:T(8,128)(2,1)}, bf16[512,1408]{1,0:T(8,128)(2,1)}, u32[]{:S(2)}, u32[]{:S(2)}) collective-permute-start(bf16[512,1408]{1,0:T(8,128)(2,1)} %reduce-scatter.13.cloned.1.call-done.refs_2_), channel_id=1, source_target_pairs={{0,4},{4,0},{1,5},{5,1},{2,6},{6,2},{3,7},{7,3},{8,12},{12,8},{9,1... | collective-permute-start | bytes 4325384 | tf_op jit(solution)/shard_map/ppermute | solution.py:534
  818.0 39.7 %collective-permute-start.62 = (bf16[512,512]{1,0:T(8,128)(2,1)S(1)}, bf16[512,512]{1,0:T(8,128)(2,1)}, u32[]{:S(2)}, u32[]{:S(2)}) collective-permute-start(bf16[512,512]{1,0:T(8,128)(2,1)S(1)} %copy-done.66), channel_id=1, source_target_pairs={{0,4},{4,0},{1,5},{5,1},{2,6},{6,2},{3,7},{7,3},{8,12},{12,8},{9,1... | collective-permute-start | bytes 1572872 | tf_op jit(solution)/shard_map/ppermute | solution.py:534
  827.3 30.4 %collective-permute-start.58 = (bf16[128,2048]{1,0:T(8,128)(2,1)}, bf16[128,2048]{1,0:T(8,128)(2,1)}, u32[]{:S(2)}, u32[]{:S(2)}) collective-permute-start(bf16[128,2048]{1,0:T(8,128)(2,1)} %add_convert_fusion.1), channel_id=1, source_target_pairs={{0,2},{2,0},{1,3},{3,1},{4,6},{6,4},{5,7},{7,5},{8,10},{10,8},{9,1... | collective-permute-start | bytes 1572872 | tf_op jit(solution)/shard_map/ppermute | solution.py:574
  869.3 139.5 %reduce-scatter.23.cloned.1.call-start = ((), (), s32[]{:S(2)}) async-start(), calls=%async_computation.16 | async-start | bytes 7208960 | tf_op jit(solution)/shard_map/reduce_scatter | solution.py:620
  869.4 40.4 %collective-permute-start.67 = (bf16[512,1536]{1,0:T(8,128)(2,1)}, bf16[512,1536]{1,0:T(8,128)(2,1)S(1)}, u32[]{:S(2)}, u32[]{:S(2)}) collective-permute-start(bf16[512,1536]{1,0:T(8,128)(2,1)} %reduce-scatter.17.cloned.1.call-done.refs_0_), channel_id=1, source_target_pairs={{0,4},{4,0},{1,5},{5,1},{2,6},{6,2},{3,7},{7,3},{8,12},{12,8},{9,1... | collective-permute-start | bytes 4718600 | tf_op jit(solution)/shard_map/ppermute | solution.py:534
  870.2 24.4 %collective-permute-start.65 = (bf16[128,2048]{1,0:T(8,128)(2,1)S(1)}, bf16[128,2048]{1,0:T(8,128)(2,1)S(1)}, u32[]{:S(2)}, u32[]{:S(2)}) collective-permute-start(bf16[128,2048]{1,0:T(8,128)(2,1)S(1)} %get-tuple-element.283), channel_id=1, source_target_pairs={{1,0},{2,1},{3,2},{5,4},{6,5},{7,6},{9,8},{10,9},{11,10},{13,12},{... | collective-permute-start | bytes 1572872 | tf_op jit(solution)/shard_map/ppermute | solution.py:558
  933.2 34.9 %collective-permute-start.68 = (bf16[1408,512]{1,0:T(8,128)(2,1)}, bf16[1408,512]{1,0:T(8,128)(2,1)}, u32[]{:S(2)}, u32[]{:S(2)}) collective-permute-start(bf16[1408,512]{1,0:T(8,128)(2,1)} %reduce-scatter.19.cloned.1.call-done.refs_0_), channel_id=1, source_target_pairs={{0,4},{4,0},{1,5},{5,1},{2,6},{6,2},{3,7},{7,3},{8,12},{12,8},{9,1... | collective-permute-start | bytes 4325384 | tf_op jit(solution)/shard_map/ppermute | solution.py:534
  935.5 53.0 %collective-permute-start.69 = (bf16[1024,512]{1,0:T(8,128)(2,1)S(1)}, bf16[1024,512]{1,0:T(8,128)(2,1)S(1)}, u32[]{:S(2)}, u32[]{:S(2)}) collective-permute-start(bf16[1024,512]{1,0:T(8,128)(2,1)S(1)} %copy-done.65), channel_id=1, source_target_pairs={{4,0},{5,1},{6,2},{7,3},{12,8},{13,9},{14,10},{15,11},{20,16},{21,... | collective-permute-start | bytes 3145736 | tf_op jit(solution)/shard_map/ppermute | solution.py:609
  1002.7 33.2 %collective-permute-start.76 = (bf16[512,1408]{1,0:T(8,128)(2,1)}, bf16[512,1408]{1,0:T(8,128)(2,1)}, u32[]{:S(2)}, u32[]{:S(2)}) collective-permute-start(bf16[512,1408]{1,0:T(8,128)(2,1)} %reduce-scatter.21.cloned.1.call-done.refs_0_), channel_id=1, source_target_pairs={{0,4},{4,0},{1,5},{5,1},{2,6},{6,2},{3,7},{7,3},{8,12},{12,8},{9,1... | collective-permute-start | bytes 4325384 | tf_op jit(solution)/shard_map/ppermute | solution.py:534
  1017.3 39.5 %collective-permute-start.77 = (bf16[512,1536]{1,0:T(8,128)(2,1)}, bf16[512,1536]{1,0:T(8,128)(2,1)}, u32[]{:S(2)}, u32[]{:S(2)}) collective-permute-start(bf16[512,1536]{1,0:T(8,128)(2,1)} %split.30), channel_id=1, source_target_pairs={{0,16},{8,24},{16,0},{24,8},{1,17},{9,25},{17,1},{25,9},{2,18},{10... | collective-permute-start | bytes 4718600 | tf_op jit(solution)/shard_map/ppermute | solution.py:534
  1025.3 31.6 %collective-permute-start.73 = (bf16[128,2048]{1,0:T(8,128)(2,1)}, bf16[128,2048]{1,0:T(8,128)(2,1)S(1)}, u32[]{:S(2)}, u32[]{:S(2)}) collective-permute-start(bf16[128,2048]{1,0:T(8,128)(2,1)} %add_convert_fusion), channel_id=1, source_target_pairs={{0,2},{2,0},{1,3},{3,1},{4,6},{6,4},{5,7},{7,5},{8,10},{10,8},{9,1... | collective-permute-start | bytes 1572872 | tf_op jit(solution)/shard_map/ppermute | solution.py:574
  1035.9 57.9 %collective-permute-start.82 = (bf16[512,1408]{1,0:T(8,128)(2,1)}, bf16[512,1408]{1,0:T(8,128)(2,1)}, u32[]{:S(2)}, u32[]{:S(2)}) collective-permute-start(bf16[512,1408]{1,0:T(8,128)(2,1)} %reduce-scatter.23.cloned.1.call-done.refs_2_), channel_id=1, source_target_pairs={{0,4},{4,0},{1,5},{5,1},{2,6},{6,2},{3,7},{7,3},{8,12},{12,8},{9,1... | collective-permute-start | bytes 4325384 | tf_op jit(solution)/shard_map/ppermute | solution.py:534
  1064.5 55.7 %collective-permute-start.84 = (bf16[512,1536]{1,0:T(8,128)(2,1)}, bf16[512,1536]{1,0:T(8,128)(2,1)}, u32[]{:S(2)}, u32[]{:S(2)}) collective-permute-start(bf16[512,1536]{1,0:T(8,128)(2,1)} %fusion.refs_0_), channel_id=1, source_target_pairs={{0,4},{4,0},{1,5},{5,1},{2,6},{6,2},{3,7},{7,3},{8,12},{12,8},{9,1... | collective-permute-start | bytes 4718600 | tf_op jit(solution)/shard_map/ppermute | solution.py:534
  1067.9 35.7 %collective-permute-start.85 = (bf16[512,512]{1,0:T(8,128)(2,1)S(1)}, bf16[512,512]{1,0:T(8,128)(2,1)S(1)}, u32[]{:S(2)}, u32[]{:S(2)}) collective-permute-start(bf16[512,512]{1,0:T(8,128)(2,1)S(1)} %split.31), channel_id=1, source_target_pairs={{0,16},{8,24},{16,0},{24,8},{1,17},{9,25},{17,1},{25,9},{2,18},{10... | collective-permute-start | bytes 1572872 | tf_op jit(solution)/shard_map/ppermute | solution.py:534
  (171 other events, 2801.7 us)
Sparse Core Ops, SparseCore 0:
  10.2 49.0 all-gather.21
  61.4 22.5 all-gather.19
  86.2 43.3 all-gather.23
  131.6 43.3 all-gather.25
  176.5 43.3 all-gather.27
  221.9 46.3 all-gather.29
  270.5 22.5 all-gather.31
  294.6 43.3 all-gather.33
  339.6 43.3 all-gather.35
  385.1 43.3 all-gather.37
  563.8 52.0 reduce-scatter.8
  619.1 54.8 reduce-scatter.10
  676.5 31.4 reduce-scatter.14
  711.1 54.8 reduce-scatter.12
  768.9 58.3 reduce-scatter.16
  830.4 54.8 reduce-scatter.18
  888.3 54.8 reduce-scatter.20
  946.4 54.8 reduce-scatter.22
